TPU v7x, 32 devices: a whole 2x2x4 slice. The times are simulated.
32 devices in a mesh: tm: 2 (over core), tile: 4 (over y, x), head: 4 (over z).
Axes of the slice: x: 2, y: 2, z: 4, core: 2. Of those that a mesh axis runs over, the one named last changes fastest.
Arguments:
- query: bfloat16 [2, 4, 2, 16, 16, 1536], P('tm', 'tile', None, None, None, 'head'), may hold values from -80 to 80
- keys: bfloat16 [2, 4, 2, 16, 16, 1536], P('tm', 'tile', None, None, None, 'head'), may hold values from -80 to 80
- values: bfloat16 [2, 4, 2, 16, 16, 1536], P('tm', 'tile', None, None, None, 'head'), may hold values from -6 to 6
- out_weight: bfloat16 [1536, 1536], P('head'), may hold values from -0.15625 to 0.15625
- radius: int32 [12], P('head'), may hold values from 1 to 4
- block_mask: int32 [12, 2, 2], P('head'), may hold values from 0 to 1, as said below
Outputs:
- mixed: bfloat16 [2, 4, 512, 1536], P('tm', 'tile', 'head')
Inputs may be any that keep to these rules, and one draw needn't show every extreme that they name: For every head, block_mask is 1 on the diagonal of its table and 0 above it.
All inputs are finite; a program needn't handle non-finite values.
Results may differ from a plain program's by a relative error of at most 0.015.
Values may be sent and summed in bfloat16 or wider, within the bound.
No kernel may reach another device: no remote copies, remote signals or barrier semaphores. Data moves between devices by JAX's collectives and lax.ppermute only.
A program may use at most 128 MiB of HBM per device.

v0:
```python
import functools
import math

import jax
import jax.numpy as jnp
from jax import lax
from jax.experimental import pallas as pl
from jax.experimental.pallas import tpu as pltpu
from jax.sharding import PartitionSpec as P

RMAX = 4
FAR = -1e30
LOG2E = 1.4426950408889634
VMEM_LIMIT = 24 * 1024 * 1024


def passed_along(value, axis, by):
    peers = lax.axis_size(axis)
    pairs = [(i, i + by) for i in range(peers) if 0 <= i + by < peers]
    return lax.ppermute(value, axis, pairs)


def widen(key_part, value_part, span, row_move, col_move):
    grid = math.isqrt(lax.axis_size("tile"))
    above = None
    below = None
    for offset in (grid, -grid):
        if offset > 0:
            face_key = key_part[:, :, key_part.shape[2] - span :]
            face_value = value_part[:, :, value_part.shape[2] - span :]
        else:
            face_key = key_part[:, :, :span]
            face_value = value_part[:, :, :span]
        got = row_move(face_key, face_value, offset)
        if offset > 0:
            above = got
        else:
            below = got
    key_rows = jnp.concatenate([above[0], key_part, below[0]], axis=2)
    value_rows = jnp.concatenate([above[1], value_part, below[1]], axis=2)
    left = None
    right = None
    for offset in (1, -1):
        if offset > 0:
            face_key = key_rows[:, :, :, key_rows.shape[3] - span :]
            face_value = value_rows[:, :, :, value_rows.shape[3] - span :]
        else:
            face_key = key_rows[:, :, :, :span]
            face_value = value_rows[:, :, :, :span]
        got = col_move(face_key, face_value, offset)
        if offset > 0:
            left = got
        else:
            right = got
    key_full = jnp.concatenate([left[0], key_rows, right[0]], axis=3)
    value_full = jnp.concatenate([left[1], value_rows, right[1]], axis=3)
    return (key_full, value_full)


def windows_of(block, half_high, half_wide, win_high, win_wide, heads_here, head_dim):
    parts = []
    for band in (0, 1):
        for strip in (0, 1):
            parts.append(
                block[
                    :,
                    band * half_high : band * half_high + win_high,
                    strip * half_wide : strip * half_wide + win_wide,
                ]
            )
    stacked = jnp.stack(parts)
    return stacked.reshape(4, -1, heads_here, head_dim)


def any_grid(query, keys, values, out_weight, radius, block_mask):
    span = RMAX
    grid = math.isqrt(lax.axis_size("tile"))
    tile_at = lax.axis_index("tile")
    row_at = tile_at // grid
    col_at = tile_at % grid
    stretch_at = lax.axis_index("tm")
    frames, high, wide, channels = query.shape[2:]
    heads_here = radius.shape[0]
    head_dim = channels // heads_here
    tokens_here = frames * high * wide
    half_high = high // 2
    half_wide = wide // 2
    win_high = half_high + 2 * span
    win_wide = half_wide + 2 * span
    quarter = frames * half_high * half_wide
    queries = query[0, 0].reshape(frames, 2, half_high, 2, half_wide, channels)
    queries = queries.transpose(1, 3, 0, 2, 4, 5).reshape(4, quarter, heads_here, head_dim)
    query_y = jnp.broadcast_to(
        jnp.arange(half_high, dtype=jnp.int32)[None, :, None], (frames, half_high, half_wide)
    ).reshape(-1)
    query_x = jnp.broadcast_to(
        jnp.arange(half_wide, dtype=jnp.int32)[None, None, :], (frames, half_high, half_wide)
    ).reshape(-1)
    key_y = jnp.broadcast_to(
        jnp.arange(win_high, dtype=jnp.int32)[None, :, None] - span, (frames, win_high, win_wide)
    ).reshape(-1)
    key_x = jnp.broadcast_to(
        jnp.arange(win_wide, dtype=jnp.int32)[None, None, :] - span, (frames, win_high, win_wide)
    ).reshape(-1)
    band_at = jnp.array([0, 0, 1, 1], dtype=jnp.int32)
    strip_at = jnp.array([0, 1, 0, 1], dtype=jnp.int32)
    global_y = row_at * high + band_at[:, None] * half_high + key_y[None, :]
    global_x = col_at * wide + strip_at[:, None] * half_wide + key_x[None, :]
    inside = (global_y >= 0) & (global_y < grid * high) & (global_x >= 0) & (global_x < grid * wide)
    distance = jnp.maximum(
        jnp.abs(query_y[:, None] - key_y[None, :]), jnp.abs(query_x[:, None] - key_x[None, :])
    )
    near = distance[None, :, :] <= radius[:, None, None]
    allowed = near[None, :, :, :] & inside[:, None, None, :]
    scale = 1.0 / math.sqrt(head_dim)
    initial = (
        jnp.full((4, heads_here, quarter), -1e30, jnp.float32),
        jnp.zeros((4, heads_here, quarter), jnp.float32),
        jnp.zeros((4, heads_here, quarter, head_dim), jnp.float32),
    )

    def tile_move(face_key, face_value, offset):
        return passed_along((face_key, face_value), "tile", offset)

    key_all, value_all = (
        lax.all_gather(keys[0], "tm", axis=0, tiled=True),
        lax.all_gather(values[0], "tm", axis=0, tiled=True),
    )
    key_full, value_full = widen(key_all, value_all, span, tile_move, tile_move)
    stretch_ids = jnp.arange(key_full.shape[0], dtype=jnp.int32)

    def one_stretch(state, item):
        key_block, value_block, stretch_id = item
        visible = (
            lax.dynamic_slice_in_dim(
                lax.dynamic_index_in_dim(block_mask, stretch_at, 1, False), stretch_id, 1, 1
            )[:, 0]
            > 0
        )
        best, total, acc = state
        key_win = windows_of(
            key_block, half_high, half_wide, win_high, win_wide, heads_here, head_dim
        )
        value_win = windows_of(
            value_block, half_high, half_wide, win_high, win_wide, heads_here, head_dim
        )
        usable = allowed & visible[None, :, None, None]
        scores = (
            jnp.einsum("nqhd,nkhd->nhqk", queries, key_win, preferred_element_type=jnp.float32)
            * scale
        )
        masked = jnp.where(usable, scores, jnp.float32(-1e30))
        fresh = jnp.maximum(best, jnp.max(masked, axis=3))
        probs = jnp.where(usable, jnp.exp(scores - fresh[..., None]), jnp.float32(0.0))
        shrink = jnp.exp(best - fresh)
        total = total * shrink + jnp.sum(probs, axis=3)
        acc = acc * shrink[..., None] + jnp.einsum(
            "nhqk,nkhd->nhqd",
            probs.astype(jnp.bfloat16),
            value_win,
            preferred_element_type=jnp.float32,
        )
        return ((fresh, total, acc), None)

    final, unused = lax.scan(one_stretch, initial, (key_full, value_full, stretch_ids))
    best, total, acc = final
    attn = (acc / total[..., None]).astype(jnp.bfloat16)
    attn = attn.transpose(0, 2, 1, 3).reshape(
        2, 2, frames, half_high, half_wide, heads_here * head_dim
    )
    attn = attn.transpose(2, 0, 3, 1, 4, 5).reshape(tokens_here, heads_here * head_dim)
    mixed = lax.psum_scatter(
        jnp.dot(attn, out_weight, preferred_element_type=jnp.float32).astype(jnp.bfloat16),
        "head",
        scatter_dimension=0,
        tiled=True,
    )
    return mixed.reshape(1, 1, -1, out_weight.shape[1])


def tile_place():
    tile_at = lax.axis_index("tile")
    return tile_at // 2, tile_at % 2


def face_kernel(
    k_ref, v_ref, w_ref, row_ref, col_ref, corner_ref, tile_ref, part_ref, sems, *, geometry
):
    high, wide, span, frames = geometry[:4]
    cells = high * wide
    row_at, col_at = tile_place()
    y0 = jnp.where(row_at == 0, high - span, 0)
    x0 = jnp.where(col_at == 0, wide - span, 0)
    tall, broad = part_ref.shape
    top = pl.multiple_of(lax.axis_index("tile") * tall, 16)
    edge = pl.multiple_of(lax.axis_index("tm") * broad, 128)
    copies = [
        pltpu.make_async_copy(ref, tile_ref.at[which], sems.at[which])
        for which, ref in enumerate((k_ref, v_ref))
    ]
    copies.append(
        pltpu.make_async_copy(
            w_ref.at[pl.ds(top, tall), pl.ds(edge, broad)], part_ref, sems.at[2]
        )
    )
    for copy in copies:
        copy.start()

    def picker(count, cell_of):
        row = lax.broadcasted_iota(jnp.int32, (count, cells), 0)
        col = lax.broadcasted_iota(jnp.int32, (count, cells), 1)
        return (col == cell_of(row)).astype(jnp.bfloat16)

    beside = picker(high * span, lambda i: (i // span) * wide + x0 + i % span)
    across = picker(span * span, lambda i: (y0 + i // span) * wide + x0 + i % span)
    for which in range(2):
        copies[which].wait()
        for f in range(frames):
            start = pl.multiple_of(f * cells + y0 * wide, 16)
            row_ref[which, f] = tile_ref[which, pl.ds(start, span * wide)]
            whole = tile_ref[which, f * cells : (f + 1) * cells]
            col_ref[which, f] = jnp.dot(
                beside, whole, preferred_element_type=jnp.float32
            ).astype(jnp.bfloat16)
            corner_ref[which, f] = jnp.dot(
                across, whole, preferred_element_type=jnp.float32
            ).astype(jnp.bfloat16)
    copies[2].wait()


def edge_kernel(row_ref, col_ref, corner_ref, out_ref):
    for which in range(2):
        at = 0
        for part in (row_ref, col_ref, corner_ref):
            for f in range(part.shape[1]):
                size = part.shape[2]
                out_ref[which, at : at + size] = part[which, f]
                at += size


def distances(high, wide, span, frames):
    row_at, col_at = tile_place()
    cells = high * wide
    count = frames * (cells + span * (wide + high + span))
    j = lax.broadcasted_iota(jnp.int32, (1, count), 1)
    y_off = jnp.where(row_at == 0, high, -span)
    x_off = jnp.where(col_at == 0, wide, -span)
    c = j % cells
    ky, kx = c // wide, c % wide
    base = frames * cells
    c = (j - base) % (span * wide)
    ky = jnp.where(j >= base, y_off + c // wide, ky)
    kx = jnp.where(j >= base, c % wide, kx)
    base += frames * span * wide
    c = (j - base) % (span * high)
    ky = jnp.where(j >= base, c // span, ky)
    kx = jnp.where(j >= base, x_off + c % span, kx)
    base += frames * span * high
    c = (j - base) % (span * span)
    ky = jnp.where(j >= base, y_off + c // span, ky)
    kx = jnp.where(j >= base, x_off + c % span, kx)
    i = lax.broadcasted_iota(jnp.int32, (cells, 1), 0)
    return jnp.maximum(jnp.abs(i // wide - ky), jnp.abs(i % wide - kx))


def attend(q, pieces, factor, before):
    scores = []
    m = before
    for k, v, dist, reach in pieces:
        s = lax.dot_general(q, k, (((1,), (1,)), ((), ())), preferred_element_type=jnp.float32)
        s = jnp.where(dist <= reach, s * factor, FAR)
        top = jnp.max(s, axis=1, keepdims=True)
        m = top if m is None else jnp.maximum(m, top)
        scores.append(s)
    total = None
    for s, (k, v, dist, reach) in zip(scores, pieces):
        p = jnp.exp2(s - m).astype(jnp.bfloat16)
        both = jnp.concatenate([v, jnp.ones_like(v)], axis=1)
        got = jnp.dot(p, both, preferred_element_type=jnp.float32)
        total = got if total is None else total + got
    return m, total


def attend_tile(q_ref, tile_ref, dist_ref, reach_of, heads, state, geometry):
    high, wide, span, frames, head_dim, factor, step = geometry
    cells = high * wide
    acc_ref, sum_ref, max_ref = state
    for at, head in enumerate(heads):
        cols = slice(head * head_dim, (head + 1) * head_dim)
        outs = slice(at * head_dim, (at + 1) * head_dim)
        for start in range(0, q_ref.shape[0], step):
            rows = slice(start, start + step)
            near = dist_ref[start % cells : start % cells + step, : tile_ref.shape[1]]
            piece = (tile_ref[0, :, cols], tile_ref[1, :, cols], near, reach_of(head))
            m, got = attend(q_ref[rows, cols], [piece], factor, None)
            acc_ref[rows, outs] = got[:, :head_dim]
            sum_ref[rows, outs] = got[:, head_dim:]
            max_ref[rows, outs] = jnp.broadcast_to(m, (step, head_dim))


def begin_kernel(radius_ref, mask_ref, q_ref, tile_ref, *outs, geometry, heads):
    *state, dist_ref, reach_ref = outs
    high, wide, span, frames = geometry[:4]
    dist_ref[...] = distances(high, wide, span, frames)
    stretch_at = lax.axis_index("tm")
    line = (1, reach_ref.shape[1])
    for head in range(heads):
        radius = radius_ref[head]
        seen = mask_ref[stretch_at, 0, head] > 0
        reach_ref[head : head + 1] = jnp.full(line, radius, jnp.int32)
        reach_ref[heads + head : heads + head + 1] = jnp.full(
            line, jnp.where(seen, radius, -1), jnp.int32
        )
    attend_tile(q_ref, tile_ref, dist_ref, lambda h: radius_ref[h], (0,), state, geometry)


def tile_kernel(q_ref, tile_ref, dist_ref, reach_ref, *state, geometry, heads):
    attend_tile(
        q_ref,
        tile_ref,
        dist_ref,
        lambda h: reach_ref[h : h + 1, :1],
        range(1, heads),
        state,
        geometry,
    )


def pick_state(head_state, state, head, rows, head_dim):
    refs = head_state if head == 0 else state
    at = max(head - 1, 0) * head_dim
    return [ref[rows, at : at + head_dim] for ref in refs]


def merge(q, pieces, factor, old):
    old_acc, old_total, old_max = old
    m, got = attend(q, pieces, factor, old_max[:, :1])
    shrink = jnp.exp2(old_max - m)
    head_dim = old_acc.shape[1]
    acc = old_acc * shrink + got[:, :head_dim]
    total = old_total * shrink + got[:, head_dim:]
    return acc, total, jnp.broadcast_to(m, old_max.shape)


def rest_kernel(
    q_ref,
    edge_ref,
    first_tile_ref,
    first_edge_ref,
    *rest,
    geometry,
    heads,
    flips,
):
    head_state, dist_ref, reach_ref, state, outs = rest[:3], rest[3], rest[4], rest[5:8], rest[8:]
    high, wide, span, frames, head_dim, factor, step = geometry
    cells = high * wide
    base = frames * cells
    head_at = lax.axis_index("head")
    stretch_at = lax.axis_index("tm")

    def run(with_first):
        for flip, out_ref in zip(flips, outs):
            start = pl.multiple_of(jnp.bitwise_xor(head_at, flip) * step, step)
            rows = pl.ds(start, step)
            near = dist_ref[pl.ds(pl.multiple_of(lax.rem(start, cells), step), step)]
            beyond = near[:, base:]
            for head in range(heads):
                cols = slice(head * head_dim, (head + 1) * head_dim)
                sources = [(edge_ref, beyond, head)]
                if with_first:
                    sources.append((first_tile_ref, near[:, :base], heads + head))
                    sources.append((first_edge_ref, beyond, heads + head))
                pieces = [
                    (ref[0, :, cols], ref[1, :, cols], dist, reach_ref[row : row + 1, :1])
                    for ref, dist, row in sources
                ]
                old = pick_state(head_state, state, head, rows, head_dim)
                acc, total, m = merge(q_ref[rows, cols], pieces, factor, old)
                out_ref[:, cols] = (acc / total).astype(jnp.bfloat16)

    @pl.when(stretch_at > 0)
    def _():
        run(True)

    @pl.when(stretch_at == 0)
    def _():
        run(False)


def copy_kernel(in_ref, out_ref):
    out_ref[...] = in_ref[...]


def stack_kernel(*refs):
    *parts, out_ref = refs
    tile_at = lax.axis_index("tile")
    for flip, part in enumerate(parts):
        tall = part.shape[0]
        top = pl.multiple_of(jnp.bitwise_xor(tile_at, flip) * tall, 16)
        out_ref[pl.ds(top, tall)] = part[...]


def project_kernel(w_ref, part_ref, own_ref, got_ref, out_ref, *, flip):
    broad = part_ref.shape[1]
    half = jnp.bitwise_xor(lax.axis_index("tm"), flip)
    cols = pl.ds(pl.multiple_of(half * broad, 128), broad)
    total = jnp.dot(own_ref[...], w_ref[:, cols], preferred_element_type=jnp.float32)
    total += jnp.dot(got_ref[...], part_ref[...], preferred_element_type=jnp.float32)
    out_ref[...] = total.astype(out_ref.dtype)


def add_kernel(mine_ref, got_ref, *rest, flip):
    out_ref, sum_ref, sems = rest[-3:]
    pieces, tall, broad = sum_ref.shape
    half = jnp.bitwise_xor(lax.axis_index("tm"), flip)
    cols = pl.ds(pl.multiple_of(half * broad, 128), broad)
    copies = []
    for i in range(pieces):
        rows = slice(i * tall, (i + 1) * tall)
        sum_ref[i] = (mine_ref[rows] + got_ref[rows].astype(jnp.float32)).astype(jnp.bfloat16)
        copies.append(pltpu.make_async_copy(sum_ref.at[i], out_ref.at[rows, cols], sems.at[i]))
        copies[-1].start()
    for copy in copies:
        copy.wait()


def two_by_two(query, keys, values, out_weight, radius, block_mask):
    span = RMAX
    frames, high, wide, channels = query.shape[2:]
    heads = radius.shape[0]
    head_dim = channels // heads
    cells = high * wide
    tokens = frames * cells
    groups = lax.axis_size("head")
    tiles = lax.axis_size("tile")
    depth, width = out_weight.shape
    step = tokens // groups
    geometry = (high, wide, span, frames, head_dim, LOG2E / math.sqrt(head_dim), step)
    count = frames * (cells + span * (wide + high + span))
    smem = pl.BlockSpec(memory_space=pltpu.SMEM)
    vmem = pl.BlockSpec(memory_space=pltpu.VMEM)
    hbm = pl.BlockSpec(memory_space=pltpu.HBM)
    bf16, f32 = jnp.bfloat16, jnp.float32
    shape = jax.ShapeDtypeStruct

    def call(kernel, out_shape, specs, *args, name, scratch=(), flops=0, **keys_of):
        return pl.pallas_call(
            functools.partial(kernel, **keys_of) if keys_of else kernel,
            out_shape=out_shape,
            in_specs=specs,
            out_specs=jax.tree.map(lambda _: vmem, out_shape),
            scratch_shapes=scratch,
            cost_estimate=pl.CostEstimate(flops=flops, bytes_accessed=0, transcendentals=0),
            compiler_params=pltpu.CompilerParams(vmem_limit_bytes=VMEM_LIMIT),
            name=name,
        )(*args)

    def flipped(value, axis, flip):
        return lax.ppermute(value, axis, [(i, i ^ flip) for i in range(lax.axis_size(axis))])

    q = query.reshape(tokens, channels)
    k = keys.reshape(tokens, channels)
    v = values.reshape(tokens, channels)

    tall, broad = depth // tiles, width // 2
    part_shape = shape((tall, broad), bf16)
    *faces, tile, part = call(
        face_kernel,
        [
            shape((2, frames, span * wide, channels), bf16),
            shape((2, frames, span * high, channels), bf16),
            shape((2, frames, span * span, channels), bf16),
            shape((2, tokens, channels), bf16),
            part_shape,
        ],
        [hbm] * 3,
        *[pltpu.with_memory_space_constraint(x, pltpu.HBM) for x in (k, v, out_weight)],
        name="faces",
        scratch=[pltpu.SemaphoreType.DMA((3,))],
        geometry=geometry,
    )
    faces = [flipped(face, "tile", flip) for face, flip in zip(faces, (2, 1, 3))]
    lone = flipped(part, "head", 2)
    begun = call(
        begin_kernel,
        [shape((tokens, head_dim), f32)] * 3
        + [shape((cells, count), jnp.int32), shape((2 * heads, head_dim), jnp.int32)],
        [smem] * 2 + [vmem] * 2,
        radius,
        block_mask.transpose(1, 2, 0),
        q,
        tile,
        name="begin",
        geometry=geometry,
        heads=heads,
    )
    begun, tile = lax.optimization_barrier((begun, tile))
    first_tile = lax.ppermute(tile, "tm", [(0, 1)])
    state = call(
        tile_kernel,
        [shape((tokens, channels - head_dim), f32)] * 3,
        [vmem] * 4,
        q,
        tile,
        *begun[3:],
        name="tile",
        geometry=geometry,
        heads=heads,
    )
    lone, state = lax.optimization_barrier((lone, state))
    lone = call(copy_kernel, part_shape, [vmem], lone, name="lone", flops=20 * 10**9)
    lone, state, faces = lax.optimization_barrier((lone, state, faces))
    edge = call(
        edge_kernel, shape((2, count - tokens, channels), bf16), [vmem] * 3, *faces, name="edges"
    )
    first_edge = lax.ppermute(edge, "tm", [(0, 1)])
    parts = [lone] + [flipped(lone, "tile", flip) for flip in range(1, tiles)]

    def rest(state, *flips, flops=0):
        return call(
            rest_kernel,
            [shape((step, channels), bf16)] * len(flips),
            [vmem] * 12,
            q,
            edge,
            first_tile,
            first_edge,
            *begun,
            *state,
            name="rest",
            geometry=geometry,
            heads=heads,
            flips=flips,
            flops=flops,
        )

    (for_side,) = rest(state, 3)
    got_side = flipped(for_side, "head", 2)
    state, for_side = lax.optimization_barrier((state, for_side))
    for_far, own_side = rest(state, 2, 1)
    got_far = flipped(for_far, "head", 2)
    parts, own_side = lax.optimization_barrier((parts, own_side))
    here = call(
        stack_kernel, shape((depth, broad), bf16), [vmem] * tiles, *parts, name="stack"
    )

    def project(part, mine, got, kind, flip, flops=0):
        return call(
            project_kernel,
            shape((step, broad), kind),
            [vmem] * 4,
            out_weight,
            part,
            mine,
            got,
            name="project",
            flops=flops,
            flip=flip,
        )

    for_side = [project(here, own_side, got_side, bf16, 0, 20 * 10**9)]
    from_side = [flipped(for_side[0], "head", 1)]
    state, here, for_side[0] = lax.optimization_barrier((state, here, for_side[0]))
    there = flipped(here, "tm", 1)
    (own,) = rest(state, 0, flops=20 * 10**9)
    own_side, own = lax.optimization_barrier((own_side, own))
    for_side.append(project(there, own_side, got_side, bf16, 1))
    from_side.append(flipped(for_side[1], "head", 1))
    own, for_side[1] = lax.optimization_barrier((own, for_side[1]))
    mine = [
        project(here, own, got_far, f32, 0),
        project(there, own, got_far, f32, 1, 20 * 10**9),
    ]
    pieces = 2
    mixed = []
    for flip in range(2):
        mixed = [
            pl.pallas_call(
                functools.partial(add_kernel, flip=flip),
                out_shape=shape((step, width), bf16),
                in_specs=[vmem] * 2 + [hbm] * flip,
                out_specs=hbm,
                input_output_aliases={2: 0} if flip else {},
                scratch_shapes=[
                    pltpu.VMEM((pieces, step // pieces, broad), bf16),
                    pltpu.SemaphoreType.DMA((pieces,)),
                ],
                compiler_params=pltpu.CompilerParams(vmem_limit_bytes=VMEM_LIMIT),
                name="add",
            )(mine[flip], from_side[flip], *mixed)
        ]
    (mixed,) = mixed
    return mixed.reshape(1, 1, step, width)


def solution(mesh):
    in_specs = (
        P("tm", "tile", None, None, None, "head"),
        P("tm", "tile", None, None, None, "head"),
        P("tm", "tile", None, None, None, "head"),
        P("head", None),
        P("head"),
        P("head", None, None),
    )
    out_specs = P("tm", "tile", "head", None)
    small = dict(mesh.shape) == {"tm": 2, "tile": 4, "head": 4}
    return jax.shard_map(
        two_by_two if small else any_grid,
        mesh=mesh,
        in_specs=in_specs,
        out_specs=out_specs,
        check_vma=False,
    )
```

profile of v0, /device:TPU:0, one launch (start us, length us, event | category | flops | bytes accessed | tf_op | source)
XLA Modules:
  0.0 39.1 jit_solution(16036486744233105629)
XLA Ops:
  0.0 0.0 copy-start.2
  0.0 0.0 copy-start.3
  0.0 0.0 copy-start.1
  0.0 1.5 %faces.1 = (bf16[2,2,64,384]{3,2,1,0:T(8,128)(2,1)S(1)}, bf16[2,2,64,384]{3,2,1,0:T(8,128)(2,1)S(1)}, bf16[2,2,16,384]{3,2,1,0:T(8,128)(2,1)S(1)}, bf16[2,512,384]{2,1,0:T(8,128)(2,1)S(1)}, bf16[96,768]{1,0:T(8,128)(2,1)S(1)}) custom-call(bf16[512,384]{1,0:T(8,128)(2,1)} %bitcast.11, bf16[512,384]{1,0:T(8,128)(2,1)} %bitcast.12, bf16[384,1536]{1,0:T(8,128)(2,1)} %w_ref.9), custom_call_target="tpu_custom_call" | custom-call | tf_op jit(solution)/shard_map/faces/pallas_call | solution.py:448
  1.6 4.1 %collective-permute-start = (bf16[96,768]{1,0:T(8,128)(2,1)S(1)}, bf16[96,768]{1,0:T(8,128)(2,1)S(1)}, u32[]{:S(2)}, u32[]{:S(2)}) collective-permute-start(bf16[96,768]{1,0:T(8,128)(2,1)S(1)} %get-tuple-element.52), channel_id=1, source_target_pairs={{0,2},{1,3},{2,0},{3,1},{4,6},{5,7},{6,4},{7,5},{8,10},{9,11},{10,... | collective-permute-start | bytes 442376 | tf_op jit(solution)/shard_map/ppermute | solution.py:460
  5.7 2.4 %collective-permute-start.3 = (bf16[2,2,16,384]{3,2,1,0:T(8,128)(2,1)S(1)}, bf16[2,2,16,384]{3,2,1,0:T(8,128)(2,1)S(1)}, u32[]{:S(2)}, u32[]{:S(2)}) collective-permute-start(bf16[2,2,16,384]{3,2,1,0:T(8,128)(2,1)S(1)} %get-tuple-element.71), channel_id=1, source_target_pairs={{0,12},{4,8},{8,4},{12,0},{1,13},{5,9},{9,5},{13,1},{2,14},{6,10},... | collective-permute-start | bytes 147464 | tf_op jit(solution)/shard_map/ppermute | solution.py:460
  8.1 0.5 %collective-permute-start.1 = (bf16[2,2,64,384]{3,2,1,0:T(8,128)(2,1)S(1)}, bf16[2,2,64,384]{3,2,1,0:T(8,128)(2,1)S(1)}, u32[]{:S(2)}, u32[]{:S(2)}) collective-permute-start(bf16[2,2,64,384]{3,2,1,0:T(8,128)(2,1)S(1)} %get-tuple-element.69), channel_id=1, source_target_pairs={{0,8},{4,12},{8,0},{12,4},{1,9},{5,13},{9,1},{13,5},{2,10},{6,14},... | collective-permute-start | bytes 589832 | tf_op jit(solution)/shard_map/ppermute | solution.py:460
  8.6 0.5 %collective-permute-start.2 = (bf16[2,2,64,384]{3,2,1,0:T(8,128)(2,1)S(1)}, bf16[2,2,64,384]{3,2,1,0:T(8,128)(2,1)S(1)}, u32[]{:S(2)}, u32[]{:S(2)}) collective-permute-start(bf16[2,2,64,384]{3,2,1,0:T(8,128)(2,1)S(1)} %get-tuple-element.70), channel_id=1, source_target_pairs={{0,4},{4,0},{8,12},{12,8},{1,5},{5,1},{9,13},{13,9},{2,6},{6,2},{1... | collective-permute-start | bytes 589832 | tf_op jit(solution)/shard_map/ppermute | solution.py:460
  9.1 0.0 copy-done.2
  9.2 0.0 copy-done.3
  9.2 0.0 copy-done.1
  9.2 1.4 %begin.1 = (f32[512,128]{1,0:T(8,128)S(1)}, f32[512,128]{1,0:T(8,128)S(1)}, f32[512,128]{1,0:T(8,128)S(1)}, s32[256,800]{1,0:T(8,128)S(1)}, s32[6,128]{1,0:T(8,128)S(1)}) custom-call(s32[3]{0:T(128)S(1)} %copy-done.3, s32[2,2,3]{2,1,0:T(2,128)S(1)} %bitcast.10, bf16[512,384]{1,0:T(8,128)(2,1)S(1)} %bitcast.5, bf16[2,512,384]{2,1,0:T(8,128)(2,1)S(1)} %get-tuple-element.59.tile_ref), custom_call_target="tpu_custom_call" | custom-call | tf_op jit(solution)/shard_map/begin/pallas_call | solution.py:448
  10.6 1.3 %collective-permute-start.4 = (bf16[2,512,384]{2,1,0:T(8,128)(2,1)S(1)}, bf16[2,512,384]{2,1,0:T(8,128)(2,1)S(1)}, u32[]{:S(2)}, u32[]{:S(2)}) collective-permute-start(bf16[2,512,384]{2,1,0:T(8,128)(2,1)S(1)} %get-tuple-element.59.tile_ref), channel_id=1, source_target_pairs={{0,16},{1,17},{2,18},{3,19},{4,20},{5,21},{6,22},{7,23},{8,24},{9,... | collective-permute-start | bytes 2359304 | tf_op jit(solution)/shard_map/ppermute | solution.py:499
  11.9 1.1 %tile.1 = (f32[512,256]{1,0:T(8,128)S(1)}, f32[512,256]{1,0:T(8,128)S(1)}, f32[512,256]{1,0:T(8,128)S(1)}) custom-call(bf16[512,384]{1,0:T(8,128)(2,1)S(1)} %bitcast.6, bf16[2,512,384]{2,1,0:T(8,128)(2,1)S(1)} %get-tuple-element.59.tile_ref, s32[256,800]{1,0:T(8,128)S(1)} %get-tuple-element.60.dist_ref.rest_3_, s32[6,128]{1,0:T(8,128)S(1)} %get-tuple-element.61.reach_ref.rest_4_), custom_call_target="tpu_custom_call" | custom-call | tf_op jit(solution)/shard_map/tile/pallas_call | solution.py:448
  13.0 0.0 collective-permute-done.in_ref
  13.0 0.0 collective-permute-done.3.corner_ref
  13.0 1.7 %collective-permute-done.1.row_ref = bf16[2,2,64,384]{3,2,1,0:T(8,128)(2,1)S(1)} collective-permute-done((bf16[2,2,64,384]{3,2,1,0:T(8,128)(2,1)S(1)}, bf16[2,2,64,384]{3,2,1,0:T(8,128)(2,1)S(1)}, u32[]{:S(2)}, u32[]{:S(2)}) %collective-permute-start.1) | collective-permute-done | bytes 196640 | tf_op jit(solution)/shard_map/ppermute | solution.py:460
  14.7 0.2 collective-permute-done.2.col_ref
  15.0 1.3 %collective-permute-start.5 = (bf16[2,288,384]{2,1,0:T(8,128)(2,1)S(1)}, bf16[2,288,384]{2,1,0:T(8,128)(2,1)S(1)}, u32[]{:S(2)}, u32[]{:S(2)}) collective-permute-start(bf16[2,288,384]{2,1,0:T(8,128)(2,1)S(1)} %edges.1.edge_ref), channel_id=1, source_target_pairs={{0,16},{1,17},{2,18},{3,19},{4,20},{5,21},{6,22},{7,23},{8,24},{9,... | collective-permute-start | bytes 1327112 | tf_op jit(solution)/shard_map/ppermute | solution.py:517
  16.3 1.5 %collective-permute-start.8 = (bf16[96,768]{1,0:T(8,128)(2,1)S(1)}, bf16[96,768]{1,0:T(8,128)(2,1)S(1)}, u32[]{:S(2)}, u32[]{:S(2)}) collective-permute-start(bf16[96,768]{1,0:T(8,128)(2,1)S(1)} %lone.1.refs_0_), channel_id=1, source_target_pairs={{0,12},{4,8},{8,4},{12,0},{1,13},{5,9},{9,5},{13,1},{2,14},{6,10},... | collective-permute-start | bytes 442376 | tf_op jit(solution)/shard_map/ppermute | solution.py:460
  17.8 0.6 %collective-permute-start.7 = (bf16[96,768]{1,0:T(8,128)(2,1)S(1)}, bf16[96,768]{1,0:T(8,128)(2,1)S(1)}, u32[]{:S(2)}, u32[]{:S(2)}) collective-permute-start(bf16[96,768]{1,0:T(8,128)(2,1)S(1)} %lone.1.refs_0_), channel_id=1, source_target_pairs={{0,8},{4,12},{8,0},{12,4},{1,9},{5,13},{9,1},{13,5},{2,10},{6,14},... | collective-permute-start | bytes 442376 | tf_op jit(solution)/shard_map/ppermute | solution.py:460
  18.4 1.4 %collective-permute-start.6 = (bf16[96,768]{1,0:T(8,128)(2,1)S(1)}, bf16[96,768]{1,0:T(8,128)(2,1)S(1)}, u32[]{:S(2)}, u32[]{:S(2)}) collective-permute-start(bf16[96,768]{1,0:T(8,128)(2,1)S(1)} %lone.1.refs_0_), channel_id=1, source_target_pairs={{0,4},{4,0},{8,12},{12,8},{1,5},{5,1},{9,13},{13,9},{2,6},{6,2},{1... | collective-permute-start | bytes 442376 | tf_op jit(solution)/shard_map/ppermute | solution.py:460
  19.8 0.0 collective-permute-done.5.first_edge_ref
  19.8 0.0 collective-permute-done.4.first_tile_ref
  19.9 1.0 %rest.3 = bf16[128,384]{1,0:T(8,128)(2,1)S(1)} custom-call(bf16[512,384]{1,0:T(8,128)(2,1)S(1)} %bitcast.7, bf16[2,288,384]{2,1,0:T(8,128)(2,1)S(1)} %edges.1.edge_ref, bf16[2,512,384]{2,1,0:T(8,128)(2,1)S(1)} %collective-permute-done.4.first_tile_ref, bf16[2,288,384]{2,1,0:T(8,128)(2,1)S(1)} %collective-permute-done.5.first_edge_ref, ...), custom_call_target="tpu_custom_call" | custom-call | tf_op jit(solution)/shard_map/rest/pallas_call | solution.py:448
  20.8 0.4 %collective-permute-start.9 = (bf16[128,384]{1,0:T(8,128)(2,1)S(1)}, bf16[128,384]{1,0:T(8,128)(2,1)S(1)}, u32[]{:S(2)}, u32[]{:S(2)}) collective-permute-start(bf16[128,384]{1,0:T(8,128)(2,1)S(1)} %rest.3), channel_id=1, source_target_pairs={{0,2},{1,3},{2,0},{3,1},{4,6},{5,7},{6,4},{7,5},{8,10},{9,11},{10,... | collective-permute-start | bytes 294920 | tf_op jit(solution)/shard_map/ppermute | solution.py:460
  21.2 1.4 %rest.4 = (bf16[128,384]{1,0:T(8,128)(2,1)S(1)}, bf16[128,384]{1,0:T(8,128)(2,1)S(1)}) custom-call(bf16[512,384]{1,0:T(8,128)(2,1)S(1)} %bitcast.8, bf16[2,288,384]{2,1,0:T(8,128)(2,1)S(1)} %edges.1.edge_ref, bf16[2,512,384]{2,1,0:T(8,128)(2,1)S(1)} %collective-permute-done.4.first_tile_ref, bf16[2,288,384]{2,1,0:T(8,128)(2,1)S(1)} %collective-permute-done.5.first_edge_ref, ...), custom_call_target="tpu_custom_call" | custom-call | tf_op jit(solution)/shard_map/rest/pallas_call | solution.py:448
  22.6 0.0 copy-start
  22.6 0.7 %collective-permute-done.8.refs_3_ = bf16[96,768]{1,0:T(8,128)(2,1)S(1)} collective-permute-done((bf16[96,768]{1,0:T(8,128)(2,1)S(1)}, bf16[96,768]{1,0:T(8,128)(2,1)S(1)}, u32[]{:S(2)}, u32[]{:S(2)}) %collective-permute-start.8) | collective-permute-done | bytes 147488 | tf_op jit(solution)/shard_map/ppermute | solution.py:460
  23.3 1.5 %collective-permute-done.7.refs_2_ = bf16[96,768]{1,0:T(8,128)(2,1)S(1)} collective-permute-done((bf16[96,768]{1,0:T(8,128)(2,1)S(1)}, bf16[96,768]{1,0:T(8,128)(2,1)S(1)}, u32[]{:S(2)}, u32[]{:S(2)}) %collective-permute-start.7) | collective-permute-done | bytes 147488 | tf_op jit(solution)/shard_map/ppermute | solution.py:460
  24.8 0.0 collective-permute-done.6.refs_1_
  24.8 0.5 %collective-permute-start.11 = (bf16[128,384]{1,0:T(8,128)(2,1)S(1)}, bf16[128,384]{1,0:T(8,128)(2,1)S(1)}, u32[]{:S(2)}, u32[]{:S(2)}) collective-permute-start(bf16[128,384]{1,0:T(8,128)(2,1)S(1)} %get-tuple-element.98), channel_id=1, source_target_pairs={{0,2},{1,3},{2,0},{3,1},{4,6},{5,7},{6,4},{7,5},{8,10},{9,11},{10,... | collective-permute-start | bytes 294920 | tf_op jit(solution)/shard_map/ppermute | solution.py:460
  25.3 0.1 stack.1.part_ref
  25.3 1.1 %collective-permute-done.9.got_ref = bf16[128,384]{1,0:T(8,128)(2,1)S(1)} collective-permute-done((bf16[128,384]{1,0:T(8,128)(2,1)S(1)}, bf16[128,384]{1,0:T(8,128)(2,1)S(1)}, u32[]{:S(2)}, u32[]{:S(2)}) %collective-permute-start.9) | collective-permute-done | bytes 98336 | tf_op jit(solution)/shard_map/ppermute | solution.py:460
  26.4 0.0 copy-done
  26.4 0.4 project.4
  26.8 1.9 %collective-permute-start.13 = (bf16[128,768]{1,0:T(8,128)(2,1)S(1)}, bf16[128,768]{1,0:T(8,128)(2,1)S(1)}, u32[]{:S(2)}, u32[]{:S(2)}) collective-permute-start(bf16[128,768]{1,0:T(8,128)(2,1)S(1)} %project.4), channel_id=1, source_target_pairs={{0,1},{1,0},{2,3},{3,2},{4,5},{5,4},{6,7},{7,6},{8,9},{9,8},{10,11... | collective-permute-start | bytes 589832 | tf_op jit(solution)/shard_map/ppermute | solution.py:460
  28.6 0.0 collective-permute-start.10
  28.6 0.9 %rest.5.own_ref = bf16[128,384]{1,0:T(8,128)(2,1)S(1)} custom-call(bf16[512,384]{1,0:T(8,128)(2,1)S(1)} %bitcast.9, bf16[2,288,384]{2,1,0:T(8,128)(2,1)S(1)} %edges.1.edge_ref, bf16[2,512,384]{2,1,0:T(8,128)(2,1)S(1)} %collective-permute-done.4.first_tile_ref, bf16[2,288,384]{2,1,0:T(8,128)(2,1)S(1)} %collective-permute-done.5.first_edge_ref, ...), custom_call_target="tpu_custom_call" | custom-call | flops 20000000000 | tf_op jit(solution)/shard_map/rest/pallas_call | solution.py:448
  29.6 1.0 %collective-permute-done.10.part_ref = bf16[384,768]{1,0:T(8,128)(2,1)S(1)} collective-permute-done((bf16[384,768]{1,0:T(8,128)(2,1)S(1)}, bf16[384,768]{1,0:T(8,128)(2,1)S(1)}, u32[]{:S(2)}, u32[]{:S(2)}) %collective-permute-start.10) | collective-permute-done | bytes 589856 | tf_op jit(solution)/shard_map/ppermute | solution.py:460
  30.6 0.4 project.5
  31.0 0.3 collective-permute-start.12
  31.3 0.0 collective-permute-done.11.got_ref
  31.3 0.4 project.6.mine_ref
  31.7 0.4 project.7.mine_ref
  32.0 2.4 %collective-permute-done.13.got_ref = bf16[128,768]{1,0:T(8,128)(2,1)S(1)} collective-permute-done((bf16[128,768]{1,0:T(8,128)(2,1)S(1)}, bf16[128,768]{1,0:T(8,128)(2,1)S(1)}, u32[]{:S(2)}, u32[]{:S(2)}) %collective-permute-start.13) | collective-permute-done | bytes 196640 | tf_op jit(solution)/shard_map/ppermute | solution.py:460
  34.4 0.7 %add.2.rest_0_ = bf16[128,1536]{1,0:T(8,128)(2,1)} custom-call(f32[128,768]{1,0:T(8,128)S(1)} %project.7.mine_ref, bf16[128,768]{1,0:T(8,128)(2,1)S(1)} %collective-permute-done.13.got_ref), custom_call_target="tpu_custom_call" | custom-call | tf_op jit(solution)/shard_map/add/pallas_call | solution.py:579
  35.1 3.2 %collective-permute-done.12.got_ref = bf16[128,768]{1,0:T(8,128)(2,1)S(1)} collective-permute-done((bf16[128,768]{1,0:T(8,128)(2,1)S(1)}, bf16[128,768]{1,0:T(8,128)(2,1)S(1)}, u32[]{:S(2)}, u32[]{:S(2)}) %collective-permute-start.12) | collective-permute-done | bytes 196640 | tf_op jit(solution)/shard_map/ppermute | solution.py:460
  38.3 0.7 %add.3 = bf16[128,1536]{1,0:T(8,128)(2,1)} custom-call(f32[128,768]{1,0:T(8,128)S(1)} %project.6.mine_ref, bf16[128,768]{1,0:T(8,128)(2,1)S(1)} %collective-permute-done.12.got_ref, bf16[128,1536]{1,0:T(8,128)(2,1)} %add.2.rest_0_), custom_call_target="tpu_custom_call", output_to_operand_aliasing={{}: (2, {})} | custom-call | tf_op jit(solution)/shard_map/add/pallas_call | solution.py:579
  (2 shorter events, 0.1 us)
Async XLA Ops:
  0.0 9.2 %copy-start.2 = (s32[3,2,2]{0,2,1:T(2,128)S(1)}, s32[3,2,2]{0,2,1:T(2,128)}, u32[]{:S(2)}) copy-start(s32[3,2,2]{0,2,1:T(2,128)} %param.11) | copy-start | bytes 148
  0.0 9.2 %copy-start.3 = (s32[3]{0:T(128)S(1)}, s32[3]{0:T(128)}, u32[]{:S(2)}) copy-start(s32[3]{0:T(128)} %radius_ref.1) | copy-start | bytes 40
  0.0 9.2 %copy-start.1 = (bf16[1,1,2,16,16,384]{5,4,3,2,1,0:T(8,128)(2,1)S(1)}, bf16[1,1,2,16,16,384]{5,4,3,2,1,0:T(8,128)(2,1)}, u32[]{:S(2)}) copy-start(bf16[1,1,2,16,16,384]{5,4,3,2,1,0:T(8,128)(2,1)} %param.6) | copy-start | bytes 1179652
  1.6 11.5 %collective-permute-start = (bf16[96,768]{1,0:T(8,128)(2,1)S(1)}, bf16[96,768]{1,0:T(8,128)(2,1)S(1)}, u32[]{:S(2)}, u32[]{:S(2)}) collective-permute-start(bf16[96,768]{1,0:T(8,128)(2,1)S(1)} %get-tuple-element.52), channel_id=1, source_target_pairs={{0,2},{1,3},{2,0},{3,1},{4,6},{5,7},{6,4},{7,5},{8,10},{9,11},{10,... | collective-permute-start | bytes 442376 | tf_op jit(solution)/shard_map/ppermute | solution.py:460
  5.7 7.4 %collective-permute-start.3 = (bf16[2,2,16,384]{3,2,1,0:T(8,128)(2,1)S(1)}, bf16[2,2,16,384]{3,2,1,0:T(8,128)(2,1)S(1)}, u32[]{:S(2)}, u32[]{:S(2)}) collective-permute-start(bf16[2,2,16,384]{3,2,1,0:T(8,128)(2,1)S(1)} %get-tuple-element.71), channel_id=1, source_target_pairs={{0,12},{4,8},{8,4},{12,0},{1,13},{5,9},{9,5},{13,1},{2,14},{6,10},... | collective-permute-start | bytes 147464 | tf_op jit(solution)/shard_map/ppermute | solution.py:460
  8.1 6.6 %collective-permute-start.1 = (bf16[2,2,64,384]{3,2,1,0:T(8,128)(2,1)S(1)}, bf16[2,2,64,384]{3,2,1,0:T(8,128)(2,1)S(1)}, u32[]{:S(2)}, u32[]{:S(2)}) collective-permute-start(bf16[2,2,64,384]{3,2,1,0:T(8,128)(2,1)S(1)} %get-tuple-element.69), channel_id=1, source_target_pairs={{0,8},{4,12},{8,0},{12,4},{1,9},{5,13},{9,1},{13,5},{2,10},{6,14},... | collective-permute-start | bytes 589832 | tf_op jit(solution)/shard_map/ppermute | solution.py:460
  8.6 6.3 %collective-permute-start.2 = (bf16[2,2,64,384]{3,2,1,0:T(8,128)(2,1)S(1)}, bf16[2,2,64,384]{3,2,1,0:T(8,128)(2,1)S(1)}, u32[]{:S(2)}, u32[]{:S(2)}) collective-permute-start(bf16[2,2,64,384]{3,2,1,0:T(8,128)(2,1)S(1)} %get-tuple-element.70), channel_id=1, source_target_pairs={{0,4},{4,0},{8,12},{12,8},{1,5},{5,1},{9,13},{13,9},{2,6},{6,2},{1... | collective-permute-start | bytes 589832 | tf_op jit(solution)/shard_map/ppermute | solution.py:460
  10.6 9.3 %collective-permute-start.4 = (bf16[2,512,384]{2,1,0:T(8,128)(2,1)S(1)}, bf16[2,512,384]{2,1,0:T(8,128)(2,1)S(1)}, u32[]{:S(2)}, u32[]{:S(2)}) collective-permute-start(bf16[2,512,384]{2,1,0:T(8,128)(2,1)S(1)} %get-tuple-element.59.tile_ref), channel_id=1, source_target_pairs={{0,16},{1,17},{2,18},{3,19},{4,20},{5,21},{6,22},{7,23},{8,24},{9,... | collective-permute-start | bytes 2359304 | tf_op jit(solution)/shard_map/ppermute | solution.py:499
  15.0 4.9 %collective-permute-start.5 = (bf16[2,288,384]{2,1,0:T(8,128)(2,1)S(1)}, bf16[2,288,384]{2,1,0:T(8,128)(2,1)S(1)}, u32[]{:S(2)}, u32[]{:S(2)}) collective-permute-start(bf16[2,288,384]{2,1,0:T(8,128)(2,1)S(1)} %edges.1.edge_ref), channel_id=1, source_target_pairs={{0,16},{1,17},{2,18},{3,19},{4,20},{5,21},{6,22},{7,23},{8,24},{9,... | collective-permute-start | bytes 1327112 | tf_op jit(solution)/shard_map/ppermute | solution.py:517
  16.3 7.1 %collective-permute-start.8 = (bf16[96,768]{1,0:T(8,128)(2,1)S(1)}, bf16[96,768]{1,0:T(8,128)(2,1)S(1)}, u32[]{:S(2)}, u32[]{:S(2)}) collective-permute-start(bf16[96,768]{1,0:T(8,128)(2,1)S(1)} %lone.1.refs_0_), channel_id=1, source_target_pairs={{0,12},{4,8},{8,4},{12,0},{1,13},{5,9},{9,5},{13,1},{2,14},{6,10},... | collective-permute-start | bytes 442376 | tf_op jit(solution)/shard_map/ppermute | solution.py:460
  17.8 7.0 %collective-permute-start.7 = (bf16[96,768]{1,0:T(8,128)(2,1)S(1)}, bf16[96,768]{1,0:T(8,128)(2,1)S(1)}, u32[]{:S(2)}, u32[]{:S(2)}) collective-permute-start(bf16[96,768]{1,0:T(8,128)(2,1)S(1)} %lone.1.refs_0_), channel_id=1, source_target_pairs={{0,8},{4,12},{8,0},{12,4},{1,9},{5,13},{9,1},{13,5},{2,10},{6,14},... | collective-permute-start | bytes 442376 | tf_op jit(solution)/shard_map/ppermute | solution.py:460
  18.4 6.4 %collective-permute-start.6 = (bf16[96,768]{1,0:T(8,128)(2,1)S(1)}, bf16[96,768]{1,0:T(8,128)(2,1)S(1)}, u32[]{:S(2)}, u32[]{:S(2)}) collective-permute-start(bf16[96,768]{1,0:T(8,128)(2,1)S(1)} %lone.1.refs_0_), channel_id=1, source_target_pairs={{0,4},{4,0},{8,12},{12,8},{1,5},{5,1},{9,13},{13,9},{2,6},{6,2},{1... | collective-permute-start | bytes 442376 | tf_op jit(solution)/shard_map/ppermute | solution.py:460
  20.8 5.6 %collective-permute-start.9 = (bf16[128,384]{1,0:T(8,128)(2,1)S(1)}, bf16[128,384]{1,0:T(8,128)(2,1)S(1)}, u32[]{:S(2)}, u32[]{:S(2)}) collective-permute-start(bf16[128,384]{1,0:T(8,128)(2,1)S(1)} %rest.3), channel_id=1, source_target_pairs={{0,2},{1,3},{2,0},{3,1},{4,6},{5,7},{6,4},{7,5},{8,10},{9,11},{10,... | collective-permute-start | bytes 294920 | tf_op jit(solution)/shard_map/ppermute | solution.py:460
  22.6 3.8 %copy-start = (bf16[384,1536]{1,0:T(8,128)(2,1)S(1)}, bf16[384,1536]{1,0:T(8,128)(2,1)}, u32[]{:S(2)}) copy-start(bf16[384,1536]{1,0:T(8,128)(2,1)} %w_ref.9) | copy-start | bytes 3538948
  24.8 6.5 %collective-permute-start.11 = (bf16[128,384]{1,0:T(8,128)(2,1)S(1)}, bf16[128,384]{1,0:T(8,128)(2,1)S(1)}, u32[]{:S(2)}, u32[]{:S(2)}) collective-permute-start(bf16[128,384]{1,0:T(8,128)(2,1)S(1)} %get-tuple-element.98), channel_id=1, source_target_pairs={{0,2},{1,3},{2,0},{3,1},{4,6},{5,7},{6,4},{7,5},{8,10},{9,11},{10,... | collective-permute-start | bytes 294920 | tf_op jit(solution)/shard_map/ppermute | solution.py:460
  26.8 7.6 %collective-permute-start.13 = (bf16[128,768]{1,0:T(8,128)(2,1)S(1)}, bf16[128,768]{1,0:T(8,128)(2,1)S(1)}, u32[]{:S(2)}, u32[]{:S(2)}) collective-permute-start(bf16[128,768]{1,0:T(8,128)(2,1)S(1)} %project.4), channel_id=1, source_target_pairs={{0,1},{1,0},{2,3},{3,2},{4,5},{5,4},{6,7},{7,6},{8,9},{9,8},{10,11... | collective-permute-start | bytes 589832 | tf_op jit(solution)/shard_map/ppermute | solution.py:460
  28.6 2.0 %collective-permute-start.10 = (bf16[384,768]{1,0:T(8,128)(2,1)S(1)}, bf16[384,768]{1,0:T(8,128)(2,1)S(1)}, u32[]{:S(2)}, u32[]{:S(2)}) collective-permute-start(bf16[384,768]{1,0:T(8,128)(2,1)S(1)} %stack.1.part_ref), channel_id=1, source_target_pairs={{0,16},{16,0},{1,17},{17,1},{2,18},{18,2},{3,19},{19,3},{4,20},{20... | collective-permute-start | bytes 1769480 | tf_op jit(solution)/shard_map/ppermute | solution.py:460
  31.0 7.3 %collective-permute-start.12 = (bf16[128,768]{1,0:T(8,128)(2,1)S(1)}, bf16[128,768]{1,0:T(8,128)(2,1)S(1)}, u32[]{:S(2)}, u32[]{:S(2)}) collective-permute-start(bf16[128,768]{1,0:T(8,128)(2,1)S(1)} %project.5), channel_id=1, source_target_pairs={{0,1},{1,0},{2,3},{3,2},{4,5},{5,4},{6,7},{7,6},{8,9},{9,8},{10,11... | collective-permute-start | bytes 589832 | tf_op jit(solution)/shard_map/ppermute | solution.py:460
where the time goes:
time: 39.2 us; the launch traced here: 39.1 us
  starting transfers between devices  16.8 us (43%)
  waiting for transfers between devices  11.8 us (30%)
  Pallas kernels  10.3 us (26%)
    ppermute x12, starting transfers between devices, flipped(): lax.ppermute(value, axis, [(i, i ^ flip) for i in range(lax.axis_size(axi...  14.2 us
    ppermute x12, waiting for transfers between devices, flipped(): lax.ppermute(value, axis, [(i, i ^ flip) for i in range(lax.axis_size(axi...  11.8 us
    pallas_call x13, Pallas kernels, call(): pl.pallas_call(functools.partial(kernel, **keys_of) if keys_of else kerne...  8.84 us
    pallas_call x2, Pallas kernels, two_by_two(): pl.pallas_call(functools.partial(add_kernel, flip=flip), out_shape=shape(...  1.42 us
    ppermute x1, starting transfers between devices, two_by_two(): first_tile = lax.ppermute(tile, 'tm', [(0, 1)])  1.34 us
    ppermute x1, starting transfers between devices, two_by_two(): first_edge = lax.ppermute(edge, 'tm', [(0, 1)])  1.32 us
  transfers between devices with their start and end apart: 14, of which 8 were waited for; matrix products, arithmetic and copies ran while one was open for 0% of the time, Pallas kernels for 20%

commit v1 on v0

--- a/solution.py
+++ b/solution.py
@@ -183,28 +183,29 @@
     return tile_at // 2, tile_at % 2
 
 
-def face_kernel(
-    k_ref, v_ref, w_ref, row_ref, col_ref, corner_ref, tile_ref, part_ref, sems, *, geometry
-):
+def load_kernel(k_ref, v_ref, w_ref, tile_ref, part_ref, sems):
+    tall, broad = part_ref.shape
+    top = pl.multiple_of(lax.axis_index("tile") * tall, 16)
+    left = pl.multiple_of(lax.axis_index("tm") * broad, 128)
+    copies = [
+        pltpu.make_async_copy(
+            w_ref.at[pl.ds(top, tall), pl.ds(left, broad)], part_ref, sems.at[2]
+        )
+    ]
+    for which, ref in enumerate((k_ref, v_ref)):
+        copies.append(pltpu.make_async_copy(ref, tile_ref.at[which], sems.at[which]))
+    for copy in copies:
+        copy.start()
+    for copy in copies:
+        copy.wait()
+
+
+def face_kernel(tile_ref, row_ref, col_ref, corner_ref, *, geometry):
     high, wide, span, frames = geometry[:4]
     cells = high * wide
     row_at, col_at = tile_place()
     y0 = jnp.where(row_at == 0, high - span, 0)
     x0 = jnp.where(col_at == 0, wide - span, 0)
-    tall, broad = part_ref.shape
-    top = pl.multiple_of(lax.axis_index("tile") * tall, 16)
-    edge = pl.multiple_of(lax.axis_index("tm") * broad, 128)
-    copies = [
-        pltpu.make_async_copy(ref, tile_ref.at[which], sems.at[which])
-        for which, ref in enumerate((k_ref, v_ref))
-    ]
-    copies.append(
-        pltpu.make_async_copy(
-            w_ref.at[pl.ds(top, tall), pl.ds(edge, broad)], part_ref, sems.at[2]
-        )
-    )
-    for copy in copies:
-        copy.start()
 
     def picker(count, cell_of):
         row = lax.broadcasted_iota(jnp.int32, (count, cells), 0)
@@ -214,7 +215,6 @@
     beside = picker(high * span, lambda i: (i // span) * wide + x0 + i % span)
     across = picker(span * span, lambda i: (y0 + i // span) * wide + x0 + i % span)
     for which in range(2):
-        copies[which].wait()
         for f in range(frames):
             start = pl.multiple_of(f * cells + y0 * wide, 16)
             row_ref[which, f] = tile_ref[which, pl.ds(start, span * wide)]
@@ -225,7 +225,6 @@
             corner_ref[which, f] = jnp.dot(
                 across, whole, preferred_element_type=jnp.float32
             ).astype(jnp.bfloat16)
-    copies[2].wait()
 
 
 def edge_kernel(row_ref, col_ref, corner_ref, out_ref):
@@ -465,19 +464,24 @@
 
     tall, broad = depth // tiles, width // 2
     part_shape = shape((tall, broad), bf16)
-    *faces, tile, part = call(
+    tile, part = call(
+        load_kernel,
+        [shape((2, tokens, channels), bf16), part_shape],
+        [hbm] * 3,
+        *[pltpu.with_memory_space_constraint(x, pltpu.HBM) for x in (k, v, out_weight)],
+        name="load",
+        scratch=[pltpu.SemaphoreType.DMA((3,))],
+    )
+    faces = call(
         face_kernel,
         [
             shape((2, frames, span * wide, channels), bf16),
             shape((2, frames, span * high, channels), bf16),
             shape((2, frames, span * span, channels), bf16),
-            shape((2, tokens, channels), bf16),
-            part_shape,
         ],
-        [hbm] * 3,
-        *[pltpu.with_memory_space_constraint(x, pltpu.HBM) for x in (k, v, out_weight)],
+        [vmem],
+        tile,
         name="faces",
-        scratch=[pltpu.SemaphoreType.DMA((3,))],
         geometry=geometry,
     )
     faces = [flipped(face, "tile", flip) for face, flip in zip(faces, (2, 1, 3))]

time: 39.2 us -> 39 us (level)
  waiting for transfers between devices: 11.8 us -> 11.4 us
    pallas_call x13 -> x14, Pallas kernels: 8.84 us -> 8.91 us  [call(): pl.pallas_call(functools.partial(kernel, **keys_of) if keys_of else kerne...]
  transfers between devices with their start and end apart: 14 -> 14, of which waited for: 8 -> 8; matrix products, arithmetic and copies ran while one was open for 0% -> 0% of each run, Pallas kernels for 20% -> 22%
where the time goes in v1:
time: 39 us; the launch traced here: 38.8 us
  starting transfers between devices  16.9 us (43%)
  waiting for transfers between devices  11.4 us (29%)
  Pallas kernels  10.3 us (26%)
    ppermute x12, starting transfers between devices, flipped(): lax.ppermute(value, axis, [(i, i ^ flip) for i in range(lax.axis_size(axi...  14.3 us
    ppermute x12, waiting for transfers between devices, flipped(): lax.ppermute(value, axis, [(i, i ^ flip) for i in range(lax.axis_size(axi...  11.4 us
    pallas_call x14, Pallas kernels, call(): pl.pallas_call(functools.partial(kernel, **keys_of) if keys_of else kerne...  8.91 us
    pallas_call x2, Pallas kernels, two_by_two(): pl.pallas_call(functools.partial(add_kernel, flip=flip), out_shape=shape(...  1.42 us
    ppermute x1, starting transfers between devices, two_by_two(): first_tile = lax.ppermute(tile, 'tm', [(0, 1)])  1.34 us
    ppermute x1, starting transfers between devices, two_by_two(): first_edge = lax.ppermute(edge, 'tm', [(0, 1)])  1.32 us
  transfers between devices with their start and end apart: 14, of which 8 were waited for; matrix products, arithmetic and copies ran while one was open for 0% of the time, Pallas kernels for 22%

profile of v1, /device:TPU:0, one launch (start us, length us, event | category | flops | bytes accessed | tf_op | source)
XLA Modules:
  0.0 38.8 jit_solution(17150464611446669104)
XLA Ops:
  0.0 0.0 copy-start.1
  0.0 0.0 copy-start.2
  0.0 0.0 copy-start.3
  0.0 1.3 %load.1 = (bf16[2,512,384]{2,1,0:T(8,128)(2,1)S(1)}, bf16[96,768]{1,0:T(8,128)(2,1)S(1)}) custom-call(bf16[512,384]{1,0:T(8,128)(2,1)} %bitcast.11, bf16[512,384]{1,0:T(8,128)(2,1)} %bitcast.12, bf16[384,1536]{1,0:T(8,128)(2,1)} %w_ref.9), custom_call_target="tpu_custom_call" | custom-call | tf_op jit(solution)/shard_map/load/pallas_call | solution.py:447
  1.3 4.1 %collective-permute-start = (bf16[96,768]{1,0:T(8,128)(2,1)S(1)}, bf16[96,768]{1,0:T(8,128)(2,1)S(1)}, u32[]{:S(2)}, u32[]{:S(2)}) collective-permute-start(bf16[96,768]{1,0:T(8,128)(2,1)S(1)} %get-tuple-element.52), channel_id=1, source_target_pairs={{0,2},{1,3},{2,0},{3,1},{4,6},{5,7},{6,4},{7,5},{8,10},{9,11},{10,... | collective-permute-start | bytes 442376 | tf_op jit(solution)/shard_map/ppermute | solution.py:459
  5.4 0.3 faces.1
  5.7 2.5 %collective-permute-start.3 = (bf16[2,2,16,384]{3,2,1,0:T(8,128)(2,1)S(1)}, bf16[2,2,16,384]{3,2,1,0:T(8,128)(2,1)S(1)}, u32[]{:S(2)}, u32[]{:S(2)}) collective-permute-start(bf16[2,2,16,384]{3,2,1,0:T(8,128)(2,1)S(1)} %get-tuple-element.71), channel_id=1, source_target_pairs={{0,12},{4,8},{8,4},{12,0},{1,13},{5,9},{9,5},{13,1},{2,14},{6,10},... | collective-permute-start | bytes 147464 | tf_op jit(solution)/shard_map/ppermute | solution.py:459
  8.3 0.5 %collective-permute-start.1 = (bf16[2,2,64,384]{3,2,1,0:T(8,128)(2,1)S(1)}, bf16[2,2,64,384]{3,2,1,0:T(8,128)(2,1)S(1)}, u32[]{:S(2)}, u32[]{:S(2)}) collective-permute-start(bf16[2,2,64,384]{3,2,1,0:T(8,128)(2,1)S(1)} %get-tuple-element.69), channel_id=1, source_target_pairs={{0,8},{4,12},{8,0},{12,4},{1,9},{5,13},{9,1},{13,5},{2,10},{6,14},... | collective-permute-start | bytes 589832 | tf_op jit(solution)/shard_map/ppermute | solution.py:459
  8.8 0.5 %collective-permute-start.2 = (bf16[2,2,64,384]{3,2,1,0:T(8,128)(2,1)S(1)}, bf16[2,2,64,384]{3,2,1,0:T(8,128)(2,1)S(1)}, u32[]{:S(2)}, u32[]{:S(2)}) collective-permute-start(bf16[2,2,64,384]{3,2,1,0:T(8,128)(2,1)S(1)} %get-tuple-element.70), channel_id=1, source_target_pairs={{0,4},{4,0},{8,12},{12,8},{1,5},{5,1},{9,13},{13,9},{2,6},{6,2},{1... | collective-permute-start | bytes 589832 | tf_op jit(solution)/shard_map/ppermute | solution.py:459
  9.3 0.0 copy-done.1
  9.3 0.0 copy-done.2
  9.3 0.0 copy-done.3
  9.3 1.4 %begin.1 = (f32[512,128]{1,0:T(8,128)S(1)}, f32[512,128]{1,0:T(8,128)S(1)}, f32[512,128]{1,0:T(8,128)S(1)}, s32[256,800]{1,0:T(8,128)S(1)}, s32[6,128]{1,0:T(8,128)S(1)}) custom-call(s32[3]{0:T(128)S(1)} %copy-done.3, s32[2,2,3]{2,1,0:T(2,128)S(1)} %bitcast.10, bf16[512,384]{1,0:T(8,128)(2,1)S(1)} %bitcast.5, bf16[2,512,384]{2,1,0:T(8,128)(2,1)S(1)} %get-tuple-element.59.tile_ref), custom_call_target="tpu_custom_call" | custom-call | tf_op jit(solution)/shard_map/begin/pallas_call | solution.py:447
  10.7 1.3 %collective-permute-start.4 = (bf16[2,512,384]{2,1,0:T(8,128)(2,1)S(1)}, bf16[2,512,384]{2,1,0:T(8,128)(2,1)S(1)}, u32[]{:S(2)}, u32[]{:S(2)}) collective-permute-start(bf16[2,512,384]{2,1,0:T(8,128)(2,1)S(1)} %get-tuple-element.59.tile_ref), channel_id=1, source_target_pairs={{0,16},{1,17},{2,18},{3,19},{4,20},{5,21},{6,22},{7,23},{8,24},{9,... | collective-permute-start | bytes 2359304 | tf_op jit(solution)/shard_map/ppermute | solution.py:503
  12.1 1.1 %tile.1 = (f32[512,256]{1,0:T(8,128)S(1)}, f32[512,256]{1,0:T(8,128)S(1)}, f32[512,256]{1,0:T(8,128)S(1)}) custom-call(bf16[512,384]{1,0:T(8,128)(2,1)S(1)} %bitcast.6, bf16[2,512,384]{2,1,0:T(8,128)(2,1)S(1)} %get-tuple-element.59.tile_ref, s32[256,800]{1,0:T(8,128)S(1)} %get-tuple-element.60.dist_ref.rest_3_, s32[6,128]{1,0:T(8,128)S(1)} %get-tuple-element.61.reach_ref.rest_4_), custom_call_target="tpu_custom_call" | custom-call | tf_op jit(solution)/shard_map/tile/pallas_call | solution.py:447
  13.2 0.0 collective-permute-done.in_ref
  13.2 0.0 collective-permute-done.3.corner_ref
  13.2 1.7 %collective-permute-done.1.row_ref = bf16[2,2,64,384]{3,2,1,0:T(8,128)(2,1)S(1)} collective-permute-done((bf16[2,2,64,384]{3,2,1,0:T(8,128)(2,1)S(1)}, bf16[2,2,64,384]{3,2,1,0:T(8,128)(2,1)S(1)}, u32[]{:S(2)}, u32[]{:S(2)}) %collective-permute-start.1) | collective-permute-done | bytes 196640 | tf_op jit(solution)/shard_map/ppermute | solution.py:459
  14.9 0.2 collective-permute-done.2.col_ref
  15.1 1.3 %collective-permute-start.5 = (bf16[2,288,384]{2,1,0:T(8,128)(2,1)S(1)}, bf16[2,288,384]{2,1,0:T(8,128)(2,1)S(1)}, u32[]{:S(2)}, u32[]{:S(2)}) collective-permute-start(bf16[2,288,384]{2,1,0:T(8,128)(2,1)S(1)} %edges.1.edge_ref), channel_id=1, source_target_pairs={{0,16},{1,17},{2,18},{3,19},{4,20},{5,21},{6,22},{7,23},{8,24},{9,... | collective-permute-start | bytes 1327112 | tf_op jit(solution)/shard_map/ppermute | solution.py:521
  16.4 1.5 %collective-permute-start.8 = (bf16[96,768]{1,0:T(8,128)(2,1)S(1)}, bf16[96,768]{1,0:T(8,128)(2,1)S(1)}, u32[]{:S(2)}, u32[]{:S(2)}) collective-permute-start(bf16[96,768]{1,0:T(8,128)(2,1)S(1)} %lone.1.refs_0_), channel_id=1, source_target_pairs={{0,12},{4,8},{8,4},{12,0},{1,13},{5,9},{9,5},{13,1},{2,14},{6,10},... | collective-permute-start | bytes 442376 | tf_op jit(solution)/shard_map/ppermute | solution.py:459
  17.9 0.6 %collective-permute-start.7 = (bf16[96,768]{1,0:T(8,128)(2,1)S(1)}, bf16[96,768]{1,0:T(8,128)(2,1)S(1)}, u32[]{:S(2)}, u32[]{:S(2)}) collective-permute-start(bf16[96,768]{1,0:T(8,128)(2,1)S(1)} %lone.1.refs_0_), channel_id=1, source_target_pairs={{0,8},{4,12},{8,0},{12,4},{1,9},{5,13},{9,1},{13,5},{2,10},{6,14},... | collective-permute-start | bytes 442376 | tf_op jit(solution)/shard_map/ppermute | solution.py:459
  18.6 1.4 %collective-permute-start.6 = (bf16[96,768]{1,0:T(8,128)(2,1)S(1)}, bf16[96,768]{1,0:T(8,128)(2,1)S(1)}, u32[]{:S(2)}, u32[]{:S(2)}) collective-permute-start(bf16[96,768]{1,0:T(8,128)(2,1)S(1)} %lone.1.refs_0_), channel_id=1, source_target_pairs={{0,4},{4,0},{8,12},{12,8},{1,5},{5,1},{9,13},{13,9},{2,6},{6,2},{1... | collective-permute-start | bytes 442376 | tf_op jit(solution)/shard_map/ppermute | solution.py:459
  20.0 0.0 collective-permute-done.5.first_edge_ref
  20.0 0.0 collective-permute-done.4.first_tile_ref
  20.0 1.0 %rest.3 = bf16[128,384]{1,0:T(8,128)(2,1)S(1)} custom-call(bf16[512,384]{1,0:T(8,128)(2,1)S(1)} %bitcast.7, bf16[2,288,384]{2,1,0:T(8,128)(2,1)S(1)} %edges.1.edge_ref, bf16[2,512,384]{2,1,0:T(8,128)(2,1)S(1)} %collective-permute-done.4.first_tile_ref, bf16[2,288,384]{2,1,0:T(8,128)(2,1)S(1)} %collective-permute-done.5.first_edge_ref, ...), custom_call_target="tpu_custom_call" | custom-call | tf_op jit(solution)/shard_map/rest/pallas_call | solution.py:447
  21.0 0.4 %collective-permute-start.9 = (bf16[128,384]{1,0:T(8,128)(2,1)S(1)}, bf16[128,384]{1,0:T(8,128)(2,1)S(1)}, u32[]{:S(2)}, u32[]{:S(2)}) collective-permute-start(bf16[128,384]{1,0:T(8,128)(2,1)S(1)} %rest.3), channel_id=1, source_target_pairs={{0,2},{1,3},{2,0},{3,1},{4,6},{5,7},{6,4},{7,5},{8,10},{9,11},{10,... | collective-permute-start | bytes 294920 | tf_op jit(solution)/shard_map/ppermute | solution.py:459
  21.4 1.4 %rest.4 = (bf16[128,384]{1,0:T(8,128)(2,1)S(1)}, bf16[128,384]{1,0:T(8,128)(2,1)S(1)}) custom-call(bf16[512,384]{1,0:T(8,128)(2,1)S(1)} %bitcast.8, bf16[2,288,384]{2,1,0:T(8,128)(2,1)S(1)} %edges.1.edge_ref, bf16[2,512,384]{2,1,0:T(8,128)(2,1)S(1)} %collective-permute-done.4.first_tile_ref, bf16[2,288,384]{2,1,0:T(8,128)(2,1)S(1)} %collective-permute-done.5.first_edge_ref, ...), custom_call_target="tpu_custom_call" | custom-call | tf_op jit(solution)/shard_map/rest/pallas_call | solution.py:447
  22.7 0.0 copy-start
  22.8 0.7 %collective-permute-done.8.refs_3_ = bf16[96,768]{1,0:T(8,128)(2,1)S(1)} collective-permute-done((bf16[96,768]{1,0:T(8,128)(2,1)S(1)}, bf16[96,768]{1,0:T(8,128)(2,1)S(1)}, u32[]{:S(2)}, u32[]{:S(2)}) %collective-permute-start.8) | collective-permute-done | bytes 147488 | tf_op jit(solution)/shard_map/ppermute | solution.py:459
  23.5 1.5 %collective-permute-done.7.refs_2_ = bf16[96,768]{1,0:T(8,128)(2,1)S(1)} collective-permute-done((bf16[96,768]{1,0:T(8,128)(2,1)S(1)}, bf16[96,768]{1,0:T(8,128)(2,1)S(1)}, u32[]{:S(2)}, u32[]{:S(2)}) %collective-permute-start.7) | collective-permute-done | bytes 147488 | tf_op jit(solution)/shard_map/ppermute | solution.py:459
  25.0 0.0 collective-permute-done.6.refs_1_
  25.0 0.5 %collective-permute-start.11 = (bf16[128,384]{1,0:T(8,128)(2,1)S(1)}, bf16[128,384]{1,0:T(8,128)(2,1)S(1)}, u32[]{:S(2)}, u32[]{:S(2)}) collective-permute-start(bf16[128,384]{1,0:T(8,128)(2,1)S(1)} %get-tuple-element.98), channel_id=1, source_target_pairs={{0,2},{1,3},{2,0},{3,1},{4,6},{5,7},{6,4},{7,5},{8,10},{9,11},{10,... | collective-permute-start | bytes 294920 | tf_op jit(solution)/shard_map/ppermute | solution.py:459
  25.4 0.1 stack.1.part_ref
  25.5 1.1 %collective-permute-done.9.got_ref = bf16[128,384]{1,0:T(8,128)(2,1)S(1)} collective-permute-done((bf16[128,384]{1,0:T(8,128)(2,1)S(1)}, bf16[128,384]{1,0:T(8,128)(2,1)S(1)}, u32[]{:S(2)}, u32[]{:S(2)}) %collective-permute-start.9) | collective-permute-done | bytes 98336 | tf_op jit(solution)/shard_map/ppermute | solution.py:459
  26.6 0.0 copy-done
  26.6 0.4 project.4
  26.9 1.7 %collective-permute-start.13 = (bf16[128,768]{1,0:T(8,128)(2,1)S(1)}, bf16[128,768]{1,0:T(8,128)(2,1)S(1)}, u32[]{:S(2)}, u32[]{:S(2)}) collective-permute-start(bf16[128,768]{1,0:T(8,128)(2,1)S(1)} %project.4), channel_id=1, source_target_pairs={{0,1},{1,0},{2,3},{3,2},{4,5},{5,4},{6,7},{7,6},{8,9},{9,8},{10,11... | collective-permute-start | bytes 589832 | tf_op jit(solution)/shard_map/ppermute | solution.py:459
  28.6 0.0 collective-permute-start.10
  28.6 0.9 %rest.5.own_ref = bf16[128,384]{1,0:T(8,128)(2,1)S(1)} custom-call(bf16[512,384]{1,0:T(8,128)(2,1)S(1)} %bitcast.9, bf16[2,288,384]{2,1,0:T(8,128)(2,1)S(1)} %edges.1.edge_ref, bf16[2,512,384]{2,1,0:T(8,128)(2,1)S(1)} %collective-permute-done.4.first_tile_ref, bf16[2,288,384]{2,1,0:T(8,128)(2,1)S(1)} %collective-permute-done.5.first_edge_ref, ...), custom_call_target="tpu_custom_call" | custom-call | flops 20000000000 | tf_op jit(solution)/shard_map/rest/pallas_call | solution.py:447
  29.6 1.0 %collective-permute-done.10.part_ref = bf16[384,768]{1,0:T(8,128)(2,1)S(1)} collective-permute-done((bf16[384,768]{1,0:T(8,128)(2,1)S(1)}, bf16[384,768]{1,0:T(8,128)(2,1)S(1)}, u32[]{:S(2)}, u32[]{:S(2)}) %collective-permute-start.10) | collective-permute-done | bytes 589856 | tf_op jit(solution)/shard_map/ppermute | solution.py:459
  30.6 0.4 project.5
  31.0 0.5 %collective-permute-start.12 = (bf16[128,768]{1,0:T(8,128)(2,1)S(1)}, bf16[128,768]{1,0:T(8,128)(2,1)S(1)}, u32[]{:S(2)}, u32[]{:S(2)}) collective-permute-start(bf16[128,768]{1,0:T(8,128)(2,1)S(1)} %project.5), channel_id=1, source_target_pairs={{0,1},{1,0},{2,3},{3,2},{4,5},{5,4},{6,7},{7,6},{8,9},{9,8},{10,11... | collective-permute-start | bytes 589832 | tf_op jit(solution)/shard_map/ppermute | solution.py:459
  31.5 0.0 collective-permute-done.11.got_ref
  31.5 0.4 project.6.mine_ref
  31.8 0.4 project.7.mine_ref
  32.2 1.8 %collective-permute-done.13.got_ref = bf16[128,768]{1,0:T(8,128)(2,1)S(1)} collective-permute-done((bf16[128,768]{1,0:T(8,128)(2,1)S(1)}, bf16[128,768]{1,0:T(8,128)(2,1)S(1)}, u32[]{:S(2)}, u32[]{:S(2)}) %collective-permute-start.13) | collective-permute-done | bytes 196640 | tf_op jit(solution)/shard_map/ppermute | solution.py:459
  34.0 0.7 %add.2.rest_0_ = bf16[128,1536]{1,0:T(8,128)(2,1)} custom-call(f32[128,768]{1,0:T(8,128)S(1)} %project.7.mine_ref, bf16[128,768]{1,0:T(8,128)(2,1)S(1)} %collective-permute-done.13.got_ref), custom_call_target="tpu_custom_call" | custom-call | tf_op jit(solution)/shard_map/add/pallas_call | solution.py:583
  34.7 3.4 %collective-permute-done.12.got_ref = bf16[128,768]{1,0:T(8,128)(2,1)S(1)} collective-permute-done((bf16[128,768]{1,0:T(8,128)(2,1)S(1)}, bf16[128,768]{1,0:T(8,128)(2,1)S(1)}, u32[]{:S(2)}, u32[]{:S(2)}) %collective-permute-start.12) | collective-permute-done | bytes 196640 | tf_op jit(solution)/shard_map/ppermute | solution.py:459
  38.1 0.7 %add.3 = bf16[128,1536]{1,0:T(8,128)(2,1)} custom-call(f32[128,768]{1,0:T(8,128)S(1)} %project.6.mine_ref, bf16[128,768]{1,0:T(8,128)(2,1)S(1)} %collective-permute-done.12.got_ref, bf16[128,1536]{1,0:T(8,128)(2,1)} %add.2.rest_0_), custom_call_target="tpu_custom_call", output_to_operand_aliasing={{}: (2, {})} | custom-call | tf_op jit(solution)/shard_map/add/pallas_call | solution.py:583
  (2 shorter events, 0.1 us)
Async XLA Ops:
  0.0 9.3 %copy-start.1 = (bf16[1,1,2,16,16,384]{5,4,3,2,1,0:T(8,128)(2,1)S(1)}, bf16[1,1,2,16,16,384]{5,4,3,2,1,0:T(8,128)(2,1)}, u32[]{:S(2)}) copy-start(bf16[1,1,2,16,16,384]{5,4,3,2,1,0:T(8,128)(2,1)} %param.6) | copy-start | bytes 1179652
  0.0 9.3 %copy-start.2 = (s32[3,2,2]{0,2,1:T(2,128)S(1)}, s32[3,2,2]{0,2,1:T(2,128)}, u32[]{:S(2)}) copy-start(s32[3,2,2]{0,2,1:T(2,128)} %param.11) | copy-start | bytes 148
  0.0 9.3 %copy-start.3 = (s32[3]{0:T(128)S(1)}, s32[3]{0:T(128)}, u32[]{:S(2)}) copy-start(s32[3]{0:T(128)} %radius_ref.1) | copy-start | bytes 40
  1.3 11.9 %collective-permute-start = (bf16[96,768]{1,0:T(8,128)(2,1)S(1)}, bf16[96,768]{1,0:T(8,128)(2,1)S(1)}, u32[]{:S(2)}, u32[]{:S(2)}) collective-permute-start(bf16[96,768]{1,0:T(8,128)(2,1)S(1)} %get-tuple-element.52), channel_id=1, source_target_pairs={{0,2},{1,3},{2,0},{3,1},{4,6},{5,7},{6,4},{7,5},{8,10},{9,11},{10,... | collective-permute-start | bytes 442376 | tf_op jit(solution)/shard_map/ppermute | solution.py:459
  5.7 7.4 %collective-permute-start.3 = (bf16[2,2,16,384]{3,2,1,0:T(8,128)(2,1)S(1)}, bf16[2,2,16,384]{3,2,1,0:T(8,128)(2,1)S(1)}, u32[]{:S(2)}, u32[]{:S(2)}) collective-permute-start(bf16[2,2,16,384]{3,2,1,0:T(8,128)(2,1)S(1)} %get-tuple-element.71), channel_id=1, source_target_pairs={{0,12},{4,8},{8,4},{12,0},{1,13},{5,9},{9,5},{13,1},{2,14},{6,10},... | collective-permute-start | bytes 147464 | tf_op jit(solution)/shard_map/ppermute | solution.py:459
  8.3 6.6 %collective-permute-start.1 = (bf16[2,2,64,384]{3,2,1,0:T(8,128)(2,1)S(1)}, bf16[2,2,64,384]{3,2,1,0:T(8,128)(2,1)S(1)}, u32[]{:S(2)}, u32[]{:S(2)}) collective-permute-start(bf16[2,2,64,384]{3,2,1,0:T(8,128)(2,1)S(1)} %get-tuple-element.69), channel_id=1, source_target_pairs={{0,8},{4,12},{8,0},{12,4},{1,9},{5,13},{9,1},{13,5},{2,10},{6,14},... | collective-permute-start | bytes 589832 | tf_op jit(solution)/shard_map/ppermute | solution.py:459
  8.8 6.3 %collective-permute-start.2 = (bf16[2,2,64,384]{3,2,1,0:T(8,128)(2,1)S(1)}, bf16[2,2,64,384]{3,2,1,0:T(8,128)(2,1)S(1)}, u32[]{:S(2)}, u32[]{:S(2)}) collective-permute-start(bf16[2,2,64,384]{3,2,1,0:T(8,128)(2,1)S(1)} %get-tuple-element.70), channel_id=1, source_target_pairs={{0,4},{4,0},{8,12},{12,8},{1,5},{5,1},{9,13},{13,9},{2,6},{6,2},{1... | collective-permute-start | bytes 589832 | tf_op jit(solution)/shard_map/ppermute | solution.py:459
  10.7 9.3 %collective-permute-start.4 = (bf16[2,512,384]{2,1,0:T(8,128)(2,1)S(1)}, bf16[2,512,384]{2,1,0:T(8,128)(2,1)S(1)}, u32[]{:S(2)}, u32[]{:S(2)}) collective-permute-start(bf16[2,512,384]{2,1,0:T(8,128)(2,1)S(1)} %get-tuple-element.59.tile_ref), channel_id=1, source_target_pairs={{0,16},{1,17},{2,18},{3,19},{4,20},{5,21},{6,22},{7,23},{8,24},{9,... | collective-permute-start | bytes 2359304 | tf_op jit(solution)/shard_map/ppermute | solution.py:503
  15.1 4.9 %collective-permute-start.5 = (bf16[2,288,384]{2,1,0:T(8,128)(2,1)S(1)}, bf16[2,288,384]{2,1,0:T(8,128)(2,1)S(1)}, u32[]{:S(2)}, u32[]{:S(2)}) collective-permute-start(bf16[2,288,384]{2,1,0:T(8,128)(2,1)S(1)} %edges.1.edge_ref), channel_id=1, source_target_pairs={{0,16},{1,17},{2,18},{3,19},{4,20},{5,21},{6,22},{7,23},{8,24},{9,... | collective-permute-start | bytes 1327112 | tf_op jit(solution)/shard_map/ppermute | solution.py:521
  16.4 7.1 %collective-permute-start.8 = (bf16[96,768]{1,0:T(8,128)(2,1)S(1)}, bf16[96,768]{1,0:T(8,128)(2,1)S(1)}, u32[]{:S(2)}, u32[]{:S(2)}) collective-permute-start(bf16[96,768]{1,0:T(8,128)(2,1)S(1)} %lone.1.refs_0_), channel_id=1, source_target_pairs={{0,12},{4,8},{8,4},{12,0},{1,13},{5,9},{9,5},{13,1},{2,14},{6,10},... | collective-permute-start | bytes 442376 | tf_op jit(solution)/shard_map/ppermute | solution.py:459
  17.9 7.0 %collective-permute-start.7 = (bf16[96,768]{1,0:T(8,128)(2,1)S(1)}, bf16[96,768]{1,0:T(8,128)(2,1)S(1)}, u32[]{:S(2)}, u32[]{:S(2)}) collective-permute-start(bf16[96,768]{1,0:T(8,128)(2,1)S(1)} %lone.1.refs_0_), channel_id=1, source_target_pairs={{0,8},{4,12},{8,0},{12,4},{1,9},{5,13},{9,1},{13,5},{2,10},{6,14},... | collective-permute-start | bytes 442376 | tf_op jit(solution)/shard_map/ppermute | solution.py:459
  18.6 6.4 %collective-permute-start.6 = (bf16[96,768]{1,0:T(8,128)(2,1)S(1)}, bf16[96,768]{1,0:T(8,128)(2,1)S(1)}, u32[]{:S(2)}, u32[]{:S(2)}) collective-permute-start(bf16[96,768]{1,0:T(8,128)(2,1)S(1)} %lone.1.refs_0_), channel_id=1, source_target_pairs={{0,4},{4,0},{8,12},{12,8},{1,5},{5,1},{9,13},{13,9},{2,6},{6,2},{1... | collective-permute-start | bytes 442376 | tf_op jit(solution)/shard_map/ppermute | solution.py:459
  21.0 5.6 %collective-permute-start.9 = (bf16[128,384]{1,0:T(8,128)(2,1)S(1)}, bf16[128,384]{1,0:T(8,128)(2,1)S(1)}, u32[]{:S(2)}, u32[]{:S(2)}) collective-permute-start(bf16[128,384]{1,0:T(8,128)(2,1)S(1)} %rest.3), channel_id=1, source_target_pairs={{0,2},{1,3},{2,0},{3,1},{4,6},{5,7},{6,4},{7,5},{8,10},{9,11},{10,... | collective-permute-start | bytes 294920 | tf_op jit(solution)/shard_map/ppermute | solution.py:459
  22.7 3.8 %copy-start = (bf16[384,1536]{1,0:T(8,128)(2,1)S(1)}, bf16[384,1536]{1,0:T(8,128)(2,1)}, u32[]{:S(2)}) copy-start(bf16[384,1536]{1,0:T(8,128)(2,1)} %w_ref.9) | copy-start | bytes 3538948
  25.0 6.5 %collective-permute-start.11 = (bf16[128,384]{1,0:T(8,128)(2,1)S(1)}, bf16[128,384]{1,0:T(8,128)(2,1)S(1)}, u32[]{:S(2)}, u32[]{:S(2)}) collective-permute-start(bf16[128,384]{1,0:T(8,128)(2,1)S(1)} %get-tuple-element.98), channel_id=1, source_target_pairs={{0,2},{1,3},{2,0},{3,1},{4,6},{5,7},{6,4},{7,5},{8,10},{9,11},{10,... | collective-permute-start | bytes 294920 | tf_op jit(solution)/shard_map/ppermute | solution.py:459
  26.9 7.1 %collective-permute-start.13 = (bf16[128,768]{1,0:T(8,128)(2,1)S(1)}, bf16[128,768]{1,0:T(8,128)(2,1)S(1)}, u32[]{:S(2)}, u32[]{:S(2)}) collective-permute-start(bf16[128,768]{1,0:T(8,128)(2,1)S(1)} %project.4), channel_id=1, source_target_pairs={{0,1},{1,0},{2,3},{3,2},{4,5},{5,4},{6,7},{7,6},{8,9},{9,8},{10,11... | collective-permute-start | bytes 589832 | tf_op jit(solution)/shard_map/ppermute | solution.py:459
  28.6 2.0 %collective-permute-start.10 = (bf16[384,768]{1,0:T(8,128)(2,1)S(1)}, bf16[384,768]{1,0:T(8,128)(2,1)S(1)}, u32[]{:S(2)}, u32[]{:S(2)}) collective-permute-start(bf16[384,768]{1,0:T(8,128)(2,1)S(1)} %stack.1.part_ref), channel_id=1, source_target_pairs={{0,16},{16,0},{1,17},{17,1},{2,18},{18,2},{3,19},{19,3},{4,20},{20... | collective-permute-start | bytes 1769480 | tf_op jit(solution)/shard_map/ppermute | solution.py:459
  31.0 7.2 %collective-permute-start.12 = (bf16[128,768]{1,0:T(8,128)(2,1)S(1)}, bf16[128,768]{1,0:T(8,128)(2,1)S(1)}, u32[]{:S(2)}, u32[]{:S(2)}) collective-permute-start(bf16[128,768]{1,0:T(8,128)(2,1)S(1)} %project.5), channel_id=1, source_target_pairs={{0,1},{1,0},{2,3},{3,2},{4,5},{5,4},{6,7},{7,6},{8,9},{9,8},{10,11... | collective-permute-start | bytes 589832 | tf_op jit(solution)/shard_map/ppermute | solution.py:459

commit v2 on v1

--- a/solution.py
+++ b/solution.py
@@ -513,10 +513,10 @@
         heads=heads,
     )
     lone, state = lax.optimization_barrier((lone, state))
-    lone = call(copy_kernel, part_shape, [vmem], lone, name="lone", flops=20 * 10**9)
+    lone = call(copy_kernel, part_shape, [vmem], lone, name="lone", flops=2 * 10**9)
     lone, state, faces = lax.optimization_barrier((lone, state, faces))
     edge = call(
-        edge_kernel, shape((2, count - tokens, channels), bf16), [vmem] * 3, *faces, name="edges"
+        edge_kernel, shape((2, count - tokens, channels), bf16), [vmem] * 3, *faces, name="edges", flops=20 * 10**9
     )
     first_edge = lax.ppermute(edge, "tm", [(0, 1)])
     parts = [lone] + [flipped(lone, "tile", flip) for flip in range(1, tiles)]
@@ -544,7 +544,8 @@
     state, for_side = lax.optimization_barrier((state, for_side))
     for_far, own_side = rest(state, 2, 1)
     got_far = flipped(for_far, "head", 2)
-    parts, own_side = lax.optimization_barrier((parts, own_side))
+    parts, own_side = lax.optimization_barrier((parts[::-1], own_side))
+    parts = parts[::-1]
     here = call(
         stack_kernel, shape((depth, broad), bf16), [vmem] * tiles, *parts, name="stack"
     )

time: 39 us -> 39.2 us (level)
  starting transfers between devices: 16.9 us -> 17.3 us
    ppermute x12, starting transfers between devices: 14.3 us -> 14.7 us  [flipped(): lax.ppermute(value, axis, [(i, i ^ flip) for i in range(lax.axis_size(axi...]
  transfers between devices with their start and end apart: 14 -> 14, of which waited for: 8 -> 8; matrix products, arithmetic and copies ran while one was open for 0% -> 0% of each run, Pallas kernels for 22% -> 21%
where the time goes in v2:
time: 39.2 us; the launch traced here: 39 us
  starting transfers between devices  17.3 us (44%)
  waiting for transfers between devices  11.2 us (29%)
  Pallas kernels  10.3 us (26%)
    ppermute x12, starting transfers between devices, flipped(): lax.ppermute(value, axis, [(i, i ^ flip) for i in range(lax.axis_size(axi...  14.7 us
    ppermute x12, waiting for transfers between devices, flipped(): lax.ppermute(value, axis, [(i, i ^ flip) for i in range(lax.axis_size(axi...  11.2 us
    pallas_call x14, Pallas kernels, call(): pl.pallas_call(functools.partial(kernel, **keys_of) if keys_of else kerne...  8.91 us
    pallas_call x2, Pallas kernels, two_by_two(): pl.pallas_call(functools.partial(add_kernel, flip=flip), out_shape=shape(...  1.42 us
    ppermute x1, starting transfers between devices, two_by_two(): first_tile = lax.ppermute(tile, 'tm', [(0, 1)])  1.34 us
    ppermute x1, starting transfers between devices, two_by_two(): first_edge = lax.ppermute(edge, 'tm', [(0, 1)])  1.32 us
  transfers between devices with their start and end apart: 14, of which 8 were waited for; matrix products, arithmetic and copies ran while one was open for 0% of the time, Pallas kernels for 21%

profile of v2, /device:TPU:0, one launch (start us, length us, event | category | flops | bytes accessed | tf_op | source)
XLA Modules:
  0.0 39.0 jit_solution(9660425531889583176)
XLA Ops:
  0.0 0.0 copy-start.1
  0.0 0.0 copy-start.2
  0.0 0.0 copy-start.3
  0.0 1.3 %load.1 = (bf16[2,512,384]{2,1,0:T(8,128)(2,1)S(1)}, bf16[96,768]{1,0:T(8,128)(2,1)S(1)}) custom-call(bf16[512,384]{1,0:T(8,128)(2,1)} %bitcast.11, bf16[512,384]{1,0:T(8,128)(2,1)} %bitcast.12, bf16[384,1536]{1,0:T(8,128)(2,1)} %w_ref.9), custom_call_target="tpu_custom_call" | custom-call | tf_op jit(solution)/shard_map/load/pallas_call | solution.py:447
  1.3 4.1 %collective-permute-start = (bf16[96,768]{1,0:T(8,128)(2,1)S(1)}, bf16[96,768]{1,0:T(8,128)(2,1)S(1)}, u32[]{:S(2)}, u32[]{:S(2)}) collective-permute-start(bf16[96,768]{1,0:T(8,128)(2,1)S(1)} %get-tuple-element.52), channel_id=1, source_target_pairs={{0,2},{1,3},{2,0},{3,1},{4,6},{5,7},{6,4},{7,5},{8,10},{9,11},{10,... | collective-permute-start | bytes 442376 | tf_op jit(solution)/shard_map/ppermute | solution.py:459
  5.4 0.3 faces.1
  5.7 1.6 %collective-permute-start.1 = (bf16[2,2,64,384]{3,2,1,0:T(8,128)(2,1)S(1)}, bf16[2,2,64,384]{3,2,1,0:T(8,128)(2,1)S(1)}, u32[]{:S(2)}, u32[]{:S(2)}) collective-permute-start(bf16[2,2,64,384]{3,2,1,0:T(8,128)(2,1)S(1)} %get-tuple-element.69), channel_id=1, source_target_pairs={{0,8},{4,12},{8,0},{12,4},{1,9},{5,13},{9,1},{13,5},{2,10},{6,14},... | collective-permute-start | bytes 589832 | tf_op jit(solution)/shard_map/ppermute | solution.py:459
  7.3 1.5 %collective-permute-start.2 = (bf16[2,2,64,384]{3,2,1,0:T(8,128)(2,1)S(1)}, bf16[2,2,64,384]{3,2,1,0:T(8,128)(2,1)S(1)}, u32[]{:S(2)}, u32[]{:S(2)}) collective-permute-start(bf16[2,2,64,384]{3,2,1,0:T(8,128)(2,1)S(1)} %get-tuple-element.70), channel_id=1, source_target_pairs={{0,4},{4,0},{8,12},{12,8},{1,5},{5,1},{9,13},{13,9},{2,6},{6,2},{1... | collective-permute-start | bytes 589832 | tf_op jit(solution)/shard_map/ppermute | solution.py:459
  8.8 0.5 %collective-permute-start.3 = (bf16[2,2,16,384]{3,2,1,0:T(8,128)(2,1)S(1)}, bf16[2,2,16,384]{3,2,1,0:T(8,128)(2,1)S(1)}, u32[]{:S(2)}, u32[]{:S(2)}) collective-permute-start(bf16[2,2,16,384]{3,2,1,0:T(8,128)(2,1)S(1)} %get-tuple-element.71), channel_id=1, source_target_pairs={{0,12},{4,8},{8,4},{12,0},{1,13},{5,9},{9,5},{13,1},{2,14},{6,10},... | collective-permute-start | bytes 147464 | tf_op jit(solution)/shard_map/ppermute | solution.py:459
  9.3 0.0 copy-done.1
  9.3 0.0 copy-done.2
  9.3 0.0 copy-done.3
  9.3 1.4 %begin.1 = (f32[512,128]{1,0:T(8,128)S(1)}, f32[512,128]{1,0:T(8,128)S(1)}, f32[512,128]{1,0:T(8,128)S(1)}, s32[256,800]{1,0:T(8,128)S(1)}, s32[6,128]{1,0:T(8,128)S(1)}) custom-call(s32[3]{0:T(128)S(1)} %copy-done.3, s32[2,2,3]{2,1,0:T(2,128)S(1)} %bitcast.10, bf16[512,384]{1,0:T(8,128)(2,1)S(1)} %bitcast.5, bf16[2,512,384]{2,1,0:T(8,128)(2,1)S(1)} %get-tuple-element.59.tile_ref), custom_call_target="tpu_custom_call" | custom-call | tf_op jit(solution)/shard_map/begin/pallas_call | solution.py:447
  10.7 1.3 %collective-permute-start.4 = (bf16[2,512,384]{2,1,0:T(8,128)(2,1)S(1)}, bf16[2,512,384]{2,1,0:T(8,128)(2,1)S(1)}, u32[]{:S(2)}, u32[]{:S(2)}) collective-permute-start(bf16[2,512,384]{2,1,0:T(8,128)(2,1)S(1)} %get-tuple-element.59.tile_ref), channel_id=1, source_target_pairs={{0,16},{1,17},{2,18},{3,19},{4,20},{5,21},{6,22},{7,23},{8,24},{9,... | collective-permute-start | bytes 2359304 | tf_op jit(solution)/shard_map/ppermute | solution.py:503
  12.1 1.1 %tile.1 = (f32[512,256]{1,0:T(8,128)S(1)}, f32[512,256]{1,0:T(8,128)S(1)}, f32[512,256]{1,0:T(8,128)S(1)}) custom-call(bf16[512,384]{1,0:T(8,128)(2,1)S(1)} %bitcast.6, bf16[2,512,384]{2,1,0:T(8,128)(2,1)S(1)} %get-tuple-element.59.tile_ref, s32[256,800]{1,0:T(8,128)S(1)} %get-tuple-element.60.dist_ref.rest_3_, s32[6,128]{1,0:T(8,128)S(1)} %get-tuple-element.61.reach_ref.rest_4_), custom_call_target="tpu_custom_call" | custom-call | tf_op jit(solution)/shard_map/tile/pallas_call | solution.py:447
  13.2 0.0 collective-permute-done.in_ref
  13.2 1.2 %collective-permute-done.3.corner_ref = bf16[2,2,16,384]{3,2,1,0:T(8,128)(2,1)S(1)} collective-permute-done((bf16[2,2,16,384]{3,2,1,0:T(8,128)(2,1)S(1)}, bf16[2,2,16,384]{3,2,1,0:T(8,128)(2,1)S(1)}, u32[]{:S(2)}, u32[]{:S(2)}) %collective-permute-start.3) | collective-permute-done | bytes 49184 | tf_op jit(solution)/shard_map/ppermute | solution.py:459
  14.4 0.0 collective-permute-done.1.row_ref
  14.4 0.0 collective-permute-done.2.col_ref
  14.5 1.3 %collective-permute-start.5 = (bf16[2,288,384]{2,1,0:T(8,128)(2,1)S(1)}, bf16[2,288,384]{2,1,0:T(8,128)(2,1)S(1)}, u32[]{:S(2)}, u32[]{:S(2)}) collective-permute-start(bf16[2,288,384]{2,1,0:T(8,128)(2,1)S(1)} %edges.1.edge_ref), channel_id=1, source_target_pairs={{0,16},{1,17},{2,18},{3,19},{4,20},{5,21},{6,22},{7,23},{8,24},{9,... | collective-permute-start | bytes 1327112 | tf_op jit(solution)/shard_map/ppermute | solution.py:521
  15.8 1.6 %collective-permute-start.8 = (bf16[96,768]{1,0:T(8,128)(2,1)S(1)}, bf16[96,768]{1,0:T(8,128)(2,1)S(1)}, u32[]{:S(2)}, u32[]{:S(2)}) collective-permute-start(bf16[96,768]{1,0:T(8,128)(2,1)S(1)} %lone.1.refs_0_), channel_id=1, source_target_pairs={{0,4},{4,0},{8,12},{12,8},{1,5},{5,1},{9,13},{13,9},{2,6},{6,2},{1... | collective-permute-start | bytes 442376 | tf_op jit(solution)/shard_map/ppermute | solution.py:459
  17.3 1.5 %collective-permute-start.7 = (bf16[96,768]{1,0:T(8,128)(2,1)S(1)}, bf16[96,768]{1,0:T(8,128)(2,1)S(1)}, u32[]{:S(2)}, u32[]{:S(2)}) collective-permute-start(bf16[96,768]{1,0:T(8,128)(2,1)S(1)} %lone.1.refs_0_), channel_id=1, source_target_pairs={{0,8},{4,12},{8,0},{12,4},{1,9},{5,13},{9,1},{13,5},{2,10},{6,14},... | collective-permute-start | bytes 442376 | tf_op jit(solution)/shard_map/ppermute | solution.py:459
  18.9 0.5 %collective-permute-start.6 = (bf16[96,768]{1,0:T(8,128)(2,1)S(1)}, bf16[96,768]{1,0:T(8,128)(2,1)S(1)}, u32[]{:S(2)}, u32[]{:S(2)}) collective-permute-start(bf16[96,768]{1,0:T(8,128)(2,1)S(1)} %lone.1.refs_0_), channel_id=1, source_target_pairs={{0,12},{4,8},{8,4},{12,0},{1,13},{5,9},{9,5},{13,1},{2,14},{6,10},... | collective-permute-start | bytes 442376 | tf_op jit(solution)/shard_map/ppermute | solution.py:459
  19.3 0.0 collective-permute-done.5.first_edge_ref
  19.3 0.0 collective-permute-done.4.first_tile_ref
  19.3 1.0 %rest.3 = bf16[128,384]{1,0:T(8,128)(2,1)S(1)} custom-call(bf16[512,384]{1,0:T(8,128)(2,1)S(1)} %bitcast.7, bf16[2,288,384]{2,1,0:T(8,128)(2,1)S(1)} %edges.1.edge_ref, bf16[2,512,384]{2,1,0:T(8,128)(2,1)S(1)} %collective-permute-done.4.first_tile_ref, bf16[2,288,384]{2,1,0:T(8,128)(2,1)S(1)} %collective-permute-done.5.first_edge_ref, ...), custom_call_target="tpu_custom_call" | custom-call | tf_op jit(solution)/shard_map/rest/pallas_call | solution.py:447
  20.3 0.4 collective-permute-start.9
  20.7 1.4 %rest.4 = (bf16[128,384]{1,0:T(8,128)(2,1)S(1)}, bf16[128,384]{1,0:T(8,128)(2,1)S(1)}) custom-call(bf16[512,384]{1,0:T(8,128)(2,1)S(1)} %bitcast.8, bf16[2,288,384]{2,1,0:T(8,128)(2,1)S(1)} %edges.1.edge_ref, bf16[2,512,384]{2,1,0:T(8,128)(2,1)S(1)} %collective-permute-done.4.first_tile_ref, bf16[2,288,384]{2,1,0:T(8,128)(2,1)S(1)} %collective-permute-done.5.first_edge_ref, ...), custom_call_target="tpu_custom_call" | custom-call | tf_op jit(solution)/shard_map/rest/pallas_call | solution.py:447
  22.1 0.0 copy-start
  22.1 0.1 collective-permute-done.8.refs_1_
  22.1 1.4 %collective-permute-done.7.refs_2_ = bf16[96,768]{1,0:T(8,128)(2,1)S(1)} collective-permute-done((bf16[96,768]{1,0:T(8,128)(2,1)S(1)}, bf16[96,768]{1,0:T(8,128)(2,1)S(1)}, u32[]{:S(2)}, u32[]{:S(2)}) %collective-permute-start.7) | collective-permute-done | bytes 147488 | tf_op jit(solution)/shard_map/ppermute | solution.py:459
  23.5 1.4 %collective-permute-done.6.refs_3_ = bf16[96,768]{1,0:T(8,128)(2,1)S(1)} collective-permute-done((bf16[96,768]{1,0:T(8,128)(2,1)S(1)}, bf16[96,768]{1,0:T(8,128)(2,1)S(1)}, u32[]{:S(2)}, u32[]{:S(2)}) %collective-permute-start.6) | collective-permute-done | bytes 147488 | tf_op jit(solution)/shard_map/ppermute | solution.py:459
  25.0 0.3 collective-permute-start.11
  25.2 0.1 stack.1.part_ref
  25.3 0.6 %collective-permute-done.9.got_ref = bf16[128,384]{1,0:T(8,128)(2,1)S(1)} collective-permute-done((bf16[128,384]{1,0:T(8,128)(2,1)S(1)}, bf16[128,384]{1,0:T(8,128)(2,1)S(1)}, u32[]{:S(2)}, u32[]{:S(2)}) %collective-permute-start.9) | collective-permute-done | bytes 98336 | tf_op jit(solution)/shard_map/ppermute | solution.py:459
  25.9 0.0 copy-done
  25.9 0.4 project.4
  26.3 2.7 %collective-permute-start.13 = (bf16[128,768]{1,0:T(8,128)(2,1)S(1)}, bf16[128,768]{1,0:T(8,128)(2,1)S(1)}, u32[]{:S(2)}, u32[]{:S(2)}) collective-permute-start(bf16[128,768]{1,0:T(8,128)(2,1)S(1)} %project.4), channel_id=1, source_target_pairs={{0,1},{1,0},{2,3},{3,2},{4,5},{5,4},{6,7},{7,6},{8,9},{9,8},{10,11... | collective-permute-start | bytes 589832 | tf_op jit(solution)/shard_map/ppermute | solution.py:459
  28.9 0.0 collective-permute-start.10
  28.9 0.9 %rest.5.own_ref = bf16[128,384]{1,0:T(8,128)(2,1)S(1)} custom-call(bf16[512,384]{1,0:T(8,128)(2,1)S(1)} %bitcast.9, bf16[2,288,384]{2,1,0:T(8,128)(2,1)S(1)} %edges.1.edge_ref, bf16[2,512,384]{2,1,0:T(8,128)(2,1)S(1)} %collective-permute-done.4.first_tile_ref, bf16[2,288,384]{2,1,0:T(8,128)(2,1)S(1)} %collective-permute-done.5.first_edge_ref, ...), custom_call_target="tpu_custom_call" | custom-call | flops 20000000000 | tf_op jit(solution)/shard_map/rest/pallas_call | solution.py:447
  29.9 1.0 %collective-permute-done.10.part_ref = bf16[384,768]{1,0:T(8,128)(2,1)S(1)} collective-permute-done((bf16[384,768]{1,0:T(8,128)(2,1)S(1)}, bf16[384,768]{1,0:T(8,128)(2,1)S(1)}, u32[]{:S(2)}, u32[]{:S(2)}) %collective-permute-start.10) | collective-permute-done | bytes 589856 | tf_op jit(solution)/shard_map/ppermute | solution.py:459
  30.9 0.4 project.5
  31.3 0.1 collective-permute-start.12
  31.4 0.0 collective-permute-done.11.got_ref
  31.4 0.4 project.6.mine_ref
  31.8 0.4 project.7.mine_ref
  32.2 1.1 %collective-permute-done.13.got_ref = bf16[128,768]{1,0:T(8,128)(2,1)S(1)} collective-permute-done((bf16[128,768]{1,0:T(8,128)(2,1)S(1)}, bf16[128,768]{1,0:T(8,128)(2,1)S(1)}, u32[]{:S(2)}, u32[]{:S(2)}) %collective-permute-start.13) | collective-permute-done | bytes 196640 | tf_op jit(solution)/shard_map/ppermute | solution.py:459
  33.3 0.7 %add.2.rest_0_ = bf16[128,1536]{1,0:T(8,128)(2,1)} custom-call(f32[128,768]{1,0:T(8,128)S(1)} %project.7.mine_ref, bf16[128,768]{1,0:T(8,128)(2,1)S(1)} %collective-permute-done.13.got_ref), custom_call_target="tpu_custom_call" | custom-call | tf_op jit(solution)/shard_map/add/pallas_call | solution.py:584
  34.0 4.3 %collective-permute-done.12.got_ref = bf16[128,768]{1,0:T(8,128)(2,1)S(1)} collective-permute-done((bf16[128,768]{1,0:T(8,128)(2,1)S(1)}, bf16[128,768]{1,0:T(8,128)(2,1)S(1)}, u32[]{:S(2)}, u32[]{:S(2)}) %collective-permute-start.12) | collective-permute-done | bytes 196640 | tf_op jit(solution)/shard_map/ppermute | solution.py:459
  38.3 0.7 %add.3 = bf16[128,1536]{1,0:T(8,128)(2,1)} custom-call(f32[128,768]{1,0:T(8,128)S(1)} %project.6.mine_ref, bf16[128,768]{1,0:T(8,128)(2,1)S(1)} %collective-permute-done.12.got_ref, bf16[128,1536]{1,0:T(8,128)(2,1)} %add.2.rest_0_), custom_call_target="tpu_custom_call", output_to_operand_aliasing={{}: (2, {})} | custom-call | tf_op jit(solution)/shard_map/add/pallas_call | solution.py:584
  (2 shorter events, 0.1 us)
Async XLA Ops:
  0.0 9.3 %copy-start.1 = (bf16[1,1,2,16,16,384]{5,4,3,2,1,0:T(8,128)(2,1)S(1)}, bf16[1,1,2,16,16,384]{5,4,3,2,1,0:T(8,128)(2,1)}, u32[]{:S(2)}) copy-start(bf16[1,1,2,16,16,384]{5,4,3,2,1,0:T(8,128)(2,1)} %param.6) | copy-start | bytes 1179652
  0.0 9.3 %copy-start.2 = (s32[3,2,2]{0,2,1:T(2,128)S(1)}, s32[3,2,2]{0,2,1:T(2,128)}, u32[]{:S(2)}) copy-start(s32[3,2,2]{0,2,1:T(2,128)} %param.11) | copy-start | bytes 148
  0.0 9.3 %copy-start.3 = (s32[3]{0:T(128)S(1)}, s32[3]{0:T(128)}, u32[]{:S(2)}) copy-start(s32[3]{0:T(128)} %radius_ref.1) | copy-start | bytes 40
  1.3 11.9 %collective-permute-start = (bf16[96,768]{1,0:T(8,128)(2,1)S(1)}, bf16[96,768]{1,0:T(8,128)(2,1)S(1)}, u32[]{:S(2)}, u32[]{:S(2)}) collective-permute-start(bf16[96,768]{1,0:T(8,128)(2,1)S(1)} %get-tuple-element.52), channel_id=1, source_target_pairs={{0,2},{1,3},{2,0},{3,1},{4,6},{5,7},{6,4},{7,5},{8,10},{9,11},{10,... | collective-permute-start | bytes 442376 | tf_op jit(solution)/shard_map/ppermute | solution.py:459
  5.7 8.7 %collective-permute-start.1 = (bf16[2,2,64,384]{3,2,1,0:T(8,128)(2,1)S(1)}, bf16[2,2,64,384]{3,2,1,0:T(8,128)(2,1)S(1)}, u32[]{:S(2)}, u32[]{:S(2)}) collective-permute-start(bf16[2,2,64,384]{3,2,1,0:T(8,128)(2,1)S(1)} %get-tuple-element.69), channel_id=1, source_target_pairs={{0,8},{4,12},{8,0},{12,4},{1,9},{5,13},{9,1},{13,5},{2,10},{6,14},... | collective-permute-start | bytes 589832 | tf_op jit(solution)/shard_map/ppermute | solution.py:459
  7.3 7.1 %collective-permute-start.2 = (bf16[2,2,64,384]{3,2,1,0:T(8,128)(2,1)S(1)}, bf16[2,2,64,384]{3,2,1,0:T(8,128)(2,1)S(1)}, u32[]{:S(2)}, u32[]{:S(2)}) collective-permute-start(bf16[2,2,64,384]{3,2,1,0:T(8,128)(2,1)S(1)} %get-tuple-element.70), channel_id=1, source_target_pairs={{0,4},{4,0},{8,12},{12,8},{1,5},{5,1},{9,13},{13,9},{2,6},{6,2},{1... | collective-permute-start | bytes 589832 | tf_op jit(solution)/shard_map/ppermute | solution.py:459
  8.8 5.6 %collective-permute-start.3 = (bf16[2,2,16,384]{3,2,1,0:T(8,128)(2,1)S(1)}, bf16[2,2,16,384]{3,2,1,0:T(8,128)(2,1)S(1)}, u32[]{:S(2)}, u32[]{:S(2)}) collective-permute-start(bf16[2,2,16,384]{3,2,1,0:T(8,128)(2,1)S(1)} %get-tuple-element.71), channel_id=1, source_target_pairs={{0,12},{4,8},{8,4},{12,0},{1,13},{5,9},{9,5},{13,1},{2,14},{6,10},... | collective-permute-start | bytes 147464 | tf_op jit(solution)/shard_map/ppermute | solution.py:459
  10.7 8.6 %collective-permute-start.4 = (bf16[2,512,384]{2,1,0:T(8,128)(2,1)S(1)}, bf16[2,512,384]{2,1,0:T(8,128)(2,1)S(1)}, u32[]{:S(2)}, u32[]{:S(2)}) collective-permute-start(bf16[2,512,384]{2,1,0:T(8,128)(2,1)S(1)} %get-tuple-element.59.tile_ref), channel_id=1, source_target_pairs={{0,16},{1,17},{2,18},{3,19},{4,20},{5,21},{6,22},{7,23},{8,24},{9,... | collective-permute-start | bytes 2359304 | tf_op jit(solution)/shard_map/ppermute | solution.py:503
  14.5 4.9 %collective-permute-start.5 = (bf16[2,288,384]{2,1,0:T(8,128)(2,1)S(1)}, bf16[2,288,384]{2,1,0:T(8,128)(2,1)S(1)}, u32[]{:S(2)}, u32[]{:S(2)}) collective-permute-start(bf16[2,288,384]{2,1,0:T(8,128)(2,1)S(1)} %edges.1.edge_ref), channel_id=1, source_target_pairs={{0,16},{1,17},{2,18},{3,19},{4,20},{5,21},{6,22},{7,23},{8,24},{9,... | collective-permute-start | bytes 1327112 | tf_op jit(solution)/shard_map/ppermute | solution.py:521
  15.8 6.3 %collective-permute-start.8 = (bf16[96,768]{1,0:T(8,128)(2,1)S(1)}, bf16[96,768]{1,0:T(8,128)(2,1)S(1)}, u32[]{:S(2)}, u32[]{:S(2)}) collective-permute-start(bf16[96,768]{1,0:T(8,128)(2,1)S(1)} %lone.1.refs_0_), channel_id=1, source_target_pairs={{0,4},{4,0},{8,12},{12,8},{1,5},{5,1},{9,13},{13,9},{2,6},{6,2},{1... | collective-permute-start | bytes 442376 | tf_op jit(solution)/shard_map/ppermute | solution.py:459
  17.3 6.2 %collective-permute-start.7 = (bf16[96,768]{1,0:T(8,128)(2,1)S(1)}, bf16[96,768]{1,0:T(8,128)(2,1)S(1)}, u32[]{:S(2)}, u32[]{:S(2)}) collective-permute-start(bf16[96,768]{1,0:T(8,128)(2,1)S(1)} %lone.1.refs_0_), channel_id=1, source_target_pairs={{0,8},{4,12},{8,0},{12,4},{1,9},{5,13},{9,1},{13,5},{2,10},{6,14},... | collective-permute-start | bytes 442376 | tf_op jit(solution)/shard_map/ppermute | solution.py:459
  18.9 6.1 %collective-permute-start.6 = (bf16[96,768]{1,0:T(8,128)(2,1)S(1)}, bf16[96,768]{1,0:T(8,128)(2,1)S(1)}, u32[]{:S(2)}, u32[]{:S(2)}) collective-permute-start(bf16[96,768]{1,0:T(8,128)(2,1)S(1)} %lone.1.refs_0_), channel_id=1, source_target_pairs={{0,12},{4,8},{8,4},{12,0},{1,13},{5,9},{9,5},{13,1},{2,14},{6,10},... | collective-permute-start | bytes 442376 | tf_op jit(solution)/shard_map/ppermute | solution.py:459
  20.3 5.6 %collective-permute-start.9 = (bf16[128,384]{1,0:T(8,128)(2,1)S(1)}, bf16[128,384]{1,0:T(8,128)(2,1)S(1)}, u32[]{:S(2)}, u32[]{:S(2)}) collective-permute-start(bf16[128,384]{1,0:T(8,128)(2,1)S(1)} %rest.3), channel_id=1, source_target_pairs={{0,2},{1,3},{2,0},{3,1},{4,6},{5,7},{6,4},{7,5},{8,10},{9,11},{10,... | collective-permute-start | bytes 294920 | tf_op jit(solution)/shard_map/ppermute | solution.py:459
  22.1 3.9 %copy-start = (bf16[384,1536]{1,0:T(8,128)(2,1)S(1)}, bf16[384,1536]{1,0:T(8,128)(2,1)}, u32[]{:S(2)}) copy-start(bf16[384,1536]{1,0:T(8,128)(2,1)} %w_ref.9) | copy-start | bytes 3538948
  25.0 6.5 %collective-permute-start.11 = (bf16[128,384]{1,0:T(8,128)(2,1)S(1)}, bf16[128,384]{1,0:T(8,128)(2,1)S(1)}, u32[]{:S(2)}, u32[]{:S(2)}) collective-permute-start(bf16[128,384]{1,0:T(8,128)(2,1)S(1)} %get-tuple-element.98), channel_id=1, source_target_pairs={{0,2},{1,3},{2,0},{3,1},{4,6},{5,7},{6,4},{7,5},{8,10},{9,11},{10,... | collective-permute-start | bytes 294920 | tf_op jit(solution)/shard_map/ppermute | solution.py:459
  26.3 7.0 %collective-permute-start.13 = (bf16[128,768]{1,0:T(8,128)(2,1)S(1)}, bf16[128,768]{1,0:T(8,128)(2,1)S(1)}, u32[]{:S(2)}, u32[]{:S(2)}) collective-permute-start(bf16[128,768]{1,0:T(8,128)(2,1)S(1)} %project.4), channel_id=1, source_target_pairs={{0,1},{1,0},{2,3},{3,2},{4,5},{5,4},{6,7},{7,6},{8,9},{9,8},{10,11... | collective-permute-start | bytes 589832 | tf_op jit(solution)/shard_map/ppermute | solution.py:459
  28.9 2.0 %collective-permute-start.10 = (bf16[384,768]{1,0:T(8,128)(2,1)S(1)}, bf16[384,768]{1,0:T(8,128)(2,1)S(1)}, u32[]{:S(2)}, u32[]{:S(2)}) collective-permute-start(bf16[384,768]{1,0:T(8,128)(2,1)S(1)} %stack.1.part_ref), channel_id=1, source_target_pairs={{0,16},{16,0},{1,17},{17,1},{2,18},{18,2},{3,19},{19,3},{4,20},{20... | collective-permute-start | bytes 1769480 | tf_op jit(solution)/shard_map/ppermute | solution.py:459
  31.3 7.0 %collective-permute-start.12 = (bf16[128,768]{1,0:T(8,128)(2,1)S(1)}, bf16[128,768]{1,0:T(8,128)(2,1)S(1)}, u32[]{:S(2)}, u32[]{:S(2)}) collective-permute-start(bf16[128,768]{1,0:T(8,128)(2,1)S(1)} %project.5), channel_id=1, source_target_pairs={{0,1},{1,0},{2,3},{3,2},{4,5},{5,4},{6,7},{7,6},{8,9},{9,8},{10,11... | collective-permute-start | bytes 589832 | tf_op jit(solution)/shard_map/ppermute | solution.py:459

commit v3 on v0

--- a/solution.py
+++ b/solution.py
@@ -183,26 +183,27 @@
     return tile_at // 2, tile_at % 2
 
 
+def part_kernel(w_ref, part_ref, sem):
+    tall, broad = part_ref.shape
+    top = pl.multiple_of(lax.axis_index("tile") * tall, 16)
+    left = pl.multiple_of(lax.axis_index("tm") * broad, 128)
+    copy = pltpu.make_async_copy(w_ref.at[pl.ds(top, tall), pl.ds(left, broad)], part_ref, sem)
+    copy.start()
+    copy.wait()
+
+
 def face_kernel(
-    k_ref, v_ref, w_ref, row_ref, col_ref, corner_ref, tile_ref, part_ref, sems, *, geometry
+    k_ref, v_ref, part_ref, row_ref, col_ref, corner_ref, tile_ref, sems, *, geometry
 ):
     high, wide, span, frames = geometry[:4]
     cells = high * wide
     row_at, col_at = tile_place()
     y0 = jnp.where(row_at == 0, high - span, 0)
     x0 = jnp.where(col_at == 0, wide - span, 0)
-    tall, broad = part_ref.shape
-    top = pl.multiple_of(lax.axis_index("tile") * tall, 16)
-    edge = pl.multiple_of(lax.axis_index("tm") * broad, 128)
     copies = [
         pltpu.make_async_copy(ref, tile_ref.at[which], sems.at[which])
         for which, ref in enumerate((k_ref, v_ref))
     ]
-    copies.append(
-        pltpu.make_async_copy(
-            w_ref.at[pl.ds(top, tall), pl.ds(edge, broad)], part_ref, sems.at[2]
-        )
-    )
     for copy in copies:
         copy.start()
 
@@ -225,7 +226,6 @@
             corner_ref[which, f] = jnp.dot(
                 across, whole, preferred_element_type=jnp.float32
             ).astype(jnp.bfloat16)
-    copies[2].wait()
 
 
 def edge_kernel(row_ref, col_ref, corner_ref, out_ref):
@@ -465,19 +465,31 @@
 
     tall, broad = depth // tiles, width // 2
     part_shape = shape((tall, broad), bf16)
-    *faces, tile, part = call(
+    k, v, far_weight = (
+        pltpu.with_memory_space_constraint(x, pltpu.HBM) for x in (k, v, out_weight)
+    )
+    part = call(
+        part_kernel,
+        part_shape,
+        [hbm],
+        far_weight,
+        name="part",
+        scratch=[pltpu.SemaphoreType.DMA],
+    )
+    *faces, tile = call(
         face_kernel,
         [
             shape((2, frames, span * wide, channels), bf16),
             shape((2, frames, span * high, channels), bf16),
             shape((2, frames, span * span, channels), bf16),
             shape((2, tokens, channels), bf16),
-            part_shape,
         ],
-        [hbm] * 3,
-        *[pltpu.with_memory_space_constraint(x, pltpu.HBM) for x in (k, v, out_weight)],
+        [hbm] * 2 + [vmem],
+        k,
+        v,
+        part,
         name="faces",
-        scratch=[pltpu.SemaphoreType.DMA((3,))],
+        scratch=[pltpu.SemaphoreType.DMA((2,))],
         geometry=geometry,
     )
     faces = [flipped(face, "tile", flip) for face, flip in zip(faces, (2, 1, 3))]
@@ -509,10 +521,10 @@
         heads=heads,
     )
     lone, state = lax.optimization_barrier((lone, state))
-    lone = call(copy_kernel, part_shape, [vmem], lone, name="lone", flops=20 * 10**9)
+    lone = call(copy_kernel, part_shape, [vmem], lone, name="lone", flops=2 * 10**9)
     lone, state, faces = lax.optimization_barrier((lone, state, faces))
     edge = call(
-        edge_kernel, shape((2, count - tokens, channels), bf16), [vmem] * 3, *faces, name="edges"
+        edge_kernel, shape((2, count - tokens, channels), bf16), [vmem] * 3, *faces, name="edges", flops=20 * 10**9
     )
     first_edge = lax.ppermute(edge, "tm", [(0, 1)])
     parts = [lone] + [flipped(lone, "tile", flip) for flip in range(1, tiles)]
@@ -540,7 +552,8 @@
     state, for_side = lax.optimization_barrier((state, for_side))
     for_far, own_side = rest(state, 2, 1)
     got_far = flipped(for_far, "head", 2)
-    parts, own_side = lax.optimization_barrier((parts, own_side))
+    parts, own_side = lax.optimization_barrier((parts[::-1], own_side))
+    parts = parts[::-1]
     here = call(
         stack_kernel, shape((depth, broad), bf16), [vmem] * tiles, *parts, name="stack"
     )

time: 39.2 us -> 40.1 us (1.023)
  Pallas kernels: 10.3 us -> 11.2 us
    pallas_call x13 -> x14, Pallas kernels: 8.84 us -> 9.77 us  [call(): pl.pallas_call(functools.partial(kernel, **keys_of) if keys_of else kerne...]
  transfers between devices with their start and end apart: 14 -> 14, of which waited for: 8 -> 7; matrix products, arithmetic and copies ran while one was open for 0% -> 0% of each run, Pallas kernels for 20% -> 24%
where the time goes in v3:
time: 40.1 us; the launch traced here: 39.9 us
  starting transfers between devices  16.7 us (42%)
  waiting for transfers between devices  11.8 us (29%)
  Pallas kernels  11.2 us (28%)
    ppermute x12, starting transfers between devices, flipped(): lax.ppermute(value, axis, [(i, i ^ flip) for i in range(lax.axis_size(axi...  14.1 us
    ppermute x12, waiting for transfers between devices, flipped(): lax.ppermute(value, axis, [(i, i ^ flip) for i in range(lax.axis_size(axi...  11.8 us
    pallas_call x14, Pallas kernels, call(): pl.pallas_call(functools.partial(kernel, **keys_of) if keys_of else kerne...  9.77 us
    pallas_call x2, Pallas kernels, two_by_two(): pl.pallas_call(functools.partial(add_kernel, flip=flip), out_shape=shape(...  1.42 us
    ppermute x1, starting transfers between devices, two_by_two(): first_tile = lax.ppermute(tile, 'tm', [(0, 1)])  1.34 us
    ppermute x1, starting transfers between devices, two_by_two(): first_edge = lax.ppermute(edge, 'tm', [(0, 1)])  1.32 us
  transfers between devices with their start and end apart: 14, of which 7 were waited for; matrix products, arithmetic and copies ran while one was open for 0% of the time, Pallas kernels for 24%

profile of v3, /device:TPU:0, one launch (start us, length us, event | category | flops | bytes accessed | tf_op | source)
XLA Modules:
  0.0 39.9 jit_solution(1116461125587974089)
XLA Ops:
  0.0 0.0 copy-start.2
  0.0 0.0 copy-start.3
  0.0 0.0 copy-start.1
  0.0 1.0 %part.1.part_ref = bf16[96,768]{1,0:T(8,128)(2,1)S(1)} custom-call(bf16[384,1536]{1,0:T(8,128)(2,1)} %w_ref.9), custom_call_target="tpu_custom_call" | custom-call | tf_op jit(solution)/shard_map/part/pallas_call | solution.py:448
  1.0 4.1 %collective-permute-start = (bf16[96,768]{1,0:T(8,128)(2,1)S(1)}, bf16[96,768]{1,0:T(8,128)(2,1)S(1)}, u32[]{:S(2)}, u32[]{:S(2)}) collective-permute-start(bf16[96,768]{1,0:T(8,128)(2,1)S(1)} %part.1.part_ref), channel_id=1, source_target_pairs={{0,2},{1,3},{2,0},{3,1},{4,6},{5,7},{6,4},{7,5},{8,10},{9,11},{10,... | collective-permute-start | bytes 442376 | tf_op jit(solution)/shard_map/ppermute | solution.py:460
  5.1 1.5 %faces.1 = (bf16[2,2,64,384]{3,2,1,0:T(8,128)(2,1)S(1)}, bf16[2,2,64,384]{3,2,1,0:T(8,128)(2,1)S(1)}, bf16[2,2,16,384]{3,2,1,0:T(8,128)(2,1)S(1)}, bf16[2,512,384]{2,1,0:T(8,128)(2,1)S(1)}) custom-call(bf16[512,384]{1,0:T(8,128)(2,1)} %bitcast.11, bf16[512,384]{1,0:T(8,128)(2,1)} %bitcast.12, bf16[96,768]{1,0:T(8,128)(2,1)S(1)} %part.1.part_ref), custom_call_target="tpu_custom_call" | custom-call | tf_op jit(solution)/shard_map/faces/pallas_call | solution.py:448
  6.6 1.6 %collective-permute-start.1 = (bf16[2,2,64,384]{3,2,1,0:T(8,128)(2,1)S(1)}, bf16[2,2,64,384]{3,2,1,0:T(8,128)(2,1)S(1)}, u32[]{:S(2)}, u32[]{:S(2)}) collective-permute-start(bf16[2,2,64,384]{3,2,1,0:T(8,128)(2,1)S(1)} %get-tuple-element.67), channel_id=1, source_target_pairs={{0,8},{4,12},{8,0},{12,4},{1,9},{5,13},{9,1},{13,5},{2,10},{6,14},... | collective-permute-start | bytes 589832 | tf_op jit(solution)/shard_map/ppermute | solution.py:460
  8.2 1.5 %collective-permute-start.2 = (bf16[2,2,64,384]{3,2,1,0:T(8,128)(2,1)S(1)}, bf16[2,2,64,384]{3,2,1,0:T(8,128)(2,1)S(1)}, u32[]{:S(2)}, u32[]{:S(2)}) collective-permute-start(bf16[2,2,64,384]{3,2,1,0:T(8,128)(2,1)S(1)} %get-tuple-element.68), channel_id=1, source_target_pairs={{0,4},{4,0},{8,12},{12,8},{1,5},{5,1},{9,13},{13,9},{2,6},{6,2},{1... | collective-permute-start | bytes 589832 | tf_op jit(solution)/shard_map/ppermute | solution.py:460
  9.7 0.5 %collective-permute-start.3 = (bf16[2,2,16,384]{3,2,1,0:T(8,128)(2,1)S(1)}, bf16[2,2,16,384]{3,2,1,0:T(8,128)(2,1)S(1)}, u32[]{:S(2)}, u32[]{:S(2)}) collective-permute-start(bf16[2,2,16,384]{3,2,1,0:T(8,128)(2,1)S(1)} %get-tuple-element.69), channel_id=1, source_target_pairs={{0,12},{4,8},{8,4},{12,0},{1,13},{5,9},{9,5},{13,1},{2,14},{6,10},... | collective-permute-start | bytes 147464 | tf_op jit(solution)/shard_map/ppermute | solution.py:460
  10.1 0.0 copy-done.2
  10.1 0.0 copy-done.3
  10.1 0.0 copy-done.1
  10.1 1.4 %begin.1 = (f32[512,128]{1,0:T(8,128)S(1)}, f32[512,128]{1,0:T(8,128)S(1)}, f32[512,128]{1,0:T(8,128)S(1)}, s32[256,800]{1,0:T(8,128)S(1)}, s32[6,128]{1,0:T(8,128)S(1)}) custom-call(s32[3]{0:T(128)S(1)} %copy-done.3, s32[2,2,3]{2,1,0:T(2,128)S(1)} %bitcast.10, bf16[512,384]{1,0:T(8,128)(2,1)S(1)} %bitcast.5, bf16[2,512,384]{2,1,0:T(8,128)(2,1)S(1)} %get-tuple-element.57.tile_ref), custom_call_target="tpu_custom_call" | custom-call | tf_op jit(solution)/shard_map/begin/pallas_call | solution.py:448
  11.6 1.3 %collective-permute-start.4 = (bf16[2,512,384]{2,1,0:T(8,128)(2,1)S(1)}, bf16[2,512,384]{2,1,0:T(8,128)(2,1)S(1)}, u32[]{:S(2)}, u32[]{:S(2)}) collective-permute-start(bf16[2,512,384]{2,1,0:T(8,128)(2,1)S(1)} %get-tuple-element.57.tile_ref), channel_id=1, source_target_pairs={{0,16},{1,17},{2,18},{3,19},{4,20},{5,21},{6,22},{7,23},{8,24},{9,... | collective-permute-start | bytes 2359304 | tf_op jit(solution)/shard_map/ppermute | solution.py:511
  12.9 1.1 %tile.1 = (f32[512,256]{1,0:T(8,128)S(1)}, f32[512,256]{1,0:T(8,128)S(1)}, f32[512,256]{1,0:T(8,128)S(1)}) custom-call(bf16[512,384]{1,0:T(8,128)(2,1)S(1)} %bitcast.6, bf16[2,512,384]{2,1,0:T(8,128)(2,1)S(1)} %get-tuple-element.57.tile_ref, s32[256,800]{1,0:T(8,128)S(1)} %get-tuple-element.58.dist_ref.rest_3_, s32[6,128]{1,0:T(8,128)S(1)} %get-tuple-element.59.reach_ref.rest_4_), custom_call_target="tpu_custom_call" | custom-call | tf_op jit(solution)/shard_map/tile/pallas_call | solution.py:448
  14.0 0.0 collective-permute-done.in_ref
  14.0 1.2 %collective-permute-done.3.corner_ref = bf16[2,2,16,384]{3,2,1,0:T(8,128)(2,1)S(1)} collective-permute-done((bf16[2,2,16,384]{3,2,1,0:T(8,128)(2,1)S(1)}, bf16[2,2,16,384]{3,2,1,0:T(8,128)(2,1)S(1)}, u32[]{:S(2)}, u32[]{:S(2)}) %collective-permute-start.3) | collective-permute-done | bytes 49184 | tf_op jit(solution)/shard_map/ppermute | solution.py:460
  15.2 0.0 collective-permute-done.1.row_ref
  15.3 0.0 collective-permute-done.2.col_ref
  15.3 1.3 %collective-permute-start.5 = (bf16[2,288,384]{2,1,0:T(8,128)(2,1)S(1)}, bf16[2,288,384]{2,1,0:T(8,128)(2,1)S(1)}, u32[]{:S(2)}, u32[]{:S(2)}) collective-permute-start(bf16[2,288,384]{2,1,0:T(8,128)(2,1)S(1)} %edges.1.edge_ref), channel_id=1, source_target_pairs={{0,16},{1,17},{2,18},{3,19},{4,20},{5,21},{6,22},{7,23},{8,24},{9,... | collective-permute-start | bytes 1327112 | tf_op jit(solution)/shard_map/ppermute | solution.py:529
  16.6 1.6 %collective-permute-start.8 = (bf16[96,768]{1,0:T(8,128)(2,1)S(1)}, bf16[96,768]{1,0:T(8,128)(2,1)S(1)}, u32[]{:S(2)}, u32[]{:S(2)}) collective-permute-start(bf16[96,768]{1,0:T(8,128)(2,1)S(1)} %lone.1.refs_0_), channel_id=1, source_target_pairs={{0,4},{4,0},{8,12},{12,8},{1,5},{5,1},{9,13},{13,9},{2,6},{6,2},{1... | collective-permute-start | bytes 442376 | tf_op jit(solution)/shard_map/ppermute | solution.py:460
  18.2 1.5 %collective-permute-start.7 = (bf16[96,768]{1,0:T(8,128)(2,1)S(1)}, bf16[96,768]{1,0:T(8,128)(2,1)S(1)}, u32[]{:S(2)}, u32[]{:S(2)}) collective-permute-start(bf16[96,768]{1,0:T(8,128)(2,1)S(1)} %lone.1.refs_0_), channel_id=1, source_target_pairs={{0,8},{4,12},{8,0},{12,4},{1,9},{5,13},{9,1},{13,5},{2,10},{6,14},... | collective-permute-start | bytes 442376 | tf_op jit(solution)/shard_map/ppermute | solution.py:460
  19.7 0.5 %collective-permute-start.6 = (bf16[96,768]{1,0:T(8,128)(2,1)S(1)}, bf16[96,768]{1,0:T(8,128)(2,1)S(1)}, u32[]{:S(2)}, u32[]{:S(2)}) collective-permute-start(bf16[96,768]{1,0:T(8,128)(2,1)S(1)} %lone.1.refs_0_), channel_id=1, source_target_pairs={{0,12},{4,8},{8,4},{12,0},{1,13},{5,9},{9,5},{13,1},{2,14},{6,10},... | collective-permute-start | bytes 442376 | tf_op jit(solution)/shard_map/ppermute | solution.py:460
  20.2 0.0 collective-permute-done.5.first_edge_ref
  20.2 0.0 collective-permute-done.4.first_tile_ref
  20.2 1.0 %rest.3 = bf16[128,384]{1,0:T(8,128)(2,1)S(1)} custom-call(bf16[512,384]{1,0:T(8,128)(2,1)S(1)} %bitcast.7, bf16[2,288,384]{2,1,0:T(8,128)(2,1)S(1)} %edges.1.edge_ref, bf16[2,512,384]{2,1,0:T(8,128)(2,1)S(1)} %collective-permute-done.4.first_tile_ref, bf16[2,288,384]{2,1,0:T(8,128)(2,1)S(1)} %collective-permute-done.5.first_edge_ref, ...), custom_call_target="tpu_custom_call" | custom-call | tf_op jit(solution)/shard_map/rest/pallas_call | solution.py:448
  21.1 0.4 collective-permute-start.9
  21.5 1.4 %rest.4 = (bf16[128,384]{1,0:T(8,128)(2,1)S(1)}, bf16[128,384]{1,0:T(8,128)(2,1)S(1)}) custom-call(bf16[512,384]{1,0:T(8,128)(2,1)S(1)} %bitcast.8, bf16[2,288,384]{2,1,0:T(8,128)(2,1)S(1)} %edges.1.edge_ref, bf16[2,512,384]{2,1,0:T(8,128)(2,1)S(1)} %collective-permute-done.4.first_tile_ref, bf16[2,288,384]{2,1,0:T(8,128)(2,1)S(1)} %collective-permute-done.5.first_edge_ref, ...), custom_call_target="tpu_custom_call" | custom-call | tf_op jit(solution)/shard_map/rest/pallas_call | solution.py:448
  22.9 0.0 copy-start
  22.9 0.0 collective-permute-done.8.refs_1_
  22.9 1.4 %collective-permute-done.7.refs_2_ = bf16[96,768]{1,0:T(8,128)(2,1)S(1)} collective-permute-done((bf16[96,768]{1,0:T(8,128)(2,1)S(1)}, bf16[96,768]{1,0:T(8,128)(2,1)S(1)}, u32[]{:S(2)}, u32[]{:S(2)}) %collective-permute-start.7) | collective-permute-done | bytes 147488 | tf_op jit(solution)/shard_map/ppermute | solution.py:460
  24.3 1.5 %collective-permute-done.6.refs_3_ = bf16[96,768]{1,0:T(8,128)(2,1)S(1)} collective-permute-done((bf16[96,768]{1,0:T(8,128)(2,1)S(1)}, bf16[96,768]{1,0:T(8,128)(2,1)S(1)}, u32[]{:S(2)}, u32[]{:S(2)}) %collective-permute-start.6) | collective-permute-done | bytes 147488 | tf_op jit(solution)/shard_map/ppermute | solution.py:460
  25.7 0.3 collective-permute-start.11
  26.1 0.1 stack.1.part_ref
  26.1 2.8 %collective-permute-done.9.got_ref = bf16[128,384]{1,0:T(8,128)(2,1)S(1)} collective-permute-done((bf16[128,384]{1,0:T(8,128)(2,1)S(1)}, bf16[128,384]{1,0:T(8,128)(2,1)S(1)}, u32[]{:S(2)}, u32[]{:S(2)}) %collective-permute-start.9) | collective-permute-done | bytes 98336 | tf_op jit(solution)/shard_map/ppermute | solution.py:460
  28.9 0.0 copy-done
  28.9 0.4 project.4
  29.3 0.1 collective-permute-start.13
  29.4 0.1 collective-permute-start.10
  29.4 1.0 %rest.5.own_ref = bf16[128,384]{1,0:T(8,128)(2,1)S(1)} custom-call(bf16[512,384]{1,0:T(8,128)(2,1)S(1)} %bitcast.9, bf16[2,288,384]{2,1,0:T(8,128)(2,1)S(1)} %edges.1.edge_ref, bf16[2,512,384]{2,1,0:T(8,128)(2,1)S(1)} %collective-permute-done.4.first_tile_ref, bf16[2,288,384]{2,1,0:T(8,128)(2,1)S(1)} %collective-permute-done.5.first_edge_ref, ...), custom_call_target="tpu_custom_call" | custom-call | flops 20000000000 | tf_op jit(solution)/shard_map/rest/pallas_call | solution.py:448
  30.4 1.0 %collective-permute-done.10.part_ref = bf16[384,768]{1,0:T(8,128)(2,1)S(1)} collective-permute-done((bf16[384,768]{1,0:T(8,128)(2,1)S(1)}, bf16[384,768]{1,0:T(8,128)(2,1)S(1)}, u32[]{:S(2)}, u32[]{:S(2)}) %collective-permute-start.10) | collective-permute-done | bytes 589856 | tf_op jit(solution)/shard_map/ppermute | solution.py:460
  31.4 0.4 project.5
  31.8 2.0 %collective-permute-start.12 = (bf16[128,768]{1,0:T(8,128)(2,1)S(1)}, bf16[128,768]{1,0:T(8,128)(2,1)S(1)}, u32[]{:S(2)}, u32[]{:S(2)}) collective-permute-start(bf16[128,768]{1,0:T(8,128)(2,1)S(1)} %project.5), channel_id=1, source_target_pairs={{0,1},{1,0},{2,3},{3,2},{4,5},{5,4},{6,7},{7,6},{8,9},{9,8},{10,11... | collective-permute-start | bytes 589832 | tf_op jit(solution)/shard_map/ppermute | solution.py:460
  33.8 0.0 collective-permute-done.11.got_ref
  33.8 0.4 project.6.mine_ref
  34.2 0.4 project.7.mine_ref
  34.5 0.6 %collective-permute-done.13.got_ref = bf16[128,768]{1,0:T(8,128)(2,1)S(1)} collective-permute-done((bf16[128,768]{1,0:T(8,128)(2,1)S(1)}, bf16[128,768]{1,0:T(8,128)(2,1)S(1)}, u32[]{:S(2)}, u32[]{:S(2)}) %collective-permute-start.13) | collective-permute-done | bytes 196640 | tf_op jit(solution)/shard_map/ppermute | solution.py:460
  35.2 0.7 %add.2.rest_0_ = bf16[128,1536]{1,0:T(8,128)(2,1)} custom-call(f32[128,768]{1,0:T(8,128)S(1)} %project.7.mine_ref, bf16[128,768]{1,0:T(8,128)(2,1)S(1)} %collective-permute-done.13.got_ref), custom_call_target="tpu_custom_call" | custom-call | tf_op jit(solution)/shard_map/add/pallas_call | solution.py:592
  35.9 3.3 %collective-permute-done.12.got_ref = bf16[128,768]{1,0:T(8,128)(2,1)S(1)} collective-permute-done((bf16[128,768]{1,0:T(8,128)(2,1)S(1)}, bf16[128,768]{1,0:T(8,128)(2,1)S(1)}, u32[]{:S(2)}, u32[]{:S(2)}) %collective-permute-start.12) | collective-permute-done | bytes 196640 | tf_op jit(solution)/shard_map/ppermute | solution.py:460
  39.2 0.7 %add.3 = bf16[128,1536]{1,0:T(8,128)(2,1)} custom-call(f32[128,768]{1,0:T(8,128)S(1)} %project.6.mine_ref, bf16[128,768]{1,0:T(8,128)(2,1)S(1)} %collective-permute-done.12.got_ref, bf16[128,1536]{1,0:T(8,128)(2,1)} %add.2.rest_0_), custom_call_target="tpu_custom_call", output_to_operand_aliasing={{}: (2, {})} | custom-call | tf_op jit(solution)/shard_map/add/pallas_call | solution.py:592
  (2 shorter events, 0.1 us)
Async XLA Ops:
  0.0 10.1 %copy-start.2 = (s32[3,2,2]{0,2,1:T(2,128)S(1)}, s32[3,2,2]{0,2,1:T(2,128)}, u32[]{:S(2)}) copy-start(s32[3,2,2]{0,2,1:T(2,128)} %param.11) | copy-start | bytes 148
  0.0 10.1 %copy-start.3 = (s32[3]{0:T(128)S(1)}, s32[3]{0:T(128)}, u32[]{:S(2)}) copy-start(s32[3]{0:T(128)} %radius_ref.1) | copy-start | bytes 40
  0.0 10.1 %copy-start.1 = (bf16[1,1,2,16,16,384]{5,4,3,2,1,0:T(8,128)(2,1)S(1)}, bf16[1,1,2,16,16,384]{5,4,3,2,1,0:T(8,128)(2,1)}, u32[]{:S(2)}) copy-start(bf16[1,1,2,16,16,384]{5,4,3,2,1,0:T(8,128)(2,1)} %param.6) | copy-start | bytes 1179652
  1.0 13.0 %collective-permute-start = (bf16[96,768]{1,0:T(8,128)(2,1)S(1)}, bf16[96,768]{1,0:T(8,128)(2,1)S(1)}, u32[]{:S(2)}, u32[]{:S(2)}) collective-permute-start(bf16[96,768]{1,0:T(8,128)(2,1)S(1)} %part.1.part_ref), channel_id=1, source_target_pairs={{0,2},{1,3},{2,0},{3,1},{4,6},{5,7},{6,4},{7,5},{8,10},{9,11},{10,... | collective-permute-start | bytes 442376 | tf_op jit(solution)/shard_map/ppermute | solution.py:460
  6.6 8.7 %collective-permute-start.1 = (bf16[2,2,64,384]{3,2,1,0:T(8,128)(2,1)S(1)}, bf16[2,2,64,384]{3,2,1,0:T(8,128)(2,1)S(1)}, u32[]{:S(2)}, u32[]{:S(2)}) collective-permute-start(bf16[2,2,64,384]{3,2,1,0:T(8,128)(2,1)S(1)} %get-tuple-element.67), channel_id=1, source_target_pairs={{0,8},{4,12},{8,0},{12,4},{1,9},{5,13},{9,1},{13,5},{2,10},{6,14},... | collective-permute-start | bytes 589832 | tf_op jit(solution)/shard_map/ppermute | solution.py:460
  8.2 7.1 %collective-permute-start.2 = (bf16[2,2,64,384]{3,2,1,0:T(8,128)(2,1)S(1)}, bf16[2,2,64,384]{3,2,1,0:T(8,128)(2,1)S(1)}, u32[]{:S(2)}, u32[]{:S(2)}) collective-permute-start(bf16[2,2,64,384]{3,2,1,0:T(8,128)(2,1)S(1)} %get-tuple-element.68), channel_id=1, source_target_pairs={{0,4},{4,0},{8,12},{12,8},{1,5},{5,1},{9,13},{13,9},{2,6},{6,2},{1... | collective-permute-start | bytes 589832 | tf_op jit(solution)/shard_map/ppermute | solution.py:460
  9.7 5.6 %collective-permute-start.3 = (bf16[2,2,16,384]{3,2,1,0:T(8,128)(2,1)S(1)}, bf16[2,2,16,384]{3,2,1,0:T(8,128)(2,1)S(1)}, u32[]{:S(2)}, u32[]{:S(2)}) collective-permute-start(bf16[2,2,16,384]{3,2,1,0:T(8,128)(2,1)S(1)} %get-tuple-element.69), channel_id=1, source_target_pairs={{0,12},{4,8},{8,4},{12,0},{1,13},{5,9},{9,5},{13,1},{2,14},{6,10},... | collective-permute-start | bytes 147464 | tf_op jit(solution)/shard_map/ppermute | solution.py:460
  11.6 8.6 %collective-permute-start.4 = (bf16[2,512,384]{2,1,0:T(8,128)(2,1)S(1)}, bf16[2,512,384]{2,1,0:T(8,128)(2,1)S(1)}, u32[]{:S(2)}, u32[]{:S(2)}) collective-permute-start(bf16[2,512,384]{2,1,0:T(8,128)(2,1)S(1)} %get-tuple-element.57.tile_ref), channel_id=1, source_target_pairs={{0,16},{1,17},{2,18},{3,19},{4,20},{5,21},{6,22},{7,23},{8,24},{9,... | collective-permute-start | bytes 2359304 | tf_op jit(solution)/shard_map/ppermute | solution.py:511
  15.3 4.9 %collective-permute-start.5 = (bf16[2,288,384]{2,1,0:T(8,128)(2,1)S(1)}, bf16[2,288,384]{2,1,0:T(8,128)(2,1)S(1)}, u32[]{:S(2)}, u32[]{:S(2)}) collective-permute-start(bf16[2,288,384]{2,1,0:T(8,128)(2,1)S(1)} %edges.1.edge_ref), channel_id=1, source_target_pairs={{0,16},{1,17},{2,18},{3,19},{4,20},{5,21},{6,22},{7,23},{8,24},{9,... | collective-permute-start | bytes 1327112 | tf_op jit(solution)/shard_map/ppermute | solution.py:529
  16.6 6.3 %collective-permute-start.8 = (bf16[96,768]{1,0:T(8,128)(2,1)S(1)}, bf16[96,768]{1,0:T(8,128)(2,1)S(1)}, u32[]{:S(2)}, u32[]{:S(2)}) collective-permute-start(bf16[96,768]{1,0:T(8,128)(2,1)S(1)} %lone.1.refs_0_), channel_id=1, source_target_pairs={{0,4},{4,0},{8,12},{12,8},{1,5},{5,1},{9,13},{13,9},{2,6},{6,2},{1... | collective-permute-start | bytes 442376 | tf_op jit(solution)/shard_map/ppermute | solution.py:460
  18.2 6.1 %collective-permute-start.7 = (bf16[96,768]{1,0:T(8,128)(2,1)S(1)}, bf16[96,768]{1,0:T(8,128)(2,1)S(1)}, u32[]{:S(2)}, u32[]{:S(2)}) collective-permute-start(bf16[96,768]{1,0:T(8,128)(2,1)S(1)} %lone.1.refs_0_), channel_id=1, source_target_pairs={{0,8},{4,12},{8,0},{12,4},{1,9},{5,13},{9,1},{13,5},{2,10},{6,14},... | collective-permute-start | bytes 442376 | tf_op jit(solution)/shard_map/ppermute | solution.py:460
  19.7 6.0 %collective-permute-start.6 = (bf16[96,768]{1,0:T(8,128)(2,1)S(1)}, bf16[96,768]{1,0:T(8,128)(2,1)S(1)}, u32[]{:S(2)}, u32[]{:S(2)}) collective-permute-start(bf16[96,768]{1,0:T(8,128)(2,1)S(1)} %lone.1.refs_0_), channel_id=1, source_target_pairs={{0,12},{4,8},{8,4},{12,0},{1,13},{5,9},{9,5},{13,1},{2,14},{6,10},... | collective-permute-start | bytes 442376 | tf_op jit(solution)/shard_map/ppermute | solution.py:460
  21.1 7.8 %collective-permute-start.9 = (bf16[128,384]{1,0:T(8,128)(2,1)S(1)}, bf16[128,384]{1,0:T(8,128)(2,1)S(1)}, u32[]{:S(2)}, u32[]{:S(2)}) collective-permute-start(bf16[128,384]{1,0:T(8,128)(2,1)S(1)} %rest.3), channel_id=1, source_target_pairs={{0,2},{1,3},{2,0},{3,1},{4,6},{5,7},{6,4},{7,5},{8,10},{9,11},{10,... | collective-permute-start | bytes 294920 | tf_op jit(solution)/shard_map/ppermute | solution.py:460
  22.9 6.0 %copy-start = (bf16[384,1536]{1,0:T(8,128)(2,1)S(1)}, bf16[384,1536]{1,0:T(8,128)(2,1)}, u32[]{:S(2)}) copy-start(bf16[384,1536]{1,0:T(8,128)(2,1)} %w_ref.9) | copy-start | bytes 3538948
  25.7 8.1 %collective-permute-start.11 = (bf16[128,384]{1,0:T(8,128)(2,1)S(1)}, bf16[128,384]{1,0:T(8,128)(2,1)S(1)}, u32[]{:S(2)}, u32[]{:S(2)}) collective-permute-start(bf16[128,384]{1,0:T(8,128)(2,1)S(1)} %get-tuple-element.96), channel_id=1, source_target_pairs={{0,2},{1,3},{2,0},{3,1},{4,6},{5,7},{6,4},{7,5},{8,10},{9,11},{10,... | collective-permute-start | bytes 294920 | tf_op jit(solution)/shard_map/ppermute | solution.py:460
  29.3 5.9 %collective-permute-start.13 = (bf16[128,768]{1,0:T(8,128)(2,1)S(1)}, bf16[128,768]{1,0:T(8,128)(2,1)S(1)}, u32[]{:S(2)}, u32[]{:S(2)}) collective-permute-start(bf16[128,768]{1,0:T(8,128)(2,1)S(1)} %project.4), channel_id=1, source_target_pairs={{0,1},{1,0},{2,3},{3,2},{4,5},{5,4},{6,7},{7,6},{8,9},{9,8},{10,11... | collective-permute-start | bytes 589832 | tf_op jit(solution)/shard_map/ppermute | solution.py:460
  29.4 2.1 %collective-permute-start.10 = (bf16[384,768]{1,0:T(8,128)(2,1)S(1)}, bf16[384,768]{1,0:T(8,128)(2,1)S(1)}, u32[]{:S(2)}, u32[]{:S(2)}) collective-permute-start(bf16[384,768]{1,0:T(8,128)(2,1)S(1)} %stack.1.part_ref), channel_id=1, source_target_pairs={{0,16},{16,0},{1,17},{17,1},{2,18},{18,2},{3,19},{19,3},{4,20},{20... | collective-permute-start | bytes 1769480 | tf_op jit(solution)/shard_map/ppermute | solution.py:460
  31.8 7.4 %collective-permute-start.12 = (bf16[128,768]{1,0:T(8,128)(2,1)S(1)}, bf16[128,768]{1,0:T(8,128)(2,1)S(1)}, u32[]{:S(2)}, u32[]{:S(2)}) collective-permute-start(bf16[128,768]{1,0:T(8,128)(2,1)S(1)} %project.5), channel_id=1, source_target_pairs={{0,1},{1,0},{2,3},{3,2},{4,5},{5,4},{6,7},{7,6},{8,9},{9,8},{10,11... | collective-permute-start | bytes 589832 | tf_op jit(solution)/shard_map/ppermute | solution.py:460

commit v4 on v2

--- a/solution.py
+++ b/solution.py
@@ -262,22 +262,39 @@
     return jnp.maximum(jnp.abs(i // wide - ky), jnp.abs(i % wide - kx))
 
 
-def attend(q, pieces, factor, before):
-    scores = []
-    m = before
-    for k, v, dist, reach in pieces:
-        s = lax.dot_general(q, k, (((1,), (1,)), ((), ())), preferred_element_type=jnp.float32)
-        s = jnp.where(dist <= reach, s * factor, FAR)
-        top = jnp.max(s, axis=1, keepdims=True)
-        m = top if m is None else jnp.maximum(m, top)
-        scores.append(s)
-    total = None
-    for s, (k, v, dist, reach) in zip(scores, pieces):
-        p = jnp.exp2(s - m).astype(jnp.bfloat16)
-        both = jnp.concatenate([v, jnp.ones_like(v)], axis=1)
-        got = jnp.dot(p, both, preferred_element_type=jnp.float32)
-        total = got if total is None else total + got
-    return m, total
+def attend(units, factor):
+    scores = [
+        [
+            jnp.where(
+                dist <= reach,
+                lax.dot_general(
+                    q, k, (((1,), (1,)), ((), ())), preferred_element_type=jnp.float32
+                )
+                * factor,
+                FAR,
+            )
+            for k, v, dist, reach in pieces
+        ]
+        for q, pieces, before in units
+    ]
+    tops = []
+    for parts, (q, pieces, before) in zip(scores, units):
+        found = [jnp.max(s, axis=1, keepdims=True) for s in parts]
+        if before is not None:
+            found.append(before)
+        tops.append(functools.reduce(jnp.maximum, found))
+    probs = [
+        [jnp.exp2(s - m).astype(jnp.bfloat16) for s in parts] for parts, m in zip(scores, tops)
+    ]
+    sums = []
+    for parts, (q, pieces, before) in zip(probs, units):
+        total = None
+        for p, (k, v, dist, reach) in zip(parts, pieces):
+            both = jnp.concatenate([v, jnp.ones_like(v)], axis=1)
+            got = jnp.dot(p, both, preferred_element_type=jnp.float32)
+            total = got if total is None else total + got
+        sums.append(total)
+    return tops, sums
 
 
 def attend_tile(q_ref, tile_ref, dist_ref, reach_of, heads, state, geometry):
@@ -287,11 +304,14 @@
     for at, head in enumerate(heads):
         cols = slice(head * head_dim, (head + 1) * head_dim)
         outs = slice(at * head_dim, (at + 1) * head_dim)
-        for start in range(0, q_ref.shape[0], step):
-            rows = slice(start, start + step)
+        starts = range(0, q_ref.shape[0], step)
+        units = []
+        for start in starts:
             near = dist_ref[start % cells : start % cells + step, : tile_ref.shape[1]]
             piece = (tile_ref[0, :, cols], tile_ref[1, :, cols], near, reach_of(head))
-            m, got = attend(q_ref[rows, cols], [piece], factor, None)
+            units.append((q_ref[start : start + step, cols], [piece], None))
+        for start, m, got in zip(starts, *attend(units, factor)):
+            rows = slice(start, start + step)
             acc_ref[rows, outs] = got[:, :head_dim]
             sum_ref[rows, outs] = got[:, head_dim:]
             max_ref[rows, outs] = jnp.broadcast_to(m, (step, head_dim))
@@ -329,16 +349,6 @@
     refs = head_state if head == 0 else state
     at = max(head - 1, 0) * head_dim
     return [ref[rows, at : at + head_dim] for ref in refs]
-
-
-def merge(q, pieces, factor, old):
-    old_acc, old_total, old_max = old
-    m, got = attend(q, pieces, factor, old_max[:, :1])
-    shrink = jnp.exp2(old_max - m)
-    head_dim = old_acc.shape[1]
-    acc = old_acc * shrink + got[:, :head_dim]
-    total = old_total * shrink + got[:, head_dim:]
-    return acc, total, jnp.broadcast_to(m, old_max.shape)
 
 
 def rest_kernel(
@@ -364,6 +374,8 @@
             rows = pl.ds(start, step)
             near = dist_ref[pl.ds(pl.multiple_of(lax.rem(start, cells), step), step)]
             beyond = near[:, base:]
+            units = []
+            olds = []
             for head in range(heads):
                 cols = slice(head * head_dim, (head + 1) * head_dim)
                 sources = [(edge_ref, beyond, head)]
@@ -374,8 +386,14 @@
                     (ref[0, :, cols], ref[1, :, cols], dist, reach_ref[row : row + 1, :1])
                     for ref, dist, row in sources
                 ]
-                old = pick_state(head_state, state, head, rows, head_dim)
-                acc, total, m = merge(q_ref[rows, cols], pieces, factor, old)
+                olds.append(pick_state(head_state, state, head, rows, head_dim))
+                units.append((q_ref[rows, cols], pieces, olds[-1][2][:, :1]))
+            for head, (m, got) in enumerate(zip(*attend(units, factor))):
+                old_acc, old_total, old_max = olds[head]
+                shrink = jnp.exp2(old_max - m)
+                acc = old_acc * shrink + got[:, :head_dim]
+                total = old_total * shrink + got[:, head_dim:]
+                cols = slice(head * head_dim, (head + 1) * head_dim)
                 out_ref[:, cols] = (acc / total).astype(jnp.bfloat16)
 
     @pl.when(stretch_at > 0)
@@ -544,8 +562,7 @@
     state, for_side = lax.optimization_barrier((state, for_side))
     for_far, own_side = rest(state, 2, 1)
     got_far = flipped(for_far, "head", 2)
-    parts, own_side = lax.optimization_barrier((parts[::-1], own_side))
-    parts = parts[::-1]
+    parts, own_side = lax.optimization_barrier((parts, own_side))
     here = call(
         stack_kernel, shape((depth, broad), bf16), [vmem] * tiles, *parts, name="stack"
     )

time: 39.2 us -> 38.9 us (level)
  waiting for transfers between devices: 11.2 us -> 12.4 us
  Pallas kernels: 10.3 us -> 9.49 us
  starting transfers between devices: 17.3 us -> 16.7 us
    ppermute x12, waiting for transfers between devices: 11.2 us -> 12.3 us  [flipped(): lax.ppermute(value, axis, [(i, i ^ flip) for i in range(lax.axis_size(axi...]
    pallas_call x14, Pallas kernels: 8.91 us -> 8.08 us  [call(): pl.pallas_call(functools.partial(kernel, **keys_of) if keys_of else kerne...]
    ppermute x12, starting transfers between devices: 14.7 us -> 14.1 us  [flipped(): lax.ppermute(value, axis, [(i, i ^ flip) for i in range(lax.axis_size(axi...]
  transfers between devices with their start and end apart: 14 -> 14, of which waited for: 8 -> 7; matrix products, arithmetic and copies ran while one was open for 0% -> 0% of each run, Pallas kernels for 21% -> 19%
where the time goes in v4:
time: 38.9 us; the launch traced here: 38.7 us
  starting transfers between devices  16.7 us (43%)
  waiting for transfers between devices  12.4 us (32%)
  Pallas kernels  9.49 us (24%)
    ppermute x12, starting transfers between devices, flipped(): lax.ppermute(value, axis, [(i, i ^ flip) for i in range(lax.axis_size(axi...  14.1 us
    ppermute x12, waiting for transfers between devices, flipped(): lax.ppermute(value, axis, [(i, i ^ flip) for i in range(lax.axis_size(axi...  12.3 us
    pallas_call x14, Pallas kernels, call(): pl.pallas_call(functools.partial(kernel, **keys_of) if keys_of else kerne...  8.08 us
    pallas_call x2, Pallas kernels, two_by_two(): pl.pallas_call(functools.partial(add_kernel, flip=flip), out_shape=shape(...  1.42 us
    ppermute x1, starting transfers between devices, two_by_two(): first_tile = lax.ppermute(tile, 'tm', [(0, 1)])  1.34 us
    ppermute x1, starting transfers between devices, two_by_two(): first_edge = lax.ppermute(edge, 'tm', [(0, 1)])  1.32 us
  transfers between devices with their start and end apart: 14, of which 7 were waited for; matrix products, arithmetic and copies ran while one was open for 0% of the time, Pallas kernels for 19%

profile of v4, /device:TPU:0, one launch (start us, length us, event | category | flops | bytes accessed | tf_op | source)
XLA Modules:
  0.0 38.7 jit_solution(9089896174727994591)
XLA Ops:
  0.0 0.0 copy-start.1
  0.0 0.0 copy-start.2
  0.0 0.0 copy-start.3
  0.0 1.3 %load.1 = (bf16[2,512,384]{2,1,0:T(8,128)(2,1)S(1)}, bf16[96,768]{1,0:T(8,128)(2,1)S(1)}) custom-call(bf16[512,384]{1,0:T(8,128)(2,1)} %bitcast.11, bf16[512,384]{1,0:T(8,128)(2,1)} %bitcast.12, bf16[384,1536]{1,0:T(8,128)(2,1)} %w_ref.9), custom_call_target="tpu_custom_call" | custom-call | tf_op jit(solution)/shard_map/load/pallas_call | solution.py:465
  1.3 4.1 %collective-permute-start = (bf16[96,768]{1,0:T(8,128)(2,1)S(1)}, bf16[96,768]{1,0:T(8,128)(2,1)S(1)}, u32[]{:S(2)}, u32[]{:S(2)}) collective-permute-start(bf16[96,768]{1,0:T(8,128)(2,1)S(1)} %get-tuple-element.52), channel_id=1, source_target_pairs={{0,2},{1,3},{2,0},{3,1},{4,6},{5,7},{6,4},{7,5},{8,10},{9,11},{10,... | collective-permute-start | bytes 442376 | tf_op jit(solution)/shard_map/ppermute | solution.py:477
  5.4 0.3 faces.1
  5.7 1.6 %collective-permute-start.1 = (bf16[2,2,64,384]{3,2,1,0:T(8,128)(2,1)S(1)}, bf16[2,2,64,384]{3,2,1,0:T(8,128)(2,1)S(1)}, u32[]{:S(2)}, u32[]{:S(2)}) collective-permute-start(bf16[2,2,64,384]{3,2,1,0:T(8,128)(2,1)S(1)} %get-tuple-element.69), channel_id=1, source_target_pairs={{0,8},{4,12},{8,0},{12,4},{1,9},{5,13},{9,1},{13,5},{2,10},{6,14},... | collective-permute-start | bytes 589832 | tf_op jit(solution)/shard_map/ppermute | solution.py:477
  7.3 1.5 %collective-permute-start.2 = (bf16[2,2,64,384]{3,2,1,0:T(8,128)(2,1)S(1)}, bf16[2,2,64,384]{3,2,1,0:T(8,128)(2,1)S(1)}, u32[]{:S(2)}, u32[]{:S(2)}) collective-permute-start(bf16[2,2,64,384]{3,2,1,0:T(8,128)(2,1)S(1)} %get-tuple-element.70), channel_id=1, source_target_pairs={{0,4},{4,0},{8,12},{12,8},{1,5},{5,1},{9,13},{13,9},{2,6},{6,2},{1... | collective-permute-start | bytes 589832 | tf_op jit(solution)/shard_map/ppermute | solution.py:477
  8.8 0.5 %collective-permute-start.3 = (bf16[2,2,16,384]{3,2,1,0:T(8,128)(2,1)S(1)}, bf16[2,2,16,384]{3,2,1,0:T(8,128)(2,1)S(1)}, u32[]{:S(2)}, u32[]{:S(2)}) collective-permute-start(bf16[2,2,16,384]{3,2,1,0:T(8,128)(2,1)S(1)} %get-tuple-element.71), channel_id=1, source_target_pairs={{0,12},{4,8},{8,4},{12,0},{1,13},{5,9},{9,5},{13,1},{2,14},{6,10},... | collective-permute-start | bytes 147464 | tf_op jit(solution)/shard_map/ppermute | solution.py:477
  9.3 0.0 copy-done.1
  9.3 0.0 copy-done.2
  9.3 0.0 copy-done.3
  9.3 1.4 %begin.1 = (f32[512,128]{1,0:T(8,128)S(1)}, f32[512,128]{1,0:T(8,128)S(1)}, f32[512,128]{1,0:T(8,128)S(1)}, s32[256,800]{1,0:T(8,128)S(1)}, s32[6,128]{1,0:T(8,128)S(1)}) custom-call(s32[3]{0:T(128)S(1)} %copy-done.3, s32[2,2,3]{2,1,0:T(2,128)S(1)} %bitcast.10, bf16[512,384]{1,0:T(8,128)(2,1)S(1)} %bitcast.5, bf16[2,512,384]{2,1,0:T(8,128)(2,1)S(1)} %get-tuple-element.59.tile_ref), custom_call_target="tpu_custom_call" | custom-call | tf_op jit(solution)/shard_map/begin/pallas_call | solution.py:465
  10.7 1.3 %collective-permute-start.4 = (bf16[2,512,384]{2,1,0:T(8,128)(2,1)S(1)}, bf16[2,512,384]{2,1,0:T(8,128)(2,1)S(1)}, u32[]{:S(2)}, u32[]{:S(2)}) collective-permute-start(bf16[2,512,384]{2,1,0:T(8,128)(2,1)S(1)} %get-tuple-element.59.tile_ref), channel_id=1, source_target_pairs={{0,16},{1,17},{2,18},{3,19},{4,20},{5,21},{6,22},{7,23},{8,24},{9,... | collective-permute-start | bytes 2359304 | tf_op jit(solution)/shard_map/ppermute | solution.py:521
  12.0 1.1 %tile.1 = (f32[512,256]{1,0:T(8,128)S(1)}, f32[512,256]{1,0:T(8,128)S(1)}, f32[512,256]{1,0:T(8,128)S(1)}) custom-call(bf16[512,384]{1,0:T(8,128)(2,1)S(1)} %bitcast.6, bf16[2,512,384]{2,1,0:T(8,128)(2,1)S(1)} %get-tuple-element.59.tile_ref, s32[256,800]{1,0:T(8,128)S(1)} %get-tuple-element.60.dist_ref.rest_3_, s32[6,128]{1,0:T(8,128)S(1)} %get-tuple-element.61.reach_ref.rest_4_), custom_call_target="tpu_custom_call" | custom-call | tf_op jit(solution)/shard_map/tile/pallas_call | solution.py:465
  13.1 0.0 collective-permute-done.in_ref
  13.2 1.3 %collective-permute-done.3.corner_ref = bf16[2,2,16,384]{3,2,1,0:T(8,128)(2,1)S(1)} collective-permute-done((bf16[2,2,16,384]{3,2,1,0:T(8,128)(2,1)S(1)}, bf16[2,2,16,384]{3,2,1,0:T(8,128)(2,1)S(1)}, u32[]{:S(2)}, u32[]{:S(2)}) %collective-permute-start.3) | collective-permute-done | bytes 49184 | tf_op jit(solution)/shard_map/ppermute | solution.py:477
  14.4 0.0 collective-permute-done.1.row_ref
  14.4 0.0 collective-permute-done.2.col_ref
  14.5 1.3 %collective-permute-start.5 = (bf16[2,288,384]{2,1,0:T(8,128)(2,1)S(1)}, bf16[2,288,384]{2,1,0:T(8,128)(2,1)S(1)}, u32[]{:S(2)}, u32[]{:S(2)}) collective-permute-start(bf16[2,288,384]{2,1,0:T(8,128)(2,1)S(1)} %edges.1.edge_ref), channel_id=1, source_target_pairs={{0,16},{1,17},{2,18},{3,19},{4,20},{5,21},{6,22},{7,23},{8,24},{9,... | collective-permute-start | bytes 1327112 | tf_op jit(solution)/shard_map/ppermute | solution.py:539
  15.8 2.5 %collective-permute-start.8 = (bf16[96,768]{1,0:T(8,128)(2,1)S(1)}, bf16[96,768]{1,0:T(8,128)(2,1)S(1)}, u32[]{:S(2)}, u32[]{:S(2)}) collective-permute-start(bf16[96,768]{1,0:T(8,128)(2,1)S(1)} %lone.1.refs_0_), channel_id=1, source_target_pairs={{0,12},{4,8},{8,4},{12,0},{1,13},{5,9},{9,5},{13,1},{2,14},{6,10},... | collective-permute-start | bytes 442376 | tf_op jit(solution)/shard_map/ppermute | solution.py:477
  18.3 0.5 %collective-permute-start.7 = (bf16[96,768]{1,0:T(8,128)(2,1)S(1)}, bf16[96,768]{1,0:T(8,128)(2,1)S(1)}, u32[]{:S(2)}, u32[]{:S(2)}) collective-permute-start(bf16[96,768]{1,0:T(8,128)(2,1)S(1)} %lone.1.refs_0_), channel_id=1, source_target_pairs={{0,8},{4,12},{8,0},{12,4},{1,9},{5,13},{9,1},{13,5},{2,10},{6,14},... | collective-permute-start | bytes 442376 | tf_op jit(solution)/shard_map/ppermute | solution.py:477
  18.8 0.5 %collective-permute-start.6 = (bf16[96,768]{1,0:T(8,128)(2,1)S(1)}, bf16[96,768]{1,0:T(8,128)(2,1)S(1)}, u32[]{:S(2)}, u32[]{:S(2)}) collective-permute-start(bf16[96,768]{1,0:T(8,128)(2,1)S(1)} %lone.1.refs_0_), channel_id=1, source_target_pairs={{0,4},{4,0},{8,12},{12,8},{1,5},{5,1},{9,13},{13,9},{2,6},{6,2},{1... | collective-permute-start | bytes 442376 | tf_op jit(solution)/shard_map/ppermute | solution.py:477
  19.3 0.0 collective-permute-done.5.first_edge_ref
  19.3 0.0 collective-permute-done.4.first_tile_ref
  19.3 0.7 %rest.3 = bf16[128,384]{1,0:T(8,128)(2,1)S(1)} custom-call(bf16[512,384]{1,0:T(8,128)(2,1)S(1)} %bitcast.7, bf16[2,288,384]{2,1,0:T(8,128)(2,1)S(1)} %edges.1.edge_ref, bf16[2,512,384]{2,1,0:T(8,128)(2,1)S(1)} %collective-permute-done.4.first_tile_ref, bf16[2,288,384]{2,1,0:T(8,128)(2,1)S(1)} %collective-permute-done.5.first_edge_ref, ...), custom_call_target="tpu_custom_call" | custom-call | tf_op jit(solution)/shard_map/rest/pallas_call | solution.py:465
  20.0 0.4 collective-permute-start.9
  20.4 1.2 %rest.4 = (bf16[128,384]{1,0:T(8,128)(2,1)S(1)}, bf16[128,384]{1,0:T(8,128)(2,1)S(1)}) custom-call(bf16[512,384]{1,0:T(8,128)(2,1)S(1)} %bitcast.8, bf16[2,288,384]{2,1,0:T(8,128)(2,1)S(1)} %edges.1.edge_ref, bf16[2,512,384]{2,1,0:T(8,128)(2,1)S(1)} %collective-permute-done.4.first_tile_ref, bf16[2,288,384]{2,1,0:T(8,128)(2,1)S(1)} %collective-permute-done.5.first_edge_ref, ...), custom_call_target="tpu_custom_call" | custom-call | tf_op jit(solution)/shard_map/rest/pallas_call | solution.py:465
  21.5 0.0 copy-start
  21.5 1.6 %collective-permute-done.8.refs_3_ = bf16[96,768]{1,0:T(8,128)(2,1)S(1)} collective-permute-done((bf16[96,768]{1,0:T(8,128)(2,1)S(1)}, bf16[96,768]{1,0:T(8,128)(2,1)S(1)}, u32[]{:S(2)}, u32[]{:S(2)}) %collective-permute-start.8) | collective-permute-done | bytes 147488 | tf_op jit(solution)/shard_map/ppermute | solution.py:477
  23.1 1.1 %collective-permute-done.7.refs_2_ = bf16[96,768]{1,0:T(8,128)(2,1)S(1)} collective-permute-done((bf16[96,768]{1,0:T(8,128)(2,1)S(1)}, bf16[96,768]{1,0:T(8,128)(2,1)S(1)}, u32[]{:S(2)}, u32[]{:S(2)}) %collective-permute-start.7) | collective-permute-done | bytes 147488 | tf_op jit(solution)/shard_map/ppermute | solution.py:477
  24.2 0.0 collective-permute-done.6.refs_1_
  24.2 0.3 collective-permute-start.11
  24.5 0.1 stack.1.part_ref
  24.6 2.8 %collective-permute-done.9.got_ref = bf16[128,384]{1,0:T(8,128)(2,1)S(1)} collective-permute-done((bf16[128,384]{1,0:T(8,128)(2,1)S(1)}, bf16[128,384]{1,0:T(8,128)(2,1)S(1)}, u32[]{:S(2)}, u32[]{:S(2)}) %collective-permute-start.9) | collective-permute-done | bytes 98336 | tf_op jit(solution)/shard_map/ppermute | solution.py:477
  27.4 0.0 copy-done
  27.4 0.4 project.4
  27.8 0.6 %collective-permute-start.13 = (bf16[128,768]{1,0:T(8,128)(2,1)S(1)}, bf16[128,768]{1,0:T(8,128)(2,1)S(1)}, u32[]{:S(2)}, u32[]{:S(2)}) collective-permute-start(bf16[128,768]{1,0:T(8,128)(2,1)S(1)} %project.4), channel_id=1, source_target_pairs={{0,1},{1,0},{2,3},{3,2},{4,5},{5,4},{6,7},{7,6},{8,9},{9,8},{10,11... | collective-permute-start | bytes 589832 | tf_op jit(solution)/shard_map/ppermute | solution.py:477
  28.4 0.0 collective-permute-start.10
  28.4 0.7 %rest.5.own_ref = bf16[128,384]{1,0:T(8,128)(2,1)S(1)} custom-call(bf16[512,384]{1,0:T(8,128)(2,1)S(1)} %bitcast.9, bf16[2,288,384]{2,1,0:T(8,128)(2,1)S(1)} %edges.1.edge_ref, bf16[2,512,384]{2,1,0:T(8,128)(2,1)S(1)} %collective-permute-done.4.first_tile_ref, bf16[2,288,384]{2,1,0:T(8,128)(2,1)S(1)} %collective-permute-done.5.first_edge_ref, ...), custom_call_target="tpu_custom_call" | custom-call | flops 20000000000 | tf_op jit(solution)/shard_map/rest/pallas_call | solution.py:465
  29.0 1.3 %collective-permute-done.10.part_ref = bf16[384,768]{1,0:T(8,128)(2,1)S(1)} collective-permute-done((bf16[384,768]{1,0:T(8,128)(2,1)S(1)}, bf16[384,768]{1,0:T(8,128)(2,1)S(1)}, u32[]{:S(2)}, u32[]{:S(2)}) %collective-permute-start.10) | collective-permute-done | bytes 589856 | tf_op jit(solution)/shard_map/ppermute | solution.py:477
  30.4 0.4 project.5
  30.7 1.6 %collective-permute-start.12 = (bf16[128,768]{1,0:T(8,128)(2,1)S(1)}, bf16[128,768]{1,0:T(8,128)(2,1)S(1)}, u32[]{:S(2)}, u32[]{:S(2)}) collective-permute-start(bf16[128,768]{1,0:T(8,128)(2,1)S(1)} %project.5), channel_id=1, source_target_pairs={{0,1},{1,0},{2,3},{3,2},{4,5},{5,4},{6,7},{7,6},{8,9},{9,8},{10,11... | collective-permute-start | bytes 589832 | tf_op jit(solution)/shard_map/ppermute | solution.py:477
  32.3 0.0 collective-permute-done.11.got_ref
  32.3 0.4 project.6.mine_ref
  32.7 0.4 project.7.mine_ref
  33.1 0.9 %collective-permute-done.13.got_ref = bf16[128,768]{1,0:T(8,128)(2,1)S(1)} collective-permute-done((bf16[128,768]{1,0:T(8,128)(2,1)S(1)}, bf16[128,768]{1,0:T(8,128)(2,1)S(1)}, u32[]{:S(2)}, u32[]{:S(2)}) %collective-permute-start.13) | collective-permute-done | bytes 196640 | tf_op jit(solution)/shard_map/ppermute | solution.py:477
  34.0 0.7 %add.2.rest_0_ = bf16[128,1536]{1,0:T(8,128)(2,1)} custom-call(f32[128,768]{1,0:T(8,128)S(1)} %project.7.mine_ref, bf16[128,768]{1,0:T(8,128)(2,1)S(1)} %collective-permute-done.13.got_ref), custom_call_target="tpu_custom_call" | custom-call | tf_op jit(solution)/shard_map/add/pallas_call | solution.py:601
  34.7 3.3 %collective-permute-done.12.got_ref = bf16[128,768]{1,0:T(8,128)(2,1)S(1)} collective-permute-done((bf16[128,768]{1,0:T(8,128)(2,1)S(1)}, bf16[128,768]{1,0:T(8,128)(2,1)S(1)}, u32[]{:S(2)}, u32[]{:S(2)}) %collective-permute-start.12) | collective-permute-done | bytes 196640 | tf_op jit(solution)/shard_map/ppermute | solution.py:477
  38.0 0.7 %add.3 = bf16[128,1536]{1,0:T(8,128)(2,1)} custom-call(f32[128,768]{1,0:T(8,128)S(1)} %project.6.mine_ref, bf16[128,768]{1,0:T(8,128)(2,1)S(1)} %collective-permute-done.12.got_ref, bf16[128,1536]{1,0:T(8,128)(2,1)} %add.2.rest_0_), custom_call_target="tpu_custom_call", output_to_operand_aliasing={{}: (2, {})} | custom-call | tf_op jit(solution)/shard_map/add/pallas_call | solution.py:601
  (2 shorter events, 0.1 us)
Async XLA Ops:
  0.0 9.3 %copy-start.1 = (bf16[1,1,2,16,16,384]{5,4,3,2,1,0:T(8,128)(2,1)S(1)}, bf16[1,1,2,16,16,384]{5,4,3,2,1,0:T(8,128)(2,1)}, u32[]{:S(2)}) copy-start(bf16[1,1,2,16,16,384]{5,4,3,2,1,0:T(8,128)(2,1)} %param.6) | copy-start | bytes 1179652
  0.0 9.3 %copy-start.2 = (s32[3,2,2]{0,2,1:T(2,128)S(1)}, s32[3,2,2]{0,2,1:T(2,128)}, u32[]{:S(2)}) copy-start(s32[3,2,2]{0,2,1:T(2,128)} %param.11) | copy-start | bytes 148
  0.0 9.3 %copy-start.3 = (s32[3]{0:T(128)S(1)}, s32[3]{0:T(128)}, u32[]{:S(2)}) copy-start(s32[3]{0:T(128)} %radius_ref.1) | copy-start | bytes 40
  1.3 11.9 %collective-permute-start = (bf16[96,768]{1,0:T(8,128)(2,1)S(1)}, bf16[96,768]{1,0:T(8,128)(2,1)S(1)}, u32[]{:S(2)}, u32[]{:S(2)}) collective-permute-start(bf16[96,768]{1,0:T(8,128)(2,1)S(1)} %get-tuple-element.52), channel_id=1, source_target_pairs={{0,2},{1,3},{2,0},{3,1},{4,6},{5,7},{6,4},{7,5},{8,10},{9,11},{10,... | collective-permute-start | bytes 442376 | tf_op jit(solution)/shard_map/ppermute | solution.py:477
  5.7 8.7 %collective-permute-start.1 = (bf16[2,2,64,384]{3,2,1,0:T(8,128)(2,1)S(1)}, bf16[2,2,64,384]{3,2,1,0:T(8,128)(2,1)S(1)}, u32[]{:S(2)}, u32[]{:S(2)}) collective-permute-start(bf16[2,2,64,384]{3,2,1,0:T(8,128)(2,1)S(1)} %get-tuple-element.69), channel_id=1, source_target_pairs={{0,8},{4,12},{8,0},{12,4},{1,9},{5,13},{9,1},{13,5},{2,10},{6,14},... | collective-permute-start | bytes 589832 | tf_op jit(solution)/shard_map/ppermute | solution.py:477
  7.3 7.1 %collective-permute-start.2 = (bf16[2,2,64,384]{3,2,1,0:T(8,128)(2,1)S(1)}, bf16[2,2,64,384]{3,2,1,0:T(8,128)(2,1)S(1)}, u32[]{:S(2)}, u32[]{:S(2)}) collective-permute-start(bf16[2,2,64,384]{3,2,1,0:T(8,128)(2,1)S(1)} %get-tuple-element.70), channel_id=1, source_target_pairs={{0,4},{4,0},{8,12},{12,8},{1,5},{5,1},{9,13},{13,9},{2,6},{6,2},{1... | collective-permute-start | bytes 589832 | tf_op jit(solution)/shard_map/ppermute | solution.py:477
  8.8 5.6 %collective-permute-start.3 = (bf16[2,2,16,384]{3,2,1,0:T(8,128)(2,1)S(1)}, bf16[2,2,16,384]{3,2,1,0:T(8,128)(2,1)S(1)}, u32[]{:S(2)}, u32[]{:S(2)}) collective-permute-start(bf16[2,2,16,384]{3,2,1,0:T(8,128)(2,1)S(1)} %get-tuple-element.71), channel_id=1, source_target_pairs={{0,12},{4,8},{8,4},{12,0},{1,13},{5,9},{9,5},{13,1},{2,14},{6,10},... | collective-permute-start | bytes 147464 | tf_op jit(solution)/shard_map/ppermute | solution.py:477
  10.7 8.7 %collective-permute-start.4 = (bf16[2,512,384]{2,1,0:T(8,128)(2,1)S(1)}, bf16[2,512,384]{2,1,0:T(8,128)(2,1)S(1)}, u32[]{:S(2)}, u32[]{:S(2)}) collective-permute-start(bf16[2,512,384]{2,1,0:T(8,128)(2,1)S(1)} %get-tuple-element.59.tile_ref), channel_id=1, source_target_pairs={{0,16},{1,17},{2,18},{3,19},{4,20},{5,21},{6,22},{7,23},{8,24},{9,... | collective-permute-start | bytes 2359304 | tf_op jit(solution)/shard_map/ppermute | solution.py:521
  14.5 4.9 %collective-permute-start.5 = (bf16[2,288,384]{2,1,0:T(8,128)(2,1)S(1)}, bf16[2,288,384]{2,1,0:T(8,128)(2,1)S(1)}, u32[]{:S(2)}, u32[]{:S(2)}) collective-permute-start(bf16[2,288,384]{2,1,0:T(8,128)(2,1)S(1)} %edges.1.edge_ref), channel_id=1, source_target_pairs={{0,16},{1,17},{2,18},{3,19},{4,20},{5,21},{6,22},{7,23},{8,24},{9,... | collective-permute-start | bytes 1327112 | tf_op jit(solution)/shard_map/ppermute | solution.py:539
  15.8 7.3 %collective-permute-start.8 = (bf16[96,768]{1,0:T(8,128)(2,1)S(1)}, bf16[96,768]{1,0:T(8,128)(2,1)S(1)}, u32[]{:S(2)}, u32[]{:S(2)}) collective-permute-start(bf16[96,768]{1,0:T(8,128)(2,1)S(1)} %lone.1.refs_0_), channel_id=1, source_target_pairs={{0,12},{4,8},{8,4},{12,0},{1,13},{5,9},{9,5},{13,1},{2,14},{6,10},... | collective-permute-start | bytes 442376 | tf_op jit(solution)/shard_map/ppermute | solution.py:477
  18.3 5.9 %collective-permute-start.7 = (bf16[96,768]{1,0:T(8,128)(2,1)S(1)}, bf16[96,768]{1,0:T(8,128)(2,1)S(1)}, u32[]{:S(2)}, u32[]{:S(2)}) collective-permute-start(bf16[96,768]{1,0:T(8,128)(2,1)S(1)} %lone.1.refs_0_), channel_id=1, source_target_pairs={{0,8},{4,12},{8,0},{12,4},{1,9},{5,13},{9,1},{13,5},{2,10},{6,14},... | collective-permute-start | bytes 442376 | tf_op jit(solution)/shard_map/ppermute | solution.py:477
  18.8 5.4 %collective-permute-start.6 = (bf16[96,768]{1,0:T(8,128)(2,1)S(1)}, bf16[96,768]{1,0:T(8,128)(2,1)S(1)}, u32[]{:S(2)}, u32[]{:S(2)}) collective-permute-start(bf16[96,768]{1,0:T(8,128)(2,1)S(1)} %lone.1.refs_0_), channel_id=1, source_target_pairs={{0,4},{4,0},{8,12},{12,8},{1,5},{5,1},{9,13},{13,9},{2,6},{6,2},{1... | collective-permute-start | bytes 442376 | tf_op jit(solution)/shard_map/ppermute | solution.py:477
  20.0 7.4 %collective-permute-start.9 = (bf16[128,384]{1,0:T(8,128)(2,1)S(1)}, bf16[128,384]{1,0:T(8,128)(2,1)S(1)}, u32[]{:S(2)}, u32[]{:S(2)}) collective-permute-start(bf16[128,384]{1,0:T(8,128)(2,1)S(1)} %rest.3), channel_id=1, source_target_pairs={{0,2},{1,3},{2,0},{3,1},{4,6},{5,7},{6,4},{7,5},{8,10},{9,11},{10,... | collective-permute-start | bytes 294920 | tf_op jit(solution)/shard_map/ppermute | solution.py:477
  21.5 5.9 %copy-start = (bf16[384,1536]{1,0:T(8,128)(2,1)S(1)}, bf16[384,1536]{1,0:T(8,128)(2,1)}, u32[]{:S(2)}) copy-start(bf16[384,1536]{1,0:T(8,128)(2,1)} %w_ref.9) | copy-start | bytes 3538948
  24.2 8.1 %collective-permute-start.11 = (bf16[128,384]{1,0:T(8,128)(2,1)S(1)}, bf16[128,384]{1,0:T(8,128)(2,1)S(1)}, u32[]{:S(2)}, u32[]{:S(2)}) collective-permute-start(bf16[128,384]{1,0:T(8,128)(2,1)S(1)} %get-tuple-element.98), channel_id=1, source_target_pairs={{0,2},{1,3},{2,0},{3,1},{4,6},{5,7},{6,4},{7,5},{8,10},{9,11},{10,... | collective-permute-start | bytes 294920 | tf_op jit(solution)/shard_map/ppermute | solution.py:477
  27.8 6.2 %collective-permute-start.13 = (bf16[128,768]{1,0:T(8,128)(2,1)S(1)}, bf16[128,768]{1,0:T(8,128)(2,1)S(1)}, u32[]{:S(2)}, u32[]{:S(2)}) collective-permute-start(bf16[128,768]{1,0:T(8,128)(2,1)S(1)} %project.4), channel_id=1, source_target_pairs={{0,1},{1,0},{2,3},{3,2},{4,5},{5,4},{6,7},{7,6},{8,9},{9,8},{10,11... | collective-permute-start | bytes 589832 | tf_op jit(solution)/shard_map/ppermute | solution.py:477
  28.4 2.0 %collective-permute-start.10 = (bf16[384,768]{1,0:T(8,128)(2,1)S(1)}, bf16[384,768]{1,0:T(8,128)(2,1)S(1)}, u32[]{:S(2)}, u32[]{:S(2)}) collective-permute-start(bf16[384,768]{1,0:T(8,128)(2,1)S(1)} %stack.1.part_ref), channel_id=1, source_target_pairs={{0,16},{16,0},{1,17},{17,1},{2,18},{18,2},{3,19},{19,3},{4,20},{20... | collective-permute-start | bytes 1769480 | tf_op jit(solution)/shard_map/ppermute | solution.py:477
  30.7 7.3 %collective-permute-start.12 = (bf16[128,768]{1,0:T(8,128)(2,1)S(1)}, bf16[128,768]{1,0:T(8,128)(2,1)S(1)}, u32[]{:S(2)}, u32[]{:S(2)}) collective-permute-start(bf16[128,768]{1,0:T(8,128)(2,1)S(1)} %project.5), channel_id=1, source_target_pairs={{0,1},{1,0},{2,3},{3,2},{4,5},{5,4},{6,7},{7,6},{8,9},{9,8},{10,11... | collective-permute-start | bytes 589832 | tf_op jit(solution)/shard_map/ppermute | solution.py:477

commit v5 on v4

--- a/solution.py
+++ b/solution.py
@@ -561,7 +561,6 @@
     got_side = flipped(for_side, "head", 2)
     state, for_side = lax.optimization_barrier((state, for_side))
     for_far, own_side = rest(state, 2, 1)
-    got_far = flipped(for_far, "head", 2)
     parts, own_side = lax.optimization_barrier((parts, own_side))
     here = call(
         stack_kernel, shape((depth, broad), bf16), [vmem] * tiles, *parts, name="stack"
@@ -583,7 +582,10 @@
 
     for_side = [project(here, own_side, got_side, bf16, 0, 20 * 10**9)]
     from_side = [flipped(for_side[0], "head", 1)]
-    state, here, for_side[0] = lax.optimization_barrier((state, here, for_side[0]))
+    state, here, for_far, for_side[0] = lax.optimization_barrier(
+        (state, here, for_far, for_side[0])
+    )
+    got_far = flipped(for_far, "head", 2)
     there = flipped(here, "tm", 1)
     (own,) = rest(state, 0, flops=20 * 10**9)
     own_side, own = lax.optimization_barrier((own_side, own))

time: 38.9 us -> 39.4 us (1.013)
  starting transfers between devices: 16.7 us -> 17.5 us
  waiting for transfers between devices: 12.4 us -> 12 us
    ppermute x12, starting transfers between devices: 14.1 us -> 14.8 us  [flipped(): lax.ppermute(value, axis, [(i, i ^ flip) for i in range(lax.axis_size(axi...]
  transfers between devices with their start and end apart: 14 -> 14, of which waited for: 7 -> 7; matrix products, arithmetic and copies ran while one was open for 0% -> 0% of each run, Pallas kernels for 19% -> 18%
where the time goes in v5:
time: 39.4 us; the launch traced here: 39.2 us
  starting transfers between devices  17.5 us (44%)
  waiting for transfers between devices  12 us (30%)
  Pallas kernels  9.49 us (24%)
    ppermute x12, starting transfers between devices, flipped(): lax.ppermute(value, axis, [(i, i ^ flip) for i in range(lax.axis_size(axi...  14.8 us
    ppermute x12, waiting for transfers between devices, flipped(): lax.ppermute(value, axis, [(i, i ^ flip) for i in range(lax.axis_size(axi...  12 us
    pallas_call x14, Pallas kernels, call(): pl.pallas_call(functools.partial(kernel, **keys_of) if keys_of else kerne...  8.07 us
    pallas_call x2, Pallas kernels, two_by_two(): pl.pallas_call(functools.partial(add_kernel, flip=flip), out_shape=shape(...  1.42 us
    ppermute x1, starting transfers between devices, two_by_two(): first_tile = lax.ppermute(tile, 'tm', [(0, 1)])  1.34 us
    ppermute x1, starting transfers between devices, two_by_two(): first_edge = lax.ppermute(edge, 'tm', [(0, 1)])  1.32 us
  transfers between devices with their start and end apart: 14, of which 7 were waited for; matrix products, arithmetic and copies ran while one was open for 0% of the time, Pallas kernels for 18%

profile of v5, /device:TPU:0, one launch (start us, length us, event | category | flops | bytes accessed | tf_op | source)
XLA Modules:
  0.0 39.2 jit_solution(12026762833884175603)
XLA Ops:
  0.0 0.0 copy-start.1
  0.0 0.0 copy-start.2
  0.0 0.0 copy-start.3
  0.0 1.3 %load.1 = (bf16[2,512,384]{2,1,0:T(8,128)(2,1)S(1)}, bf16[96,768]{1,0:T(8,128)(2,1)S(1)}) custom-call(bf16[512,384]{1,0:T(8,128)(2,1)} %bitcast.11, bf16[512,384]{1,0:T(8,128)(2,1)} %bitcast.12, bf16[384,1536]{1,0:T(8,128)(2,1)} %w_ref.9), custom_call_target="tpu_custom_call" | custom-call | tf_op jit(solution)/shard_map/load/pallas_call | solution.py:465
  1.3 4.1 %collective-permute-start = (bf16[96,768]{1,0:T(8,128)(2,1)S(1)}, bf16[96,768]{1,0:T(8,128)(2,1)S(1)}, u32[]{:S(2)}, u32[]{:S(2)}) collective-permute-start(bf16[96,768]{1,0:T(8,128)(2,1)S(1)} %get-tuple-element.53), channel_id=1, source_target_pairs={{0,2},{1,3},{2,0},{3,1},{4,6},{5,7},{6,4},{7,5},{8,10},{9,11},{10,... | collective-permute-start | bytes 442376 | tf_op jit(solution)/shard_map/ppermute | solution.py:477
  5.4 0.3 faces.1
  5.7 1.6 %collective-permute-start.1 = (bf16[2,2,64,384]{3,2,1,0:T(8,128)(2,1)S(1)}, bf16[2,2,64,384]{3,2,1,0:T(8,128)(2,1)S(1)}, u32[]{:S(2)}, u32[]{:S(2)}) collective-permute-start(bf16[2,2,64,384]{3,2,1,0:T(8,128)(2,1)S(1)} %get-tuple-element.70), channel_id=1, source_target_pairs={{0,8},{4,12},{8,0},{12,4},{1,9},{5,13},{9,1},{13,5},{2,10},{6,14},... | collective-permute-start | bytes 589832 | tf_op jit(solution)/shard_map/ppermute | solution.py:477
  7.3 1.5 %collective-permute-start.2 = (bf16[2,2,64,384]{3,2,1,0:T(8,128)(2,1)S(1)}, bf16[2,2,64,384]{3,2,1,0:T(8,128)(2,1)S(1)}, u32[]{:S(2)}, u32[]{:S(2)}) collective-permute-start(bf16[2,2,64,384]{3,2,1,0:T(8,128)(2,1)S(1)} %get-tuple-element.71), channel_id=1, source_target_pairs={{0,4},{4,0},{8,12},{12,8},{1,5},{5,1},{9,13},{13,9},{2,6},{6,2},{1... | collective-permute-start | bytes 589832 | tf_op jit(solution)/shard_map/ppermute | solution.py:477
  8.8 0.5 %collective-permute-start.3 = (bf16[2,2,16,384]{3,2,1,0:T(8,128)(2,1)S(1)}, bf16[2,2,16,384]{3,2,1,0:T(8,128)(2,1)S(1)}, u32[]{:S(2)}, u32[]{:S(2)}) collective-permute-start(bf16[2,2,16,384]{3,2,1,0:T(8,128)(2,1)S(1)} %get-tuple-element.72), channel_id=1, source_target_pairs={{0,12},{4,8},{8,4},{12,0},{1,13},{5,9},{9,5},{13,1},{2,14},{6,10},... | collective-permute-start | bytes 147464 | tf_op jit(solution)/shard_map/ppermute | solution.py:477
  9.3 0.0 copy-done.1
  9.3 0.0 copy-done.2
  9.3 0.0 copy-done.3
  9.3 1.4 %begin.1 = (f32[512,128]{1,0:T(8,128)S(1)}, f32[512,128]{1,0:T(8,128)S(1)}, f32[512,128]{1,0:T(8,128)S(1)}, s32[256,800]{1,0:T(8,128)S(1)}, s32[6,128]{1,0:T(8,128)S(1)}) custom-call(s32[3]{0:T(128)S(1)} %copy-done.3, s32[2,2,3]{2,1,0:T(2,128)S(1)} %bitcast.10, bf16[512,384]{1,0:T(8,128)(2,1)S(1)} %bitcast.5, bf16[2,512,384]{2,1,0:T(8,128)(2,1)S(1)} %get-tuple-element.60.tile_ref), custom_call_target="tpu_custom_call" | custom-call | tf_op jit(solution)/shard_map/begin/pallas_call | solution.py:465
  10.7 1.3 %collective-permute-start.4 = (bf16[2,512,384]{2,1,0:T(8,128)(2,1)S(1)}, bf16[2,512,384]{2,1,0:T(8,128)(2,1)S(1)}, u32[]{:S(2)}, u32[]{:S(2)}) collective-permute-start(bf16[2,512,384]{2,1,0:T(8,128)(2,1)S(1)} %get-tuple-element.60.tile_ref), channel_id=1, source_target_pairs={{0,16},{1,17},{2,18},{3,19},{4,20},{5,21},{6,22},{7,23},{8,24},{9,... | collective-permute-start | bytes 2359304 | tf_op jit(solution)/shard_map/ppermute | solution.py:521
  12.0 1.1 %tile.1 = (f32[512,256]{1,0:T(8,128)S(1)}, f32[512,256]{1,0:T(8,128)S(1)}, f32[512,256]{1,0:T(8,128)S(1)}) custom-call(bf16[512,384]{1,0:T(8,128)(2,1)S(1)} %bitcast.6, bf16[2,512,384]{2,1,0:T(8,128)(2,1)S(1)} %get-tuple-element.60.tile_ref, s32[256,800]{1,0:T(8,128)S(1)} %get-tuple-element.61.dist_ref.rest_3_, s32[6,128]{1,0:T(8,128)S(1)} %get-tuple-element.62.reach_ref.rest_4_), custom_call_target="tpu_custom_call" | custom-call | tf_op jit(solution)/shard_map/tile/pallas_call | solution.py:465
  13.1 0.0 collective-permute-done.in_ref
  13.2 1.3 %collective-permute-done.3.corner_ref = bf16[2,2,16,384]{3,2,1,0:T(8,128)(2,1)S(1)} collective-permute-done((bf16[2,2,16,384]{3,2,1,0:T(8,128)(2,1)S(1)}, bf16[2,2,16,384]{3,2,1,0:T(8,128)(2,1)S(1)}, u32[]{:S(2)}, u32[]{:S(2)}) %collective-permute-start.3) | collective-permute-done | bytes 49184 | tf_op jit(solution)/shard_map/ppermute | solution.py:477
  14.4 0.0 collective-permute-done.1.row_ref
  14.4 0.0 collective-permute-done.2.col_ref
  14.5 1.3 %collective-permute-start.5 = (bf16[2,288,384]{2,1,0:T(8,128)(2,1)S(1)}, bf16[2,288,384]{2,1,0:T(8,128)(2,1)S(1)}, u32[]{:S(2)}, u32[]{:S(2)}) collective-permute-start(bf16[2,288,384]{2,1,0:T(8,128)(2,1)S(1)} %edges.1.edge_ref), channel_id=1, source_target_pairs={{0,16},{1,17},{2,18},{3,19},{4,20},{5,21},{6,22},{7,23},{8,24},{9,... | collective-permute-start | bytes 1327112 | tf_op jit(solution)/shard_map/ppermute | solution.py:539
  15.8 2.5 %collective-permute-start.8 = (bf16[96,768]{1,0:T(8,128)(2,1)S(1)}, bf16[96,768]{1,0:T(8,128)(2,1)S(1)}, u32[]{:S(2)}, u32[]{:S(2)}) collective-permute-start(bf16[96,768]{1,0:T(8,128)(2,1)S(1)} %lone.1.refs_0_), channel_id=1, source_target_pairs={{0,12},{4,8},{8,4},{12,0},{1,13},{5,9},{9,5},{13,1},{2,14},{6,10},... | collective-permute-start | bytes 442376 | tf_op jit(solution)/shard_map/ppermute | solution.py:477
  18.3 0.5 %collective-permute-start.7 = (bf16[96,768]{1,0:T(8,128)(2,1)S(1)}, bf16[96,768]{1,0:T(8,128)(2,1)S(1)}, u32[]{:S(2)}, u32[]{:S(2)}) collective-permute-start(bf16[96,768]{1,0:T(8,128)(2,1)S(1)} %lone.1.refs_0_), channel_id=1, source_target_pairs={{0,8},{4,12},{8,0},{12,4},{1,9},{5,13},{9,1},{13,5},{2,10},{6,14},... | collective-permute-start | bytes 442376 | tf_op jit(solution)/shard_map/ppermute | solution.py:477
  18.8 0.5 %collective-permute-start.6 = (bf16[96,768]{1,0:T(8,128)(2,1)S(1)}, bf16[96,768]{1,0:T(8,128)(2,1)S(1)}, u32[]{:S(2)}, u32[]{:S(2)}) collective-permute-start(bf16[96,768]{1,0:T(8,128)(2,1)S(1)} %lone.1.refs_0_), channel_id=1, source_target_pairs={{0,4},{4,0},{8,12},{12,8},{1,5},{5,1},{9,13},{13,9},{2,6},{6,2},{1... | collective-permute-start | bytes 442376 | tf_op jit(solution)/shard_map/ppermute | solution.py:477
  19.3 0.0 collective-permute-done.5.first_edge_ref
  19.3 0.0 collective-permute-done.4.first_tile_ref
  19.3 0.7 %rest.3 = bf16[128,384]{1,0:T(8,128)(2,1)S(1)} custom-call(bf16[512,384]{1,0:T(8,128)(2,1)S(1)} %bitcast.7, bf16[2,288,384]{2,1,0:T(8,128)(2,1)S(1)} %edges.1.edge_ref, bf16[2,512,384]{2,1,0:T(8,128)(2,1)S(1)} %collective-permute-done.4.first_tile_ref, bf16[2,288,384]{2,1,0:T(8,128)(2,1)S(1)} %collective-permute-done.5.first_edge_ref, ...), custom_call_target="tpu_custom_call" | custom-call | tf_op jit(solution)/shard_map/rest/pallas_call | solution.py:465
  20.0 0.4 collective-permute-start.9
  20.4 1.2 %rest.4 = (bf16[128,384]{1,0:T(8,128)(2,1)S(1)}, bf16[128,384]{1,0:T(8,128)(2,1)S(1)}) custom-call(bf16[512,384]{1,0:T(8,128)(2,1)S(1)} %bitcast.8, bf16[2,288,384]{2,1,0:T(8,128)(2,1)S(1)} %edges.1.edge_ref, bf16[2,512,384]{2,1,0:T(8,128)(2,1)S(1)} %collective-permute-done.4.first_tile_ref, bf16[2,288,384]{2,1,0:T(8,128)(2,1)S(1)} %collective-permute-done.5.first_edge_ref, ...), custom_call_target="tpu_custom_call" | custom-call | tf_op jit(solution)/shard_map/rest/pallas_call | solution.py:465
  21.5 0.0 copy-start
  21.5 1.6 %collective-permute-done.8.refs_3_ = bf16[96,768]{1,0:T(8,128)(2,1)S(1)} collective-permute-done((bf16[96,768]{1,0:T(8,128)(2,1)S(1)}, bf16[96,768]{1,0:T(8,128)(2,1)S(1)}, u32[]{:S(2)}, u32[]{:S(2)}) %collective-permute-start.8) | collective-permute-done | bytes 147488 | tf_op jit(solution)/shard_map/ppermute | solution.py:477
  23.1 1.1 %collective-permute-done.7.refs_2_ = bf16[96,768]{1,0:T(8,128)(2,1)S(1)} collective-permute-done((bf16[96,768]{1,0:T(8,128)(2,1)S(1)}, bf16[96,768]{1,0:T(8,128)(2,1)S(1)}, u32[]{:S(2)}, u32[]{:S(2)}) %collective-permute-start.7) | collective-permute-done | bytes 147488 | tf_op jit(solution)/shard_map/ppermute | solution.py:477
  24.2 0.0 collective-permute-done.6.refs_1_
  24.2 0.1 stack.1.part_ref
  24.3 1.3 %collective-permute-done.9.got_ref = bf16[128,384]{1,0:T(8,128)(2,1)S(1)} collective-permute-done((bf16[128,384]{1,0:T(8,128)(2,1)S(1)}, bf16[128,384]{1,0:T(8,128)(2,1)S(1)}, u32[]{:S(2)}, u32[]{:S(2)}) %collective-permute-start.9) | collective-permute-done | bytes 98336 | tf_op jit(solution)/shard_map/ppermute | solution.py:477
  25.6 0.0 copy-done
  25.6 0.4 project.4
  26.0 1.7 %collective-permute-start.13 = (bf16[128,768]{1,0:T(8,128)(2,1)S(1)}, bf16[128,768]{1,0:T(8,128)(2,1)S(1)}, u32[]{:S(2)}, u32[]{:S(2)}) collective-permute-start(bf16[128,768]{1,0:T(8,128)(2,1)S(1)} %project.4), channel_id=1, source_target_pairs={{0,1},{1,0},{2,3},{3,2},{4,5},{5,4},{6,7},{7,6},{8,9},{9,8},{10,11... | collective-permute-start | bytes 589832 | tf_op jit(solution)/shard_map/ppermute | solution.py:477
  27.6 1.4 %collective-permute-start.11 = (bf16[128,384]{1,0:T(8,128)(2,1)S(1)}, bf16[128,384]{1,0:T(8,128)(2,1)S(1)}, u32[]{:S(2)}, u32[]{:S(2)}) collective-permute-start(bf16[128,384]{1,0:T(8,128)(2,1)S(1)} %get-tuple-element.100), channel_id=1, source_target_pairs={{0,2},{1,3},{2,0},{3,1},{4,6},{5,7},{6,4},{7,5},{8,10},{9,11},{10,... | collective-permute-start | bytes 294920 | tf_op jit(solution)/shard_map/ppermute | solution.py:477
  29.1 0.0 collective-permute-start.10
  29.1 0.7 %rest.5.own_ref = bf16[128,384]{1,0:T(8,128)(2,1)S(1)} custom-call(bf16[512,384]{1,0:T(8,128)(2,1)S(1)} %bitcast.9, bf16[2,288,384]{2,1,0:T(8,128)(2,1)S(1)} %edges.1.edge_ref, bf16[2,512,384]{2,1,0:T(8,128)(2,1)S(1)} %collective-permute-done.4.first_tile_ref, bf16[2,288,384]{2,1,0:T(8,128)(2,1)S(1)} %collective-permute-done.5.first_edge_ref, ...), custom_call_target="tpu_custom_call" | custom-call | flops 20000000000 | tf_op jit(solution)/shard_map/rest/pallas_call | solution.py:465
  29.8 1.3 %collective-permute-done.10.part_ref = bf16[384,768]{1,0:T(8,128)(2,1)S(1)} collective-permute-done((bf16[384,768]{1,0:T(8,128)(2,1)S(1)}, bf16[384,768]{1,0:T(8,128)(2,1)S(1)}, u32[]{:S(2)}, u32[]{:S(2)}) %collective-permute-start.10) | collective-permute-done | bytes 589856 | tf_op jit(solution)/shard_map/ppermute | solution.py:477
  31.1 0.4 project.5
  31.5 0.1 collective-permute-start.12
  31.6 2.1 %collective-permute-done.11.got_ref = bf16[128,384]{1,0:T(8,128)(2,1)S(1)} collective-permute-done((bf16[128,384]{1,0:T(8,128)(2,1)S(1)}, bf16[128,384]{1,0:T(8,128)(2,1)S(1)}, u32[]{:S(2)}, u32[]{:S(2)}) %collective-permute-start.11) | collective-permute-done | bytes 98336 | tf_op jit(solution)/shard_map/ppermute | solution.py:477
  33.7 0.4 project.6.mine_ref
  34.1 0.4 project.7.mine_ref
  34.5 0.0 collective-permute-done.13.got_ref
  34.5 0.7 %add.2.rest_0_ = bf16[128,1536]{1,0:T(8,128)(2,1)} custom-call(f32[128,768]{1,0:T(8,128)S(1)} %project.7.mine_ref, bf16[128,768]{1,0:T(8,128)(2,1)S(1)} %collective-permute-done.13.got_ref), custom_call_target="tpu_custom_call" | custom-call | tf_op jit(solution)/shard_map/add/pallas_call | solution.py:603
  35.2 3.3 %collective-permute-done.12.got_ref = bf16[128,768]{1,0:T(8,128)(2,1)S(1)} collective-permute-done((bf16[128,768]{1,0:T(8,128)(2,1)S(1)}, bf16[128,768]{1,0:T(8,128)(2,1)S(1)}, u32[]{:S(2)}, u32[]{:S(2)}) %collective-permute-start.12) | collective-permute-done | bytes 196640 | tf_op jit(solution)/shard_map/ppermute | solution.py:477
  38.5 0.7 %add.3 = bf16[128,1536]{1,0:T(8,128)(2,1)} custom-call(f32[128,768]{1,0:T(8,128)S(1)} %project.6.mine_ref, bf16[128,768]{1,0:T(8,128)(2,1)S(1)} %collective-permute-done.12.got_ref, bf16[128,1536]{1,0:T(8,128)(2,1)} %add.2.rest_0_), custom_call_target="tpu_custom_call", output_to_operand_aliasing={{}: (2, {})} | custom-call | tf_op jit(solution)/shard_map/add/pallas_call | solution.py:603
  (2 shorter events, 0.1 us)
Async XLA Ops:
  0.0 9.3 %copy-start.1 = (bf16[1,1,2,16,16,384]{5,4,3,2,1,0:T(8,128)(2,1)S(1)}, bf16[1,1,2,16,16,384]{5,4,3,2,1,0:T(8,128)(2,1)}, u32[]{:S(2)}) copy-start(bf16[1,1,2,16,16,384]{5,4,3,2,1,0:T(8,128)(2,1)} %param.6) | copy-start | bytes 1179652
  0.0 9.3 %copy-start.2 = (s32[3,2,2]{0,2,1:T(2,128)S(1)}, s32[3,2,2]{0,2,1:T(2,128)}, u32[]{:S(2)}) copy-start(s32[3,2,2]{0,2,1:T(2,128)} %param.11) | copy-start | bytes 148
  0.0 9.3 %copy-start.3 = (s32[3]{0:T(128)S(1)}, s32[3]{0:T(128)}, u32[]{:S(2)}) copy-start(s32[3]{0:T(128)} %radius_ref.1) | copy-start | bytes 40
  1.3 11.9 %collective-permute-start = (bf16[96,768]{1,0:T(8,128)(2,1)S(1)}, bf16[96,768]{1,0:T(8,128)(2,1)S(1)}, u32[]{:S(2)}, u32[]{:S(2)}) collective-permute-start(bf16[96,768]{1,0:T(8,128)(2,1)S(1)} %get-tuple-element.53), channel_id=1, source_target_pairs={{0,2},{1,3},{2,0},{3,1},{4,6},{5,7},{6,4},{7,5},{8,10},{9,11},{10,... | collective-permute-start | bytes 442376 | tf_op jit(solution)/shard_map/ppermute | solution.py:477
  5.7 8.7 %collective-permute-start.1 = (bf16[2,2,64,384]{3,2,1,0:T(8,128)(2,1)S(1)}, bf16[2,2,64,384]{3,2,1,0:T(8,128)(2,1)S(1)}, u32[]{:S(2)}, u32[]{:S(2)}) collective-permute-start(bf16[2,2,64,384]{3,2,1,0:T(8,128)(2,1)S(1)} %get-tuple-element.70), channel_id=1, source_target_pairs={{0,8},{4,12},{8,0},{12,4},{1,9},{5,13},{9,1},{13,5},{2,10},{6,14},... | collective-permute-start | bytes 589832 | tf_op jit(solution)/shard_map/ppermute | solution.py:477
  7.3 7.1 %collective-permute-start.2 = (bf16[2,2,64,384]{3,2,1,0:T(8,128)(2,1)S(1)}, bf16[2,2,64,384]{3,2,1,0:T(8,128)(2,1)S(1)}, u32[]{:S(2)}, u32[]{:S(2)}) collective-permute-start(bf16[2,2,64,384]{3,2,1,0:T(8,128)(2,1)S(1)} %get-tuple-element.71), channel_id=1, source_target_pairs={{0,4},{4,0},{8,12},{12,8},{1,5},{5,1},{9,13},{13,9},{2,6},{6,2},{1... | collective-permute-start | bytes 589832 | tf_op jit(solution)/shard_map/ppermute | solution.py:477
  8.8 5.6 %collective-permute-start.3 = (bf16[2,2,16,384]{3,2,1,0:T(8,128)(2,1)S(1)}, bf16[2,2,16,384]{3,2,1,0:T(8,128)(2,1)S(1)}, u32[]{:S(2)}, u32[]{:S(2)}) collective-permute-start(bf16[2,2,16,384]{3,2,1,0:T(8,128)(2,1)S(1)} %get-tuple-element.72), channel_id=1, source_target_pairs={{0,12},{4,8},{8,4},{12,0},{1,13},{5,9},{9,5},{13,1},{2,14},{6,10},... | collective-permute-start | bytes 147464 | tf_op jit(solution)/shard_map/ppermute | solution.py:477
  10.7 8.7 %collective-permute-start.4 = (bf16[2,512,384]{2,1,0:T(8,128)(2,1)S(1)}, bf16[2,512,384]{2,1,0:T(8,128)(2,1)S(1)}, u32[]{:S(2)}, u32[]{:S(2)}) collective-permute-start(bf16[2,512,384]{2,1,0:T(8,128)(2,1)S(1)} %get-tuple-element.60.tile_ref), channel_id=1, source_target_pairs={{0,16},{1,17},{2,18},{3,19},{4,20},{5,21},{6,22},{7,23},{8,24},{9,... | collective-permute-start | bytes 2359304 | tf_op jit(solution)/shard_map/ppermute | solution.py:521
  14.5 4.9 %collective-permute-start.5 = (bf16[2,288,384]{2,1,0:T(8,128)(2,1)S(1)}, bf16[2,288,384]{2,1,0:T(8,128)(2,1)S(1)}, u32[]{:S(2)}, u32[]{:S(2)}) collective-permute-start(bf16[2,288,384]{2,1,0:T(8,128)(2,1)S(1)} %edges.1.edge_ref), channel_id=1, source_target_pairs={{0,16},{1,17},{2,18},{3,19},{4,20},{5,21},{6,22},{7,23},{8,24},{9,... | collective-permute-start | bytes 1327112 | tf_op jit(solution)/shard_map/ppermute | solution.py:539
  15.8 7.3 %collective-permute-start.8 = (bf16[96,768]{1,0:T(8,128)(2,1)S(1)}, bf16[96,768]{1,0:T(8,128)(2,1)S(1)}, u32[]{:S(2)}, u32[]{:S(2)}) collective-permute-start(bf16[96,768]{1,0:T(8,128)(2,1)S(1)} %lone.1.refs_0_), channel_id=1, source_target_pairs={{0,12},{4,8},{8,4},{12,0},{1,13},{5,9},{9,5},{13,1},{2,14},{6,10},... | collective-permute-start | bytes 442376 | tf_op jit(solution)/shard_map/ppermute | solution.py:477
  18.3 5.9 %collective-permute-start.7 = (bf16[96,768]{1,0:T(8,128)(2,1)S(1)}, bf16[96,768]{1,0:T(8,128)(2,1)S(1)}, u32[]{:S(2)}, u32[]{:S(2)}) collective-permute-start(bf16[96,768]{1,0:T(8,128)(2,1)S(1)} %lone.1.refs_0_), channel_id=1, source_target_pairs={{0,8},{4,12},{8,0},{12,4},{1,9},{5,13},{9,1},{13,5},{2,10},{6,14},... | collective-permute-start | bytes 442376 | tf_op jit(solution)/shard_map/ppermute | solution.py:477
  18.8 5.4 %collective-permute-start.6 = (bf16[96,768]{1,0:T(8,128)(2,1)S(1)}, bf16[96,768]{1,0:T(8,128)(2,1)S(1)}, u32[]{:S(2)}, u32[]{:S(2)}) collective-permute-start(bf16[96,768]{1,0:T(8,128)(2,1)S(1)} %lone.1.refs_0_), channel_id=1, source_target_pairs={{0,4},{4,0},{8,12},{12,8},{1,5},{5,1},{9,13},{13,9},{2,6},{6,2},{1... | collective-permute-start | bytes 442376 | tf_op jit(solution)/shard_map/ppermute | solution.py:477
  20.0 5.6 %collective-permute-start.9 = (bf16[128,384]{1,0:T(8,128)(2,1)S(1)}, bf16[128,384]{1,0:T(8,128)(2,1)S(1)}, u32[]{:S(2)}, u32[]{:S(2)}) collective-permute-start(bf16[128,384]{1,0:T(8,128)(2,1)S(1)} %rest.3), channel_id=1, source_target_pairs={{0,2},{1,3},{2,0},{3,1},{4,6},{5,7},{6,4},{7,5},{8,10},{9,11},{10,... | collective-permute-start | bytes 294920 | tf_op jit(solution)/shard_map/ppermute | solution.py:477
  21.5 4.1 %copy-start = (bf16[384,1536]{1,0:T(8,128)(2,1)S(1)}, bf16[384,1536]{1,0:T(8,128)(2,1)}, u32[]{:S(2)}) copy-start(bf16[384,1536]{1,0:T(8,128)(2,1)} %w_ref.9) | copy-start | bytes 3538948
  26.0 8.5 %collective-permute-start.13 = (bf16[128,768]{1,0:T(8,128)(2,1)S(1)}, bf16[128,768]{1,0:T(8,128)(2,1)S(1)}, u32[]{:S(2)}, u32[]{:S(2)}) collective-permute-start(bf16[128,768]{1,0:T(8,128)(2,1)S(1)} %project.4), channel_id=1, source_target_pairs={{0,1},{1,0},{2,3},{3,2},{4,5},{5,4},{6,7},{7,6},{8,9},{9,8},{10,11... | collective-permute-start | bytes 589832 | tf_op jit(solution)/shard_map/ppermute | solution.py:477
  27.6 6.1 %collective-permute-start.11 = (bf16[128,384]{1,0:T(8,128)(2,1)S(1)}, bf16[128,384]{1,0:T(8,128)(2,1)S(1)}, u32[]{:S(2)}, u32[]{:S(2)}) collective-permute-start(bf16[128,384]{1,0:T(8,128)(2,1)S(1)} %get-tuple-element.100), channel_id=1, source_target_pairs={{0,2},{1,3},{2,0},{3,1},{4,6},{5,7},{6,4},{7,5},{8,10},{9,11},{10,... | collective-permute-start | bytes 294920 | tf_op jit(solution)/shard_map/ppermute | solution.py:477
  29.1 2.0 %collective-permute-start.10 = (bf16[384,768]{1,0:T(8,128)(2,1)S(1)}, bf16[384,768]{1,0:T(8,128)(2,1)S(1)}, u32[]{:S(2)}, u32[]{:S(2)}) collective-permute-start(bf16[384,768]{1,0:T(8,128)(2,1)S(1)} %stack.1.part_ref), channel_id=1, source_target_pairs={{0,16},{16,0},{1,17},{17,1},{2,18},{18,2},{3,19},{19,3},{4,20},{20... | collective-permute-start | bytes 1769480 | tf_op jit(solution)/shard_map/ppermute | solution.py:477
  31.5 7.0 %collective-permute-start.12 = (bf16[128,768]{1,0:T(8,128)(2,1)S(1)}, bf16[128,768]{1,0:T(8,128)(2,1)S(1)}, u32[]{:S(2)}, u32[]{:S(2)}) collective-permute-start(bf16[128,768]{1,0:T(8,128)(2,1)S(1)} %project.5), channel_id=1, source_target_pairs={{0,1},{1,0},{2,3},{3,2},{4,5},{5,4},{6,7},{7,6},{8,9},{9,8},{10,11... | collective-permute-start | bytes 589832 | tf_op jit(solution)/shard_map/ppermute | solution.py:477

commit v6 on v4

--- a/solution.py
+++ b/solution.py
@@ -567,6 +567,8 @@
         stack_kernel, shape((depth, broad), bf16), [vmem] * tiles, *parts, name="stack"
     )
 
+    there = flipped(here, "tm", 1)
+
     def project(part, mine, got, kind, flip, flops=0):
         return call(
             project_kernel,
@@ -583,13 +585,11 @@
 
     for_side = [project(here, own_side, got_side, bf16, 0, 20 * 10**9)]
     from_side = [flipped(for_side[0], "head", 1)]
-    state, here, for_side[0] = lax.optimization_barrier((state, here, for_side[0]))
-    there = flipped(here, "tm", 1)
-    (own,) = rest(state, 0, flops=20 * 10**9)
-    own_side, own = lax.optimization_barrier((own_side, own))
+    state, for_side[0] = lax.optimization_barrier((state, for_side[0]))
     for_side.append(project(there, own_side, got_side, bf16, 1))
     from_side.append(flipped(for_side[1], "head", 1))
-    own, for_side[1] = lax.optimization_barrier((own, for_side[1]))
+    state, for_side[1] = lax.optimization_barrier((state, for_side[1]))
+    (own,) = rest(state, 0, flops=20 * 10**9)
     mine = [
         project(here, own, got_far, f32, 0),
         project(there, own, got_far, f32, 1, 20 * 10**9),

time: 38.9 us -> 39.2 us (level)
  transfers between devices with their start and end apart: 14 -> 14, of which waited for: 7 -> 6; matrix products, arithmetic and copies ran while one was open for 0% -> 0% of each run, Pallas kernels for 19% -> 19%
where the time goes in v6:
time: 39.2 us; the launch traced here: 39 us
  starting transfers between devices  16.9 us (43%)
  waiting for transfers between devices  12.5 us (32%)
  Pallas kernels  9.5 us (24%)
    ppermute x12, starting transfers between devices, flipped(): lax.ppermute(value, axis, [(i, i ^ flip) for i in range(lax.axis_size(axi...  14.2 us
    ppermute x12, waiting for transfers between devices, flipped(): lax.ppermute(value, axis, [(i, i ^ flip) for i in range(lax.axis_size(axi...  12.5 us
    pallas_call x14, Pallas kernels, call(): pl.pallas_call(functools.partial(kernel, **keys_of) if keys_of else kerne...  8.07 us
    pallas_call x2, Pallas kernels, two_by_two(): pl.pallas_call(functools.partial(add_kernel, flip=flip), out_shape=shape(...  1.42 us
    ppermute x1, starting transfers between devices, two_by_two(): first_tile = lax.ppermute(tile, 'tm', [(0, 1)])  1.34 us
    ppermute x1, starting transfers between devices, two_by_two(): first_edge = lax.ppermute(edge, 'tm', [(0, 1)])  1.32 us
  transfers between devices with their start and end apart: 14, of which 6 were waited for; matrix products, arithmetic and copies ran while one was open for 0% of the time, Pallas kernels for 19%

profile of v6, /device:TPU:0, one launch (start us, length us, event | category | flops | bytes accessed | tf_op | source)
XLA Modules:
  0.0 39.0 jit_solution(6970264384871402230)
XLA Ops:
  0.0 0.0 copy-start.1
  0.0 0.0 copy-start.2
  0.0 0.0 copy-start.3
  0.0 1.3 %load.1 = (bf16[2,512,384]{2,1,0:T(8,128)(2,1)S(1)}, bf16[96,768]{1,0:T(8,128)(2,1)S(1)}) custom-call(bf16[512,384]{1,0:T(8,128)(2,1)} %bitcast.11, bf16[512,384]{1,0:T(8,128)(2,1)} %bitcast.12, bf16[384,1536]{1,0:T(8,128)(2,1)} %w_ref.9), custom_call_target="tpu_custom_call" | custom-call | tf_op jit(solution)/shard_map/load/pallas_call | solution.py:465
  1.3 4.1 %collective-permute-start = (bf16[96,768]{1,0:T(8,128)(2,1)S(1)}, bf16[96,768]{1,0:T(8,128)(2,1)S(1)}, u32[]{:S(2)}, u32[]{:S(2)}) collective-permute-start(bf16[96,768]{1,0:T(8,128)(2,1)S(1)} %get-tuple-element.51), channel_id=1, source_target_pairs={{0,2},{1,3},{2,0},{3,1},{4,6},{5,7},{6,4},{7,5},{8,10},{9,11},{10,... | collective-permute-start | bytes 442376 | tf_op jit(solution)/shard_map/ppermute | solution.py:477
  5.4 0.3 faces.1
  5.7 1.6 %collective-permute-start.1 = (bf16[2,2,64,384]{3,2,1,0:T(8,128)(2,1)S(1)}, bf16[2,2,64,384]{3,2,1,0:T(8,128)(2,1)S(1)}, u32[]{:S(2)}, u32[]{:S(2)}) collective-permute-start(bf16[2,2,64,384]{3,2,1,0:T(8,128)(2,1)S(1)} %get-tuple-element.68), channel_id=1, source_target_pairs={{0,8},{4,12},{8,0},{12,4},{1,9},{5,13},{9,1},{13,5},{2,10},{6,14},... | collective-permute-start | bytes 589832 | tf_op jit(solution)/shard_map/ppermute | solution.py:477
  7.3 1.5 %collective-permute-start.2 = (bf16[2,2,64,384]{3,2,1,0:T(8,128)(2,1)S(1)}, bf16[2,2,64,384]{3,2,1,0:T(8,128)(2,1)S(1)}, u32[]{:S(2)}, u32[]{:S(2)}) collective-permute-start(bf16[2,2,64,384]{3,2,1,0:T(8,128)(2,1)S(1)} %get-tuple-element.69), channel_id=1, source_target_pairs={{0,4},{4,0},{8,12},{12,8},{1,5},{5,1},{9,13},{13,9},{2,6},{6,2},{1... | collective-permute-start | bytes 589832 | tf_op jit(solution)/shard_map/ppermute | solution.py:477
  8.8 0.5 %collective-permute-start.3 = (bf16[2,2,16,384]{3,2,1,0:T(8,128)(2,1)S(1)}, bf16[2,2,16,384]{3,2,1,0:T(8,128)(2,1)S(1)}, u32[]{:S(2)}, u32[]{:S(2)}) collective-permute-start(bf16[2,2,16,384]{3,2,1,0:T(8,128)(2,1)S(1)} %get-tuple-element.70), channel_id=1, source_target_pairs={{0,12},{4,8},{8,4},{12,0},{1,13},{5,9},{9,5},{13,1},{2,14},{6,10},... | collective-permute-start | bytes 147464 | tf_op jit(solution)/shard_map/ppermute | solution.py:477
  9.3 0.0 copy-done.1
  9.3 0.0 copy-done.2
  9.3 0.0 copy-done.3
  9.3 1.4 %begin.1 = (f32[512,128]{1,0:T(8,128)S(1)}, f32[512,128]{1,0:T(8,128)S(1)}, f32[512,128]{1,0:T(8,128)S(1)}, s32[256,800]{1,0:T(8,128)S(1)}, s32[6,128]{1,0:T(8,128)S(1)}) custom-call(s32[3]{0:T(128)S(1)} %copy-done.3, s32[2,2,3]{2,1,0:T(2,128)S(1)} %bitcast.10, bf16[512,384]{1,0:T(8,128)(2,1)S(1)} %bitcast.5, bf16[2,512,384]{2,1,0:T(8,128)(2,1)S(1)} %get-tuple-element.58.tile_ref), custom_call_target="tpu_custom_call" | custom-call | tf_op jit(solution)/shard_map/begin/pallas_call | solution.py:465
  10.7 1.3 %collective-permute-start.7 = (bf16[2,512,384]{2,1,0:T(8,128)(2,1)S(1)}, bf16[2,512,384]{2,1,0:T(8,128)(2,1)S(1)}, u32[]{:S(2)}, u32[]{:S(2)}) collective-permute-start(bf16[2,512,384]{2,1,0:T(8,128)(2,1)S(1)} %get-tuple-element.58.tile_ref), channel_id=1, source_target_pairs={{0,16},{1,17},{2,18},{3,19},{4,20},{5,21},{6,22},{7,23},{8,24},{9,... | collective-permute-start | bytes 2359304 | tf_op jit(solution)/shard_map/ppermute | solution.py:521
  12.0 1.1 %tile.1 = (f32[512,256]{1,0:T(8,128)S(1)}, f32[512,256]{1,0:T(8,128)S(1)}, f32[512,256]{1,0:T(8,128)S(1)}) custom-call(bf16[512,384]{1,0:T(8,128)(2,1)S(1)} %bitcast.6, bf16[2,512,384]{2,1,0:T(8,128)(2,1)S(1)} %get-tuple-element.58.tile_ref, s32[256,800]{1,0:T(8,128)S(1)} %get-tuple-element.59.dist_ref.rest_3_, s32[6,128]{1,0:T(8,128)S(1)} %get-tuple-element.60.reach_ref.rest_4_), custom_call_target="tpu_custom_call" | custom-call | tf_op jit(solution)/shard_map/tile/pallas_call | solution.py:465
  13.1 0.0 collective-permute-done.in_ref
  13.2 1.3 %collective-permute-done.3.corner_ref = bf16[2,2,16,384]{3,2,1,0:T(8,128)(2,1)S(1)} collective-permute-done((bf16[2,2,16,384]{3,2,1,0:T(8,128)(2,1)S(1)}, bf16[2,2,16,384]{3,2,1,0:T(8,128)(2,1)S(1)}, u32[]{:S(2)}, u32[]{:S(2)}) %collective-permute-start.3) | collective-permute-done | bytes 49184 | tf_op jit(solution)/shard_map/ppermute | solution.py:477
  14.4 0.0 collective-permute-done.1.row_ref
  14.4 0.0 collective-permute-done.2.col_ref
  14.5 1.3 %collective-permute-start.8 = (bf16[2,288,384]{2,1,0:T(8,128)(2,1)S(1)}, bf16[2,288,384]{2,1,0:T(8,128)(2,1)S(1)}, u32[]{:S(2)}, u32[]{:S(2)}) collective-permute-start(bf16[2,288,384]{2,1,0:T(8,128)(2,1)S(1)} %edges.1.edge_ref), channel_id=1, source_target_pairs={{0,16},{1,17},{2,18},{3,19},{4,20},{5,21},{6,22},{7,23},{8,24},{9,... | collective-permute-start | bytes 1327112 | tf_op jit(solution)/shard_map/ppermute | solution.py:539
  15.8 2.5 %collective-permute-start.6 = (bf16[96,768]{1,0:T(8,128)(2,1)S(1)}, bf16[96,768]{1,0:T(8,128)(2,1)S(1)}, u32[]{:S(2)}, u32[]{:S(2)}) collective-permute-start(bf16[96,768]{1,0:T(8,128)(2,1)S(1)} %lone.1.refs_0_), channel_id=1, source_target_pairs={{0,12},{4,8},{8,4},{12,0},{1,13},{5,9},{9,5},{13,1},{2,14},{6,10},... | collective-permute-start | bytes 442376 | tf_op jit(solution)/shard_map/ppermute | solution.py:477
  18.3 0.5 %collective-permute-start.5 = (bf16[96,768]{1,0:T(8,128)(2,1)S(1)}, bf16[96,768]{1,0:T(8,128)(2,1)S(1)}, u32[]{:S(2)}, u32[]{:S(2)}) collective-permute-start(bf16[96,768]{1,0:T(8,128)(2,1)S(1)} %lone.1.refs_0_), channel_id=1, source_target_pairs={{0,8},{4,12},{8,0},{12,4},{1,9},{5,13},{9,1},{13,5},{2,10},{6,14},... | collective-permute-start | bytes 442376 | tf_op jit(solution)/shard_map/ppermute | solution.py:477
  18.8 0.5 %collective-permute-start.4 = (bf16[96,768]{1,0:T(8,128)(2,1)S(1)}, bf16[96,768]{1,0:T(8,128)(2,1)S(1)}, u32[]{:S(2)}, u32[]{:S(2)}) collective-permute-start(bf16[96,768]{1,0:T(8,128)(2,1)S(1)} %lone.1.refs_0_), channel_id=1, source_target_pairs={{0,4},{4,0},{8,12},{12,8},{1,5},{5,1},{9,13},{13,9},{2,6},{6,2},{1... | collective-permute-start | bytes 442376 | tf_op jit(solution)/shard_map/ppermute | solution.py:477
  19.3 0.0 collective-permute-done.8.first_edge_ref
  19.3 0.0 collective-permute-done.7.first_tile_ref
  19.3 0.7 %rest.3 = bf16[128,384]{1,0:T(8,128)(2,1)S(1)} custom-call(bf16[512,384]{1,0:T(8,128)(2,1)S(1)} %bitcast.7, bf16[2,288,384]{2,1,0:T(8,128)(2,1)S(1)} %edges.1.edge_ref, bf16[2,512,384]{2,1,0:T(8,128)(2,1)S(1)} %collective-permute-done.7.first_tile_ref, bf16[2,288,384]{2,1,0:T(8,128)(2,1)S(1)} %collective-permute-done.8.first_edge_ref, ...), custom_call_target="tpu_custom_call" | custom-call | tf_op jit(solution)/shard_map/rest/pallas_call | solution.py:465
  20.0 0.4 collective-permute-start.10
  20.4 1.2 %rest.4 = (bf16[128,384]{1,0:T(8,128)(2,1)S(1)}, bf16[128,384]{1,0:T(8,128)(2,1)S(1)}) custom-call(bf16[512,384]{1,0:T(8,128)(2,1)S(1)} %bitcast.8, bf16[2,288,384]{2,1,0:T(8,128)(2,1)S(1)} %edges.1.edge_ref, bf16[2,512,384]{2,1,0:T(8,128)(2,1)S(1)} %collective-permute-done.7.first_tile_ref, bf16[2,288,384]{2,1,0:T(8,128)(2,1)S(1)} %collective-permute-done.8.first_edge_ref, ...), custom_call_target="tpu_custom_call" | custom-call | tf_op jit(solution)/shard_map/rest/pallas_call | solution.py:465
  21.5 0.0 copy-start
  21.5 1.6 %collective-permute-done.6.refs_3_ = bf16[96,768]{1,0:T(8,128)(2,1)S(1)} collective-permute-done((bf16[96,768]{1,0:T(8,128)(2,1)S(1)}, bf16[96,768]{1,0:T(8,128)(2,1)S(1)}, u32[]{:S(2)}, u32[]{:S(2)}) %collective-permute-start.6) | collective-permute-done | bytes 147488 | tf_op jit(solution)/shard_map/ppermute | solution.py:477
  23.1 1.1 %collective-permute-done.5.refs_2_ = bf16[96,768]{1,0:T(8,128)(2,1)S(1)} collective-permute-done((bf16[96,768]{1,0:T(8,128)(2,1)S(1)}, bf16[96,768]{1,0:T(8,128)(2,1)S(1)}, u32[]{:S(2)}, u32[]{:S(2)}) %collective-permute-start.5) | collective-permute-done | bytes 147488 | tf_op jit(solution)/shard_map/ppermute | solution.py:477
  24.2 0.0 collective-permute-done.4.refs_1_
  24.2 0.3 collective-permute-start.11
  24.5 0.1 stack.1.part_ref
  24.6 0.1 collective-permute-start.9
  24.7 2.8 %collective-permute-done.10.got_ref = bf16[128,384]{1,0:T(8,128)(2,1)S(1)} collective-permute-done((bf16[128,384]{1,0:T(8,128)(2,1)S(1)}, bf16[128,384]{1,0:T(8,128)(2,1)S(1)}, u32[]{:S(2)}, u32[]{:S(2)}) %collective-permute-start.10) | collective-permute-done | bytes 98336 | tf_op jit(solution)/shard_map/ppermute | solution.py:477
  27.4 0.0 copy-done
  27.4 0.4 project.4
  27.8 0.6 %collective-permute-start.13 = (bf16[128,768]{1,0:T(8,128)(2,1)S(1)}, bf16[128,768]{1,0:T(8,128)(2,1)S(1)}, u32[]{:S(2)}, u32[]{:S(2)}) collective-permute-start(bf16[128,768]{1,0:T(8,128)(2,1)S(1)} %project.4), channel_id=1, source_target_pairs={{0,1},{1,0},{2,3},{3,2},{4,5},{5,4},{6,7},{7,6},{8,9},{9,8},{10,11... | collective-permute-start | bytes 589832 | tf_op jit(solution)/shard_map/ppermute | solution.py:477
  28.4 0.0 collective-permute-done.9.part_ref
  28.4 0.4 project.5
  28.8 1.6 %collective-permute-start.12 = (bf16[128,768]{1,0:T(8,128)(2,1)S(1)}, bf16[128,768]{1,0:T(8,128)(2,1)S(1)}, u32[]{:S(2)}, u32[]{:S(2)}) collective-permute-start(bf16[128,768]{1,0:T(8,128)(2,1)S(1)} %project.5), channel_id=1, source_target_pairs={{0,1},{1,0},{2,3},{3,2},{4,5},{5,4},{6,7},{7,6},{8,9},{9,8},{10,11... | collective-permute-start | bytes 589832 | tf_op jit(solution)/shard_map/ppermute | solution.py:477
  30.4 0.7 %rest.5.own_ref = bf16[128,384]{1,0:T(8,128)(2,1)S(1)} custom-call(bf16[512,384]{1,0:T(8,128)(2,1)S(1)} %bitcast.9, bf16[2,288,384]{2,1,0:T(8,128)(2,1)S(1)} %edges.1.edge_ref, bf16[2,512,384]{2,1,0:T(8,128)(2,1)S(1)} %collective-permute-done.7.first_tile_ref, bf16[2,288,384]{2,1,0:T(8,128)(2,1)S(1)} %collective-permute-done.8.first_edge_ref, ...), custom_call_target="tpu_custom_call" | custom-call | flops 20000000000 | tf_op jit(solution)/shard_map/rest/pallas_call | solution.py:465
  31.1 0.0 collective-permute-done.11.got_ref
  31.1 0.4 project.6.mine_ref
  31.4 0.4 project.7.mine_ref
  31.8 3.9 %collective-permute-done.13.got_ref = bf16[128,768]{1,0:T(8,128)(2,1)S(1)} collective-permute-done((bf16[128,768]{1,0:T(8,128)(2,1)S(1)}, bf16[128,768]{1,0:T(8,128)(2,1)S(1)}, u32[]{:S(2)}, u32[]{:S(2)}) %collective-permute-start.13) | collective-permute-done | bytes 196640 | tf_op jit(solution)/shard_map/ppermute | solution.py:477
  35.7 0.7 %add.2.rest_0_ = bf16[128,1536]{1,0:T(8,128)(2,1)} custom-call(f32[128,768]{1,0:T(8,128)S(1)} %project.7.mine_ref, bf16[128,768]{1,0:T(8,128)(2,1)S(1)} %collective-permute-done.13.got_ref), custom_call_target="tpu_custom_call" | custom-call | tf_op jit(solution)/shard_map/add/pallas_call | solution.py:601
  36.4 1.9 %collective-permute-done.12.got_ref = bf16[128,768]{1,0:T(8,128)(2,1)S(1)} collective-permute-done((bf16[128,768]{1,0:T(8,128)(2,1)S(1)}, bf16[128,768]{1,0:T(8,128)(2,1)S(1)}, u32[]{:S(2)}, u32[]{:S(2)}) %collective-permute-start.12) | collective-permute-done | bytes 196640 | tf_op jit(solution)/shard_map/ppermute | solution.py:477
  38.3 0.7 %add.3 = bf16[128,1536]{1,0:T(8,128)(2,1)} custom-call(f32[128,768]{1,0:T(8,128)S(1)} %project.6.mine_ref, bf16[128,768]{1,0:T(8,128)(2,1)S(1)} %collective-permute-done.12.got_ref, bf16[128,1536]{1,0:T(8,128)(2,1)} %add.2.rest_0_), custom_call_target="tpu_custom_call", output_to_operand_aliasing={{}: (2, {})} | custom-call | tf_op jit(solution)/shard_map/add/pallas_call | solution.py:601
  (2 shorter events, 0.1 us)
Async XLA Ops:
  0.0 9.3 %copy-start.1 = (bf16[1,1,2,16,16,384]{5,4,3,2,1,0:T(8,128)(2,1)S(1)}, bf16[1,1,2,16,16,384]{5,4,3,2,1,0:T(8,128)(2,1)}, u32[]{:S(2)}) copy-start(bf16[1,1,2,16,16,384]{5,4,3,2,1,0:T(8,128)(2,1)} %param.6) | copy-start | bytes 1179652
  0.0 9.3 %copy-start.2 = (s32[3,2,2]{0,2,1:T(2,128)S(1)}, s32[3,2,2]{0,2,1:T(2,128)}, u32[]{:S(2)}) copy-start(s32[3,2,2]{0,2,1:T(2,128)} %param.11) | copy-start | bytes 148
  0.0 9.3 %copy-start.3 = (s32[3]{0:T(128)S(1)}, s32[3]{0:T(128)}, u32[]{:S(2)}) copy-start(s32[3]{0:T(128)} %radius_ref.1) | copy-start | bytes 40
  1.3 11.9 %collective-permute-start = (bf16[96,768]{1,0:T(8,128)(2,1)S(1)}, bf16[96,768]{1,0:T(8,128)(2,1)S(1)}, u32[]{:S(2)}, u32[]{:S(2)}) collective-permute-start(bf16[96,768]{1,0:T(8,128)(2,1)S(1)} %get-tuple-element.51), channel_id=1, source_target_pairs={{0,2},{1,3},{2,0},{3,1},{4,6},{5,7},{6,4},{7,5},{8,10},{9,11},{10,... | collective-permute-start | bytes 442376 | tf_op jit(solution)/shard_map/ppermute | solution.py:477
  5.7 8.7 %collective-permute-start.1 = (bf16[2,2,64,384]{3,2,1,0:T(8,128)(2,1)S(1)}, bf16[2,2,64,384]{3,2,1,0:T(8,128)(2,1)S(1)}, u32[]{:S(2)}, u32[]{:S(2)}) collective-permute-start(bf16[2,2,64,384]{3,2,1,0:T(8,128)(2,1)S(1)} %get-tuple-element.68), channel_id=1, source_target_pairs={{0,8},{4,12},{8,0},{12,4},{1,9},{5,13},{9,1},{13,5},{2,10},{6,14},... | collective-permute-start | bytes 589832 | tf_op jit(solution)/shard_map/ppermute | solution.py:477
  7.3 7.1 %collective-permute-start.2 = (bf16[2,2,64,384]{3,2,1,0:T(8,128)(2,1)S(1)}, bf16[2,2,64,384]{3,2,1,0:T(8,128)(2,1)S(1)}, u32[]{:S(2)}, u32[]{:S(2)}) collective-permute-start(bf16[2,2,64,384]{3,2,1,0:T(8,128)(2,1)S(1)} %get-tuple-element.69), channel_id=1, source_target_pairs={{0,4},{4,0},{8,12},{12,8},{1,5},{5,1},{9,13},{13,9},{2,6},{6,2},{1... | collective-permute-start | bytes 589832 | tf_op jit(solution)/shard_map/ppermute | solution.py:477
  8.8 5.6 %collective-permute-start.3 = (bf16[2,2,16,384]{3,2,1,0:T(8,128)(2,1)S(1)}, bf16[2,2,16,384]{3,2,1,0:T(8,128)(2,1)S(1)}, u32[]{:S(2)}, u32[]{:S(2)}) collective-permute-start(bf16[2,2,16,384]{3,2,1,0:T(8,128)(2,1)S(1)} %get-tuple-element.70), channel_id=1, source_target_pairs={{0,12},{4,8},{8,4},{12,0},{1,13},{5,9},{9,5},{13,1},{2,14},{6,10},... | collective-permute-start | bytes 147464 | tf_op jit(solution)/shard_map/ppermute | solution.py:477
  10.7 8.7 %collective-permute-start.7 = (bf16[2,512,384]{2,1,0:T(8,128)(2,1)S(1)}, bf16[2,512,384]{2,1,0:T(8,128)(2,1)S(1)}, u32[]{:S(2)}, u32[]{:S(2)}) collective-permute-start(bf16[2,512,384]{2,1,0:T(8,128)(2,1)S(1)} %get-tuple-element.58.tile_ref), channel_id=1, source_target_pairs={{0,16},{1,17},{2,18},{3,19},{4,20},{5,21},{6,22},{7,23},{8,24},{9,... | collective-permute-start | bytes 2359304 | tf_op jit(solution)/shard_map/ppermute | solution.py:521
  14.5 4.9 %collective-permute-start.8 = (bf16[2,288,384]{2,1,0:T(8,128)(2,1)S(1)}, bf16[2,288,384]{2,1,0:T(8,128)(2,1)S(1)}, u32[]{:S(2)}, u32[]{:S(2)}) collective-permute-start(bf16[2,288,384]{2,1,0:T(8,128)(2,1)S(1)} %edges.1.edge_ref), channel_id=1, source_target_pairs={{0,16},{1,17},{2,18},{3,19},{4,20},{5,21},{6,22},{7,23},{8,24},{9,... | collective-permute-start | bytes 1327112 | tf_op jit(solution)/shard_map/ppermute | solution.py:539
  15.8 7.3 %collective-permute-start.6 = (bf16[96,768]{1,0:T(8,128)(2,1)S(1)}, bf16[96,768]{1,0:T(8,128)(2,1)S(1)}, u32[]{:S(2)}, u32[]{:S(2)}) collective-permute-start(bf16[96,768]{1,0:T(8,128)(2,1)S(1)} %lone.1.refs_0_), channel_id=1, source_target_pairs={{0,12},{4,8},{8,4},{12,0},{1,13},{5,9},{9,5},{13,1},{2,14},{6,10},... | collective-permute-start | bytes 442376 | tf_op jit(solution)/shard_map/ppermute | solution.py:477
  18.3 5.9 %collective-permute-start.5 = (bf16[96,768]{1,0:T(8,128)(2,1)S(1)}, bf16[96,768]{1,0:T(8,128)(2,1)S(1)}, u32[]{:S(2)}, u32[]{:S(2)}) collective-permute-start(bf16[96,768]{1,0:T(8,128)(2,1)S(1)} %lone.1.refs_0_), channel_id=1, source_target_pairs={{0,8},{4,12},{8,0},{12,4},{1,9},{5,13},{9,1},{13,5},{2,10},{6,14},... | collective-permute-start | bytes 442376 | tf_op jit(solution)/shard_map/ppermute | solution.py:477
  18.8 5.4 %collective-permute-start.4 = (bf16[96,768]{1,0:T(8,128)(2,1)S(1)}, bf16[96,768]{1,0:T(8,128)(2,1)S(1)}, u32[]{:S(2)}, u32[]{:S(2)}) collective-permute-start(bf16[96,768]{1,0:T(8,128)(2,1)S(1)} %lone.1.refs_0_), channel_id=1, source_target_pairs={{0,4},{4,0},{8,12},{12,8},{1,5},{5,1},{9,13},{13,9},{2,6},{6,2},{1... | collective-permute-start | bytes 442376 | tf_op jit(solution)/shard_map/ppermute | solution.py:477
  20.0 7.4 %collective-permute-start.10 = (bf16[128,384]{1,0:T(8,128)(2,1)S(1)}, bf16[128,384]{1,0:T(8,128)(2,1)S(1)}, u32[]{:S(2)}, u32[]{:S(2)}) collective-permute-start(bf16[128,384]{1,0:T(8,128)(2,1)S(1)} %rest.3), channel_id=1, source_target_pairs={{0,2},{1,3},{2,0},{3,1},{4,6},{5,7},{6,4},{7,5},{8,10},{9,11},{10,... | collective-permute-start | bytes 294920 | tf_op jit(solution)/shard_map/ppermute | solution.py:477
  21.5 5.9 %copy-start = (bf16[384,1536]{1,0:T(8,128)(2,1)S(1)}, bf16[384,1536]{1,0:T(8,128)(2,1)}, u32[]{:S(2)}) copy-start(bf16[384,1536]{1,0:T(8,128)(2,1)} %w_ref.9) | copy-start | bytes 3538948
  24.2 6.9 %collective-permute-start.11 = (bf16[128,384]{1,0:T(8,128)(2,1)S(1)}, bf16[128,384]{1,0:T(8,128)(2,1)S(1)}, u32[]{:S(2)}, u32[]{:S(2)}) collective-permute-start(bf16[128,384]{1,0:T(8,128)(2,1)S(1)} %get-tuple-element.96), channel_id=1, source_target_pairs={{0,2},{1,3},{2,0},{3,1},{4,6},{5,7},{6,4},{7,5},{8,10},{9,11},{10,... | collective-permute-start | bytes 294920 | tf_op jit(solution)/shard_map/ppermute | solution.py:477
  24.6 3.9 %collective-permute-start.9 = (bf16[384,768]{1,0:T(8,128)(2,1)S(1)}, bf16[384,768]{1,0:T(8,128)(2,1)S(1)}, u32[]{:S(2)}, u32[]{:S(2)}) collective-permute-start(bf16[384,768]{1,0:T(8,128)(2,1)S(1)} %stack.1.part_ref), channel_id=1, source_target_pairs={{0,16},{16,0},{1,17},{17,1},{2,18},{18,2},{3,19},{19,3},{4,20},{20... | collective-permute-start | bytes 1769480 | tf_op jit(solution)/shard_map/ppermute | solution.py:477
  27.8 7.9 %collective-permute-start.13 = (bf16[128,768]{1,0:T(8,128)(2,1)S(1)}, bf16[128,768]{1,0:T(8,128)(2,1)S(1)}, u32[]{:S(2)}, u32[]{:S(2)}) collective-permute-start(bf16[128,768]{1,0:T(8,128)(2,1)S(1)} %project.4), channel_id=1, source_target_pairs={{0,1},{1,0},{2,3},{3,2},{4,5},{5,4},{6,7},{7,6},{8,9},{9,8},{10,11... | collective-permute-start | bytes 589832 | tf_op jit(solution)/shard_map/ppermute | solution.py:477
  28.8 9.5 %collective-permute-start.12 = (bf16[128,768]{1,0:T(8,128)(2,1)S(1)}, bf16[128,768]{1,0:T(8,128)(2,1)S(1)}, u32[]{:S(2)}, u32[]{:S(2)}) collective-permute-start(bf16[128,768]{1,0:T(8,128)(2,1)S(1)} %project.5), channel_id=1, source_target_pairs={{0,1},{1,0},{2,3},{3,2},{4,5},{5,4},{6,7},{7,6},{8,9},{9,8},{10,11... | collective-permute-start | bytes 589832 | tf_op jit(solution)/shard_map/ppermute | solution.py:477

commit v7 on v4

--- a/solution.py
+++ b/solution.py
@@ -183,24 +183,16 @@
     return tile_at // 2, tile_at % 2
 
 
-def load_kernel(k_ref, v_ref, w_ref, tile_ref, part_ref, sems):
+def part_kernel(w_ref, part_ref, sem):
     tall, broad = part_ref.shape
     top = pl.multiple_of(lax.axis_index("tile") * tall, 16)
     left = pl.multiple_of(lax.axis_index("tm") * broad, 128)
-    copies = [
-        pltpu.make_async_copy(
-            w_ref.at[pl.ds(top, tall), pl.ds(left, broad)], part_ref, sems.at[2]
-        )
-    ]
-    for which, ref in enumerate((k_ref, v_ref)):
-        copies.append(pltpu.make_async_copy(ref, tile_ref.at[which], sems.at[which]))
-    for copy in copies:
-        copy.start()
-    for copy in copies:
-        copy.wait()
-
-
-def face_kernel(tile_ref, row_ref, col_ref, corner_ref, *, geometry):
+    copy = pltpu.make_async_copy(w_ref.at[pl.ds(top, tall), pl.ds(left, broad)], part_ref, sem)
+    copy.start()
+    copy.wait()
+
+
+def face_kernel(k_ref, v_ref, part_ref, row_ref, col_ref, corner_ref, tile_ref, *, geometry):
     high, wide, span, frames = geometry[:4]
     cells = high * wide
     row_at, col_at = tile_place()
@@ -214,11 +206,12 @@
 
     beside = picker(high * span, lambda i: (i // span) * wide + x0 + i % span)
     across = picker(span * span, lambda i: (y0 + i // span) * wide + x0 + i % span)
-    for which in range(2):
+    for which, ref in enumerate((k_ref, v_ref)):
+        tile_ref[which] = ref[...]
         for f in range(frames):
             start = pl.multiple_of(f * cells + y0 * wide, 16)
-            row_ref[which, f] = tile_ref[which, pl.ds(start, span * wide)]
-            whole = tile_ref[which, f * cells : (f + 1) * cells]
+            row_ref[which, f] = ref[pl.ds(start, span * wide)]
+            whole = ref[f * cells : (f + 1) * cells]
             col_ref[which, f] = jnp.dot(
                 beside, whole, preferred_element_type=jnp.float32
             ).astype(jnp.bfloat16)
@@ -482,23 +475,26 @@
 
     tall, broad = depth // tiles, width // 2
     part_shape = shape((tall, broad), bf16)
-    tile, part = call(
-        load_kernel,
-        [shape((2, tokens, channels), bf16), part_shape],
-        [hbm] * 3,
-        *[pltpu.with_memory_space_constraint(x, pltpu.HBM) for x in (k, v, out_weight)],
-        name="load",
-        scratch=[pltpu.SemaphoreType.DMA((3,))],
-    )
-    faces = call(
+    part = call(
+        part_kernel,
+        part_shape,
+        [hbm],
+        pltpu.with_memory_space_constraint(out_weight, pltpu.HBM),
+        name="part",
+        scratch=[pltpu.SemaphoreType.DMA],
+    )
+    *faces, tile = call(
         face_kernel,
         [
             shape((2, frames, span * wide, channels), bf16),
             shape((2, frames, span * high, channels), bf16),
             shape((2, frames, span * span, channels), bf16),
+            shape((2, tokens, channels), bf16),
         ],
-        [vmem],
-        tile,
+        [vmem] * 3,
+        k,
+        v,
+        part,
         name="faces",
         geometry=geometry,
     )

time: 38.9 us -> 38.7 us (level)
  transfers between devices with their start and end apart: 14 -> 14, of which waited for: 7 -> 7; matrix products, arithmetic and copies ran while one was open for 0% -> 0% of each run, Pallas kernels for 19% -> 20%
where the time goes in v7:
time: 38.7 us; the launch traced here: 38.5 us
  starting transfers between devices  16.8 us (43%)
  waiting for transfers between devices  12.2 us (32%)
  Pallas kernels  9.31 us (24%)
    ppermute x12, starting transfers between devices, flipped(): lax.ppermute(value, axis, [(i, i ^ flip) for i in range(lax.axis_size(axi...  14.1 us
    ppermute x12, waiting for transfers between devices, flipped(): lax.ppermute(value, axis, [(i, i ^ flip) for i in range(lax.axis_size(axi...  12.2 us
    pallas_call x14, Pallas kernels, call(): pl.pallas_call(functools.partial(kernel, **keys_of) if keys_of else kerne...  7.89 us
    pallas_call x2, Pallas kernels, two_by_two(): pl.pallas_call(functools.partial(add_kernel, flip=flip), out_shape=shape(...  1.42 us
    ppermute x1, starting transfers between devices, two_by_two(): first_tile = lax.ppermute(tile, 'tm', [(0, 1)])  1.34 us
    ppermute x1, starting transfers between devices, two_by_two(): first_edge = lax.ppermute(edge, 'tm', [(0, 1)])  1.32 us
  transfers between devices with their start and end apart: 14, of which 7 were waited for; matrix products, arithmetic and copies ran while one was open for 0% of the time, Pallas kernels for 20%

profile of v7, /device:TPU:0, one launch (start us, length us, event | category | flops | bytes accessed | tf_op | source)
XLA Modules:
  0.0 38.5 jit_solution(13879501228875637873)
XLA Ops:
  0.0 0.0 copy-start.3
  0.0 0.0 copy-start.2
  0.0 0.0 copy-start.4
  0.0 0.0 copy-start.5
  0.0 0.0 copy-start.1
  0.0 1.0 %part.1.part_ref = bf16[96,768]{1,0:T(8,128)(2,1)S(1)} custom-call(bf16[384,1536]{1,0:T(8,128)(2,1)} %w_ref.9), custom_call_target="tpu_custom_call" | custom-call | tf_op jit(solution)/shard_map/part/pallas_call | solution.py:458
  1.0 4.1 %collective-permute-start = (bf16[96,768]{1,0:T(8,128)(2,1)S(1)}, bf16[96,768]{1,0:T(8,128)(2,1)S(1)}, u32[]{:S(2)}, u32[]{:S(2)}) collective-permute-start(bf16[96,768]{1,0:T(8,128)(2,1)S(1)} %part.1.part_ref), channel_id=1, source_target_pairs={{0,2},{1,3},{2,0},{3,1},{4,6},{5,7},{6,4},{7,5},{8,10},{9,11},{10,... | collective-permute-start | bytes 442376 | tf_op jit(solution)/shard_map/ppermute | solution.py:470
  5.2 0.0 copy-done.3
  5.2 0.0 copy-done.2
  5.2 0.4 %faces.1 = (bf16[2,2,64,384]{3,2,1,0:T(8,128)(2,1)S(1)}, bf16[2,2,64,384]{3,2,1,0:T(8,128)(2,1)S(1)}, bf16[2,2,16,384]{3,2,1,0:T(8,128)(2,1)S(1)}, bf16[2,512,384]{2,1,0:T(8,128)(2,1)S(1)}) custom-call(bf16[512,384]{1,0:T(8,128)(2,1)S(1)} %bitcast.10, bf16[512,384]{1,0:T(8,128)(2,1)S(1)} %bitcast.11, bf16[96,768]{1,0:T(8,128)(2,1)S(1)} %part.1.part_ref), custom_call_target="tpu_custom_call" | custom-call | tf_op jit(solution)/shard_map/faces/pallas_call | solution.py:458
  5.6 1.6 %collective-permute-start.1 = (bf16[2,2,64,384]{3,2,1,0:T(8,128)(2,1)S(1)}, bf16[2,2,64,384]{3,2,1,0:T(8,128)(2,1)S(1)}, u32[]{:S(2)}, u32[]{:S(2)}) collective-permute-start(bf16[2,2,64,384]{3,2,1,0:T(8,128)(2,1)S(1)} %get-tuple-element.67), channel_id=1, source_target_pairs={{0,8},{4,12},{8,0},{12,4},{1,9},{5,13},{9,1},{13,5},{2,10},{6,14},... | collective-permute-start | bytes 589832 | tf_op jit(solution)/shard_map/ppermute | solution.py:470
  7.1 1.5 %collective-permute-start.2 = (bf16[2,2,64,384]{3,2,1,0:T(8,128)(2,1)S(1)}, bf16[2,2,64,384]{3,2,1,0:T(8,128)(2,1)S(1)}, u32[]{:S(2)}, u32[]{:S(2)}) collective-permute-start(bf16[2,2,64,384]{3,2,1,0:T(8,128)(2,1)S(1)} %get-tuple-element.68), channel_id=1, source_target_pairs={{0,4},{4,0},{8,12},{12,8},{1,5},{5,1},{9,13},{13,9},{2,6},{6,2},{1... | collective-permute-start | bytes 589832 | tf_op jit(solution)/shard_map/ppermute | solution.py:470
  8.6 0.5 %collective-permute-start.3 = (bf16[2,2,16,384]{3,2,1,0:T(8,128)(2,1)S(1)}, bf16[2,2,16,384]{3,2,1,0:T(8,128)(2,1)S(1)}, u32[]{:S(2)}, u32[]{:S(2)}) collective-permute-start(bf16[2,2,16,384]{3,2,1,0:T(8,128)(2,1)S(1)} %get-tuple-element.69), channel_id=1, source_target_pairs={{0,12},{4,8},{8,4},{12,0},{1,13},{5,9},{9,5},{13,1},{2,14},{6,10},... | collective-permute-start | bytes 147464 | tf_op jit(solution)/shard_map/ppermute | solution.py:470
  9.1 0.0 copy-done.4
  9.1 0.0 copy-done.5
  9.1 0.0 copy-done.1
  9.1 1.4 %begin.1 = (f32[512,128]{1,0:T(8,128)S(1)}, f32[512,128]{1,0:T(8,128)S(1)}, f32[512,128]{1,0:T(8,128)S(1)}, s32[256,800]{1,0:T(8,128)S(1)}, s32[6,128]{1,0:T(8,128)S(1)}) custom-call(s32[3]{0:T(128)S(1)} %copy-done.5, s32[2,2,3]{2,1,0:T(2,128)S(1)} %bitcast.12, bf16[512,384]{1,0:T(8,128)(2,1)S(1)} %bitcast.5, bf16[2,512,384]{2,1,0:T(8,128)(2,1)S(1)} %get-tuple-element.57.tile_ref), custom_call_target="tpu_custom_call" | custom-call | tf_op jit(solution)/shard_map/begin/pallas_call | solution.py:458
  10.5 1.3 %collective-permute-start.4 = (bf16[2,512,384]{2,1,0:T(8,128)(2,1)S(1)}, bf16[2,512,384]{2,1,0:T(8,128)(2,1)S(1)}, u32[]{:S(2)}, u32[]{:S(2)}) collective-permute-start(bf16[2,512,384]{2,1,0:T(8,128)(2,1)S(1)} %get-tuple-element.57.tile_ref), channel_id=1, source_target_pairs={{0,16},{1,17},{2,18},{3,19},{4,20},{5,21},{6,22},{7,23},{8,24},{9,... | collective-permute-start | bytes 2359304 | tf_op jit(solution)/shard_map/ppermute | solution.py:517
  11.9 1.1 %tile.1 = (f32[512,256]{1,0:T(8,128)S(1)}, f32[512,256]{1,0:T(8,128)S(1)}, f32[512,256]{1,0:T(8,128)S(1)}) custom-call(bf16[512,384]{1,0:T(8,128)(2,1)S(1)} %bitcast.6, bf16[2,512,384]{2,1,0:T(8,128)(2,1)S(1)} %get-tuple-element.57.tile_ref, s32[256,800]{1,0:T(8,128)S(1)} %get-tuple-element.58.dist_ref.rest_3_, s32[6,128]{1,0:T(8,128)S(1)} %get-tuple-element.59.reach_ref.rest_4_), custom_call_target="tpu_custom_call" | custom-call | tf_op jit(solution)/shard_map/tile/pallas_call | solution.py:458
  12.9 0.0 collective-permute-done.in_ref
  13.0 1.2 %collective-permute-done.3.corner_ref = bf16[2,2,16,384]{3,2,1,0:T(8,128)(2,1)S(1)} collective-permute-done((bf16[2,2,16,384]{3,2,1,0:T(8,128)(2,1)S(1)}, bf16[2,2,16,384]{3,2,1,0:T(8,128)(2,1)S(1)}, u32[]{:S(2)}, u32[]{:S(2)}) %collective-permute-start.3) | collective-permute-done | bytes 49184 | tf_op jit(solution)/shard_map/ppermute | solution.py:470
  14.2 0.0 collective-permute-done.1.row_ref
  14.2 0.0 collective-permute-done.2.col_ref
  14.3 1.3 %collective-permute-start.5 = (bf16[2,288,384]{2,1,0:T(8,128)(2,1)S(1)}, bf16[2,288,384]{2,1,0:T(8,128)(2,1)S(1)}, u32[]{:S(2)}, u32[]{:S(2)}) collective-permute-start(bf16[2,288,384]{2,1,0:T(8,128)(2,1)S(1)} %edges.1.edge_ref), channel_id=1, source_target_pairs={{0,16},{1,17},{2,18},{3,19},{4,20},{5,21},{6,22},{7,23},{8,24},{9,... | collective-permute-start | bytes 1327112 | tf_op jit(solution)/shard_map/ppermute | solution.py:535
  15.6 2.5 %collective-permute-start.8 = (bf16[96,768]{1,0:T(8,128)(2,1)S(1)}, bf16[96,768]{1,0:T(8,128)(2,1)S(1)}, u32[]{:S(2)}, u32[]{:S(2)}) collective-permute-start(bf16[96,768]{1,0:T(8,128)(2,1)S(1)} %lone.1.refs_0_), channel_id=1, source_target_pairs={{0,12},{4,8},{8,4},{12,0},{1,13},{5,9},{9,5},{13,1},{2,14},{6,10},... | collective-permute-start | bytes 442376 | tf_op jit(solution)/shard_map/ppermute | solution.py:470
  18.1 0.5 %collective-permute-start.7 = (bf16[96,768]{1,0:T(8,128)(2,1)S(1)}, bf16[96,768]{1,0:T(8,128)(2,1)S(1)}, u32[]{:S(2)}, u32[]{:S(2)}) collective-permute-start(bf16[96,768]{1,0:T(8,128)(2,1)S(1)} %lone.1.refs_0_), channel_id=1, source_target_pairs={{0,8},{4,12},{8,0},{12,4},{1,9},{5,13},{9,1},{13,5},{2,10},{6,14},... | collective-permute-start | bytes 442376 | tf_op jit(solution)/shard_map/ppermute | solution.py:470
  18.6 0.5 %collective-permute-start.6 = (bf16[96,768]{1,0:T(8,128)(2,1)S(1)}, bf16[96,768]{1,0:T(8,128)(2,1)S(1)}, u32[]{:S(2)}, u32[]{:S(2)}) collective-permute-start(bf16[96,768]{1,0:T(8,128)(2,1)S(1)} %lone.1.refs_0_), channel_id=1, source_target_pairs={{0,4},{4,0},{8,12},{12,8},{1,5},{5,1},{9,13},{13,9},{2,6},{6,2},{1... | collective-permute-start | bytes 442376 | tf_op jit(solution)/shard_map/ppermute | solution.py:470
  19.2 0.0 collective-permute-done.5.first_edge_ref
  19.2 0.0 collective-permute-done.4.first_tile_ref
  19.2 0.7 %rest.3 = bf16[128,384]{1,0:T(8,128)(2,1)S(1)} custom-call(bf16[512,384]{1,0:T(8,128)(2,1)S(1)} %bitcast.7, bf16[2,288,384]{2,1,0:T(8,128)(2,1)S(1)} %edges.1.edge_ref, bf16[2,512,384]{2,1,0:T(8,128)(2,1)S(1)} %collective-permute-done.4.first_tile_ref, bf16[2,288,384]{2,1,0:T(8,128)(2,1)S(1)} %collective-permute-done.5.first_edge_ref, ...), custom_call_target="tpu_custom_call" | custom-call | tf_op jit(solution)/shard_map/rest/pallas_call | solution.py:458
  19.8 0.4 %collective-permute-start.9 = (bf16[128,384]{1,0:T(8,128)(2,1)S(1)}, bf16[128,384]{1,0:T(8,128)(2,1)S(1)}, u32[]{:S(2)}, u32[]{:S(2)}) collective-permute-start(bf16[128,384]{1,0:T(8,128)(2,1)S(1)} %rest.3), channel_id=1, source_target_pairs={{0,2},{1,3},{2,0},{3,1},{4,6},{5,7},{6,4},{7,5},{8,10},{9,11},{10,... | collective-permute-start | bytes 294920 | tf_op jit(solution)/shard_map/ppermute | solution.py:470
  20.2 1.2 %rest.4 = (bf16[128,384]{1,0:T(8,128)(2,1)S(1)}, bf16[128,384]{1,0:T(8,128)(2,1)S(1)}) custom-call(bf16[512,384]{1,0:T(8,128)(2,1)S(1)} %bitcast.8, bf16[2,288,384]{2,1,0:T(8,128)(2,1)S(1)} %edges.1.edge_ref, bf16[2,512,384]{2,1,0:T(8,128)(2,1)S(1)} %collective-permute-done.4.first_tile_ref, bf16[2,288,384]{2,1,0:T(8,128)(2,1)S(1)} %collective-permute-done.5.first_edge_ref, ...), custom_call_target="tpu_custom_call" | custom-call | tf_op jit(solution)/shard_map/rest/pallas_call | solution.py:458
  21.4 0.0 copy-start
  21.4 1.5 %collective-permute-done.8.refs_3_ = bf16[96,768]{1,0:T(8,128)(2,1)S(1)} collective-permute-done((bf16[96,768]{1,0:T(8,128)(2,1)S(1)}, bf16[96,768]{1,0:T(8,128)(2,1)S(1)}, u32[]{:S(2)}, u32[]{:S(2)}) %collective-permute-start.8) | collective-permute-done | bytes 147488 | tf_op jit(solution)/shard_map/ppermute | solution.py:470
  22.9 1.1 %collective-permute-done.7.refs_2_ = bf16[96,768]{1,0:T(8,128)(2,1)S(1)} collective-permute-done((bf16[96,768]{1,0:T(8,128)(2,1)S(1)}, bf16[96,768]{1,0:T(8,128)(2,1)S(1)}, u32[]{:S(2)}, u32[]{:S(2)}) %collective-permute-start.7) | collective-permute-done | bytes 147488 | tf_op jit(solution)/shard_map/ppermute | solution.py:470
  24.0 0.0 collective-permute-done.6.refs_1_
  24.0 0.3 collective-permute-start.11
  24.4 0.1 stack.1.part_ref
  24.4 2.8 %collective-permute-done.9.got_ref = bf16[128,384]{1,0:T(8,128)(2,1)S(1)} collective-permute-done((bf16[128,384]{1,0:T(8,128)(2,1)S(1)}, bf16[128,384]{1,0:T(8,128)(2,1)S(1)}, u32[]{:S(2)}, u32[]{:S(2)}) %collective-permute-start.9) | collective-permute-done | bytes 98336 | tf_op jit(solution)/shard_map/ppermute | solution.py:470
  27.2 0.0 copy-done
  27.2 0.4 project.4
  27.6 0.5 %collective-permute-start.13 = (bf16[128,768]{1,0:T(8,128)(2,1)S(1)}, bf16[128,768]{1,0:T(8,128)(2,1)S(1)}, u32[]{:S(2)}, u32[]{:S(2)}) collective-permute-start(bf16[128,768]{1,0:T(8,128)(2,1)S(1)} %project.4), channel_id=1, source_target_pairs={{0,1},{1,0},{2,3},{3,2},{4,5},{5,4},{6,7},{7,6},{8,9},{9,8},{10,11... | collective-permute-start | bytes 589832 | tf_op jit(solution)/shard_map/ppermute | solution.py:470
  28.1 0.0 collective-permute-start.10
  28.1 0.7 %rest.5.own_ref = bf16[128,384]{1,0:T(8,128)(2,1)S(1)} custom-call(bf16[512,384]{1,0:T(8,128)(2,1)S(1)} %bitcast.9, bf16[2,288,384]{2,1,0:T(8,128)(2,1)S(1)} %edges.1.edge_ref, bf16[2,512,384]{2,1,0:T(8,128)(2,1)S(1)} %collective-permute-done.4.first_tile_ref, bf16[2,288,384]{2,1,0:T(8,128)(2,1)S(1)} %collective-permute-done.5.first_edge_ref, ...), custom_call_target="tpu_custom_call" | custom-call | flops 20000000000 | tf_op jit(solution)/shard_map/rest/pallas_call | solution.py:458
  28.8 1.3 %collective-permute-done.10.part_ref = bf16[384,768]{1,0:T(8,128)(2,1)S(1)} collective-permute-done((bf16[384,768]{1,0:T(8,128)(2,1)S(1)}, bf16[384,768]{1,0:T(8,128)(2,1)S(1)}, u32[]{:S(2)}, u32[]{:S(2)}) %collective-permute-start.10) | collective-permute-done | bytes 589856 | tf_op jit(solution)/shard_map/ppermute | solution.py:470
  30.1 0.4 project.5
  30.5 1.6 %collective-permute-start.12 = (bf16[128,768]{1,0:T(8,128)(2,1)S(1)}, bf16[128,768]{1,0:T(8,128)(2,1)S(1)}, u32[]{:S(2)}, u32[]{:S(2)}) collective-permute-start(bf16[128,768]{1,0:T(8,128)(2,1)S(1)} %project.5), channel_id=1, source_target_pairs={{0,1},{1,0},{2,3},{3,2},{4,5},{5,4},{6,7},{7,6},{8,9},{9,8},{10,11... | collective-permute-start | bytes 589832 | tf_op jit(solution)/shard_map/ppermute | solution.py:470
  32.1 0.0 collective-permute-done.11.got_ref
  32.1 0.4 project.6.mine_ref
  32.5 0.4 project.7.mine_ref
  32.9 0.9 %collective-permute-done.13.got_ref = bf16[128,768]{1,0:T(8,128)(2,1)S(1)} collective-permute-done((bf16[128,768]{1,0:T(8,128)(2,1)S(1)}, bf16[128,768]{1,0:T(8,128)(2,1)S(1)}, u32[]{:S(2)}, u32[]{:S(2)}) %collective-permute-start.13) | collective-permute-done | bytes 196640 | tf_op jit(solution)/shard_map/ppermute | solution.py:470
  33.8 0.7 %add.2.rest_0_ = bf16[128,1536]{1,0:T(8,128)(2,1)} custom-call(f32[128,768]{1,0:T(8,128)S(1)} %project.7.mine_ref, bf16[128,768]{1,0:T(8,128)(2,1)S(1)} %collective-permute-done.13.got_ref), custom_call_target="tpu_custom_call" | custom-call | tf_op jit(solution)/shard_map/add/pallas_call | solution.py:597
  34.5 3.3 %collective-permute-done.12.got_ref = bf16[128,768]{1,0:T(8,128)(2,1)S(1)} collective-permute-done((bf16[128,768]{1,0:T(8,128)(2,1)S(1)}, bf16[128,768]{1,0:T(8,128)(2,1)S(1)}, u32[]{:S(2)}, u32[]{:S(2)}) %collective-permute-start.12) | collective-permute-done | bytes 196640 | tf_op jit(solution)/shard_map/ppermute | solution.py:470
  37.8 0.7 %add.3 = bf16[128,1536]{1,0:T(8,128)(2,1)} custom-call(f32[128,768]{1,0:T(8,128)S(1)} %project.6.mine_ref, bf16[128,768]{1,0:T(8,128)(2,1)S(1)} %collective-permute-done.12.got_ref, bf16[128,1536]{1,0:T(8,128)(2,1)} %add.2.rest_0_), custom_call_target="tpu_custom_call", output_to_operand_aliasing={{}: (2, {})} | custom-call | tf_op jit(solution)/shard_map/add/pallas_call | solution.py:597
  (2 shorter events, 0.1 us)
Async XLA Ops:
  0.0 5.2 %copy-start.3 = (bf16[1,1,2,16,16,384]{5,4,3,2,1,0:T(8,128)(2,1)S(1)}, bf16[1,1,2,16,16,384]{5,4,3,2,1,0:T(8,128)(2,1)}, u32[]{:S(2)}) copy-start(bf16[1,1,2,16,16,384]{5,4,3,2,1,0:T(8,128)(2,1)} %param.8) | copy-start | bytes 1179652
  0.0 5.2 %copy-start.2 = (bf16[1,1,2,16,16,384]{5,4,3,2,1,0:T(8,128)(2,1)S(1)}, bf16[1,1,2,16,16,384]{5,4,3,2,1,0:T(8,128)(2,1)}, u32[]{:S(2)}) copy-start(bf16[1,1,2,16,16,384]{5,4,3,2,1,0:T(8,128)(2,1)} %param.7) | copy-start | bytes 1179652
  0.0 9.1 %copy-start.4 = (s32[3,2,2]{0,2,1:T(2,128)S(1)}, s32[3,2,2]{0,2,1:T(2,128)}, u32[]{:S(2)}) copy-start(s32[3,2,2]{0,2,1:T(2,128)} %param.11) | copy-start | bytes 148
  0.0 9.1 %copy-start.5 = (s32[3]{0:T(128)S(1)}, s32[3]{0:T(128)}, u32[]{:S(2)}) copy-start(s32[3]{0:T(128)} %radius_ref.1) | copy-start | bytes 40
  0.0 9.1 %copy-start.1 = (bf16[1,1,2,16,16,384]{5,4,3,2,1,0:T(8,128)(2,1)S(1)}, bf16[1,1,2,16,16,384]{5,4,3,2,1,0:T(8,128)(2,1)}, u32[]{:S(2)}) copy-start(bf16[1,1,2,16,16,384]{5,4,3,2,1,0:T(8,128)(2,1)} %param.6) | copy-start | bytes 1179652
  1.0 11.9 %collective-permute-start = (bf16[96,768]{1,0:T(8,128)(2,1)S(1)}, bf16[96,768]{1,0:T(8,128)(2,1)S(1)}, u32[]{:S(2)}, u32[]{:S(2)}) collective-permute-start(bf16[96,768]{1,0:T(8,128)(2,1)S(1)} %part.1.part_ref), channel_id=1, source_target_pairs={{0,2},{1,3},{2,0},{3,1},{4,6},{5,7},{6,4},{7,5},{8,10},{9,11},{10,... | collective-permute-start | bytes 442376 | tf_op jit(solution)/shard_map/ppermute | solution.py:470
  5.6 8.7 %collective-permute-start.1 = (bf16[2,2,64,384]{3,2,1,0:T(8,128)(2,1)S(1)}, bf16[2,2,64,384]{3,2,1,0:T(8,128)(2,1)S(1)}, u32[]{:S(2)}, u32[]{:S(2)}) collective-permute-start(bf16[2,2,64,384]{3,2,1,0:T(8,128)(2,1)S(1)} %get-tuple-element.67), channel_id=1, source_target_pairs={{0,8},{4,12},{8,0},{12,4},{1,9},{5,13},{9,1},{13,5},{2,10},{6,14},... | collective-permute-start | bytes 589832 | tf_op jit(solution)/shard_map/ppermute | solution.py:470
  7.1 7.1 %collective-permute-start.2 = (bf16[2,2,64,384]{3,2,1,0:T(8,128)(2,1)S(1)}, bf16[2,2,64,384]{3,2,1,0:T(8,128)(2,1)S(1)}, u32[]{:S(2)}, u32[]{:S(2)}) collective-permute-start(bf16[2,2,64,384]{3,2,1,0:T(8,128)(2,1)S(1)} %get-tuple-element.68), channel_id=1, source_target_pairs={{0,4},{4,0},{8,12},{12,8},{1,5},{5,1},{9,13},{13,9},{2,6},{6,2},{1... | collective-permute-start | bytes 589832 | tf_op jit(solution)/shard_map/ppermute | solution.py:470
  8.6 5.6 %collective-permute-start.3 = (bf16[2,2,16,384]{3,2,1,0:T(8,128)(2,1)S(1)}, bf16[2,2,16,384]{3,2,1,0:T(8,128)(2,1)S(1)}, u32[]{:S(2)}, u32[]{:S(2)}) collective-permute-start(bf16[2,2,16,384]{3,2,1,0:T(8,128)(2,1)S(1)} %get-tuple-element.69), channel_id=1, source_target_pairs={{0,12},{4,8},{8,4},{12,0},{1,13},{5,9},{9,5},{13,1},{2,14},{6,10},... | collective-permute-start | bytes 147464 | tf_op jit(solution)/shard_map/ppermute | solution.py:470
  10.5 8.7 %collective-permute-start.4 = (bf16[2,512,384]{2,1,0:T(8,128)(2,1)S(1)}, bf16[2,512,384]{2,1,0:T(8,128)(2,1)S(1)}, u32[]{:S(2)}, u32[]{:S(2)}) collective-permute-start(bf16[2,512,384]{2,1,0:T(8,128)(2,1)S(1)} %get-tuple-element.57.tile_ref), channel_id=1, source_target_pairs={{0,16},{1,17},{2,18},{3,19},{4,20},{5,21},{6,22},{7,23},{8,24},{9,... | collective-permute-start | bytes 2359304 | tf_op jit(solution)/shard_map/ppermute | solution.py:517
  14.3 4.9 %collective-permute-start.5 = (bf16[2,288,384]{2,1,0:T(8,128)(2,1)S(1)}, bf16[2,288,384]{2,1,0:T(8,128)(2,1)S(1)}, u32[]{:S(2)}, u32[]{:S(2)}) collective-permute-start(bf16[2,288,384]{2,1,0:T(8,128)(2,1)S(1)} %edges.1.edge_ref), channel_id=1, source_target_pairs={{0,16},{1,17},{2,18},{3,19},{4,20},{5,21},{6,22},{7,23},{8,24},{9,... | collective-permute-start | bytes 1327112 | tf_op jit(solution)/shard_map/ppermute | solution.py:535
  15.6 7.3 %collective-permute-start.8 = (bf16[96,768]{1,0:T(8,128)(2,1)S(1)}, bf16[96,768]{1,0:T(8,128)(2,1)S(1)}, u32[]{:S(2)}, u32[]{:S(2)}) collective-permute-start(bf16[96,768]{1,0:T(8,128)(2,1)S(1)} %lone.1.refs_0_), channel_id=1, source_target_pairs={{0,12},{4,8},{8,4},{12,0},{1,13},{5,9},{9,5},{13,1},{2,14},{6,10},... | collective-permute-start | bytes 442376 | tf_op jit(solution)/shard_map/ppermute | solution.py:470
  18.1 5.9 %collective-permute-start.7 = (bf16[96,768]{1,0:T(8,128)(2,1)S(1)}, bf16[96,768]{1,0:T(8,128)(2,1)S(1)}, u32[]{:S(2)}, u32[]{:S(2)}) collective-permute-start(bf16[96,768]{1,0:T(8,128)(2,1)S(1)} %lone.1.refs_0_), channel_id=1, source_target_pairs={{0,8},{4,12},{8,0},{12,4},{1,9},{5,13},{9,1},{13,5},{2,10},{6,14},... | collective-permute-start | bytes 442376 | tf_op jit(solution)/shard_map/ppermute | solution.py:470
  18.6 5.4 %collective-permute-start.6 = (bf16[96,768]{1,0:T(8,128)(2,1)S(1)}, bf16[96,768]{1,0:T(8,128)(2,1)S(1)}, u32[]{:S(2)}, u32[]{:S(2)}) collective-permute-start(bf16[96,768]{1,0:T(8,128)(2,1)S(1)} %lone.1.refs_0_), channel_id=1, source_target_pairs={{0,4},{4,0},{8,12},{12,8},{1,5},{5,1},{9,13},{13,9},{2,6},{6,2},{1... | collective-permute-start | bytes 442376 | tf_op jit(solution)/shard_map/ppermute | solution.py:470
  19.8 7.4 %collective-permute-start.9 = (bf16[128,384]{1,0:T(8,128)(2,1)S(1)}, bf16[128,384]{1,0:T(8,128)(2,1)S(1)}, u32[]{:S(2)}, u32[]{:S(2)}) collective-permute-start(bf16[128,384]{1,0:T(8,128)(2,1)S(1)} %rest.3), channel_id=1, source_target_pairs={{0,2},{1,3},{2,0},{3,1},{4,6},{5,7},{6,4},{7,5},{8,10},{9,11},{10,... | collective-permute-start | bytes 294920 | tf_op jit(solution)/shard_map/ppermute | solution.py:470
  21.4 5.8 %copy-start = (bf16[384,1536]{1,0:T(8,128)(2,1)S(1)}, bf16[384,1536]{1,0:T(8,128)(2,1)}, u32[]{:S(2)}) copy-start(bf16[384,1536]{1,0:T(8,128)(2,1)} %w_ref.9) | copy-start | bytes 3538948
  24.0 8.1 %collective-permute-start.11 = (bf16[128,384]{1,0:T(8,128)(2,1)S(1)}, bf16[128,384]{1,0:T(8,128)(2,1)S(1)}, u32[]{:S(2)}, u32[]{:S(2)}) collective-permute-start(bf16[128,384]{1,0:T(8,128)(2,1)S(1)} %get-tuple-element.96), channel_id=1, source_target_pairs={{0,2},{1,3},{2,0},{3,1},{4,6},{5,7},{6,4},{7,5},{8,10},{9,11},{10,... | collective-permute-start | bytes 294920 | tf_op jit(solution)/shard_map/ppermute | solution.py:470
  27.6 6.2 %collective-permute-start.13 = (bf16[128,768]{1,0:T(8,128)(2,1)S(1)}, bf16[128,768]{1,0:T(8,128)(2,1)S(1)}, u32[]{:S(2)}, u32[]{:S(2)}) collective-permute-start(bf16[128,768]{1,0:T(8,128)(2,1)S(1)} %project.4), channel_id=1, source_target_pairs={{0,1},{1,0},{2,3},{3,2},{4,5},{5,4},{6,7},{7,6},{8,9},{9,8},{10,11... | collective-permute-start | bytes 589832 | tf_op jit(solution)/shard_map/ppermute | solution.py:470
  28.1 2.0 %collective-permute-start.10 = (bf16[384,768]{1,0:T(8,128)(2,1)S(1)}, bf16[384,768]{1,0:T(8,128)(2,1)S(1)}, u32[]{:S(2)}, u32[]{:S(2)}) collective-permute-start(bf16[384,768]{1,0:T(8,128)(2,1)S(1)} %stack.1.part_ref), channel_id=1, source_target_pairs={{0,16},{16,0},{1,17},{17,1},{2,18},{18,2},{3,19},{19,3},{4,20},{20... | collective-permute-start | bytes 1769480 | tf_op jit(solution)/shard_map/ppermute | solution.py:470
  30.5 7.3 %collective-permute-start.12 = (bf16[128,768]{1,0:T(8,128)(2,1)S(1)}, bf16[128,768]{1,0:T(8,128)(2,1)S(1)}, u32[]{:S(2)}, u32[]{:S(2)}) collective-permute-start(bf16[128,768]{1,0:T(8,128)(2,1)S(1)} %project.5), channel_id=1, source_target_pairs={{0,1},{1,0},{2,3},{3,2},{4,5},{5,4},{6,7},{7,6},{8,9},{9,8},{10,11... | collective-permute-start | bytes 589832 | tf_op jit(solution)/shard_map/ppermute | solution.py:470

commit v8 on v7

--- a/solution.py
+++ b/solution.py
@@ -411,12 +411,17 @@
         out_ref[pl.ds(top, tall)] = part[...]
 
 
-def project_kernel(w_ref, part_ref, own_ref, got_ref, out_ref, *, flip):
+def project_kernel(w_ref, part_ref, own_ref, *rest, flip):
+    *got_refs, out_ref = rest
     broad = part_ref.shape[1]
-    half = jnp.bitwise_xor(lax.axis_index("tm"), flip)
+    core = lax.axis_index("tm")
+    half = jnp.bitwise_xor(core, flip)
     cols = pl.ds(pl.multiple_of(half * broad, 128), broad)
+    got = got_refs[0][...]
+    for at, ref in enumerate(got_refs[1:], 1):
+        got = jnp.where(core == at, ref[...], got)
     total = jnp.dot(own_ref[...], w_ref[:, cols], preferred_element_type=jnp.float32)
-    total += jnp.dot(got_ref[...], part_ref[...], preferred_element_type=jnp.float32)
+    total += jnp.dot(got, part_ref[...], preferred_element_type=jnp.float32)
     out_ref[...] = total.astype(out_ref.dtype)
 
 
@@ -469,6 +474,11 @@
     def flipped(value, axis, flip):
         return lax.ppermute(value, axis, [(i, i ^ flip) for i in range(lax.axis_size(axis))])
 
+    def flipped_head(value, flip, stretch):
+        at = [stretch * groups + i for i in range(groups)]
+        pairs = [(at[i], at[i ^ flip]) for i in range(groups)]
+        return lax.ppermute(value, ("tm", "head"), pairs)
+
     q = query.reshape(tokens, channels)
     k = keys.reshape(tokens, channels)
     v = values.reshape(tokens, channels)
@@ -557,7 +567,7 @@
     got_side = flipped(for_side, "head", 2)
     state, for_side = lax.optimization_barrier((state, for_side))
     for_far, own_side = rest(state, 2, 1)
-    got_far = flipped(for_far, "head", 2)
+    got_far = [flipped_head(for_far, 2, 0)]
     parts, own_side = lax.optimization_barrier((parts, own_side))
     here = call(
         stack_kernel, shape((depth, broad), bf16), [vmem] * tiles, *parts, name="stack"
@@ -567,23 +577,26 @@
         return call(
             project_kernel,
             shape((step, broad), kind),
-            [vmem] * 4,
+            [vmem] * (3 + len(got)),
             out_weight,
             part,
             mine,
-            got,
+            *got,
             name="project",
             flops=flops,
             flip=flip,
         )
 
-    for_side = [project(here, own_side, got_side, bf16, 0, 20 * 10**9)]
+    for_side = [project(here, own_side, [got_side], bf16, 0, 20 * 10**9)]
     from_side = [flipped(for_side[0], "head", 1)]
-    state, here, for_side[0] = lax.optimization_barrier((state, here, for_side[0]))
+    state, here, for_far, for_side[0] = lax.optimization_barrier(
+        (state, here, for_far, for_side[0])
+    )
+    got_far.append(flipped_head(for_far, 2, 1))
     there = flipped(here, "tm", 1)
     (own,) = rest(state, 0, flops=20 * 10**9)
     own_side, own = lax.optimization_barrier((own_side, own))
-    for_side.append(project(there, own_side, got_side, bf16, 1))
+    for_side.append(project(there, own_side, [got_side], bf16, 1))
     from_side.append(flipped(for_side[1], "head", 1))
     own, for_side[1] = lax.optimization_barrier((own, for_side[1]))
     mine = [

time: 38.7 us -> 41.1 us (1.062)
  starting transfers between devices: 16.8 us -> 20.6 us
  waiting for transfers between devices: 12.2 us -> 10.7 us
    ppermute x0 -> x2, starting transfers between devices: none -> 2.89 us  [flipped_head(): return lax.ppermute(value, ('tm', 'head'), pairs)]
    ppermute x12 -> x11, waiting for transfers between devices: 12.2 us -> 9.61 us  [flipped(): lax.ppermute(value, axis, [(i, i ^ flip) for i in range(lax.axis_size(axi...]
    ppermute x0 -> x2, waiting for transfers between devices: none -> 1.06 us  [flipped_head(): return lax.ppermute(value, ('tm', 'head'), pairs)]
    ppermute x12 -> x11, starting transfers between devices: 14.1 us -> 15.1 us  [flipped(): lax.ppermute(value, axis, [(i, i ^ flip) for i in range(lax.axis_size(axi...]
  transfers between devices with their start and end apart: 14 -> 15, of which waited for: 7 -> 7; matrix products, arithmetic and copies ran while one was open for 0% -> 0% of each run, Pallas kernels for 20% -> 19%
where the time goes in v8:
time: 41.1 us; the launch traced here: 40.9 us
  starting transfers between devices  20.6 us (50%)
  waiting for transfers between devices  10.7 us (26%)
  Pallas kernels  9.33 us (23%)
    ppermute x11, starting transfers between devices, flipped(): lax.ppermute(value, axis, [(i, i ^ flip) for i in range(lax.axis_size(axi...  15.1 us
    ppermute x11, waiting for transfers between devices, flipped(): lax.ppermute(value, axis, [(i, i ^ flip) for i in range(lax.axis_size(axi...  9.61 us
    pallas_call x14, Pallas kernels, call(): pl.pallas_call(functools.partial(kernel, **keys_of) if keys_of else kerne...  7.9 us
    ppermute x2, starting transfers between devices, flipped_head(): return lax.ppermute(value, ('tm', 'head'), pairs)  2.89 us
    pallas_call x2, Pallas kernels, two_by_two(): pl.pallas_call(functools.partial(add_kernel, flip=flip), out_shape=shape(...  1.43 us
    ppermute x1, starting transfers between devices, two_by_two(): first_tile = lax.ppermute(tile, 'tm', [(0, 1)])  1.34 us
    ppermute x1, starting transfers between devices, two_by_two(): first_edge = lax.ppermute(edge, 'tm', [(0, 1)])  1.32 us
    ppermute x2, waiting for transfers between devices, flipped_head(): return lax.ppermute(value, ('tm', 'head'), pairs)  1.06 us
  transfers between devices with their start and end apart: 15, of which 7 were waited for; matrix products, arithmetic and copies ran while one was open for 0% of the time, Pallas kernels for 19%

profile of v8, /device:TPU:0, one launch (start us, length us, event | category | flops | bytes accessed | tf_op | source)
XLA Modules:
  0.0 40.9 jit_solution(14978574711695831475)
XLA Ops:
  0.0 0.0 copy-start.3
  0.0 0.0 copy-start.2
  0.0 0.0 copy-start.4
  0.0 0.0 copy-start.5
  0.0 0.0 copy-start.1
  0.0 1.0 %part.1.part_ref = bf16[96,768]{1,0:T(8,128)(2,1)S(1)} custom-call(bf16[384,1536]{1,0:T(8,128)(2,1)} %w_ref.9), custom_call_target="tpu_custom_call" | custom-call | tf_op jit(solution)/shard_map/part/pallas_call | solution.py:463
  1.0 4.1 %collective-permute-start = (bf16[96,768]{1,0:T(8,128)(2,1)S(1)}, bf16[96,768]{1,0:T(8,128)(2,1)S(1)}, u32[]{:S(2)}, u32[]{:S(2)}) collective-permute-start(bf16[96,768]{1,0:T(8,128)(2,1)S(1)} %part.1.part_ref), channel_id=1, source_target_pairs={{0,2},{1,3},{2,0},{3,1},{4,6},{5,7},{6,4},{7,5},{8,10},{9,11},{10,... | collective-permute-start | bytes 442376 | tf_op jit(solution)/shard_map/ppermute | solution.py:475
  5.2 0.0 copy-done.3
  5.2 0.0 copy-done.2
  5.2 0.4 faces.1
  5.6 1.6 %collective-permute-start.1 = (bf16[2,2,64,384]{3,2,1,0:T(8,128)(2,1)S(1)}, bf16[2,2,64,384]{3,2,1,0:T(8,128)(2,1)S(1)}, u32[]{:S(2)}, u32[]{:S(2)}) collective-permute-start(bf16[2,2,64,384]{3,2,1,0:T(8,128)(2,1)S(1)} %get-tuple-element.68), channel_id=1, source_target_pairs={{0,8},{4,12},{8,0},{12,4},{1,9},{5,13},{9,1},{13,5},{2,10},{6,14},... | collective-permute-start | bytes 589832 | tf_op jit(solution)/shard_map/ppermute | solution.py:475
  7.1 1.5 %collective-permute-start.2 = (bf16[2,2,64,384]{3,2,1,0:T(8,128)(2,1)S(1)}, bf16[2,2,64,384]{3,2,1,0:T(8,128)(2,1)S(1)}, u32[]{:S(2)}, u32[]{:S(2)}) collective-permute-start(bf16[2,2,64,384]{3,2,1,0:T(8,128)(2,1)S(1)} %get-tuple-element.69), channel_id=1, source_target_pairs={{0,4},{4,0},{8,12},{12,8},{1,5},{5,1},{9,13},{13,9},{2,6},{6,2},{1... | collective-permute-start | bytes 589832 | tf_op jit(solution)/shard_map/ppermute | solution.py:475
  8.6 0.5 %collective-permute-start.3 = (bf16[2,2,16,384]{3,2,1,0:T(8,128)(2,1)S(1)}, bf16[2,2,16,384]{3,2,1,0:T(8,128)(2,1)S(1)}, u32[]{:S(2)}, u32[]{:S(2)}) collective-permute-start(bf16[2,2,16,384]{3,2,1,0:T(8,128)(2,1)S(1)} %get-tuple-element.70), channel_id=1, source_target_pairs={{0,12},{4,8},{8,4},{12,0},{1,13},{5,9},{9,5},{13,1},{2,14},{6,10},... | collective-permute-start | bytes 147464 | tf_op jit(solution)/shard_map/ppermute | solution.py:475
  9.1 0.0 copy-done.4
  9.1 0.0 copy-done.5
  9.1 0.0 copy-done.1
  9.1 1.4 %begin.1 = (f32[512,128]{1,0:T(8,128)S(1)}, f32[512,128]{1,0:T(8,128)S(1)}, f32[512,128]{1,0:T(8,128)S(1)}, s32[256,800]{1,0:T(8,128)S(1)}, s32[6,128]{1,0:T(8,128)S(1)}) custom-call(s32[3]{0:T(128)S(1)} %copy-done.5, s32[2,2,3]{2,1,0:T(2,128)S(1)} %bitcast.12, bf16[512,384]{1,0:T(8,128)(2,1)S(1)} %bitcast.5, bf16[2,512,384]{2,1,0:T(8,128)(2,1)S(1)} %get-tuple-element.58.tile_ref), custom_call_target="tpu_custom_call" | custom-call | tf_op jit(solution)/shard_map/begin/pallas_call | solution.py:463
  10.5 1.3 %collective-permute-start.4 = (bf16[2,512,384]{2,1,0:T(8,128)(2,1)S(1)}, bf16[2,512,384]{2,1,0:T(8,128)(2,1)S(1)}, u32[]{:S(2)}, u32[]{:S(2)}) collective-permute-start(bf16[2,512,384]{2,1,0:T(8,128)(2,1)S(1)} %get-tuple-element.58.tile_ref), channel_id=1, source_target_pairs={{0,16},{1,17},{2,18},{3,19},{4,20},{5,21},{6,22},{7,23},{8,24},{9,... | collective-permute-start | bytes 2359304 | tf_op jit(solution)/shard_map/ppermute | solution.py:527
  11.9 1.1 %tile.1 = (f32[512,256]{1,0:T(8,128)S(1)}, f32[512,256]{1,0:T(8,128)S(1)}, f32[512,256]{1,0:T(8,128)S(1)}) custom-call(bf16[512,384]{1,0:T(8,128)(2,1)S(1)} %bitcast.6, bf16[2,512,384]{2,1,0:T(8,128)(2,1)S(1)} %get-tuple-element.58.tile_ref, s32[256,800]{1,0:T(8,128)S(1)} %get-tuple-element.59.dist_ref.rest_3_, s32[6,128]{1,0:T(8,128)S(1)} %get-tuple-element.60.reach_ref.rest_4_), custom_call_target="tpu_custom_call" | custom-call | tf_op jit(solution)/shard_map/tile/pallas_call | solution.py:463
  12.9 0.0 collective-permute-done.in_ref
  13.0 1.2 %collective-permute-done.3.corner_ref = bf16[2,2,16,384]{3,2,1,0:T(8,128)(2,1)S(1)} collective-permute-done((bf16[2,2,16,384]{3,2,1,0:T(8,128)(2,1)S(1)}, bf16[2,2,16,384]{3,2,1,0:T(8,128)(2,1)S(1)}, u32[]{:S(2)}, u32[]{:S(2)}) %collective-permute-start.3) | collective-permute-done | bytes 49184 | tf_op jit(solution)/shard_map/ppermute | solution.py:475
  14.2 0.0 collective-permute-done.1.row_ref
  14.2 0.0 collective-permute-done.2.col_ref
  14.3 1.3 %collective-permute-start.5 = (bf16[2,288,384]{2,1,0:T(8,128)(2,1)S(1)}, bf16[2,288,384]{2,1,0:T(8,128)(2,1)S(1)}, u32[]{:S(2)}, u32[]{:S(2)}) collective-permute-start(bf16[2,288,384]{2,1,0:T(8,128)(2,1)S(1)} %edges.1.edge_ref), channel_id=1, source_target_pairs={{0,16},{1,17},{2,18},{3,19},{4,20},{5,21},{6,22},{7,23},{8,24},{9,... | collective-permute-start | bytes 1327112 | tf_op jit(solution)/shard_map/ppermute | solution.py:545
  15.6 2.5 %collective-permute-start.8 = (bf16[96,768]{1,0:T(8,128)(2,1)S(1)}, bf16[96,768]{1,0:T(8,128)(2,1)S(1)}, u32[]{:S(2)}, u32[]{:S(2)}) collective-permute-start(bf16[96,768]{1,0:T(8,128)(2,1)S(1)} %lone.1.refs_0_), channel_id=1, source_target_pairs={{0,12},{4,8},{8,4},{12,0},{1,13},{5,9},{9,5},{13,1},{2,14},{6,10},... | collective-permute-start | bytes 442376 | tf_op jit(solution)/shard_map/ppermute | solution.py:475
  18.1 0.5 %collective-permute-start.7 = (bf16[96,768]{1,0:T(8,128)(2,1)S(1)}, bf16[96,768]{1,0:T(8,128)(2,1)S(1)}, u32[]{:S(2)}, u32[]{:S(2)}) collective-permute-start(bf16[96,768]{1,0:T(8,128)(2,1)S(1)} %lone.1.refs_0_), channel_id=1, source_target_pairs={{0,8},{4,12},{8,0},{12,4},{1,9},{5,13},{9,1},{13,5},{2,10},{6,14},... | collective-permute-start | bytes 442376 | tf_op jit(solution)/shard_map/ppermute | solution.py:475
  18.6 0.5 %collective-permute-start.6 = (bf16[96,768]{1,0:T(8,128)(2,1)S(1)}, bf16[96,768]{1,0:T(8,128)(2,1)S(1)}, u32[]{:S(2)}, u32[]{:S(2)}) collective-permute-start(bf16[96,768]{1,0:T(8,128)(2,1)S(1)} %lone.1.refs_0_), channel_id=1, source_target_pairs={{0,4},{4,0},{8,12},{12,8},{1,5},{5,1},{9,13},{13,9},{2,6},{6,2},{1... | collective-permute-start | bytes 442376 | tf_op jit(solution)/shard_map/ppermute | solution.py:475
  19.2 0.0 collective-permute-done.5.first_edge_ref
  19.2 0.0 collective-permute-done.4.first_tile_ref
  19.2 0.7 %rest.3 = bf16[128,384]{1,0:T(8,128)(2,1)S(1)} custom-call(bf16[512,384]{1,0:T(8,128)(2,1)S(1)} %bitcast.7, bf16[2,288,384]{2,1,0:T(8,128)(2,1)S(1)} %edges.1.edge_ref, bf16[2,512,384]{2,1,0:T(8,128)(2,1)S(1)} %collective-permute-done.4.first_tile_ref, bf16[2,288,384]{2,1,0:T(8,128)(2,1)S(1)} %collective-permute-done.5.first_edge_ref, ...), custom_call_target="tpu_custom_call" | custom-call | tf_op jit(solution)/shard_map/rest/pallas_call | solution.py:463
  19.8 0.4 collective-permute-start.9
  20.2 1.2 %rest.4 = (bf16[128,384]{1,0:T(8,128)(2,1)S(1)}, bf16[128,384]{1,0:T(8,128)(2,1)S(1)}) custom-call(bf16[512,384]{1,0:T(8,128)(2,1)S(1)} %bitcast.8, bf16[2,288,384]{2,1,0:T(8,128)(2,1)S(1)} %edges.1.edge_ref, bf16[2,512,384]{2,1,0:T(8,128)(2,1)S(1)} %collective-permute-done.4.first_tile_ref, bf16[2,288,384]{2,1,0:T(8,128)(2,1)S(1)} %collective-permute-done.5.first_edge_ref, ...), custom_call_target="tpu_custom_call" | custom-call | tf_op jit(solution)/shard_map/rest/pallas_call | solution.py:463
  21.4 0.0 copy-start
  21.4 1.5 %collective-permute-done.8.refs_3_ = bf16[96,768]{1,0:T(8,128)(2,1)S(1)} collective-permute-done((bf16[96,768]{1,0:T(8,128)(2,1)S(1)}, bf16[96,768]{1,0:T(8,128)(2,1)S(1)}, u32[]{:S(2)}, u32[]{:S(2)}) %collective-permute-start.8) | collective-permute-done | bytes 147488 | tf_op jit(solution)/shard_map/ppermute | solution.py:475
  22.9 1.1 %collective-permute-done.7.refs_2_ = bf16[96,768]{1,0:T(8,128)(2,1)S(1)} collective-permute-done((bf16[96,768]{1,0:T(8,128)(2,1)S(1)}, bf16[96,768]{1,0:T(8,128)(2,1)S(1)}, u32[]{:S(2)}, u32[]{:S(2)}) %collective-permute-start.7) | collective-permute-done | bytes 147488 | tf_op jit(solution)/shard_map/ppermute | solution.py:475
  24.0 0.0 collective-permute-done.6.refs_1_
  24.0 2.2 %collective-permute-start.11 = (bf16[128,384]{1,0:T(8,128)(2,1)S(1)}, bf16[128,384]{1,0:T(8,128)(2,1)S(1)}, u32[]{:S(2)}, u32[]{:S(2)}) collective-permute-start(bf16[128,384]{1,0:T(8,128)(2,1)S(1)} %get-tuple-element.98), channel_id=1, source_target_pairs={{0,2},{1,3},{2,0},{3,1},{4,6},{5,7},{6,4},{7,5},{8,10},{9,11},{10,... | collective-permute-start | bytes 294920 | tf_op jit(solution)/shard_map/ppermute | solution.py:480
  26.3 0.1 stack.1.part_ref
  26.3 0.0 collective-permute-done.9.rest_0_
  26.3 0.0 copy-done
  26.4 0.4 project.4
  26.7 3.3 %collective-permute-start.14 = (bf16[128,768]{1,0:T(8,128)(2,1)S(1)}, bf16[128,768]{1,0:T(8,128)(2,1)S(1)}, u32[]{:S(2)}, u32[]{:S(2)}) collective-permute-start(bf16[128,768]{1,0:T(8,128)(2,1)S(1)} %project.4), channel_id=1, source_target_pairs={{0,1},{1,0},{2,3},{3,2},{4,5},{5,4},{6,7},{7,6},{8,9},{9,8},{10,11... | collective-permute-start | bytes 589832 | tf_op jit(solution)/shard_map/ppermute | solution.py:475
  30.0 0.7 %collective-permute-start.12 = (bf16[128,384]{1,0:T(8,128)(2,1)S(1)}, bf16[128,384]{1,0:T(8,128)(2,1)S(1)}, u32[]{:S(2)}, u32[]{:S(2)}) collective-permute-start(bf16[128,384]{1,0:T(8,128)(2,1)S(1)} %get-tuple-element.98), channel_id=1, source_target_pairs={{16,18},{17,19},{18,16},{19,17},{20,22},{21,23},{22,20},{23,21},{2... | collective-permute-start | bytes 294920 | tf_op jit(solution)/shard_map/ppermute | solution.py:480
  30.7 0.1 collective-permute-start.10
  30.8 0.7 %rest.5.own_ref = bf16[128,384]{1,0:T(8,128)(2,1)S(1)} custom-call(bf16[512,384]{1,0:T(8,128)(2,1)S(1)} %bitcast.9, bf16[2,288,384]{2,1,0:T(8,128)(2,1)S(1)} %edges.1.edge_ref, bf16[2,512,384]{2,1,0:T(8,128)(2,1)S(1)} %collective-permute-done.4.first_tile_ref, bf16[2,288,384]{2,1,0:T(8,128)(2,1)S(1)} %collective-permute-done.5.first_edge_ref, ...), custom_call_target="tpu_custom_call" | custom-call | flops 20000000000 | tf_op jit(solution)/shard_map/rest/pallas_call | solution.py:463
  31.5 1.3 %collective-permute-done.10.part_ref = bf16[384,768]{1,0:T(8,128)(2,1)S(1)} collective-permute-done((bf16[384,768]{1,0:T(8,128)(2,1)S(1)}, bf16[384,768]{1,0:T(8,128)(2,1)S(1)}, u32[]{:S(2)}, u32[]{:S(2)}) %collective-permute-start.10) | collective-permute-done | bytes 589856 | tf_op jit(solution)/shard_map/ppermute | solution.py:475
  32.8 0.4 project.5
  33.1 0.1 collective-permute-start.13
  33.2 1.1 %collective-permute-done.11.rest_0_ = bf16[128,384]{1,0:T(8,128)(2,1)S(1)} collective-permute-done((bf16[128,384]{1,0:T(8,128)(2,1)S(1)}, bf16[128,384]{1,0:T(8,128)(2,1)S(1)}, u32[]{:S(2)}, u32[]{:S(2)}) %collective-permute-start.11) | collective-permute-done | bytes 98336 | tf_op jit(solution)/shard_map/ppermute | solution.py:480
  34.3 0.0 collective-permute-done.12.rest_1_
  34.3 0.4 project.6.mine_ref
  34.6 0.4 project.7.mine_ref
  35.0 0.3 collective-permute-done.14.got_ref
  35.3 0.7 %add.2.rest_0_ = bf16[128,1536]{1,0:T(8,128)(2,1)} custom-call(f32[128,768]{1,0:T(8,128)S(1)} %project.7.mine_ref, bf16[128,768]{1,0:T(8,128)(2,1)S(1)} %collective-permute-done.14.got_ref), custom_call_target="tpu_custom_call" | custom-call | tf_op jit(solution)/shard_map/add/pallas_call | solution.py:610
  36.0 4.1 %collective-permute-done.13.got_ref = bf16[128,768]{1,0:T(8,128)(2,1)S(1)} collective-permute-done((bf16[128,768]{1,0:T(8,128)(2,1)S(1)}, bf16[128,768]{1,0:T(8,128)(2,1)S(1)}, u32[]{:S(2)}, u32[]{:S(2)}) %collective-permute-start.13) | collective-permute-done | bytes 196640 | tf_op jit(solution)/shard_map/ppermute | solution.py:475
  40.1 0.7 %add.3 = bf16[128,1536]{1,0:T(8,128)(2,1)} custom-call(f32[128,768]{1,0:T(8,128)S(1)} %project.6.mine_ref, bf16[128,768]{1,0:T(8,128)(2,1)S(1)} %collective-permute-done.13.got_ref, bf16[128,1536]{1,0:T(8,128)(2,1)} %add.2.rest_0_), custom_call_target="tpu_custom_call", output_to_operand_aliasing={{}: (2, {})} | custom-call | tf_op jit(solution)/shard_map/add/pallas_call | solution.py:610
  (2 shorter events, 0.1 us)
Async XLA Ops:
  0.0 5.2 %copy-start.3 = (bf16[1,1,2,16,16,384]{5,4,3,2,1,0:T(8,128)(2,1)S(1)}, bf16[1,1,2,16,16,384]{5,4,3,2,1,0:T(8,128)(2,1)}, u32[]{:S(2)}) copy-start(bf16[1,1,2,16,16,384]{5,4,3,2,1,0:T(8,128)(2,1)} %param.8) | copy-start | bytes 1179652
  0.0 5.2 %copy-start.2 = (bf16[1,1,2,16,16,384]{5,4,3,2,1,0:T(8,128)(2,1)S(1)}, bf16[1,1,2,16,16,384]{5,4,3,2,1,0:T(8,128)(2,1)}, u32[]{:S(2)}) copy-start(bf16[1,1,2,16,16,384]{5,4,3,2,1,0:T(8,128)(2,1)} %param.7) | copy-start | bytes 1179652
  0.0 9.1 %copy-start.4 = (s32[3,2,2]{0,2,1:T(2,128)S(1)}, s32[3,2,2]{0,2,1:T(2,128)}, u32[]{:S(2)}) copy-start(s32[3,2,2]{0,2,1:T(2,128)} %param.11) | copy-start | bytes 148
  0.0 9.1 %copy-start.5 = (s32[3]{0:T(128)S(1)}, s32[3]{0:T(128)}, u32[]{:S(2)}) copy-start(s32[3]{0:T(128)} %radius_ref.1) | copy-start | bytes 40
  0.0 9.1 %copy-start.1 = (bf16[1,1,2,16,16,384]{5,4,3,2,1,0:T(8,128)(2,1)S(1)}, bf16[1,1,2,16,16,384]{5,4,3,2,1,0:T(8,128)(2,1)}, u32[]{:S(2)}) copy-start(bf16[1,1,2,16,16,384]{5,4,3,2,1,0:T(8,128)(2,1)} %param.6) | copy-start | bytes 1179652
  1.0 11.9 %collective-permute-start = (bf16[96,768]{1,0:T(8,128)(2,1)S(1)}, bf16[96,768]{1,0:T(8,128)(2,1)S(1)}, u32[]{:S(2)}, u32[]{:S(2)}) collective-permute-start(bf16[96,768]{1,0:T(8,128)(2,1)S(1)} %part.1.part_ref), channel_id=1, source_target_pairs={{0,2},{1,3},{2,0},{3,1},{4,6},{5,7},{6,4},{7,5},{8,10},{9,11},{10,... | collective-permute-start | bytes 442376 | tf_op jit(solution)/shard_map/ppermute | solution.py:475
  5.6 8.7 %collective-permute-start.1 = (bf16[2,2,64,384]{3,2,1,0:T(8,128)(2,1)S(1)}, bf16[2,2,64,384]{3,2,1,0:T(8,128)(2,1)S(1)}, u32[]{:S(2)}, u32[]{:S(2)}) collective-permute-start(bf16[2,2,64,384]{3,2,1,0:T(8,128)(2,1)S(1)} %get-tuple-element.68), channel_id=1, source_target_pairs={{0,8},{4,12},{8,0},{12,4},{1,9},{5,13},{9,1},{13,5},{2,10},{6,14},... | collective-permute-start | bytes 589832 | tf_op jit(solution)/shard_map/ppermute | solution.py:475
  7.1 7.1 %collective-permute-start.2 = (bf16[2,2,64,384]{3,2,1,0:T(8,128)(2,1)S(1)}, bf16[2,2,64,384]{3,2,1,0:T(8,128)(2,1)S(1)}, u32[]{:S(2)}, u32[]{:S(2)}) collective-permute-start(bf16[2,2,64,384]{3,2,1,0:T(8,128)(2,1)S(1)} %get-tuple-element.69), channel_id=1, source_target_pairs={{0,4},{4,0},{8,12},{12,8},{1,5},{5,1},{9,13},{13,9},{2,6},{6,2},{1... | collective-permute-start | bytes 589832 | tf_op jit(solution)/shard_map/ppermute | solution.py:475
  8.6 5.6 %collective-permute-start.3 = (bf16[2,2,16,384]{3,2,1,0:T(8,128)(2,1)S(1)}, bf16[2,2,16,384]{3,2,1,0:T(8,128)(2,1)S(1)}, u32[]{:S(2)}, u32[]{:S(2)}) collective-permute-start(bf16[2,2,16,384]{3,2,1,0:T(8,128)(2,1)S(1)} %get-tuple-element.70), channel_id=1, source_target_pairs={{0,12},{4,8},{8,4},{12,0},{1,13},{5,9},{9,5},{13,1},{2,14},{6,10},... | collective-permute-start | bytes 147464 | tf_op jit(solution)/shard_map/ppermute | solution.py:475
  10.5 8.7 %collective-permute-start.4 = (bf16[2,512,384]{2,1,0:T(8,128)(2,1)S(1)}, bf16[2,512,384]{2,1,0:T(8,128)(2,1)S(1)}, u32[]{:S(2)}, u32[]{:S(2)}) collective-permute-start(bf16[2,512,384]{2,1,0:T(8,128)(2,1)S(1)} %get-tuple-element.58.tile_ref), channel_id=1, source_target_pairs={{0,16},{1,17},{2,18},{3,19},{4,20},{5,21},{6,22},{7,23},{8,24},{9,... | collective-permute-start | bytes 2359304 | tf_op jit(solution)/shard_map/ppermute | solution.py:527
  14.3 4.9 %collective-permute-start.5 = (bf16[2,288,384]{2,1,0:T(8,128)(2,1)S(1)}, bf16[2,288,384]{2,1,0:T(8,128)(2,1)S(1)}, u32[]{:S(2)}, u32[]{:S(2)}) collective-permute-start(bf16[2,288,384]{2,1,0:T(8,128)(2,1)S(1)} %edges.1.edge_ref), channel_id=1, source_target_pairs={{0,16},{1,17},{2,18},{3,19},{4,20},{5,21},{6,22},{7,23},{8,24},{9,... | collective-permute-start | bytes 1327112 | tf_op jit(solution)/shard_map/ppermute | solution.py:545
  15.6 7.3 %collective-permute-start.8 = (bf16[96,768]{1,0:T(8,128)(2,1)S(1)}, bf16[96,768]{1,0:T(8,128)(2,1)S(1)}, u32[]{:S(2)}, u32[]{:S(2)}) collective-permute-start(bf16[96,768]{1,0:T(8,128)(2,1)S(1)} %lone.1.refs_0_), channel_id=1, source_target_pairs={{0,12},{4,8},{8,4},{12,0},{1,13},{5,9},{9,5},{13,1},{2,14},{6,10},... | collective-permute-start | bytes 442376 | tf_op jit(solution)/shard_map/ppermute | solution.py:475
  18.1 5.9 %collective-permute-start.7 = (bf16[96,768]{1,0:T(8,128)(2,1)S(1)}, bf16[96,768]{1,0:T(8,128)(2,1)S(1)}, u32[]{:S(2)}, u32[]{:S(2)}) collective-permute-start(bf16[96,768]{1,0:T(8,128)(2,1)S(1)} %lone.1.refs_0_), channel_id=1, source_target_pairs={{0,8},{4,12},{8,0},{12,4},{1,9},{5,13},{9,1},{13,5},{2,10},{6,14},... | collective-permute-start | bytes 442376 | tf_op jit(solution)/shard_map/ppermute | solution.py:475
  18.6 5.4 %collective-permute-start.6 = (bf16[96,768]{1,0:T(8,128)(2,1)S(1)}, bf16[96,768]{1,0:T(8,128)(2,1)S(1)}, u32[]{:S(2)}, u32[]{:S(2)}) collective-permute-start(bf16[96,768]{1,0:T(8,128)(2,1)S(1)} %lone.1.refs_0_), channel_id=1, source_target_pairs={{0,4},{4,0},{8,12},{12,8},{1,5},{5,1},{9,13},{13,9},{2,6},{6,2},{1... | collective-permute-start | bytes 442376 | tf_op jit(solution)/shard_map/ppermute | solution.py:475
  19.8 6.5 %collective-permute-start.9 = (bf16[128,384]{1,0:T(8,128)(2,1)S(1)}, bf16[128,384]{1,0:T(8,128)(2,1)S(1)}, u32[]{:S(2)}, u32[]{:S(2)}) collective-permute-start(bf16[128,384]{1,0:T(8,128)(2,1)S(1)} %rest.3), channel_id=1, source_target_pairs={{0,2},{1,3},{2,0},{3,1},{4,6},{5,7},{6,4},{7,5},{8,10},{9,11},{10,... | collective-permute-start | bytes 294920 | tf_op jit(solution)/shard_map/ppermute | solution.py:475
  21.4 5.0 %copy-start = (bf16[384,1536]{1,0:T(8,128)(2,1)S(1)}, bf16[384,1536]{1,0:T(8,128)(2,1)}, u32[]{:S(2)}) copy-start(bf16[384,1536]{1,0:T(8,128)(2,1)} %w_ref.9) | copy-start | bytes 3538948
  24.0 10.3 %collective-permute-start.11 = (bf16[128,384]{1,0:T(8,128)(2,1)S(1)}, bf16[128,384]{1,0:T(8,128)(2,1)S(1)}, u32[]{:S(2)}, u32[]{:S(2)}) collective-permute-start(bf16[128,384]{1,0:T(8,128)(2,1)S(1)} %get-tuple-element.98), channel_id=1, source_target_pairs={{0,2},{1,3},{2,0},{3,1},{4,6},{5,7},{6,4},{7,5},{8,10},{9,11},{10,... | collective-permute-start | bytes 294920 | tf_op jit(solution)/shard_map/ppermute | solution.py:480
  26.7 8.6 %collective-permute-start.14 = (bf16[128,768]{1,0:T(8,128)(2,1)S(1)}, bf16[128,768]{1,0:T(8,128)(2,1)S(1)}, u32[]{:S(2)}, u32[]{:S(2)}) collective-permute-start(bf16[128,768]{1,0:T(8,128)(2,1)S(1)} %project.4), channel_id=1, source_target_pairs={{0,1},{1,0},{2,3},{3,2},{4,5},{5,4},{6,7},{7,6},{8,9},{9,8},{10,11... | collective-permute-start | bytes 589832 | tf_op jit(solution)/shard_map/ppermute | solution.py:475
  30.0 4.3 %collective-permute-start.12 = (bf16[128,384]{1,0:T(8,128)(2,1)S(1)}, bf16[128,384]{1,0:T(8,128)(2,1)S(1)}, u32[]{:S(2)}, u32[]{:S(2)}) collective-permute-start(bf16[128,384]{1,0:T(8,128)(2,1)S(1)} %get-tuple-element.98), channel_id=1, source_target_pairs={{16,18},{17,19},{18,16},{19,17},{20,22},{21,23},{22,20},{23,21},{2... | collective-permute-start | bytes 294920 | tf_op jit(solution)/shard_map/ppermute | solution.py:480
  30.7 2.1 %collective-permute-start.10 = (bf16[384,768]{1,0:T(8,128)(2,1)S(1)}, bf16[384,768]{1,0:T(8,128)(2,1)S(1)}, u32[]{:S(2)}, u32[]{:S(2)}) collective-permute-start(bf16[384,768]{1,0:T(8,128)(2,1)S(1)} %stack.1.part_ref), channel_id=1, source_target_pairs={{0,16},{16,0},{1,17},{17,1},{2,18},{18,2},{3,19},{19,3},{4,20},{20... | collective-permute-start | bytes 1769480 | tf_op jit(solution)/shard_map/ppermute | solution.py:475
  33.1 7.0 %collective-permute-start.13 = (bf16[128,768]{1,0:T(8,128)(2,1)S(1)}, bf16[128,768]{1,0:T(8,128)(2,1)S(1)}, u32[]{:S(2)}, u32[]{:S(2)}) collective-permute-start(bf16[128,768]{1,0:T(8,128)(2,1)S(1)} %project.5), channel_id=1, source_target_pairs={{0,1},{1,0},{2,3},{3,2},{4,5},{5,4},{6,7},{7,6},{8,9},{9,8},{10,11... | collective-permute-start | bytes 589832 | tf_op jit(solution)/shard_map/ppermute | solution.py:475

commit v9 on v7

--- a/solution.py
+++ b/solution.py
@@ -556,8 +556,10 @@
     (for_side,) = rest(state, 3)
     got_side = flipped(for_side, "head", 2)
     state, for_side = lax.optimization_barrier((state, for_side))
-    for_far, own_side = rest(state, 2, 1)
+    (for_far,) = rest(state, 2)
     got_far = flipped(for_far, "head", 2)
+    state, for_far = lax.optimization_barrier((state, for_far))
+    (own_side,) = rest(state, 1)
     parts, own_side = lax.optimization_barrier((parts, own_side))
     here = call(
         stack_kernel, shape((depth, broad), bf16), [vmem] * tiles, *parts, name="stack"

time: 38.7 us -> 40.9 us (1.057)
  starting transfers between devices: 16.8 us -> 19.1 us
    ppermute x12, starting transfers between devices: 14.1 us -> 16.4 us  [flipped(): lax.ppermute(value, axis, [(i, i ^ flip) for i in range(lax.axis_size(axi...]
    pallas_call x14 -> x15, Pallas kernels: 7.89 us -> 8.06 us  [call(): pl.pallas_call(functools.partial(kernel, **keys_of) if keys_of else kerne...]
  transfers between devices with their start and end apart: 14 -> 14, of which waited for: 7 -> 5; matrix products, arithmetic and copies ran while one was open for 0% -> 0% of each run, Pallas kernels for 20% -> 19%
where the time goes in v9:
time: 40.9 us; the launch traced here: 40.7 us
  starting transfers between devices  19.1 us (47%)
  waiting for transfers between devices  11.9 us (29%)
  Pallas kernels  9.49 us (23%)
    ppermute x12, starting transfers between devices, flipped(): lax.ppermute(value, axis, [(i, i ^ flip) for i in range(lax.axis_size(axi...  16.4 us
    ppermute x12, waiting for transfers between devices, flipped(): lax.ppermute(value, axis, [(i, i ^ flip) for i in range(lax.axis_size(axi...  11.9 us
    pallas_call x15, Pallas kernels, call(): pl.pallas_call(functools.partial(kernel, **keys_of) if keys_of else kerne...  8.06 us
    pallas_call x2, Pallas kernels, two_by_two(): pl.pallas_call(functools.partial(add_kernel, flip=flip), out_shape=shape(...  1.43 us
    ppermute x1, starting transfers between devices, two_by_two(): first_tile = lax.ppermute(tile, 'tm', [(0, 1)])  1.34 us
    ppermute x1, starting transfers between devices, two_by_two(): first_edge = lax.ppermute(edge, 'tm', [(0, 1)])  1.32 us
  transfers between devices with their start and end apart: 14, of which 5 were waited for; matrix products, arithmetic and copies ran while one was open for 0% of the time, Pallas kernels for 19%

profile of v9, /device:TPU:0, one launch (start us, length us, event | category | flops | bytes accessed | tf_op | source)
XLA Modules:
  0.0 40.7 jit_solution(5846070888165475919)
XLA Ops:
  0.0 0.0 copy-start.3
  0.0 0.0 copy-start.2
  0.0 0.0 copy-start.4
  0.0 0.0 copy-start.5
  0.0 0.0 copy-start.1
  0.0 1.0 %part.1.part_ref = bf16[96,768]{1,0:T(8,128)(2,1)S(1)} custom-call(bf16[384,1536]{1,0:T(8,128)(2,1)} %w_ref.9), custom_call_target="tpu_custom_call" | custom-call | tf_op jit(solution)/shard_map/part/pallas_call | solution.py:458
  1.0 4.1 %collective-permute-start = (bf16[96,768]{1,0:T(8,128)(2,1)S(1)}, bf16[96,768]{1,0:T(8,128)(2,1)S(1)}, u32[]{:S(2)}, u32[]{:S(2)}) collective-permute-start(bf16[96,768]{1,0:T(8,128)(2,1)S(1)} %part.1.part_ref), channel_id=1, source_target_pairs={{0,2},{1,3},{2,0},{3,1},{4,6},{5,7},{6,4},{7,5},{8,10},{9,11},{10,... | collective-permute-start | bytes 442376 | tf_op jit(solution)/shard_map/ppermute | solution.py:470
  5.2 0.0 copy-done.3
  5.2 0.0 copy-done.2
  5.2 0.4 faces.1
  5.6 1.6 %collective-permute-start.1 = (bf16[2,2,64,384]{3,2,1,0:T(8,128)(2,1)S(1)}, bf16[2,2,64,384]{3,2,1,0:T(8,128)(2,1)S(1)}, u32[]{:S(2)}, u32[]{:S(2)}) collective-permute-start(bf16[2,2,64,384]{3,2,1,0:T(8,128)(2,1)S(1)} %get-tuple-element.68), channel_id=1, source_target_pairs={{0,8},{4,12},{8,0},{12,4},{1,9},{5,13},{9,1},{13,5},{2,10},{6,14},... | collective-permute-start | bytes 589832 | tf_op jit(solution)/shard_map/ppermute | solution.py:470
  7.1 1.5 %collective-permute-start.2 = (bf16[2,2,64,384]{3,2,1,0:T(8,128)(2,1)S(1)}, bf16[2,2,64,384]{3,2,1,0:T(8,128)(2,1)S(1)}, u32[]{:S(2)}, u32[]{:S(2)}) collective-permute-start(bf16[2,2,64,384]{3,2,1,0:T(8,128)(2,1)S(1)} %get-tuple-element.69), channel_id=1, source_target_pairs={{0,4},{4,0},{8,12},{12,8},{1,5},{5,1},{9,13},{13,9},{2,6},{6,2},{1... | collective-permute-start | bytes 589832 | tf_op jit(solution)/shard_map/ppermute | solution.py:470
  8.6 0.5 %collective-permute-start.3 = (bf16[2,2,16,384]{3,2,1,0:T(8,128)(2,1)S(1)}, bf16[2,2,16,384]{3,2,1,0:T(8,128)(2,1)S(1)}, u32[]{:S(2)}, u32[]{:S(2)}) collective-permute-start(bf16[2,2,16,384]{3,2,1,0:T(8,128)(2,1)S(1)} %get-tuple-element.70), channel_id=1, source_target_pairs={{0,12},{4,8},{8,4},{12,0},{1,13},{5,9},{9,5},{13,1},{2,14},{6,10},... | collective-permute-start | bytes 147464 | tf_op jit(solution)/shard_map/ppermute | solution.py:470
  9.1 0.0 copy-done.4
  9.1 0.0 copy-done.5
  9.1 0.0 copy-done.1
  9.1 1.4 %begin.1 = (f32[512,128]{1,0:T(8,128)S(1)}, f32[512,128]{1,0:T(8,128)S(1)}, f32[512,128]{1,0:T(8,128)S(1)}, s32[256,800]{1,0:T(8,128)S(1)}, s32[6,128]{1,0:T(8,128)S(1)}) custom-call(s32[3]{0:T(128)S(1)} %copy-done.5, s32[2,2,3]{2,1,0:T(2,128)S(1)} %bitcast.13, bf16[512,384]{1,0:T(8,128)(2,1)S(1)} %bitcast.5, bf16[2,512,384]{2,1,0:T(8,128)(2,1)S(1)} %get-tuple-element.58.tile_ref), custom_call_target="tpu_custom_call" | custom-call | tf_op jit(solution)/shard_map/begin/pallas_call | solution.py:458
  10.5 1.3 %collective-permute-start.4 = (bf16[2,512,384]{2,1,0:T(8,128)(2,1)S(1)}, bf16[2,512,384]{2,1,0:T(8,128)(2,1)S(1)}, u32[]{:S(2)}, u32[]{:S(2)}) collective-permute-start(bf16[2,512,384]{2,1,0:T(8,128)(2,1)S(1)} %get-tuple-element.58.tile_ref), channel_id=1, source_target_pairs={{0,16},{1,17},{2,18},{3,19},{4,20},{5,21},{6,22},{7,23},{8,24},{9,... | collective-permute-start | bytes 2359304 | tf_op jit(solution)/shard_map/ppermute | solution.py:517
  11.9 1.1 %tile.1 = (f32[512,256]{1,0:T(8,128)S(1)}, f32[512,256]{1,0:T(8,128)S(1)}, f32[512,256]{1,0:T(8,128)S(1)}) custom-call(bf16[512,384]{1,0:T(8,128)(2,1)S(1)} %bitcast.6, bf16[2,512,384]{2,1,0:T(8,128)(2,1)S(1)} %get-tuple-element.58.tile_ref, s32[256,800]{1,0:T(8,128)S(1)} %get-tuple-element.59.dist_ref.rest_3_, s32[6,128]{1,0:T(8,128)S(1)} %get-tuple-element.60.reach_ref.rest_4_), custom_call_target="tpu_custom_call" | custom-call | tf_op jit(solution)/shard_map/tile/pallas_call | solution.py:458
  12.9 0.0 collective-permute-done.in_ref
  13.0 1.3 %collective-permute-done.3.corner_ref = bf16[2,2,16,384]{3,2,1,0:T(8,128)(2,1)S(1)} collective-permute-done((bf16[2,2,16,384]{3,2,1,0:T(8,128)(2,1)S(1)}, bf16[2,2,16,384]{3,2,1,0:T(8,128)(2,1)S(1)}, u32[]{:S(2)}, u32[]{:S(2)}) %collective-permute-start.3) | collective-permute-done | bytes 49184 | tf_op jit(solution)/shard_map/ppermute | solution.py:470
  14.2 0.0 collective-permute-done.1.row_ref
  14.2 0.0 collective-permute-done.2.col_ref
  14.3 1.3 %collective-permute-start.5 = (bf16[2,288,384]{2,1,0:T(8,128)(2,1)S(1)}, bf16[2,288,384]{2,1,0:T(8,128)(2,1)S(1)}, u32[]{:S(2)}, u32[]{:S(2)}) collective-permute-start(bf16[2,288,384]{2,1,0:T(8,128)(2,1)S(1)} %edges.1.edge_ref), channel_id=1, source_target_pairs={{0,16},{1,17},{2,18},{3,19},{4,20},{5,21},{6,22},{7,23},{8,24},{9,... | collective-permute-start | bytes 1327112 | tf_op jit(solution)/shard_map/ppermute | solution.py:535
  15.6 2.5 %collective-permute-start.8 = (bf16[96,768]{1,0:T(8,128)(2,1)S(1)}, bf16[96,768]{1,0:T(8,128)(2,1)S(1)}, u32[]{:S(2)}, u32[]{:S(2)}) collective-permute-start(bf16[96,768]{1,0:T(8,128)(2,1)S(1)} %lone.1.refs_0_), channel_id=1, source_target_pairs={{0,12},{4,8},{8,4},{12,0},{1,13},{5,9},{9,5},{13,1},{2,14},{6,10},... | collective-permute-start | bytes 442376 | tf_op jit(solution)/shard_map/ppermute | solution.py:470
  18.1 0.5 %collective-permute-start.7 = (bf16[96,768]{1,0:T(8,128)(2,1)S(1)}, bf16[96,768]{1,0:T(8,128)(2,1)S(1)}, u32[]{:S(2)}, u32[]{:S(2)}) collective-permute-start(bf16[96,768]{1,0:T(8,128)(2,1)S(1)} %lone.1.refs_0_), channel_id=1, source_target_pairs={{0,8},{4,12},{8,0},{12,4},{1,9},{5,13},{9,1},{13,5},{2,10},{6,14},... | collective-permute-start | bytes 442376 | tf_op jit(solution)/shard_map/ppermute | solution.py:470
  18.6 0.5 %collective-permute-start.6 = (bf16[96,768]{1,0:T(8,128)(2,1)S(1)}, bf16[96,768]{1,0:T(8,128)(2,1)S(1)}, u32[]{:S(2)}, u32[]{:S(2)}) collective-permute-start(bf16[96,768]{1,0:T(8,128)(2,1)S(1)} %lone.1.refs_0_), channel_id=1, source_target_pairs={{0,4},{4,0},{8,12},{12,8},{1,5},{5,1},{9,13},{13,9},{2,6},{6,2},{1... | collective-permute-start | bytes 442376 | tf_op jit(solution)/shard_map/ppermute | solution.py:470
  19.2 0.0 collective-permute-done.5.first_edge_ref
  19.2 0.0 collective-permute-done.4.first_tile_ref
  19.2 0.7 %rest.4 = bf16[128,384]{1,0:T(8,128)(2,1)S(1)} custom-call(bf16[512,384]{1,0:T(8,128)(2,1)S(1)} %bitcast.7, bf16[2,288,384]{2,1,0:T(8,128)(2,1)S(1)} %edges.1.edge_ref, bf16[2,512,384]{2,1,0:T(8,128)(2,1)S(1)} %collective-permute-done.4.first_tile_ref, bf16[2,288,384]{2,1,0:T(8,128)(2,1)S(1)} %collective-permute-done.5.first_edge_ref, ...), custom_call_target="tpu_custom_call" | custom-call | tf_op jit(solution)/shard_map/rest/pallas_call | solution.py:458
  19.8 0.4 collective-permute-start.9
  20.2 0.7 %rest.5 = bf16[128,384]{1,0:T(8,128)(2,1)S(1)} custom-call(bf16[512,384]{1,0:T(8,128)(2,1)S(1)} %bitcast.8, bf16[2,288,384]{2,1,0:T(8,128)(2,1)S(1)} %edges.1.edge_ref, bf16[2,512,384]{2,1,0:T(8,128)(2,1)S(1)} %collective-permute-done.4.first_tile_ref, bf16[2,288,384]{2,1,0:T(8,128)(2,1)S(1)} %collective-permute-done.5.first_edge_ref, ...), custom_call_target="tpu_custom_call" | custom-call | tf_op jit(solution)/shard_map/rest/pallas_call | solution.py:458
  20.9 2.7 %collective-permute-start.11 = (bf16[128,384]{1,0:T(8,128)(2,1)S(1)}, bf16[128,384]{1,0:T(8,128)(2,1)S(1)}, u32[]{:S(2)}, u32[]{:S(2)}) collective-permute-start(bf16[128,384]{1,0:T(8,128)(2,1)S(1)} %rest.5), channel_id=1, source_target_pairs={{0,2},{1,3},{2,0},{3,1},{4,6},{5,7},{6,4},{7,5},{8,10},{9,11},{10,... | collective-permute-start | bytes 294920 | tf_op jit(solution)/shard_map/ppermute | solution.py:470
  23.5 0.7 %rest.6.own_ref = bf16[128,384]{1,0:T(8,128)(2,1)S(1)} custom-call(bf16[512,384]{1,0:T(8,128)(2,1)S(1)} %bitcast.9, bf16[2,288,384]{2,1,0:T(8,128)(2,1)S(1)} %edges.1.edge_ref, bf16[2,512,384]{2,1,0:T(8,128)(2,1)S(1)} %collective-permute-done.4.first_tile_ref, bf16[2,288,384]{2,1,0:T(8,128)(2,1)S(1)} %collective-permute-done.5.first_edge_ref, ...), custom_call_target="tpu_custom_call" | custom-call | tf_op jit(solution)/shard_map/rest/pallas_call | solution.py:458
  24.2 0.0 copy-start
  24.2 0.0 collective-permute-done.8.refs_3_
  24.2 0.0 collective-permute-done.7.refs_2_
  24.2 0.0 collective-permute-done.6.refs_1_
  24.3 0.1 stack.1.part_ref
  24.3 5.4 %collective-permute-done.9.got_ref = bf16[128,384]{1,0:T(8,128)(2,1)S(1)} collective-permute-done((bf16[128,384]{1,0:T(8,128)(2,1)S(1)}, bf16[128,384]{1,0:T(8,128)(2,1)S(1)}, u32[]{:S(2)}, u32[]{:S(2)}) %collective-permute-start.9) | collective-permute-done | bytes 98336 | tf_op jit(solution)/shard_map/ppermute | solution.py:470
  29.7 0.0 copy-done
  29.7 0.4 project.4
  30.1 0.1 collective-permute-start.13
  30.1 0.1 collective-permute-start.10
  30.2 0.7 %rest.7.own_ref = bf16[128,384]{1,0:T(8,128)(2,1)S(1)} custom-call(bf16[512,384]{1,0:T(8,128)(2,1)S(1)} %bitcast.10, bf16[2,288,384]{2,1,0:T(8,128)(2,1)S(1)} %edges.1.edge_ref, bf16[2,512,384]{2,1,0:T(8,128)(2,1)S(1)} %collective-permute-done.4.first_tile_ref, bf16[2,288,384]{2,1,0:T(8,128)(2,1)S(1)} %collective-permute-done.5.first_edge_ref, ...), custom_call_target="tpu_custom_call" | custom-call | flops 20000000000 | tf_op jit(solution)/shard_map/rest/pallas_call | solution.py:458
  30.9 1.3 %collective-permute-done.10.part_ref = bf16[384,768]{1,0:T(8,128)(2,1)S(1)} collective-permute-done((bf16[384,768]{1,0:T(8,128)(2,1)S(1)}, bf16[384,768]{1,0:T(8,128)(2,1)S(1)}, u32[]{:S(2)}, u32[]{:S(2)}) %collective-permute-start.10) | collective-permute-done | bytes 589856 | tf_op jit(solution)/shard_map/ppermute | solution.py:470
  32.2 0.4 project.5
  32.6 2.0 %collective-permute-start.12 = (bf16[128,768]{1,0:T(8,128)(2,1)S(1)}, bf16[128,768]{1,0:T(8,128)(2,1)S(1)}, u32[]{:S(2)}, u32[]{:S(2)}) collective-permute-start(bf16[128,768]{1,0:T(8,128)(2,1)S(1)} %project.5), channel_id=1, source_target_pairs={{0,1},{1,0},{2,3},{3,2},{4,5},{5,4},{6,7},{7,6},{8,9},{9,8},{10,11... | collective-permute-start | bytes 589832 | tf_op jit(solution)/shard_map/ppermute | solution.py:470
  34.6 0.0 collective-permute-done.11.got_ref
  34.6 0.4 project.6.mine_ref
  34.9 0.4 project.7.mine_ref
  35.3 0.6 %collective-permute-done.13.got_ref = bf16[128,768]{1,0:T(8,128)(2,1)S(1)} collective-permute-done((bf16[128,768]{1,0:T(8,128)(2,1)S(1)}, bf16[128,768]{1,0:T(8,128)(2,1)S(1)}, u32[]{:S(2)}, u32[]{:S(2)}) %collective-permute-start.13) | collective-permute-done | bytes 196640 | tf_op jit(solution)/shard_map/ppermute | solution.py:470
  35.9 0.7 %add.2.rest_0_ = bf16[128,1536]{1,0:T(8,128)(2,1)} custom-call(f32[128,768]{1,0:T(8,128)S(1)} %project.7.mine_ref, bf16[128,768]{1,0:T(8,128)(2,1)S(1)} %collective-permute-done.13.got_ref), custom_call_target="tpu_custom_call" | custom-call | tf_op jit(solution)/shard_map/add/pallas_call | solution.py:599
  36.7 3.3 %collective-permute-done.12.got_ref = bf16[128,768]{1,0:T(8,128)(2,1)S(1)} collective-permute-done((bf16[128,768]{1,0:T(8,128)(2,1)S(1)}, bf16[128,768]{1,0:T(8,128)(2,1)S(1)}, u32[]{:S(2)}, u32[]{:S(2)}) %collective-permute-start.12) | collective-permute-done | bytes 196640 | tf_op jit(solution)/shard_map/ppermute | solution.py:470
  40.0 0.7 %add.3 = bf16[128,1536]{1,0:T(8,128)(2,1)} custom-call(f32[128,768]{1,0:T(8,128)S(1)} %project.6.mine_ref, bf16[128,768]{1,0:T(8,128)(2,1)S(1)} %collective-permute-done.12.got_ref, bf16[128,1536]{1,0:T(8,128)(2,1)} %add.2.rest_0_), custom_call_target="tpu_custom_call", output_to_operand_aliasing={{}: (2, {})} | custom-call | tf_op jit(solution)/shard_map/add/pallas_call | solution.py:599
  (2 shorter events, 0.1 us)
Async XLA Ops:
  0.0 5.2 %copy-start.3 = (bf16[1,1,2,16,16,384]{5,4,3,2,1,0:T(8,128)(2,1)S(1)}, bf16[1,1,2,16,16,384]{5,4,3,2,1,0:T(8,128)(2,1)}, u32[]{:S(2)}) copy-start(bf16[1,1,2,16,16,384]{5,4,3,2,1,0:T(8,128)(2,1)} %param.8) | copy-start | bytes 1179652
  0.0 5.2 %copy-start.2 = (bf16[1,1,2,16,16,384]{5,4,3,2,1,0:T(8,128)(2,1)S(1)}, bf16[1,1,2,16,16,384]{5,4,3,2,1,0:T(8,128)(2,1)}, u32[]{:S(2)}) copy-start(bf16[1,1,2,16,16,384]{5,4,3,2,1,0:T(8,128)(2,1)} %param.7) | copy-start | bytes 1179652
  0.0 9.1 %copy-start.4 = (s32[3,2,2]{0,2,1:T(2,128)S(1)}, s32[3,2,2]{0,2,1:T(2,128)}, u32[]{:S(2)}) copy-start(s32[3,2,2]{0,2,1:T(2,128)} %param.11) | copy-start | bytes 148
  0.0 9.1 %copy-start.5 = (s32[3]{0:T(128)S(1)}, s32[3]{0:T(128)}, u32[]{:S(2)}) copy-start(s32[3]{0:T(128)} %radius_ref.1) | copy-start | bytes 40
  0.0 9.1 %copy-start.1 = (bf16[1,1,2,16,16,384]{5,4,3,2,1,0:T(8,128)(2,1)S(1)}, bf16[1,1,2,16,16,384]{5,4,3,2,1,0:T(8,128)(2,1)}, u32[]{:S(2)}) copy-start(bf16[1,1,2,16,16,384]{5,4,3,2,1,0:T(8,128)(2,1)} %param.6) | copy-start | bytes 1179652
  1.0 11.9 %collective-permute-start = (bf16[96,768]{1,0:T(8,128)(2,1)S(1)}, bf16[96,768]{1,0:T(8,128)(2,1)S(1)}, u32[]{:S(2)}, u32[]{:S(2)}) collective-permute-start(bf16[96,768]{1,0:T(8,128)(2,1)S(1)} %part.1.part_ref), channel_id=1, source_target_pairs={{0,2},{1,3},{2,0},{3,1},{4,6},{5,7},{6,4},{7,5},{8,10},{9,11},{10,... | collective-permute-start | bytes 442376 | tf_op jit(solution)/shard_map/ppermute | solution.py:470
  5.6 8.7 %collective-permute-start.1 = (bf16[2,2,64,384]{3,2,1,0:T(8,128)(2,1)S(1)}, bf16[2,2,64,384]{3,2,1,0:T(8,128)(2,1)S(1)}, u32[]{:S(2)}, u32[]{:S(2)}) collective-permute-start(bf16[2,2,64,384]{3,2,1,0:T(8,128)(2,1)S(1)} %get-tuple-element.68), channel_id=1, source_target_pairs={{0,8},{4,12},{8,0},{12,4},{1,9},{5,13},{9,1},{13,5},{2,10},{6,14},... | collective-permute-start | bytes 589832 | tf_op jit(solution)/shard_map/ppermute | solution.py:470
  7.1 7.1 %collective-permute-start.2 = (bf16[2,2,64,384]{3,2,1,0:T(8,128)(2,1)S(1)}, bf16[2,2,64,384]{3,2,1,0:T(8,128)(2,1)S(1)}, u32[]{:S(2)}, u32[]{:S(2)}) collective-permute-start(bf16[2,2,64,384]{3,2,1,0:T(8,128)(2,1)S(1)} %get-tuple-element.69), channel_id=1, source_target_pairs={{0,4},{4,0},{8,12},{12,8},{1,5},{5,1},{9,13},{13,9},{2,6},{6,2},{1... | collective-permute-start | bytes 589832 | tf_op jit(solution)/shard_map/ppermute | solution.py:470
  8.6 5.6 %collective-permute-start.3 = (bf16[2,2,16,384]{3,2,1,0:T(8,128)(2,1)S(1)}, bf16[2,2,16,384]{3,2,1,0:T(8,128)(2,1)S(1)}, u32[]{:S(2)}, u32[]{:S(2)}) collective-permute-start(bf16[2,2,16,384]{3,2,1,0:T(8,128)(2,1)S(1)} %get-tuple-element.70), channel_id=1, source_target_pairs={{0,12},{4,8},{8,4},{12,0},{1,13},{5,9},{9,5},{13,1},{2,14},{6,10},... | collective-permute-start | bytes 147464 | tf_op jit(solution)/shard_map/ppermute | solution.py:470
  10.5 8.7 %collective-permute-start.4 = (bf16[2,512,384]{2,1,0:T(8,128)(2,1)S(1)}, bf16[2,512,384]{2,1,0:T(8,128)(2,1)S(1)}, u32[]{:S(2)}, u32[]{:S(2)}) collective-permute-start(bf16[2,512,384]{2,1,0:T(8,128)(2,1)S(1)} %get-tuple-element.58.tile_ref), channel_id=1, source_target_pairs={{0,16},{1,17},{2,18},{3,19},{4,20},{5,21},{6,22},{7,23},{8,24},{9,... | collective-permute-start | bytes 2359304 | tf_op jit(solution)/shard_map/ppermute | solution.py:517
  14.3 4.9 %collective-permute-start.5 = (bf16[2,288,384]{2,1,0:T(8,128)(2,1)S(1)}, bf16[2,288,384]{2,1,0:T(8,128)(2,1)S(1)}, u32[]{:S(2)}, u32[]{:S(2)}) collective-permute-start(bf16[2,288,384]{2,1,0:T(8,128)(2,1)S(1)} %edges.1.edge_ref), channel_id=1, source_target_pairs={{0,16},{1,17},{2,18},{3,19},{4,20},{5,21},{6,22},{7,23},{8,24},{9,... | collective-permute-start | bytes 1327112 | tf_op jit(solution)/shard_map/ppermute | solution.py:535
  15.6 8.6 %collective-permute-start.8 = (bf16[96,768]{1,0:T(8,128)(2,1)S(1)}, bf16[96,768]{1,0:T(8,128)(2,1)S(1)}, u32[]{:S(2)}, u32[]{:S(2)}) collective-permute-start(bf16[96,768]{1,0:T(8,128)(2,1)S(1)} %lone.1.refs_0_), channel_id=1, source_target_pairs={{0,12},{4,8},{8,4},{12,0},{1,13},{5,9},{9,5},{13,1},{2,14},{6,10},... | collective-permute-start | bytes 442376 | tf_op jit(solution)/shard_map/ppermute | solution.py:470
  18.1 6.1 %collective-permute-start.7 = (bf16[96,768]{1,0:T(8,128)(2,1)S(1)}, bf16[96,768]{1,0:T(8,128)(2,1)S(1)}, u32[]{:S(2)}, u32[]{:S(2)}) collective-permute-start(bf16[96,768]{1,0:T(8,128)(2,1)S(1)} %lone.1.refs_0_), channel_id=1, source_target_pairs={{0,8},{4,12},{8,0},{12,4},{1,9},{5,13},{9,1},{13,5},{2,10},{6,14},... | collective-permute-start | bytes 442376 | tf_op jit(solution)/shard_map/ppermute | solution.py:470
  18.6 5.6 %collective-permute-start.6 = (bf16[96,768]{1,0:T(8,128)(2,1)S(1)}, bf16[96,768]{1,0:T(8,128)(2,1)S(1)}, u32[]{:S(2)}, u32[]{:S(2)}) collective-permute-start(bf16[96,768]{1,0:T(8,128)(2,1)S(1)} %lone.1.refs_0_), channel_id=1, source_target_pairs={{0,4},{4,0},{8,12},{12,8},{1,5},{5,1},{9,13},{13,9},{2,6},{6,2},{1... | collective-permute-start | bytes 442376 | tf_op jit(solution)/shard_map/ppermute | solution.py:470
  19.8 9.9 %collective-permute-start.9 = (bf16[128,384]{1,0:T(8,128)(2,1)S(1)}, bf16[128,384]{1,0:T(8,128)(2,1)S(1)}, u32[]{:S(2)}, u32[]{:S(2)}) collective-permute-start(bf16[128,384]{1,0:T(8,128)(2,1)S(1)} %rest.4), channel_id=1, source_target_pairs={{0,2},{1,3},{2,0},{3,1},{4,6},{5,7},{6,4},{7,5},{8,10},{9,11},{10,... | collective-permute-start | bytes 294920 | tf_op jit(solution)/shard_map/ppermute | solution.py:470
  20.9 13.7 %collective-permute-start.11 = (bf16[128,384]{1,0:T(8,128)(2,1)S(1)}, bf16[128,384]{1,0:T(8,128)(2,1)S(1)}, u32[]{:S(2)}, u32[]{:S(2)}) collective-permute-start(bf16[128,384]{1,0:T(8,128)(2,1)S(1)} %rest.5), channel_id=1, source_target_pairs={{0,2},{1,3},{2,0},{3,1},{4,6},{5,7},{6,4},{7,5},{8,10},{9,11},{10,... | collective-permute-start | bytes 294920 | tf_op jit(solution)/shard_map/ppermute | solution.py:470
  24.2 5.5 %copy-start = (bf16[384,1536]{1,0:T(8,128)(2,1)S(1)}, bf16[384,1536]{1,0:T(8,128)(2,1)}, u32[]{:S(2)}) copy-start(bf16[384,1536]{1,0:T(8,128)(2,1)} %w_ref.9) | copy-start | bytes 3538948
  30.1 5.9 %collective-permute-start.13 = (bf16[128,768]{1,0:T(8,128)(2,1)S(1)}, bf16[128,768]{1,0:T(8,128)(2,1)S(1)}, u32[]{:S(2)}, u32[]{:S(2)}) collective-permute-start(bf16[128,768]{1,0:T(8,128)(2,1)S(1)} %project.4), channel_id=1, source_target_pairs={{0,1},{1,0},{2,3},{3,2},{4,5},{5,4},{6,7},{7,6},{8,9},{9,8},{10,11... | collective-permute-start | bytes 589832 | tf_op jit(solution)/shard_map/ppermute | solution.py:470
  30.1 2.1 %collective-permute-start.10 = (bf16[384,768]{1,0:T(8,128)(2,1)S(1)}, bf16[384,768]{1,0:T(8,128)(2,1)S(1)}, u32[]{:S(2)}, u32[]{:S(2)}) collective-permute-start(bf16[384,768]{1,0:T(8,128)(2,1)S(1)} %stack.1.part_ref), channel_id=1, source_target_pairs={{0,16},{16,0},{1,17},{17,1},{2,18},{18,2},{3,19},{19,3},{4,20},{20... | collective-permute-start | bytes 1769480 | tf_op jit(solution)/shard_map/ppermute | solution.py:470
  32.6 7.4 %collective-permute-start.12 = (bf16[128,768]{1,0:T(8,128)(2,1)S(1)}, bf16[128,768]{1,0:T(8,128)(2,1)S(1)}, u32[]{:S(2)}, u32[]{:S(2)}) collective-permute-start(bf16[128,768]{1,0:T(8,128)(2,1)S(1)} %project.5), channel_id=1, source_target_pairs={{0,1},{1,0},{2,3},{3,2},{4,5},{5,4},{6,7},{7,6},{8,9},{9,8},{10,11... | collective-permute-start | bytes 589832 | tf_op jit(solution)/shard_map/ppermute | solution.py:470

commit v10 on v7

--- a/solution.py
+++ b/solution.py
@@ -310,7 +310,7 @@
             max_ref[rows, outs] = jnp.broadcast_to(m, (step, head_dim))
 
 
-def begin_kernel(radius_ref, mask_ref, q_ref, tile_ref, *outs, geometry, heads):
+def tile_kernel(radius_ref, mask_ref, q_ref, tile_ref, *outs, geometry, heads):
     *state, dist_ref, reach_ref = outs
     high, wide, span, frames = geometry[:4]
     dist_ref[...] = distances(high, wide, span, frames)
@@ -323,38 +323,59 @@
         reach_ref[heads + head : heads + head + 1] = jnp.full(
             line, jnp.where(seen, radius, -1), jnp.int32
         )
-    attend_tile(q_ref, tile_ref, dist_ref, lambda h: radius_ref[h], (0,), state, geometry)
-
-
-def tile_kernel(q_ref, tile_ref, dist_ref, reach_ref, *state, geometry, heads):
     attend_tile(
-        q_ref,
-        tile_ref,
-        dist_ref,
-        lambda h: reach_ref[h : h + 1, :1],
-        range(1, heads),
-        state,
-        geometry,
-    )
-
-
-def pick_state(head_state, state, head, rows, head_dim):
-    refs = head_state if head == 0 else state
-    at = max(head - 1, 0) * head_dim
-    return [ref[rows, at : at + head_dim] for ref in refs]
+        q_ref, tile_ref, dist_ref, lambda h: radius_ref[h], range(heads), state, geometry
+    )
+
+
+def first_kernel(
+    q_ref, first_ref, acc_ref, sum_ref, max_ref, dist_ref, reach_ref, *outs, geometry, heads
+):
+    high, wide, span, frames, head_dim, factor, step = geometry
+    cells = high * wide
+    base = frames * cells
+    olds = (acc_ref, sum_ref, max_ref)
+
+    @pl.when(lax.axis_index("tm") > 0)
+    def _():
+        for head in range(heads):
+            cols = slice(head * head_dim, (head + 1) * head_dim)
+            units = []
+            starts = range(0, q_ref.shape[0], step)
+            for start in starts:
+                rows = slice(start, start + step)
+                near = dist_ref[start % cells : start % cells + step, :base]
+                reach = reach_ref[heads + head : heads + head + 1, :1]
+                piece = (first_ref[0, :, cols], first_ref[1, :, cols], near, reach)
+                units.append((q_ref[rows, cols], [piece], max_ref[rows, cols][:, :1]))
+            for start, m, got in zip(starts, *attend(units, factor)):
+                rows = slice(start, start + step)
+                acc, total, old = (ref[rows, cols] for ref in olds)
+                shrink = jnp.exp2(old - m)
+                outs[0][rows, cols] = acc * shrink + got[:, :head_dim]
+                outs[1][rows, cols] = total * shrink + got[:, head_dim:]
+                outs[2][rows, cols] = jnp.broadcast_to(m, old.shape)
+
+    @pl.when(lax.axis_index("tm") == 0)
+    def _():
+        for ref, out_ref in zip(olds, outs):
+            out_ref[...] = ref[...]
 
 
 def rest_kernel(
     q_ref,
     edge_ref,
-    first_tile_ref,
-    first_edge_ref,
-    *rest,
+    first_ref,
+    dist_ref,
+    reach_ref,
+    acc_ref,
+    sum_ref,
+    max_ref,
+    *outs,
     geometry,
     heads,
     flips,
 ):
-    head_state, dist_ref, reach_ref, state, outs = rest[:3], rest[3], rest[4], rest[5:8], rest[8:]
     high, wide, span, frames, head_dim, factor, step = geometry
     cells = high * wide
     base = frames * cells
@@ -365,21 +386,19 @@
         for flip, out_ref in zip(flips, outs):
             start = pl.multiple_of(jnp.bitwise_xor(head_at, flip) * step, step)
             rows = pl.ds(start, step)
-            near = dist_ref[pl.ds(pl.multiple_of(lax.rem(start, cells), step), step)]
-            beyond = near[:, base:]
+            near = dist_ref[pl.ds(pl.multiple_of(lax.rem(start, cells), step), step), base:]
             units = []
             olds = []
             for head in range(heads):
                 cols = slice(head * head_dim, (head + 1) * head_dim)
-                sources = [(edge_ref, beyond, head)]
+                sources = [(edge_ref, head)]
                 if with_first:
-                    sources.append((first_tile_ref, near[:, :base], heads + head))
-                    sources.append((first_edge_ref, beyond, heads + head))
+                    sources.append((first_ref, heads + head))
                 pieces = [
-                    (ref[0, :, cols], ref[1, :, cols], dist, reach_ref[row : row + 1, :1])
-                    for ref, dist, row in sources
+                    (ref[0, :, cols], ref[1, :, cols], near, reach_ref[row : row + 1, :1])
+                    for ref, row in sources
                 ]
-                olds.append(pick_state(head_state, state, head, rows, head_dim))
+                olds.append([ref[rows, cols] for ref in (acc_ref, sum_ref, max_ref)])
                 units.append((q_ref[rows, cols], pieces, olds[-1][2][:, :1]))
             for head, (m, got) in enumerate(zip(*attend(units, factor))):
                 old_acc, old_total, old_max = olds[head]
@@ -500,29 +519,31 @@
     )
     faces = [flipped(face, "tile", flip) for face, flip in zip(faces, (2, 1, 3))]
     lone = flipped(part, "head", 2)
-    begun = call(
-        begin_kernel,
-        [shape((tokens, head_dim), f32)] * 3
+    first_tile = lax.ppermute(tile, "tm", [(0, 1)])
+    *state, dist, reach = call(
+        tile_kernel,
+        [shape((tokens, channels), f32)] * 3
         + [shape((cells, count), jnp.int32), shape((2 * heads, head_dim), jnp.int32)],
         [smem] * 2 + [vmem] * 2,
         radius,
         block_mask.transpose(1, 2, 0),
         q,
         tile,
-        name="begin",
+        name="tile",
+        flops=20 * 10**9,
         geometry=geometry,
         heads=heads,
     )
-    begun, tile = lax.optimization_barrier((begun, tile))
-    first_tile = lax.ppermute(tile, "tm", [(0, 1)])
     state = call(
-        tile_kernel,
-        [shape((tokens, channels - head_dim), f32)] * 3,
-        [vmem] * 4,
+        first_kernel,
+        [shape((tokens, channels), f32)] * 3,
+        [vmem] * 7,
         q,
-        tile,
-        *begun[3:],
-        name="tile",
+        first_tile,
+        *state,
+        dist,
+        reach,
+        name="first",
         geometry=geometry,
         heads=heads,
     )
@@ -539,12 +560,12 @@
         return call(
             rest_kernel,
             [shape((step, channels), bf16)] * len(flips),
-            [vmem] * 12,
+            [vmem] * 8,
             q,
             edge,
-            first_tile,
             first_edge,
-            *begun,
+            dist,
+            reach,
             *state,
             name="rest",
             geometry=geometry,

time: 38.7 us -> 40.3 us (1.041)
  waiting for transfers between devices: 12.2 us -> 13.5 us
    ppermute x12, waiting for transfers between devices: 12.2 us -> 13.5 us  [flipped(): lax.ppermute(value, axis, [(i, i ^ flip) for i in range(lax.axis_size(axi...]
    ppermute x1, starting transfers between devices: 1.32 us -> 1.92 us  [two_by_two(): first_edge = lax.ppermute(edge, 'tm', [(0, 1)])]
  transfers between devices with their start and end apart: 14 -> 14, of which waited for: 7 -> 10; matrix products, arithmetic and copies ran while one was open for 0% -> 0% of each run, Pallas kernels for 20% -> 19%
where the time goes in v10:
time: 40.3 us; the launch traced here: 40.1 us
  starting transfers between devices  17.1 us (42%)
  waiting for transfers between devices  13.5 us (33%)
  Pallas kernels  9.3 us (23%)
    ppermute x12, starting transfers between devices, flipped(): lax.ppermute(value, axis, [(i, i ^ flip) for i in range(lax.axis_size(axi...  13.8 us
    ppermute x12, waiting for transfers between devices, flipped(): lax.ppermute(value, axis, [(i, i ^ flip) for i in range(lax.axis_size(axi...  13.5 us
    pallas_call x14, Pallas kernels, call(): pl.pallas_call(functools.partial(kernel, **keys_of) if keys_of else kerne...  7.87 us
    ppermute x1, starting transfers between devices, two_by_two(): first_edge = lax.ppermute(edge, 'tm', [(0, 1)])  1.92 us
    pallas_call x2, Pallas kernels, two_by_two(): pl.pallas_call(functools.partial(add_kernel, flip=flip), out_shape=shape(...  1.43 us
    ppermute x1, starting transfers between devices, two_by_two(): first_tile = lax.ppermute(tile, 'tm', [(0, 1)])  1.33 us
  transfers between devices with their start and end apart: 14, of which 10 were waited for; matrix products, arithmetic and copies ran while one was open for 0% of the time, Pallas kernels for 19%

profile of v10, /device:TPU:0, one launch (start us, length us, event | category | flops | bytes accessed | tf_op | source)
XLA Modules:
  0.0 40.1 jit_solution(11705533620944518667)
XLA Ops:
  0.0 0.0 copy-start.3
  0.0 0.0 copy-start.2
  0.0 0.0 copy-start.4
  0.0 0.0 copy-start.5
  0.0 0.0 copy-start.1
  0.0 1.0 %part.1.part_ref = bf16[96,768]{1,0:T(8,128)(2,1)S(1)} custom-call(bf16[384,1536]{1,0:T(8,128)(2,1)} %w_ref.9), custom_call_target="tpu_custom_call" | custom-call | tf_op jit(solution)/shard_map/part/pallas_call | solution.py:477
  1.0 4.1 %collective-permute-start = (bf16[96,768]{1,0:T(8,128)(2,1)S(1)}, bf16[96,768]{1,0:T(8,128)(2,1)S(1)}, u32[]{:S(2)}, u32[]{:S(2)}) collective-permute-start(bf16[96,768]{1,0:T(8,128)(2,1)S(1)} %part.1.part_ref), channel_id=1, source_target_pairs={{0,2},{1,3},{2,0},{3,1},{4,6},{5,7},{6,4},{7,5},{8,10},{9,11},{10,... | collective-permute-start | bytes 442376 | tf_op jit(solution)/shard_map/ppermute | solution.py:489
  5.2 0.0 copy-done.3
  5.2 0.0 copy-done.2
  5.2 0.4 faces.1
  5.6 2.5 %collective-permute-start.4 = (bf16[2,2,16,384]{3,2,1,0:T(8,128)(2,1)S(1)}, bf16[2,2,16,384]{3,2,1,0:T(8,128)(2,1)S(1)}, u32[]{:S(2)}, u32[]{:S(2)}) collective-permute-start(bf16[2,2,16,384]{3,2,1,0:T(8,128)(2,1)S(1)} %get-tuple-element.60), channel_id=1, source_target_pairs={{0,12},{4,8},{8,4},{12,0},{1,13},{5,9},{9,5},{13,1},{2,14},{6,10},... | collective-permute-start | bytes 147464 | tf_op jit(solution)/shard_map/ppermute | solution.py:489
  8.1 0.5 %collective-permute-start.2 = (bf16[2,2,64,384]{3,2,1,0:T(8,128)(2,1)S(1)}, bf16[2,2,64,384]{3,2,1,0:T(8,128)(2,1)S(1)}, u32[]{:S(2)}, u32[]{:S(2)}) collective-permute-start(bf16[2,2,64,384]{3,2,1,0:T(8,128)(2,1)S(1)} %get-tuple-element.58), channel_id=1, source_target_pairs={{0,8},{4,12},{8,0},{12,4},{1,9},{5,13},{9,1},{13,5},{2,10},{6,14},... | collective-permute-start | bytes 589832 | tf_op jit(solution)/shard_map/ppermute | solution.py:489
  8.6 0.5 %collective-permute-start.3 = (bf16[2,2,64,384]{3,2,1,0:T(8,128)(2,1)S(1)}, bf16[2,2,64,384]{3,2,1,0:T(8,128)(2,1)S(1)}, u32[]{:S(2)}, u32[]{:S(2)}) collective-permute-start(bf16[2,2,64,384]{3,2,1,0:T(8,128)(2,1)S(1)} %get-tuple-element.59), channel_id=1, source_target_pairs={{0,4},{4,0},{8,12},{12,8},{1,5},{5,1},{9,13},{13,9},{2,6},{6,2},{1... | collective-permute-start | bytes 589832 | tf_op jit(solution)/shard_map/ppermute | solution.py:489
  9.1 1.3 %collective-permute-start.1 = (bf16[2,512,384]{2,1,0:T(8,128)(2,1)S(1)}, bf16[2,512,384]{2,1,0:T(8,128)(2,1)S(1)}, u32[]{:S(2)}, u32[]{:S(2)}) collective-permute-start(bf16[2,512,384]{2,1,0:T(8,128)(2,1)S(1)} %get-tuple-element.45.tile_ref), channel_id=1, source_target_pairs={{0,16},{1,17},{2,18},{3,19},{4,20},{5,21},{6,22},{7,23},{8,24},{9,... | collective-permute-start | bytes 2359304 | tf_op jit(solution)/shard_map/ppermute | solution.py:522
  10.5 0.0 copy-done.4
  10.5 0.0 copy-done.5
  10.5 0.0 copy-done.1
  10.5 2.3 %tile.1 = (f32[512,384]{1,0:T(8,128)S(1)}, f32[512,384]{1,0:T(8,128)S(1)}, f32[512,384]{1,0:T(8,128)S(1)}, s32[256,800]{1,0:T(8,128)S(1)}, s32[6,128]{1,0:T(8,128)S(1)}) custom-call(s32[3]{0:T(128)S(1)} %copy-done.5, s32[2,2,3]{2,1,0:T(2,128)S(1)} %bitcast.12, bf16[512,384]{1,0:T(8,128)(2,1)S(1)} %bitcast.5, bf16[2,512,384]{2,1,0:T(8,128)(2,1)S(1)} %get-tuple-element.45.tile_ref), custom_call_target="tpu_custom_call" | custom-call | flops 20000000000 | tf_op jit(solution)/shard_map/tile/pallas_call | solution.py:477
  12.8 0.0 collective-permute-done.1.first_ref
  12.8 0.2 first.1
  13.0 0.0 collective-permute-done.in_ref
  13.0 0.0 collective-permute-done.4.corner_ref
  13.0 1.7 %collective-permute-done.2.row_ref = bf16[2,2,64,384]{3,2,1,0:T(8,128)(2,1)S(1)} collective-permute-done((bf16[2,2,64,384]{3,2,1,0:T(8,128)(2,1)S(1)}, bf16[2,2,64,384]{3,2,1,0:T(8,128)(2,1)S(1)}, u32[]{:S(2)}, u32[]{:S(2)}) %collective-permute-start.2) | collective-permute-done | bytes 196640 | tf_op jit(solution)/shard_map/ppermute | solution.py:489
  14.7 0.2 collective-permute-done.3.col_ref
  14.9 1.9 %collective-permute-start.5 = (bf16[2,288,384]{2,1,0:T(8,128)(2,1)S(1)}, bf16[2,288,384]{2,1,0:T(8,128)(2,1)S(1)}, u32[]{:S(2)}, u32[]{:S(2)}) collective-permute-start(bf16[2,288,384]{2,1,0:T(8,128)(2,1)S(1)} %edges.1.edge_ref), channel_id=1, source_target_pairs={{0,16},{1,17},{2,18},{3,19},{4,20},{5,21},{6,22},{7,23},{8,24},{9,... | collective-permute-start | bytes 1327112 | tf_op jit(solution)/shard_map/ppermute | solution.py:556
  16.9 2.5 %collective-permute-start.8 = (bf16[96,768]{1,0:T(8,128)(2,1)S(1)}, bf16[96,768]{1,0:T(8,128)(2,1)S(1)}, u32[]{:S(2)}, u32[]{:S(2)}) collective-permute-start(bf16[96,768]{1,0:T(8,128)(2,1)S(1)} %lone.1.refs_0_), channel_id=1, source_target_pairs={{0,12},{4,8},{8,4},{12,0},{1,13},{5,9},{9,5},{13,1},{2,14},{6,10},... | collective-permute-start | bytes 442376 | tf_op jit(solution)/shard_map/ppermute | solution.py:489
  19.4 0.5 %collective-permute-start.7 = (bf16[96,768]{1,0:T(8,128)(2,1)S(1)}, bf16[96,768]{1,0:T(8,128)(2,1)S(1)}, u32[]{:S(2)}, u32[]{:S(2)}) collective-permute-start(bf16[96,768]{1,0:T(8,128)(2,1)S(1)} %lone.1.refs_0_), channel_id=1, source_target_pairs={{0,8},{4,12},{8,0},{12,4},{1,9},{5,13},{9,1},{13,5},{2,10},{6,14},... | collective-permute-start | bytes 442376 | tf_op jit(solution)/shard_map/ppermute | solution.py:489
  19.9 0.5 %collective-permute-start.6 = (bf16[96,768]{1,0:T(8,128)(2,1)S(1)}, bf16[96,768]{1,0:T(8,128)(2,1)S(1)}, u32[]{:S(2)}, u32[]{:S(2)}) collective-permute-start(bf16[96,768]{1,0:T(8,128)(2,1)S(1)} %lone.1.refs_0_), channel_id=1, source_target_pairs={{0,4},{4,0},{8,12},{12,8},{1,5},{5,1},{9,13},{13,9},{2,6},{6,2},{1... | collective-permute-start | bytes 442376 | tf_op jit(solution)/shard_map/ppermute | solution.py:489
  20.4 0.0 collective-permute-done.5.first_ref
  20.4 0.7 %rest.3 = bf16[128,384]{1,0:T(8,128)(2,1)S(1)} custom-call(bf16[512,384]{1,0:T(8,128)(2,1)S(1)} %bitcast.7, bf16[2,288,384]{2,1,0:T(8,128)(2,1)S(1)} %edges.1.edge_ref, bf16[2,288,384]{2,1,0:T(8,128)(2,1)S(1)} %collective-permute-done.5.first_ref, s32[256,800]{1,0:T(8,128)S(1)} %get-tuple-element.49.dist_ref, s32[6,128]{1,0:T(8,128)S(1)} %get-tuple-element.50.reach_ref, ...), custom_call_target="tpu_custom_call" | custom-call | tf_op jit(solution)/shard_map/rest/pallas_call | solution.py:477
  21.1 0.1 collective-permute-start.9
  21.2 1.2 %rest.4 = (bf16[128,384]{1,0:T(8,128)(2,1)S(1)}, bf16[128,384]{1,0:T(8,128)(2,1)S(1)}) custom-call(bf16[512,384]{1,0:T(8,128)(2,1)S(1)} %bitcast.8, bf16[2,288,384]{2,1,0:T(8,128)(2,1)S(1)} %edges.1.edge_ref, bf16[2,288,384]{2,1,0:T(8,128)(2,1)S(1)} %collective-permute-done.5.first_ref, s32[256,800]{1,0:T(8,128)S(1)} %get-tuple-element.49.dist_ref, ...), custom_call_target="tpu_custom_call" | custom-call | tf_op jit(solution)/shard_map/rest/pallas_call | solution.py:477
  22.4 0.0 copy-start
  22.4 1.3 %collective-permute-done.8.refs_3_ = bf16[96,768]{1,0:T(8,128)(2,1)S(1)} collective-permute-done((bf16[96,768]{1,0:T(8,128)(2,1)S(1)}, bf16[96,768]{1,0:T(8,128)(2,1)S(1)}, u32[]{:S(2)}, u32[]{:S(2)}) %collective-permute-start.8) | collective-permute-done | bytes 147488 | tf_op jit(solution)/shard_map/ppermute | solution.py:489
  23.7 2.4 %collective-permute-done.7.refs_2_ = bf16[96,768]{1,0:T(8,128)(2,1)S(1)} collective-permute-done((bf16[96,768]{1,0:T(8,128)(2,1)S(1)}, bf16[96,768]{1,0:T(8,128)(2,1)S(1)}, u32[]{:S(2)}, u32[]{:S(2)}) %collective-permute-start.7) | collective-permute-done | bytes 147488 | tf_op jit(solution)/shard_map/ppermute | solution.py:489
  26.1 0.1 collective-permute-done.6.refs_1_
  26.1 0.3 collective-permute-start.11
  26.5 0.1 stack.1.part_ref
  26.5 0.1 collective-permute-done.9.got_ref
  26.7 0.0 copy-done
  26.7 0.4 project.4
  27.0 1.7 %collective-permute-start.13 = (bf16[128,768]{1,0:T(8,128)(2,1)S(1)}, bf16[128,768]{1,0:T(8,128)(2,1)S(1)}, u32[]{:S(2)}, u32[]{:S(2)}) collective-permute-start(bf16[128,768]{1,0:T(8,128)(2,1)S(1)} %project.4), channel_id=1, source_target_pairs={{0,1},{1,0},{2,3},{3,2},{4,5},{5,4},{6,7},{7,6},{8,9},{9,8},{10,11... | collective-permute-start | bytes 589832 | tf_op jit(solution)/shard_map/ppermute | solution.py:489
  28.7 0.0 collective-permute-start.10
  28.7 0.7 %rest.5.own_ref = bf16[128,384]{1,0:T(8,128)(2,1)S(1)} custom-call(bf16[512,384]{1,0:T(8,128)(2,1)S(1)} %bitcast.9, bf16[2,288,384]{2,1,0:T(8,128)(2,1)S(1)} %edges.1.edge_ref, bf16[2,288,384]{2,1,0:T(8,128)(2,1)S(1)} %collective-permute-done.5.first_ref, s32[256,800]{1,0:T(8,128)S(1)} %get-tuple-element.49.dist_ref, ...), custom_call_target="tpu_custom_call" | custom-call | flops 20000000000 | tf_op jit(solution)/shard_map/rest/pallas_call | solution.py:477
  29.4 1.3 %collective-permute-done.10.part_ref = bf16[384,768]{1,0:T(8,128)(2,1)S(1)} collective-permute-done((bf16[384,768]{1,0:T(8,128)(2,1)S(1)}, bf16[384,768]{1,0:T(8,128)(2,1)S(1)}, u32[]{:S(2)}, u32[]{:S(2)}) %collective-permute-start.10) | collective-permute-done | bytes 589856 | tf_op jit(solution)/shard_map/ppermute | solution.py:489
  30.7 0.4 project.5
  31.1 0.5 %collective-permute-start.12 = (bf16[128,768]{1,0:T(8,128)(2,1)S(1)}, bf16[128,768]{1,0:T(8,128)(2,1)S(1)}, u32[]{:S(2)}, u32[]{:S(2)}) collective-permute-start(bf16[128,768]{1,0:T(8,128)(2,1)S(1)} %project.5), channel_id=1, source_target_pairs={{0,1},{1,0},{2,3},{3,2},{4,5},{5,4},{6,7},{7,6},{8,9},{9,8},{10,11... | collective-permute-start | bytes 589832 | tf_op jit(solution)/shard_map/ppermute | solution.py:489
  31.6 1.7 %collective-permute-done.11.got_ref = bf16[128,384]{1,0:T(8,128)(2,1)S(1)} collective-permute-done((bf16[128,384]{1,0:T(8,128)(2,1)S(1)}, bf16[128,384]{1,0:T(8,128)(2,1)S(1)}, u32[]{:S(2)}, u32[]{:S(2)}) %collective-permute-start.11) | collective-permute-done | bytes 98336 | tf_op jit(solution)/shard_map/ppermute | solution.py:489
  33.2 0.4 project.6.mine_ref
  33.6 0.4 project.7.mine_ref
  34.0 2.0 %collective-permute-done.13.got_ref = bf16[128,768]{1,0:T(8,128)(2,1)S(1)} collective-permute-done((bf16[128,768]{1,0:T(8,128)(2,1)S(1)}, bf16[128,768]{1,0:T(8,128)(2,1)S(1)}, u32[]{:S(2)}, u32[]{:S(2)}) %collective-permute-start.13) | collective-permute-done | bytes 196640 | tf_op jit(solution)/shard_map/ppermute | solution.py:489
  36.0 0.7 %add.2.rest_0_ = bf16[128,1536]{1,0:T(8,128)(2,1)} custom-call(f32[128,768]{1,0:T(8,128)S(1)} %project.7.mine_ref, bf16[128,768]{1,0:T(8,128)(2,1)S(1)} %collective-permute-done.13.got_ref), custom_call_target="tpu_custom_call" | custom-call | tf_op jit(solution)/shard_map/add/pallas_call | solution.py:618
  36.7 2.7 %collective-permute-done.12.got_ref = bf16[128,768]{1,0:T(8,128)(2,1)S(1)} collective-permute-done((bf16[128,768]{1,0:T(8,128)(2,1)S(1)}, bf16[128,768]{1,0:T(8,128)(2,1)S(1)}, u32[]{:S(2)}, u32[]{:S(2)}) %collective-permute-start.12) | collective-permute-done | bytes 196640 | tf_op jit(solution)/shard_map/ppermute | solution.py:489
  39.4 0.7 %add.3 = bf16[128,1536]{1,0:T(8,128)(2,1)} custom-call(f32[128,768]{1,0:T(8,128)S(1)} %project.6.mine_ref, bf16[128,768]{1,0:T(8,128)(2,1)S(1)} %collective-permute-done.12.got_ref, bf16[128,1536]{1,0:T(8,128)(2,1)} %add.2.rest_0_), custom_call_target="tpu_custom_call", output_to_operand_aliasing={{}: (2, {})} | custom-call | tf_op jit(solution)/shard_map/add/pallas_call | solution.py:618
  (2 shorter events, 0.1 us)
Async XLA Ops:
  0.0 5.2 %copy-start.3 = (bf16[1,1,2,16,16,384]{5,4,3,2,1,0:T(8,128)(2,1)S(1)}, bf16[1,1,2,16,16,384]{5,4,3,2,1,0:T(8,128)(2,1)}, u32[]{:S(2)}) copy-start(bf16[1,1,2,16,16,384]{5,4,3,2,1,0:T(8,128)(2,1)} %param.8) | copy-start | bytes 1179652
  0.0 5.2 %copy-start.2 = (bf16[1,1,2,16,16,384]{5,4,3,2,1,0:T(8,128)(2,1)S(1)}, bf16[1,1,2,16,16,384]{5,4,3,2,1,0:T(8,128)(2,1)}, u32[]{:S(2)}) copy-start(bf16[1,1,2,16,16,384]{5,4,3,2,1,0:T(8,128)(2,1)} %param.7) | copy-start | bytes 1179652
  0.0 10.4 %copy-start.4 = (s32[3,2,2]{0,2,1:T(2,128)S(1)}, s32[3,2,2]{0,2,1:T(2,128)}, u32[]{:S(2)}) copy-start(s32[3,2,2]{0,2,1:T(2,128)} %param.11) | copy-start | bytes 148
  0.0 10.5 %copy-start.5 = (s32[3]{0:T(128)S(1)}, s32[3]{0:T(128)}, u32[]{:S(2)}) copy-start(s32[3]{0:T(128)} %radius_ref.1) | copy-start | bytes 40
  0.0 10.5 %copy-start.1 = (bf16[1,1,2,16,16,384]{5,4,3,2,1,0:T(8,128)(2,1)S(1)}, bf16[1,1,2,16,16,384]{5,4,3,2,1,0:T(8,128)(2,1)}, u32[]{:S(2)}) copy-start(bf16[1,1,2,16,16,384]{5,4,3,2,1,0:T(8,128)(2,1)} %param.6) | copy-start | bytes 1179652
  1.0 11.9 %collective-permute-start = (bf16[96,768]{1,0:T(8,128)(2,1)S(1)}, bf16[96,768]{1,0:T(8,128)(2,1)S(1)}, u32[]{:S(2)}, u32[]{:S(2)}) collective-permute-start(bf16[96,768]{1,0:T(8,128)(2,1)S(1)} %part.1.part_ref), channel_id=1, source_target_pairs={{0,2},{1,3},{2,0},{3,1},{4,6},{5,7},{6,4},{7,5},{8,10},{9,11},{10,... | collective-permute-start | bytes 442376 | tf_op jit(solution)/shard_map/ppermute | solution.py:489
  5.6 7.4 %collective-permute-start.4 = (bf16[2,2,16,384]{3,2,1,0:T(8,128)(2,1)S(1)}, bf16[2,2,16,384]{3,2,1,0:T(8,128)(2,1)S(1)}, u32[]{:S(2)}, u32[]{:S(2)}) collective-permute-start(bf16[2,2,16,384]{3,2,1,0:T(8,128)(2,1)S(1)} %get-tuple-element.60), channel_id=1, source_target_pairs={{0,12},{4,8},{8,4},{12,0},{1,13},{5,9},{9,5},{13,1},{2,14},{6,10},... | collective-permute-start | bytes 147464 | tf_op jit(solution)/shard_map/ppermute | solution.py:489
  8.1 6.6 %collective-permute-start.2 = (bf16[2,2,64,384]{3,2,1,0:T(8,128)(2,1)S(1)}, bf16[2,2,64,384]{3,2,1,0:T(8,128)(2,1)S(1)}, u32[]{:S(2)}, u32[]{:S(2)}) collective-permute-start(bf16[2,2,64,384]{3,2,1,0:T(8,128)(2,1)S(1)} %get-tuple-element.58), channel_id=1, source_target_pairs={{0,8},{4,12},{8,0},{12,4},{1,9},{5,13},{9,1},{13,5},{2,10},{6,14},... | collective-permute-start | bytes 589832 | tf_op jit(solution)/shard_map/ppermute | solution.py:489
  8.6 6.3 %collective-permute-start.3 = (bf16[2,2,64,384]{3,2,1,0:T(8,128)(2,1)S(1)}, bf16[2,2,64,384]{3,2,1,0:T(8,128)(2,1)S(1)}, u32[]{:S(2)}, u32[]{:S(2)}) collective-permute-start(bf16[2,2,64,384]{3,2,1,0:T(8,128)(2,1)S(1)} %get-tuple-element.59), channel_id=1, source_target_pairs={{0,4},{4,0},{8,12},{12,8},{1,5},{5,1},{9,13},{13,9},{2,6},{6,2},{1... | collective-permute-start | bytes 589832 | tf_op jit(solution)/shard_map/ppermute | solution.py:489
  9.1 3.6 %collective-permute-start.1 = (bf16[2,512,384]{2,1,0:T(8,128)(2,1)S(1)}, bf16[2,512,384]{2,1,0:T(8,128)(2,1)S(1)}, u32[]{:S(2)}, u32[]{:S(2)}) collective-permute-start(bf16[2,512,384]{2,1,0:T(8,128)(2,1)S(1)} %get-tuple-element.45.tile_ref), channel_id=1, source_target_pairs={{0,16},{1,17},{2,18},{3,19},{4,20},{5,21},{6,22},{7,23},{8,24},{9,... | collective-permute-start | bytes 2359304 | tf_op jit(solution)/shard_map/ppermute | solution.py:522
  14.9 5.5 %collective-permute-start.5 = (bf16[2,288,384]{2,1,0:T(8,128)(2,1)S(1)}, bf16[2,288,384]{2,1,0:T(8,128)(2,1)S(1)}, u32[]{:S(2)}, u32[]{:S(2)}) collective-permute-start(bf16[2,288,384]{2,1,0:T(8,128)(2,1)S(1)} %edges.1.edge_ref), channel_id=1, source_target_pairs={{0,16},{1,17},{2,18},{3,19},{4,20},{5,21},{6,22},{7,23},{8,24},{9,... | collective-permute-start | bytes 1327112 | tf_op jit(solution)/shard_map/ppermute | solution.py:556
  16.9 6.9 %collective-permute-start.8 = (bf16[96,768]{1,0:T(8,128)(2,1)S(1)}, bf16[96,768]{1,0:T(8,128)(2,1)S(1)}, u32[]{:S(2)}, u32[]{:S(2)}) collective-permute-start(bf16[96,768]{1,0:T(8,128)(2,1)S(1)} %lone.1.refs_0_), channel_id=1, source_target_pairs={{0,12},{4,8},{8,4},{12,0},{1,13},{5,9},{9,5},{13,1},{2,14},{6,10},... | collective-permute-start | bytes 442376 | tf_op jit(solution)/shard_map/ppermute | solution.py:489
  19.4 6.7 %collective-permute-start.7 = (bf16[96,768]{1,0:T(8,128)(2,1)S(1)}, bf16[96,768]{1,0:T(8,128)(2,1)S(1)}, u32[]{:S(2)}, u32[]{:S(2)}) collective-permute-start(bf16[96,768]{1,0:T(8,128)(2,1)S(1)} %lone.1.refs_0_), channel_id=1, source_target_pairs={{0,8},{4,12},{8,0},{12,4},{1,9},{5,13},{9,1},{13,5},{2,10},{6,14},... | collective-permute-start | bytes 442376 | tf_op jit(solution)/shard_map/ppermute | solution.py:489
  19.9 6.3 %collective-permute-start.6 = (bf16[96,768]{1,0:T(8,128)(2,1)S(1)}, bf16[96,768]{1,0:T(8,128)(2,1)S(1)}, u32[]{:S(2)}, u32[]{:S(2)}) collective-permute-start(bf16[96,768]{1,0:T(8,128)(2,1)S(1)} %lone.1.refs_0_), channel_id=1, source_target_pairs={{0,4},{4,0},{8,12},{12,8},{1,5},{5,1},{9,13},{13,9},{2,6},{6,2},{1... | collective-permute-start | bytes 442376 | tf_op jit(solution)/shard_map/ppermute | solution.py:489
  21.1 5.6 %collective-permute-start.9 = (bf16[128,384]{1,0:T(8,128)(2,1)S(1)}, bf16[128,384]{1,0:T(8,128)(2,1)S(1)}, u32[]{:S(2)}, u32[]{:S(2)}) collective-permute-start(bf16[128,384]{1,0:T(8,128)(2,1)S(1)} %rest.3), channel_id=1, source_target_pairs={{0,2},{1,3},{2,0},{3,1},{4,6},{5,7},{6,4},{7,5},{8,10},{9,11},{10,... | collective-permute-start | bytes 294920 | tf_op jit(solution)/shard_map/ppermute | solution.py:489
  22.4 4.3 %copy-start = (bf16[384,1536]{1,0:T(8,128)(2,1)S(1)}, bf16[384,1536]{1,0:T(8,128)(2,1)}, u32[]{:S(2)}) copy-start(bf16[384,1536]{1,0:T(8,128)(2,1)} %w_ref.9) | copy-start | bytes 3538948
  26.1 7.1 %collective-permute-start.11 = (bf16[128,384]{1,0:T(8,128)(2,1)S(1)}, bf16[128,384]{1,0:T(8,128)(2,1)S(1)}, u32[]{:S(2)}, u32[]{:S(2)}) collective-permute-start(bf16[128,384]{1,0:T(8,128)(2,1)S(1)} %get-tuple-element.84), channel_id=1, source_target_pairs={{0,2},{1,3},{2,0},{3,1},{4,6},{5,7},{6,4},{7,5},{8,10},{9,11},{10,... | collective-permute-start | bytes 294920 | tf_op jit(solution)/shard_map/ppermute | solution.py:489
  27.0 9.0 %collective-permute-start.13 = (bf16[128,768]{1,0:T(8,128)(2,1)S(1)}, bf16[128,768]{1,0:T(8,128)(2,1)S(1)}, u32[]{:S(2)}, u32[]{:S(2)}) collective-permute-start(bf16[128,768]{1,0:T(8,128)(2,1)S(1)} %project.4), channel_id=1, source_target_pairs={{0,1},{1,0},{2,3},{3,2},{4,5},{5,4},{6,7},{7,6},{8,9},{9,8},{10,11... | collective-permute-start | bytes 589832 | tf_op jit(solution)/shard_map/ppermute | solution.py:489
  28.7 2.0 %collective-permute-start.10 = (bf16[384,768]{1,0:T(8,128)(2,1)S(1)}, bf16[384,768]{1,0:T(8,128)(2,1)S(1)}, u32[]{:S(2)}, u32[]{:S(2)}) collective-permute-start(bf16[384,768]{1,0:T(8,128)(2,1)S(1)} %stack.1.part_ref), channel_id=1, source_target_pairs={{0,16},{16,0},{1,17},{17,1},{2,18},{18,2},{3,19},{19,3},{4,20},{20... | collective-permute-start | bytes 1769480 | tf_op jit(solution)/shard_map/ppermute | solution.py:489
  31.1 8.3 %collective-permute-start.12 = (bf16[128,768]{1,0:T(8,128)(2,1)S(1)}, bf16[128,768]{1,0:T(8,128)(2,1)S(1)}, u32[]{:S(2)}, u32[]{:S(2)}) collective-permute-start(bf16[128,768]{1,0:T(8,128)(2,1)S(1)} %project.5), channel_id=1, source_target_pairs={{0,1},{1,0},{2,3},{3,2},{4,5},{5,4},{6,7},{7,6},{8,9},{9,8},{10,11... | collective-permute-start | bytes 589832 | tf_op jit(solution)/shard_map/ppermute | solution.py:489

commit v11 on v7

--- a/solution.py
+++ b/solution.py
@@ -527,10 +527,10 @@
         heads=heads,
     )
     lone, state = lax.optimization_barrier((lone, state))
-    lone = call(copy_kernel, part_shape, [vmem], lone, name="lone", flops=2 * 10**9)
+    lone = call(copy_kernel, part_shape, [vmem], lone, name="lone", flops=20 * 10**9)
     lone, state, faces = lax.optimization_barrier((lone, state, faces))
     edge = call(
-        edge_kernel, shape((2, count - tokens, channels), bf16), [vmem] * 3, *faces, name="edges", flops=20 * 10**9
+        edge_kernel, shape((2, count - tokens, channels), bf16), [vmem] * 3, *faces, name="edges"
     )
     first_edge = lax.ppermute(edge, "tm", [(0, 1)])
     parts = [lone] + [flipped(lone, "tile", flip) for flip in range(1, tiles)]

time: 38.7 us -> 38.7 us (level)
  transfers between devices with their start and end apart: 14 -> 14, of which waited for: 7 -> 8; matrix products, arithmetic and copies ran while one was open for 0% -> 0% of each run, Pallas kernels for 20% -> 20%
where the time goes in v11:
time: 38.7 us; the launch traced here: 38.5 us
  starting transfers between devices  16.7 us (43%)
  waiting for transfers between devices  12.4 us (32%)
  Pallas kernels  9.3 us (24%)
    ppermute x12, starting transfers between devices, flipped(): lax.ppermute(value, axis, [(i, i ^ flip) for i in range(lax.axis_size(axi...  14 us
    ppermute x12, waiting for transfers between devices, flipped(): lax.ppermute(value, axis, [(i, i ^ flip) for i in range(lax.axis_size(axi...  12.4 us
    pallas_call x14, Pallas kernels, call(): pl.pallas_call(functools.partial(kernel, **keys_of) if keys_of else kerne...  7.88 us
    pallas_call x2, Pallas kernels, two_by_two(): pl.pallas_call(functools.partial(add_kernel, flip=flip), out_shape=shape(...  1.42 us
    ppermute x1, starting transfers between devices, two_by_two(): first_tile = lax.ppermute(tile, 'tm', [(0, 1)])  1.34 us
    ppermute x1, starting transfers between devices, two_by_two(): first_edge = lax.ppermute(edge, 'tm', [(0, 1)])  1.32 us
  transfers between devices with their start and end apart: 14, of which 8 were waited for; matrix products, arithmetic and copies ran while one was open for 0% of the time, Pallas kernels for 20%

profile of v11, /device:TPU:0, one launch (start us, length us, event | category | flops | bytes accessed | tf_op | source)
XLA Modules:
  0.0 38.5 jit_solution(7618915420336476302)
XLA Ops:
  0.0 0.0 copy-start.3
  0.0 0.0 copy-start.2
  0.0 0.0 copy-start.4
  0.0 0.0 copy-start.5
  0.0 0.0 copy-start.1
  0.0 1.0 %part.1.part_ref = bf16[96,768]{1,0:T(8,128)(2,1)S(1)} custom-call(bf16[384,1536]{1,0:T(8,128)(2,1)} %w_ref.9), custom_call_target="tpu_custom_call" | custom-call | tf_op jit(solution)/shard_map/part/pallas_call | solution.py:458
  1.0 4.1 %collective-permute-start = (bf16[96,768]{1,0:T(8,128)(2,1)S(1)}, bf16[96,768]{1,0:T(8,128)(2,1)S(1)}, u32[]{:S(2)}, u32[]{:S(2)}) collective-permute-start(bf16[96,768]{1,0:T(8,128)(2,1)S(1)} %part.1.part_ref), channel_id=1, source_target_pairs={{0,2},{1,3},{2,0},{3,1},{4,6},{5,7},{6,4},{7,5},{8,10},{9,11},{10,... | collective-permute-start | bytes 442376 | tf_op jit(solution)/shard_map/ppermute | solution.py:470
  5.2 0.0 copy-done.3
  5.2 0.0 copy-done.2
  5.2 0.4 %faces.1 = (bf16[2,2,64,384]{3,2,1,0:T(8,128)(2,1)S(1)}, bf16[2,2,64,384]{3,2,1,0:T(8,128)(2,1)S(1)}, bf16[2,2,16,384]{3,2,1,0:T(8,128)(2,1)S(1)}, bf16[2,512,384]{2,1,0:T(8,128)(2,1)S(1)}) custom-call(bf16[512,384]{1,0:T(8,128)(2,1)S(1)} %bitcast.10, bf16[512,384]{1,0:T(8,128)(2,1)S(1)} %bitcast.11, bf16[96,768]{1,0:T(8,128)(2,1)S(1)} %part.1.part_ref), custom_call_target="tpu_custom_call" | custom-call | tf_op jit(solution)/shard_map/faces/pallas_call | solution.py:458
  5.6 2.5 %collective-permute-start.3 = (bf16[2,2,16,384]{3,2,1,0:T(8,128)(2,1)S(1)}, bf16[2,2,16,384]{3,2,1,0:T(8,128)(2,1)S(1)}, u32[]{:S(2)}, u32[]{:S(2)}) collective-permute-start(bf16[2,2,16,384]{3,2,1,0:T(8,128)(2,1)S(1)} %get-tuple-element.69), channel_id=1, source_target_pairs={{0,12},{4,8},{8,4},{12,0},{1,13},{5,9},{9,5},{13,1},{2,14},{6,10},... | collective-permute-start | bytes 147464 | tf_op jit(solution)/shard_map/ppermute | solution.py:470
  8.1 0.5 %collective-permute-start.1 = (bf16[2,2,64,384]{3,2,1,0:T(8,128)(2,1)S(1)}, bf16[2,2,64,384]{3,2,1,0:T(8,128)(2,1)S(1)}, u32[]{:S(2)}, u32[]{:S(2)}) collective-permute-start(bf16[2,2,64,384]{3,2,1,0:T(8,128)(2,1)S(1)} %get-tuple-element.67), channel_id=1, source_target_pairs={{0,8},{4,12},{8,0},{12,4},{1,9},{5,13},{9,1},{13,5},{2,10},{6,14},... | collective-permute-start | bytes 589832 | tf_op jit(solution)/shard_map/ppermute | solution.py:470
  8.6 0.5 %collective-permute-start.2 = (bf16[2,2,64,384]{3,2,1,0:T(8,128)(2,1)S(1)}, bf16[2,2,64,384]{3,2,1,0:T(8,128)(2,1)S(1)}, u32[]{:S(2)}, u32[]{:S(2)}) collective-permute-start(bf16[2,2,64,384]{3,2,1,0:T(8,128)(2,1)S(1)} %get-tuple-element.68), channel_id=1, source_target_pairs={{0,4},{4,0},{8,12},{12,8},{1,5},{5,1},{9,13},{13,9},{2,6},{6,2},{1... | collective-permute-start | bytes 589832 | tf_op jit(solution)/shard_map/ppermute | solution.py:470
  9.1 0.0 copy-done.4
  9.1 0.0 copy-done.5
  9.1 0.0 copy-done.1
  9.1 1.4 %begin.1 = (f32[512,128]{1,0:T(8,128)S(1)}, f32[512,128]{1,0:T(8,128)S(1)}, f32[512,128]{1,0:T(8,128)S(1)}, s32[256,800]{1,0:T(8,128)S(1)}, s32[6,128]{1,0:T(8,128)S(1)}) custom-call(s32[3]{0:T(128)S(1)} %copy-done.5, s32[2,2,3]{2,1,0:T(2,128)S(1)} %bitcast.12, bf16[512,384]{1,0:T(8,128)(2,1)S(1)} %bitcast.5, bf16[2,512,384]{2,1,0:T(8,128)(2,1)S(1)} %get-tuple-element.57.tile_ref), custom_call_target="tpu_custom_call" | custom-call | tf_op jit(solution)/shard_map/begin/pallas_call | solution.py:458
  10.5 1.3 %collective-permute-start.4 = (bf16[2,512,384]{2,1,0:T(8,128)(2,1)S(1)}, bf16[2,512,384]{2,1,0:T(8,128)(2,1)S(1)}, u32[]{:S(2)}, u32[]{:S(2)}) collective-permute-start(bf16[2,512,384]{2,1,0:T(8,128)(2,1)S(1)} %get-tuple-element.57.tile_ref), channel_id=1, source_target_pairs={{0,16},{1,17},{2,18},{3,19},{4,20},{5,21},{6,22},{7,23},{8,24},{9,... | collective-permute-start | bytes 2359304 | tf_op jit(solution)/shard_map/ppermute | solution.py:517
  11.8 1.1 %tile.1 = (f32[512,256]{1,0:T(8,128)S(1)}, f32[512,256]{1,0:T(8,128)S(1)}, f32[512,256]{1,0:T(8,128)S(1)}) custom-call(bf16[512,384]{1,0:T(8,128)(2,1)S(1)} %bitcast.6, bf16[2,512,384]{2,1,0:T(8,128)(2,1)S(1)} %get-tuple-element.57.tile_ref, s32[256,800]{1,0:T(8,128)S(1)} %get-tuple-element.58.dist_ref.rest_3_, s32[6,128]{1,0:T(8,128)S(1)} %get-tuple-element.59.reach_ref.rest_4_), custom_call_target="tpu_custom_call" | custom-call | tf_op jit(solution)/shard_map/tile/pallas_call | solution.py:458
  12.9 0.0 collective-permute-done.in_ref
  13.0 0.0 collective-permute-done.3.corner_ref
  13.0 1.7 %collective-permute-done.1.row_ref = bf16[2,2,64,384]{3,2,1,0:T(8,128)(2,1)S(1)} collective-permute-done((bf16[2,2,64,384]{3,2,1,0:T(8,128)(2,1)S(1)}, bf16[2,2,64,384]{3,2,1,0:T(8,128)(2,1)S(1)}, u32[]{:S(2)}, u32[]{:S(2)}) %collective-permute-start.1) | collective-permute-done | bytes 196640 | tf_op jit(solution)/shard_map/ppermute | solution.py:470
  14.7 0.2 collective-permute-done.2.col_ref
  14.9 1.3 %collective-permute-start.5 = (bf16[2,288,384]{2,1,0:T(8,128)(2,1)S(1)}, bf16[2,288,384]{2,1,0:T(8,128)(2,1)S(1)}, u32[]{:S(2)}, u32[]{:S(2)}) collective-permute-start(bf16[2,288,384]{2,1,0:T(8,128)(2,1)S(1)} %edges.1.edge_ref), channel_id=1, source_target_pairs={{0,16},{1,17},{2,18},{3,19},{4,20},{5,21},{6,22},{7,23},{8,24},{9,... | collective-permute-start | bytes 1327112 | tf_op jit(solution)/shard_map/ppermute | solution.py:535
  16.3 1.5 %collective-permute-start.8 = (bf16[96,768]{1,0:T(8,128)(2,1)S(1)}, bf16[96,768]{1,0:T(8,128)(2,1)S(1)}, u32[]{:S(2)}, u32[]{:S(2)}) collective-permute-start(bf16[96,768]{1,0:T(8,128)(2,1)S(1)} %lone.1.refs_0_), channel_id=1, source_target_pairs={{0,12},{4,8},{8,4},{12,0},{1,13},{5,9},{9,5},{13,1},{2,14},{6,10},... | collective-permute-start | bytes 442376 | tf_op jit(solution)/shard_map/ppermute | solution.py:470
  17.8 0.6 %collective-permute-start.7 = (bf16[96,768]{1,0:T(8,128)(2,1)S(1)}, bf16[96,768]{1,0:T(8,128)(2,1)S(1)}, u32[]{:S(2)}, u32[]{:S(2)}) collective-permute-start(bf16[96,768]{1,0:T(8,128)(2,1)S(1)} %lone.1.refs_0_), channel_id=1, source_target_pairs={{0,8},{4,12},{8,0},{12,4},{1,9},{5,13},{9,1},{13,5},{2,10},{6,14},... | collective-permute-start | bytes 442376 | tf_op jit(solution)/shard_map/ppermute | solution.py:470
  18.4 1.4 %collective-permute-start.6 = (bf16[96,768]{1,0:T(8,128)(2,1)S(1)}, bf16[96,768]{1,0:T(8,128)(2,1)S(1)}, u32[]{:S(2)}, u32[]{:S(2)}) collective-permute-start(bf16[96,768]{1,0:T(8,128)(2,1)S(1)} %lone.1.refs_0_), channel_id=1, source_target_pairs={{0,4},{4,0},{8,12},{12,8},{1,5},{5,1},{9,13},{13,9},{2,6},{6,2},{1... | collective-permute-start | bytes 442376 | tf_op jit(solution)/shard_map/ppermute | solution.py:470
  19.8 0.0 collective-permute-done.5.first_edge_ref
  19.8 0.0 collective-permute-done.4.first_tile_ref
  19.8 0.7 %rest.3 = bf16[128,384]{1,0:T(8,128)(2,1)S(1)} custom-call(bf16[512,384]{1,0:T(8,128)(2,1)S(1)} %bitcast.7, bf16[2,288,384]{2,1,0:T(8,128)(2,1)S(1)} %edges.1.edge_ref, bf16[2,512,384]{2,1,0:T(8,128)(2,1)S(1)} %collective-permute-done.4.first_tile_ref, bf16[2,288,384]{2,1,0:T(8,128)(2,1)S(1)} %collective-permute-done.5.first_edge_ref, ...), custom_call_target="tpu_custom_call" | custom-call | tf_op jit(solution)/shard_map/rest/pallas_call | solution.py:458
  20.5 0.4 %collective-permute-start.9 = (bf16[128,384]{1,0:T(8,128)(2,1)S(1)}, bf16[128,384]{1,0:T(8,128)(2,1)S(1)}, u32[]{:S(2)}, u32[]{:S(2)}) collective-permute-start(bf16[128,384]{1,0:T(8,128)(2,1)S(1)} %rest.3), channel_id=1, source_target_pairs={{0,2},{1,3},{2,0},{3,1},{4,6},{5,7},{6,4},{7,5},{8,10},{9,11},{10,... | collective-permute-start | bytes 294920 | tf_op jit(solution)/shard_map/ppermute | solution.py:470
  20.9 1.2 %rest.4 = (bf16[128,384]{1,0:T(8,128)(2,1)S(1)}, bf16[128,384]{1,0:T(8,128)(2,1)S(1)}) custom-call(bf16[512,384]{1,0:T(8,128)(2,1)S(1)} %bitcast.8, bf16[2,288,384]{2,1,0:T(8,128)(2,1)S(1)} %edges.1.edge_ref, bf16[2,512,384]{2,1,0:T(8,128)(2,1)S(1)} %collective-permute-done.4.first_tile_ref, bf16[2,288,384]{2,1,0:T(8,128)(2,1)S(1)} %collective-permute-done.5.first_edge_ref, ...), custom_call_target="tpu_custom_call" | custom-call | tf_op jit(solution)/shard_map/rest/pallas_call | solution.py:458
  22.0 0.0 copy-start
  22.1 1.3 %collective-permute-done.8.refs_3_ = bf16[96,768]{1,0:T(8,128)(2,1)S(1)} collective-permute-done((bf16[96,768]{1,0:T(8,128)(2,1)S(1)}, bf16[96,768]{1,0:T(8,128)(2,1)S(1)}, u32[]{:S(2)}, u32[]{:S(2)}) %collective-permute-start.8) | collective-permute-done | bytes 147488 | tf_op jit(solution)/shard_map/ppermute | solution.py:470
  23.3 1.5 %collective-permute-done.7.refs_2_ = bf16[96,768]{1,0:T(8,128)(2,1)S(1)} collective-permute-done((bf16[96,768]{1,0:T(8,128)(2,1)S(1)}, bf16[96,768]{1,0:T(8,128)(2,1)S(1)}, u32[]{:S(2)}, u32[]{:S(2)}) %collective-permute-start.7) | collective-permute-done | bytes 147488 | tf_op jit(solution)/shard_map/ppermute | solution.py:470
  24.8 0.0 collective-permute-done.6.refs_1_
  24.8 0.2 collective-permute-start.11
  25.0 0.1 stack.1.part_ref
  25.1 1.0 %collective-permute-done.9.got_ref = bf16[128,384]{1,0:T(8,128)(2,1)S(1)} collective-permute-done((bf16[128,384]{1,0:T(8,128)(2,1)S(1)}, bf16[128,384]{1,0:T(8,128)(2,1)S(1)}, u32[]{:S(2)}, u32[]{:S(2)}) %collective-permute-start.9) | collective-permute-done | bytes 98336 | tf_op jit(solution)/shard_map/ppermute | solution.py:470
  26.1 0.0 copy-done
  26.1 0.4 project.4
  26.4 1.7 %collective-permute-start.13 = (bf16[128,768]{1,0:T(8,128)(2,1)S(1)}, bf16[128,768]{1,0:T(8,128)(2,1)S(1)}, u32[]{:S(2)}, u32[]{:S(2)}) collective-permute-start(bf16[128,768]{1,0:T(8,128)(2,1)S(1)} %project.4), channel_id=1, source_target_pairs={{0,1},{1,0},{2,3},{3,2},{4,5},{5,4},{6,7},{7,6},{8,9},{9,8},{10,11... | collective-permute-start | bytes 589832 | tf_op jit(solution)/shard_map/ppermute | solution.py:470
  28.1 0.0 collective-permute-start.10
  28.1 0.7 %rest.5.own_ref = bf16[128,384]{1,0:T(8,128)(2,1)S(1)} custom-call(bf16[512,384]{1,0:T(8,128)(2,1)S(1)} %bitcast.9, bf16[2,288,384]{2,1,0:T(8,128)(2,1)S(1)} %edges.1.edge_ref, bf16[2,512,384]{2,1,0:T(8,128)(2,1)S(1)} %collective-permute-done.4.first_tile_ref, bf16[2,288,384]{2,1,0:T(8,128)(2,1)S(1)} %collective-permute-done.5.first_edge_ref, ...), custom_call_target="tpu_custom_call" | custom-call | flops 20000000000 | tf_op jit(solution)/shard_map/rest/pallas_call | solution.py:458
  28.8 1.3 %collective-permute-done.10.part_ref = bf16[384,768]{1,0:T(8,128)(2,1)S(1)} collective-permute-done((bf16[384,768]{1,0:T(8,128)(2,1)S(1)}, bf16[384,768]{1,0:T(8,128)(2,1)S(1)}, u32[]{:S(2)}, u32[]{:S(2)}) %collective-permute-start.10) | collective-permute-done | bytes 589856 | tf_op jit(solution)/shard_map/ppermute | solution.py:470
  30.1 0.4 project.5
  30.5 0.5 %collective-permute-start.12 = (bf16[128,768]{1,0:T(8,128)(2,1)S(1)}, bf16[128,768]{1,0:T(8,128)(2,1)S(1)}, u32[]{:S(2)}, u32[]{:S(2)}) collective-permute-start(bf16[128,768]{1,0:T(8,128)(2,1)S(1)} %project.5), channel_id=1, source_target_pairs={{0,1},{1,0},{2,3},{3,2},{4,5},{5,4},{6,7},{7,6},{8,9},{9,8},{10,11... | collective-permute-start | bytes 589832 | tf_op jit(solution)/shard_map/ppermute | solution.py:470
  31.0 0.0 collective-permute-done.11.got_ref
  31.0 0.4 project.6.mine_ref
  31.3 0.4 project.7.mine_ref
  31.7 2.1 %collective-permute-done.13.got_ref = bf16[128,768]{1,0:T(8,128)(2,1)S(1)} collective-permute-done((bf16[128,768]{1,0:T(8,128)(2,1)S(1)}, bf16[128,768]{1,0:T(8,128)(2,1)S(1)}, u32[]{:S(2)}, u32[]{:S(2)}) %collective-permute-start.13) | collective-permute-done | bytes 196640 | tf_op jit(solution)/shard_map/ppermute | solution.py:470
  33.8 0.7 %add.2.rest_0_ = bf16[128,1536]{1,0:T(8,128)(2,1)} custom-call(f32[128,768]{1,0:T(8,128)S(1)} %project.7.mine_ref, bf16[128,768]{1,0:T(8,128)(2,1)S(1)} %collective-permute-done.13.got_ref), custom_call_target="tpu_custom_call" | custom-call | tf_op jit(solution)/shard_map/add/pallas_call | solution.py:597
  34.6 3.3 %collective-permute-done.12.got_ref = bf16[128,768]{1,0:T(8,128)(2,1)S(1)} collective-permute-done((bf16[128,768]{1,0:T(8,128)(2,1)S(1)}, bf16[128,768]{1,0:T(8,128)(2,1)S(1)}, u32[]{:S(2)}, u32[]{:S(2)}) %collective-permute-start.12) | collective-permute-done | bytes 196640 | tf_op jit(solution)/shard_map/ppermute | solution.py:470
  37.8 0.7 %add.3 = bf16[128,1536]{1,0:T(8,128)(2,1)} custom-call(f32[128,768]{1,0:T(8,128)S(1)} %project.6.mine_ref, bf16[128,768]{1,0:T(8,128)(2,1)S(1)} %collective-permute-done.12.got_ref, bf16[128,1536]{1,0:T(8,128)(2,1)} %add.2.rest_0_), custom_call_target="tpu_custom_call", output_to_operand_aliasing={{}: (2, {})} | custom-call | tf_op jit(solution)/shard_map/add/pallas_call | solution.py:597
  (2 shorter events, 0.1 us)
Async XLA Ops:
  0.0 5.2 %copy-start.3 = (bf16[1,1,2,16,16,384]{5,4,3,2,1,0:T(8,128)(2,1)S(1)}, bf16[1,1,2,16,16,384]{5,4,3,2,1,0:T(8,128)(2,1)}, u32[]{:S(2)}) copy-start(bf16[1,1,2,16,16,384]{5,4,3,2,1,0:T(8,128)(2,1)} %param.8) | copy-start | bytes 1179652
  0.0 5.2 %copy-start.2 = (bf16[1,1,2,16,16,384]{5,4,3,2,1,0:T(8,128)(2,1)S(1)}, bf16[1,1,2,16,16,384]{5,4,3,2,1,0:T(8,128)(2,1)}, u32[]{:S(2)}) copy-start(bf16[1,1,2,16,16,384]{5,4,3,2,1,0:T(8,128)(2,1)} %param.7) | copy-start | bytes 1179652
  0.0 9.1 %copy-start.4 = (s32[3,2,2]{0,2,1:T(2,128)S(1)}, s32[3,2,2]{0,2,1:T(2,128)}, u32[]{:S(2)}) copy-start(s32[3,2,2]{0,2,1:T(2,128)} %param.11) | copy-start | bytes 148
  0.0 9.1 %copy-start.5 = (s32[3]{0:T(128)S(1)}, s32[3]{0:T(128)}, u32[]{:S(2)}) copy-start(s32[3]{0:T(128)} %radius_ref.1) | copy-start | bytes 40
  0.0 9.1 %copy-start.1 = (bf16[1,1,2,16,16,384]{5,4,3,2,1,0:T(8,128)(2,1)S(1)}, bf16[1,1,2,16,16,384]{5,4,3,2,1,0:T(8,128)(2,1)}, u32[]{:S(2)}) copy-start(bf16[1,1,2,16,16,384]{5,4,3,2,1,0:T(8,128)(2,1)} %param.6) | copy-start | bytes 1179652
  1.0 11.9 %collective-permute-start = (bf16[96,768]{1,0:T(8,128)(2,1)S(1)}, bf16[96,768]{1,0:T(8,128)(2,1)S(1)}, u32[]{:S(2)}, u32[]{:S(2)}) collective-permute-start(bf16[96,768]{1,0:T(8,128)(2,1)S(1)} %part.1.part_ref), channel_id=1, source_target_pairs={{0,2},{1,3},{2,0},{3,1},{4,6},{5,7},{6,4},{7,5},{8,10},{9,11},{10,... | collective-permute-start | bytes 442376 | tf_op jit(solution)/shard_map/ppermute | solution.py:470
  5.6 7.4 %collective-permute-start.3 = (bf16[2,2,16,384]{3,2,1,0:T(8,128)(2,1)S(1)}, bf16[2,2,16,384]{3,2,1,0:T(8,128)(2,1)S(1)}, u32[]{:S(2)}, u32[]{:S(2)}) collective-permute-start(bf16[2,2,16,384]{3,2,1,0:T(8,128)(2,1)S(1)} %get-tuple-element.69), channel_id=1, source_target_pairs={{0,12},{4,8},{8,4},{12,0},{1,13},{5,9},{9,5},{13,1},{2,14},{6,10},... | collective-permute-start | bytes 147464 | tf_op jit(solution)/shard_map/ppermute | solution.py:470
  8.1 6.6 %collective-permute-start.1 = (bf16[2,2,64,384]{3,2,1,0:T(8,128)(2,1)S(1)}, bf16[2,2,64,384]{3,2,1,0:T(8,128)(2,1)S(1)}, u32[]{:S(2)}, u32[]{:S(2)}) collective-permute-start(bf16[2,2,64,384]{3,2,1,0:T(8,128)(2,1)S(1)} %get-tuple-element.67), channel_id=1, source_target_pairs={{0,8},{4,12},{8,0},{12,4},{1,9},{5,13},{9,1},{13,5},{2,10},{6,14},... | collective-permute-start | bytes 589832 | tf_op jit(solution)/shard_map/ppermute | solution.py:470
  8.6 6.3 %collective-permute-start.2 = (bf16[2,2,64,384]{3,2,1,0:T(8,128)(2,1)S(1)}, bf16[2,2,64,384]{3,2,1,0:T(8,128)(2,1)S(1)}, u32[]{:S(2)}, u32[]{:S(2)}) collective-permute-start(bf16[2,2,64,384]{3,2,1,0:T(8,128)(2,1)S(1)} %get-tuple-element.68), channel_id=1, source_target_pairs={{0,4},{4,0},{8,12},{12,8},{1,5},{5,1},{9,13},{13,9},{2,6},{6,2},{1... | collective-permute-start | bytes 589832 | tf_op jit(solution)/shard_map/ppermute | solution.py:470
  10.5 9.3 %collective-permute-start.4 = (bf16[2,512,384]{2,1,0:T(8,128)(2,1)S(1)}, bf16[2,512,384]{2,1,0:T(8,128)(2,1)S(1)}, u32[]{:S(2)}, u32[]{:S(2)}) collective-permute-start(bf16[2,512,384]{2,1,0:T(8,128)(2,1)S(1)} %get-tuple-element.57.tile_ref), channel_id=1, source_target_pairs={{0,16},{1,17},{2,18},{3,19},{4,20},{5,21},{6,22},{7,23},{8,24},{9,... | collective-permute-start | bytes 2359304 | tf_op jit(solution)/shard_map/ppermute | solution.py:517
  14.9 4.9 %collective-permute-start.5 = (bf16[2,288,384]{2,1,0:T(8,128)(2,1)S(1)}, bf16[2,288,384]{2,1,0:T(8,128)(2,1)S(1)}, u32[]{:S(2)}, u32[]{:S(2)}) collective-permute-start(bf16[2,288,384]{2,1,0:T(8,128)(2,1)S(1)} %edges.1.edge_ref), channel_id=1, source_target_pairs={{0,16},{1,17},{2,18},{3,19},{4,20},{5,21},{6,22},{7,23},{8,24},{9,... | collective-permute-start | bytes 1327112 | tf_op jit(solution)/shard_map/ppermute | solution.py:535
  16.3 7.1 %collective-permute-start.8 = (bf16[96,768]{1,0:T(8,128)(2,1)S(1)}, bf16[96,768]{1,0:T(8,128)(2,1)S(1)}, u32[]{:S(2)}, u32[]{:S(2)}) collective-permute-start(bf16[96,768]{1,0:T(8,128)(2,1)S(1)} %lone.1.refs_0_), channel_id=1, source_target_pairs={{0,12},{4,8},{8,4},{12,0},{1,13},{5,9},{9,5},{13,1},{2,14},{6,10},... | collective-permute-start | bytes 442376 | tf_op jit(solution)/shard_map/ppermute | solution.py:470
  17.8 7.0 %collective-permute-start.7 = (bf16[96,768]{1,0:T(8,128)(2,1)S(1)}, bf16[96,768]{1,0:T(8,128)(2,1)S(1)}, u32[]{:S(2)}, u32[]{:S(2)}) collective-permute-start(bf16[96,768]{1,0:T(8,128)(2,1)S(1)} %lone.1.refs_0_), channel_id=1, source_target_pairs={{0,8},{4,12},{8,0},{12,4},{1,9},{5,13},{9,1},{13,5},{2,10},{6,14},... | collective-permute-start | bytes 442376 | tf_op jit(solution)/shard_map/ppermute | solution.py:470
  18.4 6.4 %collective-permute-start.6 = (bf16[96,768]{1,0:T(8,128)(2,1)S(1)}, bf16[96,768]{1,0:T(8,128)(2,1)S(1)}, u32[]{:S(2)}, u32[]{:S(2)}) collective-permute-start(bf16[96,768]{1,0:T(8,128)(2,1)S(1)} %lone.1.refs_0_), channel_id=1, source_target_pairs={{0,4},{4,0},{8,12},{12,8},{1,5},{5,1},{9,13},{13,9},{2,6},{6,2},{1... | collective-permute-start | bytes 442376 | tf_op jit(solution)/shard_map/ppermute | solution.py:470
  20.5 5.6 %collective-permute-start.9 = (bf16[128,384]{1,0:T(8,128)(2,1)S(1)}, bf16[128,384]{1,0:T(8,128)(2,1)S(1)}, u32[]{:S(2)}, u32[]{:S(2)}) collective-permute-start(bf16[128,384]{1,0:T(8,128)(2,1)S(1)} %rest.3), channel_id=1, source_target_pairs={{0,2},{1,3},{2,0},{3,1},{4,6},{5,7},{6,4},{7,5},{8,10},{9,11},{10,... | collective-permute-start | bytes 294920 | tf_op jit(solution)/shard_map/ppermute | solution.py:470
  22.0 4.0 %copy-start = (bf16[384,1536]{1,0:T(8,128)(2,1)S(1)}, bf16[384,1536]{1,0:T(8,128)(2,1)}, u32[]{:S(2)}) copy-start(bf16[384,1536]{1,0:T(8,128)(2,1)} %w_ref.9) | copy-start | bytes 3538948
  24.8 6.2 %collective-permute-start.11 = (bf16[128,384]{1,0:T(8,128)(2,1)S(1)}, bf16[128,384]{1,0:T(8,128)(2,1)S(1)}, u32[]{:S(2)}, u32[]{:S(2)}) collective-permute-start(bf16[128,384]{1,0:T(8,128)(2,1)S(1)} %get-tuple-element.96), channel_id=1, source_target_pairs={{0,2},{1,3},{2,0},{3,1},{4,6},{5,7},{6,4},{7,5},{8,10},{9,11},{10,... | collective-permute-start | bytes 294920 | tf_op jit(solution)/shard_map/ppermute | solution.py:470
  26.4 7.4 %collective-permute-start.13 = (bf16[128,768]{1,0:T(8,128)(2,1)S(1)}, bf16[128,768]{1,0:T(8,128)(2,1)S(1)}, u32[]{:S(2)}, u32[]{:S(2)}) collective-permute-start(bf16[128,768]{1,0:T(8,128)(2,1)S(1)} %project.4), channel_id=1, source_target_pairs={{0,1},{1,0},{2,3},{3,2},{4,5},{5,4},{6,7},{7,6},{8,9},{9,8},{10,11... | collective-permute-start | bytes 589832 | tf_op jit(solution)/shard_map/ppermute | solution.py:470
  28.1 2.0 %collective-permute-start.10 = (bf16[384,768]{1,0:T(8,128)(2,1)S(1)}, bf16[384,768]{1,0:T(8,128)(2,1)S(1)}, u32[]{:S(2)}, u32[]{:S(2)}) collective-permute-start(bf16[384,768]{1,0:T(8,128)(2,1)S(1)} %stack.1.part_ref), channel_id=1, source_target_pairs={{0,16},{16,0},{1,17},{17,1},{2,18},{18,2},{3,19},{19,3},{4,20},{20... | collective-permute-start | bytes 1769480 | tf_op jit(solution)/shard_map/ppermute | solution.py:470
  30.5 7.3 %collective-permute-start.12 = (bf16[128,768]{1,0:T(8,128)(2,1)S(1)}, bf16[128,768]{1,0:T(8,128)(2,1)S(1)}, u32[]{:S(2)}, u32[]{:S(2)}) collective-permute-start(bf16[128,768]{1,0:T(8,128)(2,1)S(1)} %project.5), channel_id=1, source_target_pairs={{0,1},{1,0},{2,3},{3,2},{4,5},{5,4},{6,7},{7,6},{8,9},{9,8},{10,11... | collective-permute-start | bytes 589832 | tf_op jit(solution)/shard_map/ppermute | solution.py:470

commit v12 on v11

--- a/solution.py
+++ b/solution.py
@@ -563,6 +563,8 @@
         stack_kernel, shape((depth, broad), bf16), [vmem] * tiles, *parts, name="stack"
     )
 
+    there = flipped(here, "tm", 1)
+
     def project(part, mine, got, kind, flip, flops=0):
         return call(
             project_kernel,
@@ -579,8 +581,7 @@
 
     for_side = [project(here, own_side, got_side, bf16, 0, 20 * 10**9)]
     from_side = [flipped(for_side[0], "head", 1)]
-    state, here, for_side[0] = lax.optimization_barrier((state, here, for_side[0]))
-    there = flipped(here, "tm", 1)
+    state, for_side[0] = lax.optimization_barrier((state, for_side[0]))
     (own,) = rest(state, 0, flops=20 * 10**9)
     own_side, own = lax.optimization_barrier((own_side, own))
     for_side.append(project(there, own_side, got_side, bf16, 1))

time: 38.7 us -> 39.8 us (1.028)
  starting transfers between devices: 16.7 us -> 17.3 us
  waiting for transfers between devices: 12.4 us -> 12.8 us
    ppermute x12, starting transfers between devices: 14 us -> 14.6 us  [flipped(): lax.ppermute(value, axis, [(i, i ^ flip) for i in range(lax.axis_size(axi...]
    ppermute x12, waiting for transfers between devices: 12.4 us -> 12.8 us  [flipped(): lax.ppermute(value, axis, [(i, i ^ flip) for i in range(lax.axis_size(axi...]
  transfers between devices with their start and end apart: 14 -> 14, of which waited for: 8 -> 8; matrix products, arithmetic and copies ran while one was open for 0% -> 0% of each run, Pallas kernels for 20% -> 19%
where the time goes in v12:
time: 39.8 us; the launch traced here: 39.6 us
  starting transfers between devices  17.3 us (43%)
  waiting for transfers between devices  12.8 us (32%)
  Pallas kernels  9.29 us (23%)
    ppermute x12, starting transfers between devices, flipped(): lax.ppermute(value, axis, [(i, i ^ flip) for i in range(lax.axis_size(axi...  14.6 us
    ppermute x12, waiting for transfers between devices, flipped(): lax.ppermute(value, axis, [(i, i ^ flip) for i in range(lax.axis_size(axi...  12.8 us
    pallas_call x14, Pallas kernels, call(): pl.pallas_call(functools.partial(kernel, **keys_of) if keys_of else kerne...  7.88 us
    pallas_call x2, Pallas kernels, two_by_two(): pl.pallas_call(functools.partial(add_kernel, flip=flip), out_shape=shape(...  1.42 us
    ppermute x1, starting transfers between devices, two_by_two(): first_tile = lax.ppermute(tile, 'tm', [(0, 1)])  1.34 us
    ppermute x1, starting transfers between devices, two_by_two(): first_edge = lax.ppermute(edge, 'tm', [(0, 1)])  1.32 us
  transfers between devices with their start and end apart: 14, of which 8 were waited for; matrix products, arithmetic and copies ran while one was open for 0% of the time, Pallas kernels for 19%

profile of v12, /device:TPU:0, one launch (start us, length us, event | category | flops | bytes accessed | tf_op | source)
XLA Modules:
  0.0 39.6 jit_solution(4607645892919332956)
XLA Ops:
  0.0 0.0 copy-start.3
  0.0 0.0 copy-start.2
  0.0 0.0 copy-start.4
  0.0 0.0 copy-start.5
  0.0 0.0 copy-start.1
  0.0 1.0 %part.1.part_ref = bf16[96,768]{1,0:T(8,128)(2,1)S(1)} custom-call(bf16[384,1536]{1,0:T(8,128)(2,1)} %w_ref.9), custom_call_target="tpu_custom_call" | custom-call | tf_op jit(solution)/shard_map/part/pallas_call | solution.py:458
  1.0 4.1 %collective-permute-start = (bf16[96,768]{1,0:T(8,128)(2,1)S(1)}, bf16[96,768]{1,0:T(8,128)(2,1)S(1)}, u32[]{:S(2)}, u32[]{:S(2)}) collective-permute-start(bf16[96,768]{1,0:T(8,128)(2,1)S(1)} %part.1.part_ref), channel_id=1, source_target_pairs={{0,2},{1,3},{2,0},{3,1},{4,6},{5,7},{6,4},{7,5},{8,10},{9,11},{10,... | collective-permute-start | bytes 442376 | tf_op jit(solution)/shard_map/ppermute | solution.py:470
  5.2 0.0 copy-done.3
  5.2 0.0 copy-done.2
  5.2 0.4 faces.1
  5.6 2.5 %collective-permute-start.3 = (bf16[2,2,16,384]{3,2,1,0:T(8,128)(2,1)S(1)}, bf16[2,2,16,384]{3,2,1,0:T(8,128)(2,1)S(1)}, u32[]{:S(2)}, u32[]{:S(2)}) collective-permute-start(bf16[2,2,16,384]{3,2,1,0:T(8,128)(2,1)S(1)} %get-tuple-element.68), channel_id=1, source_target_pairs={{0,12},{4,8},{8,4},{12,0},{1,13},{5,9},{9,5},{13,1},{2,14},{6,10},... | collective-permute-start | bytes 147464 | tf_op jit(solution)/shard_map/ppermute | solution.py:470
  8.1 0.5 %collective-permute-start.1 = (bf16[2,2,64,384]{3,2,1,0:T(8,128)(2,1)S(1)}, bf16[2,2,64,384]{3,2,1,0:T(8,128)(2,1)S(1)}, u32[]{:S(2)}, u32[]{:S(2)}) collective-permute-start(bf16[2,2,64,384]{3,2,1,0:T(8,128)(2,1)S(1)} %get-tuple-element.66), channel_id=1, source_target_pairs={{0,8},{4,12},{8,0},{12,4},{1,9},{5,13},{9,1},{13,5},{2,10},{6,14},... | collective-permute-start | bytes 589832 | tf_op jit(solution)/shard_map/ppermute | solution.py:470
  8.6 0.5 %collective-permute-start.2 = (bf16[2,2,64,384]{3,2,1,0:T(8,128)(2,1)S(1)}, bf16[2,2,64,384]{3,2,1,0:T(8,128)(2,1)S(1)}, u32[]{:S(2)}, u32[]{:S(2)}) collective-permute-start(bf16[2,2,64,384]{3,2,1,0:T(8,128)(2,1)S(1)} %get-tuple-element.67), channel_id=1, source_target_pairs={{0,4},{4,0},{8,12},{12,8},{1,5},{5,1},{9,13},{13,9},{2,6},{6,2},{1... | collective-permute-start | bytes 589832 | tf_op jit(solution)/shard_map/ppermute | solution.py:470
  9.1 0.0 copy-done.4
  9.1 0.0 copy-done.5
  9.1 0.0 copy-done.1
  9.1 1.4 %begin.1 = (f32[512,128]{1,0:T(8,128)S(1)}, f32[512,128]{1,0:T(8,128)S(1)}, f32[512,128]{1,0:T(8,128)S(1)}, s32[256,800]{1,0:T(8,128)S(1)}, s32[6,128]{1,0:T(8,128)S(1)}) custom-call(s32[3]{0:T(128)S(1)} %copy-done.5, s32[2,2,3]{2,1,0:T(2,128)S(1)} %bitcast.12, bf16[512,384]{1,0:T(8,128)(2,1)S(1)} %bitcast.5, bf16[2,512,384]{2,1,0:T(8,128)(2,1)S(1)} %get-tuple-element.56.tile_ref), custom_call_target="tpu_custom_call" | custom-call | tf_op jit(solution)/shard_map/begin/pallas_call | solution.py:458
  10.5 1.3 %collective-permute-start.7 = (bf16[2,512,384]{2,1,0:T(8,128)(2,1)S(1)}, bf16[2,512,384]{2,1,0:T(8,128)(2,1)S(1)}, u32[]{:S(2)}, u32[]{:S(2)}) collective-permute-start(bf16[2,512,384]{2,1,0:T(8,128)(2,1)S(1)} %get-tuple-element.56.tile_ref), channel_id=1, source_target_pairs={{0,16},{1,17},{2,18},{3,19},{4,20},{5,21},{6,22},{7,23},{8,24},{9,... | collective-permute-start | bytes 2359304 | tf_op jit(solution)/shard_map/ppermute | solution.py:517
  11.8 1.1 %tile.1 = (f32[512,256]{1,0:T(8,128)S(1)}, f32[512,256]{1,0:T(8,128)S(1)}, f32[512,256]{1,0:T(8,128)S(1)}) custom-call(bf16[512,384]{1,0:T(8,128)(2,1)S(1)} %bitcast.6, bf16[2,512,384]{2,1,0:T(8,128)(2,1)S(1)} %get-tuple-element.56.tile_ref, s32[256,800]{1,0:T(8,128)S(1)} %get-tuple-element.57.dist_ref.rest_3_, s32[6,128]{1,0:T(8,128)S(1)} %get-tuple-element.58.reach_ref.rest_4_), custom_call_target="tpu_custom_call" | custom-call | tf_op jit(solution)/shard_map/tile/pallas_call | solution.py:458
  12.9 0.0 collective-permute-done.in_ref
  13.0 0.0 collective-permute-done.3.corner_ref
  13.0 1.7 %collective-permute-done.1.row_ref = bf16[2,2,64,384]{3,2,1,0:T(8,128)(2,1)S(1)} collective-permute-done((bf16[2,2,64,384]{3,2,1,0:T(8,128)(2,1)S(1)}, bf16[2,2,64,384]{3,2,1,0:T(8,128)(2,1)S(1)}, u32[]{:S(2)}, u32[]{:S(2)}) %collective-permute-start.1) | collective-permute-done | bytes 196640 | tf_op jit(solution)/shard_map/ppermute | solution.py:470
  14.7 0.2 collective-permute-done.2.col_ref
  14.9 1.3 %collective-permute-start.8 = (bf16[2,288,384]{2,1,0:T(8,128)(2,1)S(1)}, bf16[2,288,384]{2,1,0:T(8,128)(2,1)S(1)}, u32[]{:S(2)}, u32[]{:S(2)}) collective-permute-start(bf16[2,288,384]{2,1,0:T(8,128)(2,1)S(1)} %edges.1.edge_ref), channel_id=1, source_target_pairs={{0,16},{1,17},{2,18},{3,19},{4,20},{5,21},{6,22},{7,23},{8,24},{9,... | collective-permute-start | bytes 1327112 | tf_op jit(solution)/shard_map/ppermute | solution.py:535
  16.3 1.5 %collective-permute-start.6 = (bf16[96,768]{1,0:T(8,128)(2,1)S(1)}, bf16[96,768]{1,0:T(8,128)(2,1)S(1)}, u32[]{:S(2)}, u32[]{:S(2)}) collective-permute-start(bf16[96,768]{1,0:T(8,128)(2,1)S(1)} %lone.1.refs_0_), channel_id=1, source_target_pairs={{0,12},{4,8},{8,4},{12,0},{1,13},{5,9},{9,5},{13,1},{2,14},{6,10},... | collective-permute-start | bytes 442376 | tf_op jit(solution)/shard_map/ppermute | solution.py:470
  17.8 0.6 %collective-permute-start.5 = (bf16[96,768]{1,0:T(8,128)(2,1)S(1)}, bf16[96,768]{1,0:T(8,128)(2,1)S(1)}, u32[]{:S(2)}, u32[]{:S(2)}) collective-permute-start(bf16[96,768]{1,0:T(8,128)(2,1)S(1)} %lone.1.refs_0_), channel_id=1, source_target_pairs={{0,8},{4,12},{8,0},{12,4},{1,9},{5,13},{9,1},{13,5},{2,10},{6,14},... | collective-permute-start | bytes 442376 | tf_op jit(solution)/shard_map/ppermute | solution.py:470
  18.4 1.4 %collective-permute-start.4 = (bf16[96,768]{1,0:T(8,128)(2,1)S(1)}, bf16[96,768]{1,0:T(8,128)(2,1)S(1)}, u32[]{:S(2)}, u32[]{:S(2)}) collective-permute-start(bf16[96,768]{1,0:T(8,128)(2,1)S(1)} %lone.1.refs_0_), channel_id=1, source_target_pairs={{0,4},{4,0},{8,12},{12,8},{1,5},{5,1},{9,13},{13,9},{2,6},{6,2},{1... | collective-permute-start | bytes 442376 | tf_op jit(solution)/shard_map/ppermute | solution.py:470
  19.8 0.0 collective-permute-done.8.first_edge_ref
  19.8 0.0 collective-permute-done.7.first_tile_ref
  19.8 0.7 %rest.3 = bf16[128,384]{1,0:T(8,128)(2,1)S(1)} custom-call(bf16[512,384]{1,0:T(8,128)(2,1)S(1)} %bitcast.7, bf16[2,288,384]{2,1,0:T(8,128)(2,1)S(1)} %edges.1.edge_ref, bf16[2,512,384]{2,1,0:T(8,128)(2,1)S(1)} %collective-permute-done.7.first_tile_ref, bf16[2,288,384]{2,1,0:T(8,128)(2,1)S(1)} %collective-permute-done.8.first_edge_ref, ...), custom_call_target="tpu_custom_call" | custom-call | tf_op jit(solution)/shard_map/rest/pallas_call | solution.py:458
  20.5 0.4 %collective-permute-start.10 = (bf16[128,384]{1,0:T(8,128)(2,1)S(1)}, bf16[128,384]{1,0:T(8,128)(2,1)S(1)}, u32[]{:S(2)}, u32[]{:S(2)}) collective-permute-start(bf16[128,384]{1,0:T(8,128)(2,1)S(1)} %rest.3), channel_id=1, source_target_pairs={{0,2},{1,3},{2,0},{3,1},{4,6},{5,7},{6,4},{7,5},{8,10},{9,11},{10,... | collective-permute-start | bytes 294920 | tf_op jit(solution)/shard_map/ppermute | solution.py:470
  20.9 1.2 %rest.4 = (bf16[128,384]{1,0:T(8,128)(2,1)S(1)}, bf16[128,384]{1,0:T(8,128)(2,1)S(1)}) custom-call(bf16[512,384]{1,0:T(8,128)(2,1)S(1)} %bitcast.8, bf16[2,288,384]{2,1,0:T(8,128)(2,1)S(1)} %edges.1.edge_ref, bf16[2,512,384]{2,1,0:T(8,128)(2,1)S(1)} %collective-permute-done.7.first_tile_ref, bf16[2,288,384]{2,1,0:T(8,128)(2,1)S(1)} %collective-permute-done.8.first_edge_ref, ...), custom_call_target="tpu_custom_call" | custom-call | tf_op jit(solution)/shard_map/rest/pallas_call | solution.py:458
  22.0 0.0 copy-start
  22.1 1.3 %collective-permute-done.6.refs_3_ = bf16[96,768]{1,0:T(8,128)(2,1)S(1)} collective-permute-done((bf16[96,768]{1,0:T(8,128)(2,1)S(1)}, bf16[96,768]{1,0:T(8,128)(2,1)S(1)}, u32[]{:S(2)}, u32[]{:S(2)}) %collective-permute-start.6) | collective-permute-done | bytes 147488 | tf_op jit(solution)/shard_map/ppermute | solution.py:470
  23.3 1.5 %collective-permute-done.5.refs_2_ = bf16[96,768]{1,0:T(8,128)(2,1)S(1)} collective-permute-done((bf16[96,768]{1,0:T(8,128)(2,1)S(1)}, bf16[96,768]{1,0:T(8,128)(2,1)S(1)}, u32[]{:S(2)}, u32[]{:S(2)}) %collective-permute-start.5) | collective-permute-done | bytes 147488 | tf_op jit(solution)/shard_map/ppermute | solution.py:470
  24.8 0.0 collective-permute-done.4.refs_1_
  24.8 0.2 collective-permute-start.11
  25.0 0.1 stack.1.part_ref
  25.1 0.1 collective-permute-start.9
  25.2 0.9 %collective-permute-done.10.got_ref = bf16[128,384]{1,0:T(8,128)(2,1)S(1)} collective-permute-done((bf16[128,384]{1,0:T(8,128)(2,1)S(1)}, bf16[128,384]{1,0:T(8,128)(2,1)S(1)}, u32[]{:S(2)}, u32[]{:S(2)}) %collective-permute-start.10) | collective-permute-done | bytes 98336 | tf_op jit(solution)/shard_map/ppermute | solution.py:470
  26.1 0.0 copy-done
  26.1 0.4 project.4
  26.4 1.8 %collective-permute-start.13 = (bf16[128,768]{1,0:T(8,128)(2,1)S(1)}, bf16[128,768]{1,0:T(8,128)(2,1)S(1)}, u32[]{:S(2)}, u32[]{:S(2)}) collective-permute-start(bf16[128,768]{1,0:T(8,128)(2,1)S(1)} %project.4), channel_id=1, source_target_pairs={{0,1},{1,0},{2,3},{3,2},{4,5},{5,4},{6,7},{7,6},{8,9},{9,8},{10,11... | collective-permute-start | bytes 589832 | tf_op jit(solution)/shard_map/ppermute | solution.py:470
  28.2 0.7 %rest.5.own_ref = bf16[128,384]{1,0:T(8,128)(2,1)S(1)} custom-call(bf16[512,384]{1,0:T(8,128)(2,1)S(1)} %bitcast.9, bf16[2,288,384]{2,1,0:T(8,128)(2,1)S(1)} %edges.1.edge_ref, bf16[2,512,384]{2,1,0:T(8,128)(2,1)S(1)} %collective-permute-done.7.first_tile_ref, bf16[2,288,384]{2,1,0:T(8,128)(2,1)S(1)} %collective-permute-done.8.first_edge_ref, ...), custom_call_target="tpu_custom_call" | custom-call | flops 20000000000 | tf_op jit(solution)/shard_map/rest/pallas_call | solution.py:458
  28.9 0.0 collective-permute-done.9.part_ref
  28.9 0.4 project.5
  29.2 0.9 %collective-permute-start.12 = (bf16[128,768]{1,0:T(8,128)(2,1)S(1)}, bf16[128,768]{1,0:T(8,128)(2,1)S(1)}, u32[]{:S(2)}, u32[]{:S(2)}) collective-permute-start(bf16[128,768]{1,0:T(8,128)(2,1)S(1)} %project.5), channel_id=1, source_target_pairs={{0,1},{1,0},{2,3},{3,2},{4,5},{5,4},{6,7},{7,6},{8,9},{9,8},{10,11... | collective-permute-start | bytes 589832 | tf_op jit(solution)/shard_map/ppermute | solution.py:470
  30.2 0.9 %collective-permute-done.11.got_ref = bf16[128,384]{1,0:T(8,128)(2,1)S(1)} collective-permute-done((bf16[128,384]{1,0:T(8,128)(2,1)S(1)}, bf16[128,384]{1,0:T(8,128)(2,1)S(1)}, u32[]{:S(2)}, u32[]{:S(2)}) %collective-permute-start.11) | collective-permute-done | bytes 98336 | tf_op jit(solution)/shard_map/ppermute | solution.py:470
  31.1 0.4 project.6.mine_ref
  31.5 0.4 project.7.mine_ref
  31.8 2.9 %collective-permute-done.13.got_ref = bf16[128,768]{1,0:T(8,128)(2,1)S(1)} collective-permute-done((bf16[128,768]{1,0:T(8,128)(2,1)S(1)}, bf16[128,768]{1,0:T(8,128)(2,1)S(1)}, u32[]{:S(2)}, u32[]{:S(2)}) %collective-permute-start.13) | collective-permute-done | bytes 196640 | tf_op jit(solution)/shard_map/ppermute | solution.py:470
  34.7 0.7 %add.2.rest_0_ = bf16[128,1536]{1,0:T(8,128)(2,1)} custom-call(f32[128,768]{1,0:T(8,128)S(1)} %project.7.mine_ref, bf16[128,768]{1,0:T(8,128)(2,1)S(1)} %collective-permute-done.13.got_ref), custom_call_target="tpu_custom_call" | custom-call | tf_op jit(solution)/shard_map/add/pallas_call | solution.py:598
  35.4 3.5 %collective-permute-done.12.got_ref = bf16[128,768]{1,0:T(8,128)(2,1)S(1)} collective-permute-done((bf16[128,768]{1,0:T(8,128)(2,1)S(1)}, bf16[128,768]{1,0:T(8,128)(2,1)S(1)}, u32[]{:S(2)}, u32[]{:S(2)}) %collective-permute-start.12) | collective-permute-done | bytes 196640 | tf_op jit(solution)/shard_map/ppermute | solution.py:470
  38.9 0.7 %add.3 = bf16[128,1536]{1,0:T(8,128)(2,1)} custom-call(f32[128,768]{1,0:T(8,128)S(1)} %project.6.mine_ref, bf16[128,768]{1,0:T(8,128)(2,1)S(1)} %collective-permute-done.12.got_ref, bf16[128,1536]{1,0:T(8,128)(2,1)} %add.2.rest_0_), custom_call_target="tpu_custom_call", output_to_operand_aliasing={{}: (2, {})} | custom-call | tf_op jit(solution)/shard_map/add/pallas_call | solution.py:598
  (2 shorter events, 0.1 us)
Async XLA Ops:
  0.0 5.2 %copy-start.3 = (bf16[1,1,2,16,16,384]{5,4,3,2,1,0:T(8,128)(2,1)S(1)}, bf16[1,1,2,16,16,384]{5,4,3,2,1,0:T(8,128)(2,1)}, u32[]{:S(2)}) copy-start(bf16[1,1,2,16,16,384]{5,4,3,2,1,0:T(8,128)(2,1)} %param.8) | copy-start | bytes 1179652
  0.0 5.2 %copy-start.2 = (bf16[1,1,2,16,16,384]{5,4,3,2,1,0:T(8,128)(2,1)S(1)}, bf16[1,1,2,16,16,384]{5,4,3,2,1,0:T(8,128)(2,1)}, u32[]{:S(2)}) copy-start(bf16[1,1,2,16,16,384]{5,4,3,2,1,0:T(8,128)(2,1)} %param.7) | copy-start | bytes 1179652
  0.0 9.1 %copy-start.4 = (s32[3,2,2]{0,2,1:T(2,128)S(1)}, s32[3,2,2]{0,2,1:T(2,128)}, u32[]{:S(2)}) copy-start(s32[3,2,2]{0,2,1:T(2,128)} %param.11) | copy-start | bytes 148
  0.0 9.1 %copy-start.5 = (s32[3]{0:T(128)S(1)}, s32[3]{0:T(128)}, u32[]{:S(2)}) copy-start(s32[3]{0:T(128)} %radius_ref.1) | copy-start | bytes 40
  0.0 9.1 %copy-start.1 = (bf16[1,1,2,16,16,384]{5,4,3,2,1,0:T(8,128)(2,1)S(1)}, bf16[1,1,2,16,16,384]{5,4,3,2,1,0:T(8,128)(2,1)}, u32[]{:S(2)}) copy-start(bf16[1,1,2,16,16,384]{5,4,3,2,1,0:T(8,128)(2,1)} %param.6) | copy-start | bytes 1179652
  1.0 11.9 %collective-permute-start = (bf16[96,768]{1,0:T(8,128)(2,1)S(1)}, bf16[96,768]{1,0:T(8,128)(2,1)S(1)}, u32[]{:S(2)}, u32[]{:S(2)}) collective-permute-start(bf16[96,768]{1,0:T(8,128)(2,1)S(1)} %part.1.part_ref), channel_id=1, source_target_pairs={{0,2},{1,3},{2,0},{3,1},{4,6},{5,7},{6,4},{7,5},{8,10},{9,11},{10,... | collective-permute-start | bytes 442376 | tf_op jit(solution)/shard_map/ppermute | solution.py:470
  5.6 7.4 %collective-permute-start.3 = (bf16[2,2,16,384]{3,2,1,0:T(8,128)(2,1)S(1)}, bf16[2,2,16,384]{3,2,1,0:T(8,128)(2,1)S(1)}, u32[]{:S(2)}, u32[]{:S(2)}) collective-permute-start(bf16[2,2,16,384]{3,2,1,0:T(8,128)(2,1)S(1)} %get-tuple-element.68), channel_id=1, source_target_pairs={{0,12},{4,8},{8,4},{12,0},{1,13},{5,9},{9,5},{13,1},{2,14},{6,10},... | collective-permute-start | bytes 147464 | tf_op jit(solution)/shard_map/ppermute | solution.py:470
  8.1 6.6 %collective-permute-start.1 = (bf16[2,2,64,384]{3,2,1,0:T(8,128)(2,1)S(1)}, bf16[2,2,64,384]{3,2,1,0:T(8,128)(2,1)S(1)}, u32[]{:S(2)}, u32[]{:S(2)}) collective-permute-start(bf16[2,2,64,384]{3,2,1,0:T(8,128)(2,1)S(1)} %get-tuple-element.66), channel_id=1, source_target_pairs={{0,8},{4,12},{8,0},{12,4},{1,9},{5,13},{9,1},{13,5},{2,10},{6,14},... | collective-permute-start | bytes 589832 | tf_op jit(solution)/shard_map/ppermute | solution.py:470
  8.6 6.3 %collective-permute-start.2 = (bf16[2,2,64,384]{3,2,1,0:T(8,128)(2,1)S(1)}, bf16[2,2,64,384]{3,2,1,0:T(8,128)(2,1)S(1)}, u32[]{:S(2)}, u32[]{:S(2)}) collective-permute-start(bf16[2,2,64,384]{3,2,1,0:T(8,128)(2,1)S(1)} %get-tuple-element.67), channel_id=1, source_target_pairs={{0,4},{4,0},{8,12},{12,8},{1,5},{5,1},{9,13},{13,9},{2,6},{6,2},{1... | collective-permute-start | bytes 589832 | tf_op jit(solution)/shard_map/ppermute | solution.py:470
  10.5 9.3 %collective-permute-start.7 = (bf16[2,512,384]{2,1,0:T(8,128)(2,1)S(1)}, bf16[2,512,384]{2,1,0:T(8,128)(2,1)S(1)}, u32[]{:S(2)}, u32[]{:S(2)}) collective-permute-start(bf16[2,512,384]{2,1,0:T(8,128)(2,1)S(1)} %get-tuple-element.56.tile_ref), channel_id=1, source_target_pairs={{0,16},{1,17},{2,18},{3,19},{4,20},{5,21},{6,22},{7,23},{8,24},{9,... | collective-permute-start | bytes 2359304 | tf_op jit(solution)/shard_map/ppermute | solution.py:517
  14.9 4.9 %collective-permute-start.8 = (bf16[2,288,384]{2,1,0:T(8,128)(2,1)S(1)}, bf16[2,288,384]{2,1,0:T(8,128)(2,1)S(1)}, u32[]{:S(2)}, u32[]{:S(2)}) collective-permute-start(bf16[2,288,384]{2,1,0:T(8,128)(2,1)S(1)} %edges.1.edge_ref), channel_id=1, source_target_pairs={{0,16},{1,17},{2,18},{3,19},{4,20},{5,21},{6,22},{7,23},{8,24},{9,... | collective-permute-start | bytes 1327112 | tf_op jit(solution)/shard_map/ppermute | solution.py:535
  16.3 7.1 %collective-permute-start.6 = (bf16[96,768]{1,0:T(8,128)(2,1)S(1)}, bf16[96,768]{1,0:T(8,128)(2,1)S(1)}, u32[]{:S(2)}, u32[]{:S(2)}) collective-permute-start(bf16[96,768]{1,0:T(8,128)(2,1)S(1)} %lone.1.refs_0_), channel_id=1, source_target_pairs={{0,12},{4,8},{8,4},{12,0},{1,13},{5,9},{9,5},{13,1},{2,14},{6,10},... | collective-permute-start | bytes 442376 | tf_op jit(solution)/shard_map/ppermute | solution.py:470
  17.8 7.0 %collective-permute-start.5 = (bf16[96,768]{1,0:T(8,128)(2,1)S(1)}, bf16[96,768]{1,0:T(8,128)(2,1)S(1)}, u32[]{:S(2)}, u32[]{:S(2)}) collective-permute-start(bf16[96,768]{1,0:T(8,128)(2,1)S(1)} %lone.1.refs_0_), channel_id=1, source_target_pairs={{0,8},{4,12},{8,0},{12,4},{1,9},{5,13},{9,1},{13,5},{2,10},{6,14},... | collective-permute-start | bytes 442376 | tf_op jit(solution)/shard_map/ppermute | solution.py:470
  18.4 6.4 %collective-permute-start.4 = (bf16[96,768]{1,0:T(8,128)(2,1)S(1)}, bf16[96,768]{1,0:T(8,128)(2,1)S(1)}, u32[]{:S(2)}, u32[]{:S(2)}) collective-permute-start(bf16[96,768]{1,0:T(8,128)(2,1)S(1)} %lone.1.refs_0_), channel_id=1, source_target_pairs={{0,4},{4,0},{8,12},{12,8},{1,5},{5,1},{9,13},{13,9},{2,6},{6,2},{1... | collective-permute-start | bytes 442376 | tf_op jit(solution)/shard_map/ppermute | solution.py:470
  20.5 5.6 %collective-permute-start.10 = (bf16[128,384]{1,0:T(8,128)(2,1)S(1)}, bf16[128,384]{1,0:T(8,128)(2,1)S(1)}, u32[]{:S(2)}, u32[]{:S(2)}) collective-permute-start(bf16[128,384]{1,0:T(8,128)(2,1)S(1)} %rest.3), channel_id=1, source_target_pairs={{0,2},{1,3},{2,0},{3,1},{4,6},{5,7},{6,4},{7,5},{8,10},{9,11},{10,... | collective-permute-start | bytes 294920 | tf_op jit(solution)/shard_map/ppermute | solution.py:470
  22.0 4.0 %copy-start = (bf16[384,1536]{1,0:T(8,128)(2,1)S(1)}, bf16[384,1536]{1,0:T(8,128)(2,1)}, u32[]{:S(2)}) copy-start(bf16[384,1536]{1,0:T(8,128)(2,1)} %w_ref.9) | copy-start | bytes 3538948
  24.8 6.3 %collective-permute-start.11 = (bf16[128,384]{1,0:T(8,128)(2,1)S(1)}, bf16[128,384]{1,0:T(8,128)(2,1)S(1)}, u32[]{:S(2)}, u32[]{:S(2)}) collective-permute-start(bf16[128,384]{1,0:T(8,128)(2,1)S(1)} %get-tuple-element.94), channel_id=1, source_target_pairs={{0,2},{1,3},{2,0},{3,1},{4,6},{5,7},{6,4},{7,5},{8,10},{9,11},{10,... | collective-permute-start | bytes 294920 | tf_op jit(solution)/shard_map/ppermute | solution.py:470
  25.1 3.8 %collective-permute-start.9 = (bf16[384,768]{1,0:T(8,128)(2,1)S(1)}, bf16[384,768]{1,0:T(8,128)(2,1)S(1)}, u32[]{:S(2)}, u32[]{:S(2)}) collective-permute-start(bf16[384,768]{1,0:T(8,128)(2,1)S(1)} %stack.1.part_ref), channel_id=1, source_target_pairs={{0,16},{16,0},{1,17},{17,1},{2,18},{18,2},{3,19},{19,3},{4,20},{20... | collective-permute-start | bytes 1769480 | tf_op jit(solution)/shard_map/ppermute | solution.py:470
  26.4 8.3 %collective-permute-start.13 = (bf16[128,768]{1,0:T(8,128)(2,1)S(1)}, bf16[128,768]{1,0:T(8,128)(2,1)S(1)}, u32[]{:S(2)}, u32[]{:S(2)}) collective-permute-start(bf16[128,768]{1,0:T(8,128)(2,1)S(1)} %project.4), channel_id=1, source_target_pairs={{0,1},{1,0},{2,3},{3,2},{4,5},{5,4},{6,7},{7,6},{8,9},{9,8},{10,11... | collective-permute-start | bytes 589832 | tf_op jit(solution)/shard_map/ppermute | solution.py:470
  29.2 9.6 %collective-permute-start.12 = (bf16[128,768]{1,0:T(8,128)(2,1)S(1)}, bf16[128,768]{1,0:T(8,128)(2,1)S(1)}, u32[]{:S(2)}, u32[]{:S(2)}) collective-permute-start(bf16[128,768]{1,0:T(8,128)(2,1)S(1)} %project.5), channel_id=1, source_target_pairs={{0,1},{1,0},{2,3},{3,2},{4,5},{5,4},{6,7},{7,6},{8,9},{9,8},{10,11... | collective-permute-start | bytes 589832 | tf_op jit(solution)/shard_map/ppermute | solution.py:470

commit v13 on v11

--- a/solution.py
+++ b/solution.py
@@ -558,7 +558,8 @@
     state, for_side = lax.optimization_barrier((state, for_side))
     for_far, own_side = rest(state, 2, 1)
     got_far = flipped(for_far, "head", 2)
-    parts, own_side = lax.optimization_barrier((parts, own_side))
+    parts, own_side = lax.optimization_barrier((parts[::-1], own_side))
+    parts = parts[::-1]
     here = call(
         stack_kernel, shape((depth, broad), bf16), [vmem] * tiles, *parts, name="stack"
     )

time: 38.7 us -> 39.9 us (1.031)
  waiting for transfers between devices: 12.4 us -> 13.4 us
    ppermute x12, waiting for transfers between devices: 12.4 us -> 13.4 us  [flipped(): lax.ppermute(value, axis, [(i, i ^ flip) for i in range(lax.axis_size(axi...]
  transfers between devices with their start and end apart: 14 -> 14, of which waited for: 8 -> 8; matrix products, arithmetic and copies ran while one was open for 0% -> 0% of each run, Pallas kernels for 20% -> 19%
where the time goes in v13:
time: 39.9 us; the launch traced here: 39.7 us
  starting transfers between devices  16.8 us (42%)
  waiting for transfers between devices  13.4 us (34%)
  Pallas kernels  9.32 us (23%)
    ppermute x12, starting transfers between devices, flipped(): lax.ppermute(value, axis, [(i, i ^ flip) for i in range(lax.axis_size(axi...  14.1 us
    ppermute x12, waiting for transfers between devices, flipped(): lax.ppermute(value, axis, [(i, i ^ flip) for i in range(lax.axis_size(axi...  13.4 us
    pallas_call x14, Pallas kernels, call(): pl.pallas_call(functools.partial(kernel, **keys_of) if keys_of else kerne...  7.9 us
    pallas_call x2, Pallas kernels, two_by_two(): pl.pallas_call(functools.partial(add_kernel, flip=flip), out_shape=shape(...  1.42 us
    ppermute x1, starting transfers between devices, two_by_two(): first_tile = lax.ppermute(tile, 'tm', [(0, 1)])  1.34 us
    ppermute x1, starting transfers between devices, two_by_two(): first_edge = lax.ppermute(edge, 'tm', [(0, 1)])  1.32 us
  transfers between devices with their start and end apart: 14, of which 8 were waited for; matrix products, arithmetic and copies ran while one was open for 0% of the time, Pallas kernels for 19%

profile of v13, /device:TPU:0, one launch (start us, length us, event | category | flops | bytes accessed | tf_op | source)
XLA Modules:
  0.0 39.7 jit_solution(15991131215294929023)
XLA Ops:
  0.0 0.0 copy-start.3
  0.0 0.0 copy-start.2
  0.0 0.0 copy-start.4
  0.0 0.0 copy-start.5
  0.0 0.0 copy-start.1
  0.0 1.0 %part.1.part_ref = bf16[96,768]{1,0:T(8,128)(2,1)S(1)} custom-call(bf16[384,1536]{1,0:T(8,128)(2,1)} %w_ref.9), custom_call_target="tpu_custom_call" | custom-call | tf_op jit(solution)/shard_map/part/pallas_call | solution.py:458
  1.0 4.1 %collective-permute-start = (bf16[96,768]{1,0:T(8,128)(2,1)S(1)}, bf16[96,768]{1,0:T(8,128)(2,1)S(1)}, u32[]{:S(2)}, u32[]{:S(2)}) collective-permute-start(bf16[96,768]{1,0:T(8,128)(2,1)S(1)} %part.1.part_ref), channel_id=1, source_target_pairs={{0,2},{1,3},{2,0},{3,1},{4,6},{5,7},{6,4},{7,5},{8,10},{9,11},{10,... | collective-permute-start | bytes 442376 | tf_op jit(solution)/shard_map/ppermute | solution.py:470
  5.2 0.0 copy-done.3
  5.2 0.0 copy-done.2
  5.2 0.4 faces.1
  5.6 2.5 %collective-permute-start.3 = (bf16[2,2,16,384]{3,2,1,0:T(8,128)(2,1)S(1)}, bf16[2,2,16,384]{3,2,1,0:T(8,128)(2,1)S(1)}, u32[]{:S(2)}, u32[]{:S(2)}) collective-permute-start(bf16[2,2,16,384]{3,2,1,0:T(8,128)(2,1)S(1)} %get-tuple-element.69), channel_id=1, source_target_pairs={{0,12},{4,8},{8,4},{12,0},{1,13},{5,9},{9,5},{13,1},{2,14},{6,10},... | collective-permute-start | bytes 147464 | tf_op jit(solution)/shard_map/ppermute | solution.py:470
  8.1 0.5 %collective-permute-start.1 = (bf16[2,2,64,384]{3,2,1,0:T(8,128)(2,1)S(1)}, bf16[2,2,64,384]{3,2,1,0:T(8,128)(2,1)S(1)}, u32[]{:S(2)}, u32[]{:S(2)}) collective-permute-start(bf16[2,2,64,384]{3,2,1,0:T(8,128)(2,1)S(1)} %get-tuple-element.67), channel_id=1, source_target_pairs={{0,8},{4,12},{8,0},{12,4},{1,9},{5,13},{9,1},{13,5},{2,10},{6,14},... | collective-permute-start | bytes 589832 | tf_op jit(solution)/shard_map/ppermute | solution.py:470
  8.6 0.5 %collective-permute-start.2 = (bf16[2,2,64,384]{3,2,1,0:T(8,128)(2,1)S(1)}, bf16[2,2,64,384]{3,2,1,0:T(8,128)(2,1)S(1)}, u32[]{:S(2)}, u32[]{:S(2)}) collective-permute-start(bf16[2,2,64,384]{3,2,1,0:T(8,128)(2,1)S(1)} %get-tuple-element.68), channel_id=1, source_target_pairs={{0,4},{4,0},{8,12},{12,8},{1,5},{5,1},{9,13},{13,9},{2,6},{6,2},{1... | collective-permute-start | bytes 589832 | tf_op jit(solution)/shard_map/ppermute | solution.py:470
  9.1 0.0 copy-done.4
  9.1 0.0 copy-done.5
  9.1 0.0 copy-done.1
  9.1 1.4 %begin.1 = (f32[512,128]{1,0:T(8,128)S(1)}, f32[512,128]{1,0:T(8,128)S(1)}, f32[512,128]{1,0:T(8,128)S(1)}, s32[256,800]{1,0:T(8,128)S(1)}, s32[6,128]{1,0:T(8,128)S(1)}) custom-call(s32[3]{0:T(128)S(1)} %copy-done.5, s32[2,2,3]{2,1,0:T(2,128)S(1)} %bitcast.12, bf16[512,384]{1,0:T(8,128)(2,1)S(1)} %bitcast.5, bf16[2,512,384]{2,1,0:T(8,128)(2,1)S(1)} %get-tuple-element.57.tile_ref), custom_call_target="tpu_custom_call" | custom-call | tf_op jit(solution)/shard_map/begin/pallas_call | solution.py:458
  10.5 1.3 %collective-permute-start.4 = (bf16[2,512,384]{2,1,0:T(8,128)(2,1)S(1)}, bf16[2,512,384]{2,1,0:T(8,128)(2,1)S(1)}, u32[]{:S(2)}, u32[]{:S(2)}) collective-permute-start(bf16[2,512,384]{2,1,0:T(8,128)(2,1)S(1)} %get-tuple-element.57.tile_ref), channel_id=1, source_target_pairs={{0,16},{1,17},{2,18},{3,19},{4,20},{5,21},{6,22},{7,23},{8,24},{9,... | collective-permute-start | bytes 2359304 | tf_op jit(solution)/shard_map/ppermute | solution.py:517
  11.8 1.1 %tile.1 = (f32[512,256]{1,0:T(8,128)S(1)}, f32[512,256]{1,0:T(8,128)S(1)}, f32[512,256]{1,0:T(8,128)S(1)}) custom-call(bf16[512,384]{1,0:T(8,128)(2,1)S(1)} %bitcast.6, bf16[2,512,384]{2,1,0:T(8,128)(2,1)S(1)} %get-tuple-element.57.tile_ref, s32[256,800]{1,0:T(8,128)S(1)} %get-tuple-element.58.dist_ref.rest_3_, s32[6,128]{1,0:T(8,128)S(1)} %get-tuple-element.59.reach_ref.rest_4_), custom_call_target="tpu_custom_call" | custom-call | tf_op jit(solution)/shard_map/tile/pallas_call | solution.py:458
  12.9 0.0 collective-permute-done.in_ref
  13.0 0.0 collective-permute-done.3.corner_ref
  13.0 1.7 %collective-permute-done.1.row_ref = bf16[2,2,64,384]{3,2,1,0:T(8,128)(2,1)S(1)} collective-permute-done((bf16[2,2,64,384]{3,2,1,0:T(8,128)(2,1)S(1)}, bf16[2,2,64,384]{3,2,1,0:T(8,128)(2,1)S(1)}, u32[]{:S(2)}, u32[]{:S(2)}) %collective-permute-start.1) | collective-permute-done | bytes 196640 | tf_op jit(solution)/shard_map/ppermute | solution.py:470
  14.7 0.2 collective-permute-done.2.col_ref
  14.9 1.3 %collective-permute-start.5 = (bf16[2,288,384]{2,1,0:T(8,128)(2,1)S(1)}, bf16[2,288,384]{2,1,0:T(8,128)(2,1)S(1)}, u32[]{:S(2)}, u32[]{:S(2)}) collective-permute-start(bf16[2,288,384]{2,1,0:T(8,128)(2,1)S(1)} %edges.1.edge_ref), channel_id=1, source_target_pairs={{0,16},{1,17},{2,18},{3,19},{4,20},{5,21},{6,22},{7,23},{8,24},{9,... | collective-permute-start | bytes 1327112 | tf_op jit(solution)/shard_map/ppermute | solution.py:535
  16.3 0.7 %collective-permute-start.8 = (bf16[96,768]{1,0:T(8,128)(2,1)S(1)}, bf16[96,768]{1,0:T(8,128)(2,1)S(1)}, u32[]{:S(2)}, u32[]{:S(2)}) collective-permute-start(bf16[96,768]{1,0:T(8,128)(2,1)S(1)} %lone.1.refs_0_), channel_id=1, source_target_pairs={{0,4},{4,0},{8,12},{12,8},{1,5},{5,1},{9,13},{13,9},{2,6},{6,2},{1... | collective-permute-start | bytes 442376 | tf_op jit(solution)/shard_map/ppermute | solution.py:470
  16.9 1.4 %collective-permute-start.7 = (bf16[96,768]{1,0:T(8,128)(2,1)S(1)}, bf16[96,768]{1,0:T(8,128)(2,1)S(1)}, u32[]{:S(2)}, u32[]{:S(2)}) collective-permute-start(bf16[96,768]{1,0:T(8,128)(2,1)S(1)} %lone.1.refs_0_), channel_id=1, source_target_pairs={{0,8},{4,12},{8,0},{12,4},{1,9},{5,13},{9,1},{13,5},{2,10},{6,14},... | collective-permute-start | bytes 442376 | tf_op jit(solution)/shard_map/ppermute | solution.py:470
  18.3 1.5 %collective-permute-start.6 = (bf16[96,768]{1,0:T(8,128)(2,1)S(1)}, bf16[96,768]{1,0:T(8,128)(2,1)S(1)}, u32[]{:S(2)}, u32[]{:S(2)}) collective-permute-start(bf16[96,768]{1,0:T(8,128)(2,1)S(1)} %lone.1.refs_0_), channel_id=1, source_target_pairs={{0,12},{4,8},{8,4},{12,0},{1,13},{5,9},{9,5},{13,1},{2,14},{6,10},... | collective-permute-start | bytes 442376 | tf_op jit(solution)/shard_map/ppermute | solution.py:470
  19.8 0.0 collective-permute-done.5.first_edge_ref
  19.8 0.0 collective-permute-done.4.first_tile_ref
  19.8 0.7 %rest.3 = bf16[128,384]{1,0:T(8,128)(2,1)S(1)} custom-call(bf16[512,384]{1,0:T(8,128)(2,1)S(1)} %bitcast.7, bf16[2,288,384]{2,1,0:T(8,128)(2,1)S(1)} %edges.1.edge_ref, bf16[2,512,384]{2,1,0:T(8,128)(2,1)S(1)} %collective-permute-done.4.first_tile_ref, bf16[2,288,384]{2,1,0:T(8,128)(2,1)S(1)} %collective-permute-done.5.first_edge_ref, ...), custom_call_target="tpu_custom_call" | custom-call | tf_op jit(solution)/shard_map/rest/pallas_call | solution.py:458
  20.5 0.4 %collective-permute-start.9 = (bf16[128,384]{1,0:T(8,128)(2,1)S(1)}, bf16[128,384]{1,0:T(8,128)(2,1)S(1)}, u32[]{:S(2)}, u32[]{:S(2)}) collective-permute-start(bf16[128,384]{1,0:T(8,128)(2,1)S(1)} %rest.3), channel_id=1, source_target_pairs={{0,2},{1,3},{2,0},{3,1},{4,6},{5,7},{6,4},{7,5},{8,10},{9,11},{10,... | collective-permute-start | bytes 294920 | tf_op jit(solution)/shard_map/ppermute | solution.py:470
  20.9 1.2 %rest.4 = (bf16[128,384]{1,0:T(8,128)(2,1)S(1)}, bf16[128,384]{1,0:T(8,128)(2,1)S(1)}) custom-call(bf16[512,384]{1,0:T(8,128)(2,1)S(1)} %bitcast.8, bf16[2,288,384]{2,1,0:T(8,128)(2,1)S(1)} %edges.1.edge_ref, bf16[2,512,384]{2,1,0:T(8,128)(2,1)S(1)} %collective-permute-done.4.first_tile_ref, bf16[2,288,384]{2,1,0:T(8,128)(2,1)S(1)} %collective-permute-done.5.first_edge_ref, ...), custom_call_target="tpu_custom_call" | custom-call | tf_op jit(solution)/shard_map/rest/pallas_call | solution.py:458
  22.0 0.0 copy-start
  22.1 0.3 collective-permute-done.8.refs_1_
  22.4 2.2 %collective-permute-done.7.refs_2_ = bf16[96,768]{1,0:T(8,128)(2,1)S(1)} collective-permute-done((bf16[96,768]{1,0:T(8,128)(2,1)S(1)}, bf16[96,768]{1,0:T(8,128)(2,1)S(1)}, u32[]{:S(2)}, u32[]{:S(2)}) %collective-permute-start.7) | collective-permute-done | bytes 147488 | tf_op jit(solution)/shard_map/ppermute | solution.py:470
  24.6 0.0 collective-permute-done.6.refs_3_
  24.6 0.4 collective-permute-start.11
  24.9 0.1 stack.1.part_ref
  25.0 3.7 %collective-permute-done.9.got_ref = bf16[128,384]{1,0:T(8,128)(2,1)S(1)} collective-permute-done((bf16[128,384]{1,0:T(8,128)(2,1)S(1)}, bf16[128,384]{1,0:T(8,128)(2,1)S(1)}, u32[]{:S(2)}, u32[]{:S(2)}) %collective-permute-start.9) | collective-permute-done | bytes 98336 | tf_op jit(solution)/shard_map/ppermute | solution.py:470
  28.7 0.0 copy-done
  28.7 0.4 project.4
  29.1 0.1 collective-permute-start.13
  29.1 0.1 collective-permute-start.10
  29.2 0.7 %rest.5.own_ref = bf16[128,384]{1,0:T(8,128)(2,1)S(1)} custom-call(bf16[512,384]{1,0:T(8,128)(2,1)S(1)} %bitcast.9, bf16[2,288,384]{2,1,0:T(8,128)(2,1)S(1)} %edges.1.edge_ref, bf16[2,512,384]{2,1,0:T(8,128)(2,1)S(1)} %collective-permute-done.4.first_tile_ref, bf16[2,288,384]{2,1,0:T(8,128)(2,1)S(1)} %collective-permute-done.5.first_edge_ref, ...), custom_call_target="tpu_custom_call" | custom-call | flops 20000000000 | tf_op jit(solution)/shard_map/rest/pallas_call | solution.py:458
  29.9 1.3 %collective-permute-done.10.part_ref = bf16[384,768]{1,0:T(8,128)(2,1)S(1)} collective-permute-done((bf16[384,768]{1,0:T(8,128)(2,1)S(1)}, bf16[384,768]{1,0:T(8,128)(2,1)S(1)}, u32[]{:S(2)}, u32[]{:S(2)}) %collective-permute-start.10) | collective-permute-done | bytes 589856 | tf_op jit(solution)/shard_map/ppermute | solution.py:470
  31.2 0.4 project.5
  31.6 2.0 %collective-permute-start.12 = (bf16[128,768]{1,0:T(8,128)(2,1)S(1)}, bf16[128,768]{1,0:T(8,128)(2,1)S(1)}, u32[]{:S(2)}, u32[]{:S(2)}) collective-permute-start(bf16[128,768]{1,0:T(8,128)(2,1)S(1)} %project.5), channel_id=1, source_target_pairs={{0,1},{1,0},{2,3},{3,2},{4,5},{5,4},{6,7},{7,6},{8,9},{9,8},{10,11... | collective-permute-start | bytes 589832 | tf_op jit(solution)/shard_map/ppermute | solution.py:470
  33.6 0.0 collective-permute-done.11.got_ref
  33.6 0.4 project.6.mine_ref
  34.0 0.4 project.7.mine_ref
  34.3 0.6 %collective-permute-done.13.got_ref = bf16[128,768]{1,0:T(8,128)(2,1)S(1)} collective-permute-done((bf16[128,768]{1,0:T(8,128)(2,1)S(1)}, bf16[128,768]{1,0:T(8,128)(2,1)S(1)}, u32[]{:S(2)}, u32[]{:S(2)}) %collective-permute-start.13) | collective-permute-done | bytes 196640 | tf_op jit(solution)/shard_map/ppermute | solution.py:470
  34.9 0.7 %add.2.rest_0_ = bf16[128,1536]{1,0:T(8,128)(2,1)} custom-call(f32[128,768]{1,0:T(8,128)S(1)} %project.7.mine_ref, bf16[128,768]{1,0:T(8,128)(2,1)S(1)} %collective-permute-done.13.got_ref), custom_call_target="tpu_custom_call" | custom-call | tf_op jit(solution)/shard_map/add/pallas_call | solution.py:598
  35.7 3.3 %collective-permute-done.12.got_ref = bf16[128,768]{1,0:T(8,128)(2,1)S(1)} collective-permute-done((bf16[128,768]{1,0:T(8,128)(2,1)S(1)}, bf16[128,768]{1,0:T(8,128)(2,1)S(1)}, u32[]{:S(2)}, u32[]{:S(2)}) %collective-permute-start.12) | collective-permute-done | bytes 196640 | tf_op jit(solution)/shard_map/ppermute | solution.py:470
  39.0 0.7 %add.3 = bf16[128,1536]{1,0:T(8,128)(2,1)} custom-call(f32[128,768]{1,0:T(8,128)S(1)} %project.6.mine_ref, bf16[128,768]{1,0:T(8,128)(2,1)S(1)} %collective-permute-done.12.got_ref, bf16[128,1536]{1,0:T(8,128)(2,1)} %add.2.rest_0_), custom_call_target="tpu_custom_call", output_to_operand_aliasing={{}: (2, {})} | custom-call | tf_op jit(solution)/shard_map/add/pallas_call | solution.py:598
  (2 shorter events, 0.1 us)
Async XLA Ops:
  0.0 5.2 %copy-start.3 = (bf16[1,1,2,16,16,384]{5,4,3,2,1,0:T(8,128)(2,1)S(1)}, bf16[1,1,2,16,16,384]{5,4,3,2,1,0:T(8,128)(2,1)}, u32[]{:S(2)}) copy-start(bf16[1,1,2,16,16,384]{5,4,3,2,1,0:T(8,128)(2,1)} %param.8) | copy-start | bytes 1179652
  0.0 5.2 %copy-start.2 = (bf16[1,1,2,16,16,384]{5,4,3,2,1,0:T(8,128)(2,1)S(1)}, bf16[1,1,2,16,16,384]{5,4,3,2,1,0:T(8,128)(2,1)}, u32[]{:S(2)}) copy-start(bf16[1,1,2,16,16,384]{5,4,3,2,1,0:T(8,128)(2,1)} %param.7) | copy-start | bytes 1179652
  0.0 9.1 %copy-start.4 = (s32[3,2,2]{0,2,1:T(2,128)S(1)}, s32[3,2,2]{0,2,1:T(2,128)}, u32[]{:S(2)}) copy-start(s32[3,2,2]{0,2,1:T(2,128)} %param.11) | copy-start | bytes 148
  0.0 9.1 %copy-start.5 = (s32[3]{0:T(128)S(1)}, s32[3]{0:T(128)}, u32[]{:S(2)}) copy-start(s32[3]{0:T(128)} %radius_ref.1) | copy-start | bytes 40
  0.0 9.1 %copy-start.1 = (bf16[1,1,2,16,16,384]{5,4,3,2,1,0:T(8,128)(2,1)S(1)}, bf16[1,1,2,16,16,384]{5,4,3,2,1,0:T(8,128)(2,1)}, u32[]{:S(2)}) copy-start(bf16[1,1,2,16,16,384]{5,4,3,2,1,0:T(8,128)(2,1)} %param.6) | copy-start | bytes 1179652
  1.0 11.9 %collective-permute-start = (bf16[96,768]{1,0:T(8,128)(2,1)S(1)}, bf16[96,768]{1,0:T(8,128)(2,1)S(1)}, u32[]{:S(2)}, u32[]{:S(2)}) collective-permute-start(bf16[96,768]{1,0:T(8,128)(2,1)S(1)} %part.1.part_ref), channel_id=1, source_target_pairs={{0,2},{1,3},{2,0},{3,1},{4,6},{5,7},{6,4},{7,5},{8,10},{9,11},{10,... | collective-permute-start | bytes 442376 | tf_op jit(solution)/shard_map/ppermute | solution.py:470
  5.6 7.4 %collective-permute-start.3 = (bf16[2,2,16,384]{3,2,1,0:T(8,128)(2,1)S(1)}, bf16[2,2,16,384]{3,2,1,0:T(8,128)(2,1)S(1)}, u32[]{:S(2)}, u32[]{:S(2)}) collective-permute-start(bf16[2,2,16,384]{3,2,1,0:T(8,128)(2,1)S(1)} %get-tuple-element.69), channel_id=1, source_target_pairs={{0,12},{4,8},{8,4},{12,0},{1,13},{5,9},{9,5},{13,1},{2,14},{6,10},... | collective-permute-start | bytes 147464 | tf_op jit(solution)/shard_map/ppermute | solution.py:470
  8.1 6.6 %collective-permute-start.1 = (bf16[2,2,64,384]{3,2,1,0:T(8,128)(2,1)S(1)}, bf16[2,2,64,384]{3,2,1,0:T(8,128)(2,1)S(1)}, u32[]{:S(2)}, u32[]{:S(2)}) collective-permute-start(bf16[2,2,64,384]{3,2,1,0:T(8,128)(2,1)S(1)} %get-tuple-element.67), channel_id=1, source_target_pairs={{0,8},{4,12},{8,0},{12,4},{1,9},{5,13},{9,1},{13,5},{2,10},{6,14},... | collective-permute-start | bytes 589832 | tf_op jit(solution)/shard_map/ppermute | solution.py:470
  8.6 6.3 %collective-permute-start.2 = (bf16[2,2,64,384]{3,2,1,0:T(8,128)(2,1)S(1)}, bf16[2,2,64,384]{3,2,1,0:T(8,128)(2,1)S(1)}, u32[]{:S(2)}, u32[]{:S(2)}) collective-permute-start(bf16[2,2,64,384]{3,2,1,0:T(8,128)(2,1)S(1)} %get-tuple-element.68), channel_id=1, source_target_pairs={{0,4},{4,0},{8,12},{12,8},{1,5},{5,1},{9,13},{13,9},{2,6},{6,2},{1... | collective-permute-start | bytes 589832 | tf_op jit(solution)/shard_map/ppermute | solution.py:470
  10.5 9.3 %collective-permute-start.4 = (bf16[2,512,384]{2,1,0:T(8,128)(2,1)S(1)}, bf16[2,512,384]{2,1,0:T(8,128)(2,1)S(1)}, u32[]{:S(2)}, u32[]{:S(2)}) collective-permute-start(bf16[2,512,384]{2,1,0:T(8,128)(2,1)S(1)} %get-tuple-element.57.tile_ref), channel_id=1, source_target_pairs={{0,16},{1,17},{2,18},{3,19},{4,20},{5,21},{6,22},{7,23},{8,24},{9,... | collective-permute-start | bytes 2359304 | tf_op jit(solution)/shard_map/ppermute | solution.py:517
  14.9 4.9 %collective-permute-start.5 = (bf16[2,288,384]{2,1,0:T(8,128)(2,1)S(1)}, bf16[2,288,384]{2,1,0:T(8,128)(2,1)S(1)}, u32[]{:S(2)}, u32[]{:S(2)}) collective-permute-start(bf16[2,288,384]{2,1,0:T(8,128)(2,1)S(1)} %edges.1.edge_ref), channel_id=1, source_target_pairs={{0,16},{1,17},{2,18},{3,19},{4,20},{5,21},{6,22},{7,23},{8,24},{9,... | collective-permute-start | bytes 1327112 | tf_op jit(solution)/shard_map/ppermute | solution.py:535
  16.3 6.1 %collective-permute-start.8 = (bf16[96,768]{1,0:T(8,128)(2,1)S(1)}, bf16[96,768]{1,0:T(8,128)(2,1)S(1)}, u32[]{:S(2)}, u32[]{:S(2)}) collective-permute-start(bf16[96,768]{1,0:T(8,128)(2,1)S(1)} %lone.1.refs_0_), channel_id=1, source_target_pairs={{0,4},{4,0},{8,12},{12,8},{1,5},{5,1},{9,13},{13,9},{2,6},{6,2},{1... | collective-permute-start | bytes 442376 | tf_op jit(solution)/shard_map/ppermute | solution.py:470
  16.9 7.7 %collective-permute-start.7 = (bf16[96,768]{1,0:T(8,128)(2,1)S(1)}, bf16[96,768]{1,0:T(8,128)(2,1)S(1)}, u32[]{:S(2)}, u32[]{:S(2)}) collective-permute-start(bf16[96,768]{1,0:T(8,128)(2,1)S(1)} %lone.1.refs_0_), channel_id=1, source_target_pairs={{0,8},{4,12},{8,0},{12,4},{1,9},{5,13},{9,1},{13,5},{2,10},{6,14},... | collective-permute-start | bytes 442376 | tf_op jit(solution)/shard_map/ppermute | solution.py:470
  18.3 6.3 %collective-permute-start.6 = (bf16[96,768]{1,0:T(8,128)(2,1)S(1)}, bf16[96,768]{1,0:T(8,128)(2,1)S(1)}, u32[]{:S(2)}, u32[]{:S(2)}) collective-permute-start(bf16[96,768]{1,0:T(8,128)(2,1)S(1)} %lone.1.refs_0_), channel_id=1, source_target_pairs={{0,12},{4,8},{8,4},{12,0},{1,13},{5,9},{9,5},{13,1},{2,14},{6,10},... | collective-permute-start | bytes 442376 | tf_op jit(solution)/shard_map/ppermute | solution.py:470
  20.5 8.2 %collective-permute-start.9 = (bf16[128,384]{1,0:T(8,128)(2,1)S(1)}, bf16[128,384]{1,0:T(8,128)(2,1)S(1)}, u32[]{:S(2)}, u32[]{:S(2)}) collective-permute-start(bf16[128,384]{1,0:T(8,128)(2,1)S(1)} %rest.3), channel_id=1, source_target_pairs={{0,2},{1,3},{2,0},{3,1},{4,6},{5,7},{6,4},{7,5},{8,10},{9,11},{10,... | collective-permute-start | bytes 294920 | tf_op jit(solution)/shard_map/ppermute | solution.py:470
  22.0 6.7 %copy-start = (bf16[384,1536]{1,0:T(8,128)(2,1)S(1)}, bf16[384,1536]{1,0:T(8,128)(2,1)}, u32[]{:S(2)}) copy-start(bf16[384,1536]{1,0:T(8,128)(2,1)} %w_ref.9) | copy-start | bytes 3538948
  24.6 9.0 %collective-permute-start.11 = (bf16[128,384]{1,0:T(8,128)(2,1)S(1)}, bf16[128,384]{1,0:T(8,128)(2,1)S(1)}, u32[]{:S(2)}, u32[]{:S(2)}) collective-permute-start(bf16[128,384]{1,0:T(8,128)(2,1)S(1)} %get-tuple-element.96), channel_id=1, source_target_pairs={{0,2},{1,3},{2,0},{3,1},{4,6},{5,7},{6,4},{7,5},{8,10},{9,11},{10,... | collective-permute-start | bytes 294920 | tf_op jit(solution)/shard_map/ppermute | solution.py:470
  29.1 5.9 %collective-permute-start.13 = (bf16[128,768]{1,0:T(8,128)(2,1)S(1)}, bf16[128,768]{1,0:T(8,128)(2,1)S(1)}, u32[]{:S(2)}, u32[]{:S(2)}) collective-permute-start(bf16[128,768]{1,0:T(8,128)(2,1)S(1)} %project.4), channel_id=1, source_target_pairs={{0,1},{1,0},{2,3},{3,2},{4,5},{5,4},{6,7},{7,6},{8,9},{9,8},{10,11... | collective-permute-start | bytes 589832 | tf_op jit(solution)/shard_map/ppermute | solution.py:470
  29.1 2.1 %collective-permute-start.10 = (bf16[384,768]{1,0:T(8,128)(2,1)S(1)}, bf16[384,768]{1,0:T(8,128)(2,1)S(1)}, u32[]{:S(2)}, u32[]{:S(2)}) collective-permute-start(bf16[384,768]{1,0:T(8,128)(2,1)S(1)} %stack.1.part_ref), channel_id=1, source_target_pairs={{0,16},{16,0},{1,17},{17,1},{2,18},{18,2},{3,19},{19,3},{4,20},{20... | collective-permute-start | bytes 1769480 | tf_op jit(solution)/shard_map/ppermute | solution.py:470
  31.6 7.4 %collective-permute-start.12 = (bf16[128,768]{1,0:T(8,128)(2,1)S(1)}, bf16[128,768]{1,0:T(8,128)(2,1)S(1)}, u32[]{:S(2)}, u32[]{:S(2)}) collective-permute-start(bf16[128,768]{1,0:T(8,128)(2,1)S(1)} %project.5), channel_id=1, source_target_pairs={{0,1},{1,0},{2,3},{3,2},{4,5},{5,4},{6,7},{7,6},{8,9},{9,8},{10,11... | collective-permute-start | bytes 589832 | tf_op jit(solution)/shard_map/ppermute | solution.py:470

commit v14 on v11

--- a/solution.py
+++ b/solution.py
@@ -558,7 +558,9 @@
     state, for_side = lax.optimization_barrier((state, for_side))
     for_far, own_side = rest(state, 2, 1)
     got_far = flipped(for_far, "head", 2)
-    parts, own_side = lax.optimization_barrier((parts, own_side))
+    order = [0, 2, 1, 3]
+    parts, own_side = lax.optimization_barrier(([parts[i] for i in order], own_side))
+    parts = [parts[i] for i in order]
     here = call(
         stack_kernel, shape((depth, broad), bf16), [vmem] * tiles, *parts, name="stack"
     )

time: 38.7 us -> 38.9 us (level)
  transfers between devices with their start and end apart: 14 -> 14, of which waited for: 8 -> 9; matrix products, arithmetic and copies ran while one was open for 0% -> 0% of each run, Pallas kernels for 20% -> 19%
where the time goes in v14:
time: 38.9 us; the launch traced here: 38.8 us
  starting transfers between devices  16.7 us (43%)
  waiting for transfers between devices  12.6 us (32%)
  Pallas kernels  9.29 us (24%)
    ppermute x12, starting transfers between devices, flipped(): lax.ppermute(value, axis, [(i, i ^ flip) for i in range(lax.axis_size(axi...  14 us
    ppermute x12, waiting for transfers between devices, flipped(): lax.ppermute(value, axis, [(i, i ^ flip) for i in range(lax.axis_size(axi...  12.6 us
    pallas_call x14, Pallas kernels, call(): pl.pallas_call(functools.partial(kernel, **keys_of) if keys_of else kerne...  7.88 us
    pallas_call x2, Pallas kernels, two_by_two(): pl.pallas_call(functools.partial(add_kernel, flip=flip), out_shape=shape(...  1.42 us
    ppermute x1, starting transfers between devices, two_by_two(): first_tile = lax.ppermute(tile, 'tm', [(0, 1)])  1.34 us
    ppermute x1, starting transfers between devices, two_by_two(): first_edge = lax.ppermute(edge, 'tm', [(0, 1)])  1.32 us
  transfers between devices with their start and end apart: 14, of which 9 were waited for; matrix products, arithmetic and copies ran while one was open for 0% of the time, Pallas kernels for 19%

profile of v14, /device:TPU:0, one launch (start us, length us, event | category | flops | bytes accessed | tf_op | source)
XLA Modules:
  0.0 38.8 jit_solution(9018138571497219573)
XLA Ops:
  0.0 0.0 copy-start.3
  0.0 0.0 copy-start.2
  0.0 0.0 copy-start.4
  0.0 0.0 copy-start.5
  0.0 0.0 copy-start.1
  0.0 1.0 %part.1.part_ref = bf16[96,768]{1,0:T(8,128)(2,1)S(1)} custom-call(bf16[384,1536]{1,0:T(8,128)(2,1)} %w_ref.9), custom_call_target="tpu_custom_call" | custom-call | tf_op jit(solution)/shard_map/part/pallas_call | solution.py:458
  1.0 4.1 %collective-permute-start = (bf16[96,768]{1,0:T(8,128)(2,1)S(1)}, bf16[96,768]{1,0:T(8,128)(2,1)S(1)}, u32[]{:S(2)}, u32[]{:S(2)}) collective-permute-start(bf16[96,768]{1,0:T(8,128)(2,1)S(1)} %part.1.part_ref), channel_id=1, source_target_pairs={{0,2},{1,3},{2,0},{3,1},{4,6},{5,7},{6,4},{7,5},{8,10},{9,11},{10,... | collective-permute-start | bytes 442376 | tf_op jit(solution)/shard_map/ppermute | solution.py:470
  5.2 0.0 copy-done.3
  5.2 0.0 copy-done.2
  5.2 0.4 %faces.1 = (bf16[2,2,64,384]{3,2,1,0:T(8,128)(2,1)S(1)}, bf16[2,2,64,384]{3,2,1,0:T(8,128)(2,1)S(1)}, bf16[2,2,16,384]{3,2,1,0:T(8,128)(2,1)S(1)}, bf16[2,512,384]{2,1,0:T(8,128)(2,1)S(1)}) custom-call(bf16[512,384]{1,0:T(8,128)(2,1)S(1)} %bitcast.10, bf16[512,384]{1,0:T(8,128)(2,1)S(1)} %bitcast.11, bf16[96,768]{1,0:T(8,128)(2,1)S(1)} %part.1.part_ref), custom_call_target="tpu_custom_call" | custom-call | tf_op jit(solution)/shard_map/faces/pallas_call | solution.py:458
  5.6 2.5 %collective-permute-start.3 = (bf16[2,2,16,384]{3,2,1,0:T(8,128)(2,1)S(1)}, bf16[2,2,16,384]{3,2,1,0:T(8,128)(2,1)S(1)}, u32[]{:S(2)}, u32[]{:S(2)}) collective-permute-start(bf16[2,2,16,384]{3,2,1,0:T(8,128)(2,1)S(1)} %get-tuple-element.69), channel_id=1, source_target_pairs={{0,12},{4,8},{8,4},{12,0},{1,13},{5,9},{9,5},{13,1},{2,14},{6,10},... | collective-permute-start | bytes 147464 | tf_op jit(solution)/shard_map/ppermute | solution.py:470
  8.1 0.5 %collective-permute-start.1 = (bf16[2,2,64,384]{3,2,1,0:T(8,128)(2,1)S(1)}, bf16[2,2,64,384]{3,2,1,0:T(8,128)(2,1)S(1)}, u32[]{:S(2)}, u32[]{:S(2)}) collective-permute-start(bf16[2,2,64,384]{3,2,1,0:T(8,128)(2,1)S(1)} %get-tuple-element.67), channel_id=1, source_target_pairs={{0,8},{4,12},{8,0},{12,4},{1,9},{5,13},{9,1},{13,5},{2,10},{6,14},... | collective-permute-start | bytes 589832 | tf_op jit(solution)/shard_map/ppermute | solution.py:470
  8.6 0.5 %collective-permute-start.2 = (bf16[2,2,64,384]{3,2,1,0:T(8,128)(2,1)S(1)}, bf16[2,2,64,384]{3,2,1,0:T(8,128)(2,1)S(1)}, u32[]{:S(2)}, u32[]{:S(2)}) collective-permute-start(bf16[2,2,64,384]{3,2,1,0:T(8,128)(2,1)S(1)} %get-tuple-element.68), channel_id=1, source_target_pairs={{0,4},{4,0},{8,12},{12,8},{1,5},{5,1},{9,13},{13,9},{2,6},{6,2},{1... | collective-permute-start | bytes 589832 | tf_op jit(solution)/shard_map/ppermute | solution.py:470
  9.1 0.0 copy-done.4
  9.1 0.0 copy-done.5
  9.1 0.0 copy-done.1
  9.1 1.4 %begin.1 = (f32[512,128]{1,0:T(8,128)S(1)}, f32[512,128]{1,0:T(8,128)S(1)}, f32[512,128]{1,0:T(8,128)S(1)}, s32[256,800]{1,0:T(8,128)S(1)}, s32[6,128]{1,0:T(8,128)S(1)}) custom-call(s32[3]{0:T(128)S(1)} %copy-done.5, s32[2,2,3]{2,1,0:T(2,128)S(1)} %bitcast.12, bf16[512,384]{1,0:T(8,128)(2,1)S(1)} %bitcast.5, bf16[2,512,384]{2,1,0:T(8,128)(2,1)S(1)} %get-tuple-element.57.tile_ref), custom_call_target="tpu_custom_call" | custom-call | tf_op jit(solution)/shard_map/begin/pallas_call | solution.py:458
  10.5 1.3 %collective-permute-start.4 = (bf16[2,512,384]{2,1,0:T(8,128)(2,1)S(1)}, bf16[2,512,384]{2,1,0:T(8,128)(2,1)S(1)}, u32[]{:S(2)}, u32[]{:S(2)}) collective-permute-start(bf16[2,512,384]{2,1,0:T(8,128)(2,1)S(1)} %get-tuple-element.57.tile_ref), channel_id=1, source_target_pairs={{0,16},{1,17},{2,18},{3,19},{4,20},{5,21},{6,22},{7,23},{8,24},{9,... | collective-permute-start | bytes 2359304 | tf_op jit(solution)/shard_map/ppermute | solution.py:517
  11.8 1.1 %tile.1 = (f32[512,256]{1,0:T(8,128)S(1)}, f32[512,256]{1,0:T(8,128)S(1)}, f32[512,256]{1,0:T(8,128)S(1)}) custom-call(bf16[512,384]{1,0:T(8,128)(2,1)S(1)} %bitcast.6, bf16[2,512,384]{2,1,0:T(8,128)(2,1)S(1)} %get-tuple-element.57.tile_ref, s32[256,800]{1,0:T(8,128)S(1)} %get-tuple-element.58.dist_ref.rest_3_, s32[6,128]{1,0:T(8,128)S(1)} %get-tuple-element.59.reach_ref.rest_4_), custom_call_target="tpu_custom_call" | custom-call | tf_op jit(solution)/shard_map/tile/pallas_call | solution.py:458
  12.9 0.0 collective-permute-done.in_ref
  13.0 0.0 collective-permute-done.3.corner_ref
  13.0 1.7 %collective-permute-done.1.row_ref = bf16[2,2,64,384]{3,2,1,0:T(8,128)(2,1)S(1)} collective-permute-done((bf16[2,2,64,384]{3,2,1,0:T(8,128)(2,1)S(1)}, bf16[2,2,64,384]{3,2,1,0:T(8,128)(2,1)S(1)}, u32[]{:S(2)}, u32[]{:S(2)}) %collective-permute-start.1) | collective-permute-done | bytes 196640 | tf_op jit(solution)/shard_map/ppermute | solution.py:470
  14.7 0.2 collective-permute-done.2.col_ref
  14.9 1.3 %collective-permute-start.5 = (bf16[2,288,384]{2,1,0:T(8,128)(2,1)S(1)}, bf16[2,288,384]{2,1,0:T(8,128)(2,1)S(1)}, u32[]{:S(2)}, u32[]{:S(2)}) collective-permute-start(bf16[2,288,384]{2,1,0:T(8,128)(2,1)S(1)} %edges.1.edge_ref), channel_id=1, source_target_pairs={{0,16},{1,17},{2,18},{3,19},{4,20},{5,21},{6,22},{7,23},{8,24},{9,... | collective-permute-start | bytes 1327112 | tf_op jit(solution)/shard_map/ppermute | solution.py:535
  16.3 1.5 %collective-permute-start.8 = (bf16[96,768]{1,0:T(8,128)(2,1)S(1)}, bf16[96,768]{1,0:T(8,128)(2,1)S(1)}, u32[]{:S(2)}, u32[]{:S(2)}) collective-permute-start(bf16[96,768]{1,0:T(8,128)(2,1)S(1)} %lone.1.refs_0_), channel_id=1, source_target_pairs={{0,12},{4,8},{8,4},{12,0},{1,13},{5,9},{9,5},{13,1},{2,14},{6,10},... | collective-permute-start | bytes 442376 | tf_op jit(solution)/shard_map/ppermute | solution.py:470
  17.8 1.0 %collective-permute-start.7 = (bf16[96,768]{1,0:T(8,128)(2,1)S(1)}, bf16[96,768]{1,0:T(8,128)(2,1)S(1)}, u32[]{:S(2)}, u32[]{:S(2)}) collective-permute-start(bf16[96,768]{1,0:T(8,128)(2,1)S(1)} %lone.1.refs_0_), channel_id=1, source_target_pairs={{0,4},{4,0},{8,12},{12,8},{1,5},{5,1},{9,13},{13,9},{2,6},{6,2},{1... | collective-permute-start | bytes 442376 | tf_op jit(solution)/shard_map/ppermute | solution.py:470
  18.8 1.0 %collective-permute-start.6 = (bf16[96,768]{1,0:T(8,128)(2,1)S(1)}, bf16[96,768]{1,0:T(8,128)(2,1)S(1)}, u32[]{:S(2)}, u32[]{:S(2)}) collective-permute-start(bf16[96,768]{1,0:T(8,128)(2,1)S(1)} %lone.1.refs_0_), channel_id=1, source_target_pairs={{0,8},{4,12},{8,0},{12,4},{1,9},{5,13},{9,1},{13,5},{2,10},{6,14},... | collective-permute-start | bytes 442376 | tf_op jit(solution)/shard_map/ppermute | solution.py:470
  19.8 0.0 collective-permute-done.5.first_edge_ref
  19.8 0.0 collective-permute-done.4.first_tile_ref
  19.8 0.7 %rest.3 = bf16[128,384]{1,0:T(8,128)(2,1)S(1)} custom-call(bf16[512,384]{1,0:T(8,128)(2,1)S(1)} %bitcast.7, bf16[2,288,384]{2,1,0:T(8,128)(2,1)S(1)} %edges.1.edge_ref, bf16[2,512,384]{2,1,0:T(8,128)(2,1)S(1)} %collective-permute-done.4.first_tile_ref, bf16[2,288,384]{2,1,0:T(8,128)(2,1)S(1)} %collective-permute-done.5.first_edge_ref, ...), custom_call_target="tpu_custom_call" | custom-call | tf_op jit(solution)/shard_map/rest/pallas_call | solution.py:458
  20.5 0.4 %collective-permute-start.9 = (bf16[128,384]{1,0:T(8,128)(2,1)S(1)}, bf16[128,384]{1,0:T(8,128)(2,1)S(1)}, u32[]{:S(2)}, u32[]{:S(2)}) collective-permute-start(bf16[128,384]{1,0:T(8,128)(2,1)S(1)} %rest.3), channel_id=1, source_target_pairs={{0,2},{1,3},{2,0},{3,1},{4,6},{5,7},{6,4},{7,5},{8,10},{9,11},{10,... | collective-permute-start | bytes 294920 | tf_op jit(solution)/shard_map/ppermute | solution.py:470
  20.9 1.2 %rest.4 = (bf16[128,384]{1,0:T(8,128)(2,1)S(1)}, bf16[128,384]{1,0:T(8,128)(2,1)S(1)}) custom-call(bf16[512,384]{1,0:T(8,128)(2,1)S(1)} %bitcast.8, bf16[2,288,384]{2,1,0:T(8,128)(2,1)S(1)} %edges.1.edge_ref, bf16[2,512,384]{2,1,0:T(8,128)(2,1)S(1)} %collective-permute-done.4.first_tile_ref, bf16[2,288,384]{2,1,0:T(8,128)(2,1)S(1)} %collective-permute-done.5.first_edge_ref, ...), custom_call_target="tpu_custom_call" | custom-call | tf_op jit(solution)/shard_map/rest/pallas_call | solution.py:458
  22.0 0.0 copy-start
  22.1 1.2 %collective-permute-done.8.refs_3_ = bf16[96,768]{1,0:T(8,128)(2,1)S(1)} collective-permute-done((bf16[96,768]{1,0:T(8,128)(2,1)S(1)}, bf16[96,768]{1,0:T(8,128)(2,1)S(1)}, u32[]{:S(2)}, u32[]{:S(2)}) %collective-permute-start.8) | collective-permute-done | bytes 147488 | tf_op jit(solution)/shard_map/ppermute | solution.py:470
  23.3 0.8 %collective-permute-done.7.refs_1_ = bf16[96,768]{1,0:T(8,128)(2,1)S(1)} collective-permute-done((bf16[96,768]{1,0:T(8,128)(2,1)S(1)}, bf16[96,768]{1,0:T(8,128)(2,1)S(1)}, u32[]{:S(2)}, u32[]{:S(2)}) %collective-permute-start.7) | collective-permute-done | bytes 147488 | tf_op jit(solution)/shard_map/ppermute | solution.py:470
  24.1 0.7 %collective-permute-done.6.refs_2_ = bf16[96,768]{1,0:T(8,128)(2,1)S(1)} collective-permute-done((bf16[96,768]{1,0:T(8,128)(2,1)S(1)}, bf16[96,768]{1,0:T(8,128)(2,1)S(1)}, u32[]{:S(2)}, u32[]{:S(2)}) %collective-permute-start.6) | collective-permute-done | bytes 147488 | tf_op jit(solution)/shard_map/ppermute | solution.py:470
  24.8 0.2 collective-permute-start.11
  25.0 0.1 stack.1.part_ref
  25.1 1.0 %collective-permute-done.9.got_ref = bf16[128,384]{1,0:T(8,128)(2,1)S(1)} collective-permute-done((bf16[128,384]{1,0:T(8,128)(2,1)S(1)}, bf16[128,384]{1,0:T(8,128)(2,1)S(1)}, u32[]{:S(2)}, u32[]{:S(2)}) %collective-permute-start.9) | collective-permute-done | bytes 98336 | tf_op jit(solution)/shard_map/ppermute | solution.py:470
  26.1 0.0 copy-done
  26.1 0.4 project.4
  26.5 1.8 %collective-permute-start.13 = (bf16[128,768]{1,0:T(8,128)(2,1)S(1)}, bf16[128,768]{1,0:T(8,128)(2,1)S(1)}, u32[]{:S(2)}, u32[]{:S(2)}) collective-permute-start(bf16[128,768]{1,0:T(8,128)(2,1)S(1)} %project.4), channel_id=1, source_target_pairs={{0,1},{1,0},{2,3},{3,2},{4,5},{5,4},{6,7},{7,6},{8,9},{9,8},{10,11... | collective-permute-start | bytes 589832 | tf_op jit(solution)/shard_map/ppermute | solution.py:470
  28.3 0.0 collective-permute-start.10
  28.3 0.7 %rest.5.own_ref = bf16[128,384]{1,0:T(8,128)(2,1)S(1)} custom-call(bf16[512,384]{1,0:T(8,128)(2,1)S(1)} %bitcast.9, bf16[2,288,384]{2,1,0:T(8,128)(2,1)S(1)} %edges.1.edge_ref, bf16[2,512,384]{2,1,0:T(8,128)(2,1)S(1)} %collective-permute-done.4.first_tile_ref, bf16[2,288,384]{2,1,0:T(8,128)(2,1)S(1)} %collective-permute-done.5.first_edge_ref, ...), custom_call_target="tpu_custom_call" | custom-call | flops 20000000000 | tf_op jit(solution)/shard_map/rest/pallas_call | solution.py:458
  28.9 1.3 %collective-permute-done.10.part_ref = bf16[384,768]{1,0:T(8,128)(2,1)S(1)} collective-permute-done((bf16[384,768]{1,0:T(8,128)(2,1)S(1)}, bf16[384,768]{1,0:T(8,128)(2,1)S(1)}, u32[]{:S(2)}, u32[]{:S(2)}) %collective-permute-start.10) | collective-permute-done | bytes 589856 | tf_op jit(solution)/shard_map/ppermute | solution.py:470
  30.3 0.4 project.5
  30.6 0.4 %collective-permute-start.12 = (bf16[128,768]{1,0:T(8,128)(2,1)S(1)}, bf16[128,768]{1,0:T(8,128)(2,1)S(1)}, u32[]{:S(2)}, u32[]{:S(2)}) collective-permute-start(bf16[128,768]{1,0:T(8,128)(2,1)S(1)} %project.5), channel_id=1, source_target_pairs={{0,1},{1,0},{2,3},{3,2},{4,5},{5,4},{6,7},{7,6},{8,9},{9,8},{10,11... | collective-permute-start | bytes 589832 | tf_op jit(solution)/shard_map/ppermute | solution.py:470
  31.0 0.0 collective-permute-done.11.got_ref
  31.0 0.4 project.6.mine_ref
  31.4 0.4 project.7.mine_ref
  31.8 2.4 %collective-permute-done.13.got_ref = bf16[128,768]{1,0:T(8,128)(2,1)S(1)} collective-permute-done((bf16[128,768]{1,0:T(8,128)(2,1)S(1)}, bf16[128,768]{1,0:T(8,128)(2,1)S(1)}, u32[]{:S(2)}, u32[]{:S(2)}) %collective-permute-start.13) | collective-permute-done | bytes 196640 | tf_op jit(solution)/shard_map/ppermute | solution.py:470
  34.2 0.7 %add.2.rest_0_ = bf16[128,1536]{1,0:T(8,128)(2,1)} custom-call(f32[128,768]{1,0:T(8,128)S(1)} %project.7.mine_ref, bf16[128,768]{1,0:T(8,128)(2,1)S(1)} %collective-permute-done.13.got_ref), custom_call_target="tpu_custom_call" | custom-call | tf_op jit(solution)/shard_map/add/pallas_call | solution.py:599
  34.9 3.2 %collective-permute-done.12.got_ref = bf16[128,768]{1,0:T(8,128)(2,1)S(1)} collective-permute-done((bf16[128,768]{1,0:T(8,128)(2,1)S(1)}, bf16[128,768]{1,0:T(8,128)(2,1)S(1)}, u32[]{:S(2)}, u32[]{:S(2)}) %collective-permute-start.12) | collective-permute-done | bytes 196640 | tf_op jit(solution)/shard_map/ppermute | solution.py:470
  38.1 0.7 %add.3 = bf16[128,1536]{1,0:T(8,128)(2,1)} custom-call(f32[128,768]{1,0:T(8,128)S(1)} %project.6.mine_ref, bf16[128,768]{1,0:T(8,128)(2,1)S(1)} %collective-permute-done.12.got_ref, bf16[128,1536]{1,0:T(8,128)(2,1)} %add.2.rest_0_), custom_call_target="tpu_custom_call", output_to_operand_aliasing={{}: (2, {})} | custom-call | tf_op jit(solution)/shard_map/add/pallas_call | solution.py:599
  (2 shorter events, 0.1 us)
Async XLA Ops:
  0.0 5.2 %copy-start.3 = (bf16[1,1,2,16,16,384]{5,4,3,2,1,0:T(8,128)(2,1)S(1)}, bf16[1,1,2,16,16,384]{5,4,3,2,1,0:T(8,128)(2,1)}, u32[]{:S(2)}) copy-start(bf16[1,1,2,16,16,384]{5,4,3,2,1,0:T(8,128)(2,1)} %param.8) | copy-start | bytes 1179652
  0.0 5.2 %copy-start.2 = (bf16[1,1,2,16,16,384]{5,4,3,2,1,0:T(8,128)(2,1)S(1)}, bf16[1,1,2,16,16,384]{5,4,3,2,1,0:T(8,128)(2,1)}, u32[]{:S(2)}) copy-start(bf16[1,1,2,16,16,384]{5,4,3,2,1,0:T(8,128)(2,1)} %param.7) | copy-start | bytes 1179652
  0.0 9.1 %copy-start.4 = (s32[3,2,2]{0,2,1:T(2,128)S(1)}, s32[3,2,2]{0,2,1:T(2,128)}, u32[]{:S(2)}) copy-start(s32[3,2,2]{0,2,1:T(2,128)} %param.11) | copy-start | bytes 148
  0.0 9.1 %copy-start.5 = (s32[3]{0:T(128)S(1)}, s32[3]{0:T(128)}, u32[]{:S(2)}) copy-start(s32[3]{0:T(128)} %radius_ref.1) | copy-start | bytes 40
  0.0 9.1 %copy-start.1 = (bf16[1,1,2,16,16,384]{5,4,3,2,1,0:T(8,128)(2,1)S(1)}, bf16[1,1,2,16,16,384]{5,4,3,2,1,0:T(8,128)(2,1)}, u32[]{:S(2)}) copy-start(bf16[1,1,2,16,16,384]{5,4,3,2,1,0:T(8,128)(2,1)} %param.6) | copy-start | bytes 1179652
  1.0 11.9 %collective-permute-start = (bf16[96,768]{1,0:T(8,128)(2,1)S(1)}, bf16[96,768]{1,0:T(8,128)(2,1)S(1)}, u32[]{:S(2)}, u32[]{:S(2)}) collective-permute-start(bf16[96,768]{1,0:T(8,128)(2,1)S(1)} %part.1.part_ref), channel_id=1, source_target_pairs={{0,2},{1,3},{2,0},{3,1},{4,6},{5,7},{6,4},{7,5},{8,10},{9,11},{10,... | collective-permute-start | bytes 442376 | tf_op jit(solution)/shard_map/ppermute | solution.py:470
  5.6 7.4 %collective-permute-start.3 = (bf16[2,2,16,384]{3,2,1,0:T(8,128)(2,1)S(1)}, bf16[2,2,16,384]{3,2,1,0:T(8,128)(2,1)S(1)}, u32[]{:S(2)}, u32[]{:S(2)}) collective-permute-start(bf16[2,2,16,384]{3,2,1,0:T(8,128)(2,1)S(1)} %get-tuple-element.69), channel_id=1, source_target_pairs={{0,12},{4,8},{8,4},{12,0},{1,13},{5,9},{9,5},{13,1},{2,14},{6,10},... | collective-permute-start | bytes 147464 | tf_op jit(solution)/shard_map/ppermute | solution.py:470
  8.1 6.6 %collective-permute-start.1 = (bf16[2,2,64,384]{3,2,1,0:T(8,128)(2,1)S(1)}, bf16[2,2,64,384]{3,2,1,0:T(8,128)(2,1)S(1)}, u32[]{:S(2)}, u32[]{:S(2)}) collective-permute-start(bf16[2,2,64,384]{3,2,1,0:T(8,128)(2,1)S(1)} %get-tuple-element.67), channel_id=1, source_target_pairs={{0,8},{4,12},{8,0},{12,4},{1,9},{5,13},{9,1},{13,5},{2,10},{6,14},... | collective-permute-start | bytes 589832 | tf_op jit(solution)/shard_map/ppermute | solution.py:470
  8.6 6.3 %collective-permute-start.2 = (bf16[2,2,64,384]{3,2,1,0:T(8,128)(2,1)S(1)}, bf16[2,2,64,384]{3,2,1,0:T(8,128)(2,1)S(1)}, u32[]{:S(2)}, u32[]{:S(2)}) collective-permute-start(bf16[2,2,64,384]{3,2,1,0:T(8,128)(2,1)S(1)} %get-tuple-element.68), channel_id=1, source_target_pairs={{0,4},{4,0},{8,12},{12,8},{1,5},{5,1},{9,13},{13,9},{2,6},{6,2},{1... | collective-permute-start | bytes 589832 | tf_op jit(solution)/shard_map/ppermute | solution.py:470
  10.5 9.3 %collective-permute-start.4 = (bf16[2,512,384]{2,1,0:T(8,128)(2,1)S(1)}, bf16[2,512,384]{2,1,0:T(8,128)(2,1)S(1)}, u32[]{:S(2)}, u32[]{:S(2)}) collective-permute-start(bf16[2,512,384]{2,1,0:T(8,128)(2,1)S(1)} %get-tuple-element.57.tile_ref), channel_id=1, source_target_pairs={{0,16},{1,17},{2,18},{3,19},{4,20},{5,21},{6,22},{7,23},{8,24},{9,... | collective-permute-start | bytes 2359304 | tf_op jit(solution)/shard_map/ppermute | solution.py:517
  14.9 4.9 %collective-permute-start.5 = (bf16[2,288,384]{2,1,0:T(8,128)(2,1)S(1)}, bf16[2,288,384]{2,1,0:T(8,128)(2,1)S(1)}, u32[]{:S(2)}, u32[]{:S(2)}) collective-permute-start(bf16[2,288,384]{2,1,0:T(8,128)(2,1)S(1)} %edges.1.edge_ref), channel_id=1, source_target_pairs={{0,16},{1,17},{2,18},{3,19},{4,20},{5,21},{6,22},{7,23},{8,24},{9,... | collective-permute-start | bytes 1327112 | tf_op jit(solution)/shard_map/ppermute | solution.py:535
  16.3 7.0 %collective-permute-start.8 = (bf16[96,768]{1,0:T(8,128)(2,1)S(1)}, bf16[96,768]{1,0:T(8,128)(2,1)S(1)}, u32[]{:S(2)}, u32[]{:S(2)}) collective-permute-start(bf16[96,768]{1,0:T(8,128)(2,1)S(1)} %lone.1.refs_0_), channel_id=1, source_target_pairs={{0,12},{4,8},{8,4},{12,0},{1,13},{5,9},{9,5},{13,1},{2,14},{6,10},... | collective-permute-start | bytes 442376 | tf_op jit(solution)/shard_map/ppermute | solution.py:470
  17.8 6.4 %collective-permute-start.7 = (bf16[96,768]{1,0:T(8,128)(2,1)S(1)}, bf16[96,768]{1,0:T(8,128)(2,1)S(1)}, u32[]{:S(2)}, u32[]{:S(2)}) collective-permute-start(bf16[96,768]{1,0:T(8,128)(2,1)S(1)} %lone.1.refs_0_), channel_id=1, source_target_pairs={{0,4},{4,0},{8,12},{12,8},{1,5},{5,1},{9,13},{13,9},{2,6},{6,2},{1... | collective-permute-start | bytes 442376 | tf_op jit(solution)/shard_map/ppermute | solution.py:470
  18.8 6.0 %collective-permute-start.6 = (bf16[96,768]{1,0:T(8,128)(2,1)S(1)}, bf16[96,768]{1,0:T(8,128)(2,1)S(1)}, u32[]{:S(2)}, u32[]{:S(2)}) collective-permute-start(bf16[96,768]{1,0:T(8,128)(2,1)S(1)} %lone.1.refs_0_), channel_id=1, source_target_pairs={{0,8},{4,12},{8,0},{12,4},{1,9},{5,13},{9,1},{13,5},{2,10},{6,14},... | collective-permute-start | bytes 442376 | tf_op jit(solution)/shard_map/ppermute | solution.py:470
  20.5 5.6 %collective-permute-start.9 = (bf16[128,384]{1,0:T(8,128)(2,1)S(1)}, bf16[128,384]{1,0:T(8,128)(2,1)S(1)}, u32[]{:S(2)}, u32[]{:S(2)}) collective-permute-start(bf16[128,384]{1,0:T(8,128)(2,1)S(1)} %rest.3), channel_id=1, source_target_pairs={{0,2},{1,3},{2,0},{3,1},{4,6},{5,7},{6,4},{7,5},{8,10},{9,11},{10,... | collective-permute-start | bytes 294920 | tf_op jit(solution)/shard_map/ppermute | solution.py:470
  22.0 4.1 %copy-start = (bf16[384,1536]{1,0:T(8,128)(2,1)S(1)}, bf16[384,1536]{1,0:T(8,128)(2,1)}, u32[]{:S(2)}) copy-start(bf16[384,1536]{1,0:T(8,128)(2,1)} %w_ref.9) | copy-start | bytes 3538948
  24.8 6.2 %collective-permute-start.11 = (bf16[128,384]{1,0:T(8,128)(2,1)S(1)}, bf16[128,384]{1,0:T(8,128)(2,1)S(1)}, u32[]{:S(2)}, u32[]{:S(2)}) collective-permute-start(bf16[128,384]{1,0:T(8,128)(2,1)S(1)} %get-tuple-element.96), channel_id=1, source_target_pairs={{0,2},{1,3},{2,0},{3,1},{4,6},{5,7},{6,4},{7,5},{8,10},{9,11},{10,... | collective-permute-start | bytes 294920 | tf_op jit(solution)/shard_map/ppermute | solution.py:470
  26.5 7.7 %collective-permute-start.13 = (bf16[128,768]{1,0:T(8,128)(2,1)S(1)}, bf16[128,768]{1,0:T(8,128)(2,1)S(1)}, u32[]{:S(2)}, u32[]{:S(2)}) collective-permute-start(bf16[128,768]{1,0:T(8,128)(2,1)S(1)} %project.4), channel_id=1, source_target_pairs={{0,1},{1,0},{2,3},{3,2},{4,5},{5,4},{6,7},{7,6},{8,9},{9,8},{10,11... | collective-permute-start | bytes 589832 | tf_op jit(solution)/shard_map/ppermute | solution.py:470
  28.3 2.0 %collective-permute-start.10 = (bf16[384,768]{1,0:T(8,128)(2,1)S(1)}, bf16[384,768]{1,0:T(8,128)(2,1)S(1)}, u32[]{:S(2)}, u32[]{:S(2)}) collective-permute-start(bf16[384,768]{1,0:T(8,128)(2,1)S(1)} %stack.1.part_ref), channel_id=1, source_target_pairs={{0,16},{16,0},{1,17},{17,1},{2,18},{18,2},{3,19},{19,3},{4,20},{20... | collective-permute-start | bytes 1769480 | tf_op jit(solution)/shard_map/ppermute | solution.py:470
  30.6 7.4 %collective-permute-start.12 = (bf16[128,768]{1,0:T(8,128)(2,1)S(1)}, bf16[128,768]{1,0:T(8,128)(2,1)S(1)}, u32[]{:S(2)}, u32[]{:S(2)}) collective-permute-start(bf16[128,768]{1,0:T(8,128)(2,1)S(1)} %project.5), channel_id=1, source_target_pairs={{0,1},{1,0},{2,3},{3,2},{4,5},{5,4},{6,7},{7,6},{8,9},{9,8},{10,11... | collective-permute-start | bytes 589832 | tf_op jit(solution)/shard_map/ppermute | solution.py:470

commit v15 on v11

--- a/solution.py
+++ b/solution.py
@@ -590,7 +590,7 @@
         project(here, own, got_far, f32, 0),
         project(there, own, got_far, f32, 1, 20 * 10**9),
     ]
-    pieces = 2
+    pieces = 1
     mixed = []
     for flip in range(2):
         mixed = [

time: 38.7 us -> 38.7 us (level)
  no operation moved by 1% of the time
where the time goes in v15:
time: 38.7 us; the launch traced here: 38.5 us
  starting transfers between devices  16.7 us (43%)
  waiting for transfers between devices  12.4 us (32%)
  Pallas kernels  9.32 us (24%)
    ppermute x12, starting transfers between devices, flipped(): lax.ppermute(value, axis, [(i, i ^ flip) for i in range(lax.axis_size(axi...  14 us
    ppermute x12, waiting for transfers between devices, flipped(): lax.ppermute(value, axis, [(i, i ^ flip) for i in range(lax.axis_size(axi...  12.4 us
    pallas_call x14, Pallas kernels, call(): pl.pallas_call(functools.partial(kernel, **keys_of) if keys_of else kerne...  7.88 us
    pallas_call x2, Pallas kernels, two_by_two(): pl.pallas_call(functools.partial(add_kernel, flip=flip), out_shape=shape(...  1.44 us
    ppermute x1, starting transfers between devices, two_by_two(): first_tile = lax.ppermute(tile, 'tm', [(0, 1)])  1.34 us
    ppermute x1, starting transfers between devices, two_by_two(): first_edge = lax.ppermute(edge, 'tm', [(0, 1)])  1.32 us
  transfers between devices with their start and end apart: 14, of which 8 were waited for; matrix products, arithmetic and copies ran while one was open for 0% of the time, Pallas kernels for 20%

profile of v15, /device:TPU:0, one launch (start us, length us, event | category | flops | bytes accessed | tf_op | source)
XLA Modules:
  0.0 38.5 jit_solution(17084727848725117540)
XLA Ops:
  0.0 0.0 copy-start.3
  0.0 0.0 copy-start.2
  0.0 0.0 copy-start.4
  0.0 0.0 copy-start.5
  0.0 0.0 copy-start.1
  0.0 1.0 %part.1.part_ref = bf16[96,768]{1,0:T(8,128)(2,1)S(1)} custom-call(bf16[384,1536]{1,0:T(8,128)(2,1)} %w_ref.9), custom_call_target="tpu_custom_call" | custom-call | tf_op jit(solution)/shard_map/part/pallas_call | solution.py:458
  1.0 4.1 %collective-permute-start = (bf16[96,768]{1,0:T(8,128)(2,1)S(1)}, bf16[96,768]{1,0:T(8,128)(2,1)S(1)}, u32[]{:S(2)}, u32[]{:S(2)}) collective-permute-start(bf16[96,768]{1,0:T(8,128)(2,1)S(1)} %part.1.part_ref), channel_id=1, source_target_pairs={{0,2},{1,3},{2,0},{3,1},{4,6},{5,7},{6,4},{7,5},{8,10},{9,11},{10,... | collective-permute-start | bytes 442376 | tf_op jit(solution)/shard_map/ppermute | solution.py:470
  5.2 0.0 copy-done.3
  5.2 0.0 copy-done.2
  5.2 0.4 %faces.1 = (bf16[2,2,64,384]{3,2,1,0:T(8,128)(2,1)S(1)}, bf16[2,2,64,384]{3,2,1,0:T(8,128)(2,1)S(1)}, bf16[2,2,16,384]{3,2,1,0:T(8,128)(2,1)S(1)}, bf16[2,512,384]{2,1,0:T(8,128)(2,1)S(1)}) custom-call(bf16[512,384]{1,0:T(8,128)(2,1)S(1)} %bitcast.10, bf16[512,384]{1,0:T(8,128)(2,1)S(1)} %bitcast.11, bf16[96,768]{1,0:T(8,128)(2,1)S(1)} %part.1.part_ref), custom_call_target="tpu_custom_call" | custom-call | tf_op jit(solution)/shard_map/faces/pallas_call | solution.py:458
  5.6 2.5 %collective-permute-start.3 = (bf16[2,2,16,384]{3,2,1,0:T(8,128)(2,1)S(1)}, bf16[2,2,16,384]{3,2,1,0:T(8,128)(2,1)S(1)}, u32[]{:S(2)}, u32[]{:S(2)}) collective-permute-start(bf16[2,2,16,384]{3,2,1,0:T(8,128)(2,1)S(1)} %get-tuple-element.69), channel_id=1, source_target_pairs={{0,12},{4,8},{8,4},{12,0},{1,13},{5,9},{9,5},{13,1},{2,14},{6,10},... | collective-permute-start | bytes 147464 | tf_op jit(solution)/shard_map/ppermute | solution.py:470
  8.1 0.5 %collective-permute-start.1 = (bf16[2,2,64,384]{3,2,1,0:T(8,128)(2,1)S(1)}, bf16[2,2,64,384]{3,2,1,0:T(8,128)(2,1)S(1)}, u32[]{:S(2)}, u32[]{:S(2)}) collective-permute-start(bf16[2,2,64,384]{3,2,1,0:T(8,128)(2,1)S(1)} %get-tuple-element.67), channel_id=1, source_target_pairs={{0,8},{4,12},{8,0},{12,4},{1,9},{5,13},{9,1},{13,5},{2,10},{6,14},... | collective-permute-start | bytes 589832 | tf_op jit(solution)/shard_map/ppermute | solution.py:470
  8.6 0.5 %collective-permute-start.2 = (bf16[2,2,64,384]{3,2,1,0:T(8,128)(2,1)S(1)}, bf16[2,2,64,384]{3,2,1,0:T(8,128)(2,1)S(1)}, u32[]{:S(2)}, u32[]{:S(2)}) collective-permute-start(bf16[2,2,64,384]{3,2,1,0:T(8,128)(2,1)S(1)} %get-tuple-element.68), channel_id=1, source_target_pairs={{0,4},{4,0},{8,12},{12,8},{1,5},{5,1},{9,13},{13,9},{2,6},{6,2},{1... | collective-permute-start | bytes 589832 | tf_op jit(solution)/shard_map/ppermute | solution.py:470
  9.1 0.0 copy-done.4
  9.1 0.0 copy-done.5
  9.1 0.0 copy-done.1
  9.1 1.4 %begin.1 = (f32[512,128]{1,0:T(8,128)S(1)}, f32[512,128]{1,0:T(8,128)S(1)}, f32[512,128]{1,0:T(8,128)S(1)}, s32[256,800]{1,0:T(8,128)S(1)}, s32[6,128]{1,0:T(8,128)S(1)}) custom-call(s32[3]{0:T(128)S(1)} %copy-done.5, s32[2,2,3]{2,1,0:T(2,128)S(1)} %bitcast.12, bf16[512,384]{1,0:T(8,128)(2,1)S(1)} %bitcast.5, bf16[2,512,384]{2,1,0:T(8,128)(2,1)S(1)} %get-tuple-element.57.tile_ref), custom_call_target="tpu_custom_call" | custom-call | tf_op jit(solution)/shard_map/begin/pallas_call | solution.py:458
  10.5 1.3 %collective-permute-start.4 = (bf16[2,512,384]{2,1,0:T(8,128)(2,1)S(1)}, bf16[2,512,384]{2,1,0:T(8,128)(2,1)S(1)}, u32[]{:S(2)}, u32[]{:S(2)}) collective-permute-start(bf16[2,512,384]{2,1,0:T(8,128)(2,1)S(1)} %get-tuple-element.57.tile_ref), channel_id=1, source_target_pairs={{0,16},{1,17},{2,18},{3,19},{4,20},{5,21},{6,22},{7,23},{8,24},{9,... | collective-permute-start | bytes 2359304 | tf_op jit(solution)/shard_map/ppermute | solution.py:517
  11.8 1.1 %tile.1 = (f32[512,256]{1,0:T(8,128)S(1)}, f32[512,256]{1,0:T(8,128)S(1)}, f32[512,256]{1,0:T(8,128)S(1)}) custom-call(bf16[512,384]{1,0:T(8,128)(2,1)S(1)} %bitcast.6, bf16[2,512,384]{2,1,0:T(8,128)(2,1)S(1)} %get-tuple-element.57.tile_ref, s32[256,800]{1,0:T(8,128)S(1)} %get-tuple-element.58.dist_ref.rest_3_, s32[6,128]{1,0:T(8,128)S(1)} %get-tuple-element.59.reach_ref.rest_4_), custom_call_target="tpu_custom_call" | custom-call | tf_op jit(solution)/shard_map/tile/pallas_call | solution.py:458
  12.9 0.0 collective-permute-done.in_ref
  13.0 0.0 collective-permute-done.3.corner_ref
  13.0 1.7 %collective-permute-done.1.row_ref = bf16[2,2,64,384]{3,2,1,0:T(8,128)(2,1)S(1)} collective-permute-done((bf16[2,2,64,384]{3,2,1,0:T(8,128)(2,1)S(1)}, bf16[2,2,64,384]{3,2,1,0:T(8,128)(2,1)S(1)}, u32[]{:S(2)}, u32[]{:S(2)}) %collective-permute-start.1) | collective-permute-done | bytes 196640 | tf_op jit(solution)/shard_map/ppermute | solution.py:470
  14.7 0.2 collective-permute-done.2.col_ref
  14.9 1.3 %collective-permute-start.5 = (bf16[2,288,384]{2,1,0:T(8,128)(2,1)S(1)}, bf16[2,288,384]{2,1,0:T(8,128)(2,1)S(1)}, u32[]{:S(2)}, u32[]{:S(2)}) collective-permute-start(bf16[2,288,384]{2,1,0:T(8,128)(2,1)S(1)} %edges.1.edge_ref), channel_id=1, source_target_pairs={{0,16},{1,17},{2,18},{3,19},{4,20},{5,21},{6,22},{7,23},{8,24},{9,... | collective-permute-start | bytes 1327112 | tf_op jit(solution)/shard_map/ppermute | solution.py:535
  16.3 1.5 %collective-permute-start.8 = (bf16[96,768]{1,0:T(8,128)(2,1)S(1)}, bf16[96,768]{1,0:T(8,128)(2,1)S(1)}, u32[]{:S(2)}, u32[]{:S(2)}) collective-permute-start(bf16[96,768]{1,0:T(8,128)(2,1)S(1)} %lone.1.refs_0_), channel_id=1, source_target_pairs={{0,12},{4,8},{8,4},{12,0},{1,13},{5,9},{9,5},{13,1},{2,14},{6,10},... | collective-permute-start | bytes 442376 | tf_op jit(solution)/shard_map/ppermute | solution.py:470
  17.8 0.6 %collective-permute-start.7 = (bf16[96,768]{1,0:T(8,128)(2,1)S(1)}, bf16[96,768]{1,0:T(8,128)(2,1)S(1)}, u32[]{:S(2)}, u32[]{:S(2)}) collective-permute-start(bf16[96,768]{1,0:T(8,128)(2,1)S(1)} %lone.1.refs_0_), channel_id=1, source_target_pairs={{0,8},{4,12},{8,0},{12,4},{1,9},{5,13},{9,1},{13,5},{2,10},{6,14},... | collective-permute-start | bytes 442376 | tf_op jit(solution)/shard_map/ppermute | solution.py:470
  18.4 1.4 %collective-permute-start.6 = (bf16[96,768]{1,0:T(8,128)(2,1)S(1)}, bf16[96,768]{1,0:T(8,128)(2,1)S(1)}, u32[]{:S(2)}, u32[]{:S(2)}) collective-permute-start(bf16[96,768]{1,0:T(8,128)(2,1)S(1)} %lone.1.refs_0_), channel_id=1, source_target_pairs={{0,4},{4,0},{8,12},{12,8},{1,5},{5,1},{9,13},{13,9},{2,6},{6,2},{1... | collective-permute-start | bytes 442376 | tf_op jit(solution)/shard_map/ppermute | solution.py:470
  19.8 0.0 collective-permute-done.5.first_edge_ref
  19.8 0.0 collective-permute-done.4.first_tile_ref
  19.8 0.7 %rest.3 = bf16[128,384]{1,0:T(8,128)(2,1)S(1)} custom-call(bf16[512,384]{1,0:T(8,128)(2,1)S(1)} %bitcast.7, bf16[2,288,384]{2,1,0:T(8,128)(2,1)S(1)} %edges.1.edge_ref, bf16[2,512,384]{2,1,0:T(8,128)(2,1)S(1)} %collective-permute-done.4.first_tile_ref, bf16[2,288,384]{2,1,0:T(8,128)(2,1)S(1)} %collective-permute-done.5.first_edge_ref, ...), custom_call_target="tpu_custom_call" | custom-call | tf_op jit(solution)/shard_map/rest/pallas_call | solution.py:458
  20.5 0.4 %collective-permute-start.9 = (bf16[128,384]{1,0:T(8,128)(2,1)S(1)}, bf16[128,384]{1,0:T(8,128)(2,1)S(1)}, u32[]{:S(2)}, u32[]{:S(2)}) collective-permute-start(bf16[128,384]{1,0:T(8,128)(2,1)S(1)} %rest.3), channel_id=1, source_target_pairs={{0,2},{1,3},{2,0},{3,1},{4,6},{5,7},{6,4},{7,5},{8,10},{9,11},{10,... | collective-permute-start | bytes 294920 | tf_op jit(solution)/shard_map/ppermute | solution.py:470
  20.9 1.2 %rest.4 = (bf16[128,384]{1,0:T(8,128)(2,1)S(1)}, bf16[128,384]{1,0:T(8,128)(2,1)S(1)}) custom-call(bf16[512,384]{1,0:T(8,128)(2,1)S(1)} %bitcast.8, bf16[2,288,384]{2,1,0:T(8,128)(2,1)S(1)} %edges.1.edge_ref, bf16[2,512,384]{2,1,0:T(8,128)(2,1)S(1)} %collective-permute-done.4.first_tile_ref, bf16[2,288,384]{2,1,0:T(8,128)(2,1)S(1)} %collective-permute-done.5.first_edge_ref, ...), custom_call_target="tpu_custom_call" | custom-call | tf_op jit(solution)/shard_map/rest/pallas_call | solution.py:458
  22.0 0.0 copy-start
  22.1 1.3 %collective-permute-done.8.refs_3_ = bf16[96,768]{1,0:T(8,128)(2,1)S(1)} collective-permute-done((bf16[96,768]{1,0:T(8,128)(2,1)S(1)}, bf16[96,768]{1,0:T(8,128)(2,1)S(1)}, u32[]{:S(2)}, u32[]{:S(2)}) %collective-permute-start.8) | collective-permute-done | bytes 147488 | tf_op jit(solution)/shard_map/ppermute | solution.py:470
  23.3 1.5 %collective-permute-done.7.refs_2_ = bf16[96,768]{1,0:T(8,128)(2,1)S(1)} collective-permute-done((bf16[96,768]{1,0:T(8,128)(2,1)S(1)}, bf16[96,768]{1,0:T(8,128)(2,1)S(1)}, u32[]{:S(2)}, u32[]{:S(2)}) %collective-permute-start.7) | collective-permute-done | bytes 147488 | tf_op jit(solution)/shard_map/ppermute | solution.py:470
  24.8 0.0 collective-permute-done.6.refs_1_
  24.8 0.2 collective-permute-start.11
  25.0 0.1 stack.1.part_ref
  25.1 1.0 %collective-permute-done.9.got_ref = bf16[128,384]{1,0:T(8,128)(2,1)S(1)} collective-permute-done((bf16[128,384]{1,0:T(8,128)(2,1)S(1)}, bf16[128,384]{1,0:T(8,128)(2,1)S(1)}, u32[]{:S(2)}, u32[]{:S(2)}) %collective-permute-start.9) | collective-permute-done | bytes 98336 | tf_op jit(solution)/shard_map/ppermute | solution.py:470
  26.1 0.0 copy-done
  26.1 0.4 project.4
  26.4 1.7 %collective-permute-start.13 = (bf16[128,768]{1,0:T(8,128)(2,1)S(1)}, bf16[128,768]{1,0:T(8,128)(2,1)S(1)}, u32[]{:S(2)}, u32[]{:S(2)}) collective-permute-start(bf16[128,768]{1,0:T(8,128)(2,1)S(1)} %project.4), channel_id=1, source_target_pairs={{0,1},{1,0},{2,3},{3,2},{4,5},{5,4},{6,7},{7,6},{8,9},{9,8},{10,11... | collective-permute-start | bytes 589832 | tf_op jit(solution)/shard_map/ppermute | solution.py:470
  28.1 0.0 collective-permute-start.10
  28.1 0.7 %rest.5.own_ref = bf16[128,384]{1,0:T(8,128)(2,1)S(1)} custom-call(bf16[512,384]{1,0:T(8,128)(2,1)S(1)} %bitcast.9, bf16[2,288,384]{2,1,0:T(8,128)(2,1)S(1)} %edges.1.edge_ref, bf16[2,512,384]{2,1,0:T(8,128)(2,1)S(1)} %collective-permute-done.4.first_tile_ref, bf16[2,288,384]{2,1,0:T(8,128)(2,1)S(1)} %collective-permute-done.5.first_edge_ref, ...), custom_call_target="tpu_custom_call" | custom-call | flops 20000000000 | tf_op jit(solution)/shard_map/rest/pallas_call | solution.py:458
  28.8 1.3 %collective-permute-done.10.part_ref = bf16[384,768]{1,0:T(8,128)(2,1)S(1)} collective-permute-done((bf16[384,768]{1,0:T(8,128)(2,1)S(1)}, bf16[384,768]{1,0:T(8,128)(2,1)S(1)}, u32[]{:S(2)}, u32[]{:S(2)}) %collective-permute-start.10) | collective-permute-done | bytes 589856 | tf_op jit(solution)/shard_map/ppermute | solution.py:470
  30.1 0.4 project.5
  30.5 0.5 %collective-permute-start.12 = (bf16[128,768]{1,0:T(8,128)(2,1)S(1)}, bf16[128,768]{1,0:T(8,128)(2,1)S(1)}, u32[]{:S(2)}, u32[]{:S(2)}) collective-permute-start(bf16[128,768]{1,0:T(8,128)(2,1)S(1)} %project.5), channel_id=1, source_target_pairs={{0,1},{1,0},{2,3},{3,2},{4,5},{5,4},{6,7},{7,6},{8,9},{9,8},{10,11... | collective-permute-start | bytes 589832 | tf_op jit(solution)/shard_map/ppermute | solution.py:470
  31.0 0.0 collective-permute-done.11.got_ref
  31.0 0.4 project.6.mine_ref
  31.3 0.4 project.7.mine_ref
  31.7 2.1 %collective-permute-done.13.got_ref = bf16[128,768]{1,0:T(8,128)(2,1)S(1)} collective-permute-done((bf16[128,768]{1,0:T(8,128)(2,1)S(1)}, bf16[128,768]{1,0:T(8,128)(2,1)S(1)}, u32[]{:S(2)}, u32[]{:S(2)}) %collective-permute-start.13) | collective-permute-done | bytes 196640 | tf_op jit(solution)/shard_map/ppermute | solution.py:470
  33.8 0.7 %add.2.rest_0_ = bf16[128,1536]{1,0:T(8,128)(2,1)} custom-call(f32[128,768]{1,0:T(8,128)S(1)} %project.7.mine_ref, bf16[128,768]{1,0:T(8,128)(2,1)S(1)} %collective-permute-done.13.got_ref), custom_call_target="tpu_custom_call" | custom-call | tf_op jit(solution)/shard_map/add/pallas_call | solution.py:597
  34.6 3.2 %collective-permute-done.12.got_ref = bf16[128,768]{1,0:T(8,128)(2,1)S(1)} collective-permute-done((bf16[128,768]{1,0:T(8,128)(2,1)S(1)}, bf16[128,768]{1,0:T(8,128)(2,1)S(1)}, u32[]{:S(2)}, u32[]{:S(2)}) %collective-permute-start.12) | collective-permute-done | bytes 196640 | tf_op jit(solution)/shard_map/ppermute | solution.py:470
  37.8 0.7 %add.3 = bf16[128,1536]{1,0:T(8,128)(2,1)} custom-call(f32[128,768]{1,0:T(8,128)S(1)} %project.6.mine_ref, bf16[128,768]{1,0:T(8,128)(2,1)S(1)} %collective-permute-done.12.got_ref, bf16[128,1536]{1,0:T(8,128)(2,1)} %add.2.rest_0_), custom_call_target="tpu_custom_call", output_to_operand_aliasing={{}: (2, {})} | custom-call | tf_op jit(solution)/shard_map/add/pallas_call | solution.py:597
  (2 shorter events, 0.1 us)
Async XLA Ops:
  0.0 5.2 %copy-start.3 = (bf16[1,1,2,16,16,384]{5,4,3,2,1,0:T(8,128)(2,1)S(1)}, bf16[1,1,2,16,16,384]{5,4,3,2,1,0:T(8,128)(2,1)}, u32[]{:S(2)}) copy-start(bf16[1,1,2,16,16,384]{5,4,3,2,1,0:T(8,128)(2,1)} %param.8) | copy-start | bytes 1179652
  0.0 5.2 %copy-start.2 = (bf16[1,1,2,16,16,384]{5,4,3,2,1,0:T(8,128)(2,1)S(1)}, bf16[1,1,2,16,16,384]{5,4,3,2,1,0:T(8,128)(2,1)}, u32[]{:S(2)}) copy-start(bf16[1,1,2,16,16,384]{5,4,3,2,1,0:T(8,128)(2,1)} %param.7) | copy-start | bytes 1179652
  0.0 9.1 %copy-start.4 = (s32[3,2,2]{0,2,1:T(2,128)S(1)}, s32[3,2,2]{0,2,1:T(2,128)}, u32[]{:S(2)}) copy-start(s32[3,2,2]{0,2,1:T(2,128)} %param.11) | copy-start | bytes 148
  0.0 9.1 %copy-start.5 = (s32[3]{0:T(128)S(1)}, s32[3]{0:T(128)}, u32[]{:S(2)}) copy-start(s32[3]{0:T(128)} %radius_ref.1) | copy-start | bytes 40
  0.0 9.1 %copy-start.1 = (bf16[1,1,2,16,16,384]{5,4,3,2,1,0:T(8,128)(2,1)S(1)}, bf16[1,1,2,16,16,384]{5,4,3,2,1,0:T(8,128)(2,1)}, u32[]{:S(2)}) copy-start(bf16[1,1,2,16,16,384]{5,4,3,2,1,0:T(8,128)(2,1)} %param.6) | copy-start | bytes 1179652
  1.0 11.9 %collective-permute-start = (bf16[96,768]{1,0:T(8,128)(2,1)S(1)}, bf16[96,768]{1,0:T(8,128)(2,1)S(1)}, u32[]{:S(2)}, u32[]{:S(2)}) collective-permute-start(bf16[96,768]{1,0:T(8,128)(2,1)S(1)} %part.1.part_ref), channel_id=1, source_target_pairs={{0,2},{1,3},{2,0},{3,1},{4,6},{5,7},{6,4},{7,5},{8,10},{9,11},{10,... | collective-permute-start | bytes 442376 | tf_op jit(solution)/shard_map/ppermute | solution.py:470
  5.6 7.4 %collective-permute-start.3 = (bf16[2,2,16,384]{3,2,1,0:T(8,128)(2,1)S(1)}, bf16[2,2,16,384]{3,2,1,0:T(8,128)(2,1)S(1)}, u32[]{:S(2)}, u32[]{:S(2)}) collective-permute-start(bf16[2,2,16,384]{3,2,1,0:T(8,128)(2,1)S(1)} %get-tuple-element.69), channel_id=1, source_target_pairs={{0,12},{4,8},{8,4},{12,0},{1,13},{5,9},{9,5},{13,1},{2,14},{6,10},... | collective-permute-start | bytes 147464 | tf_op jit(solution)/shard_map/ppermute | solution.py:470
  8.1 6.6 %collective-permute-start.1 = (bf16[2,2,64,384]{3,2,1,0:T(8,128)(2,1)S(1)}, bf16[2,2,64,384]{3,2,1,0:T(8,128)(2,1)S(1)}, u32[]{:S(2)}, u32[]{:S(2)}) collective-permute-start(bf16[2,2,64,384]{3,2,1,0:T(8,128)(2,1)S(1)} %get-tuple-element.67), channel_id=1, source_target_pairs={{0,8},{4,12},{8,0},{12,4},{1,9},{5,13},{9,1},{13,5},{2,10},{6,14},... | collective-permute-start | bytes 589832 | tf_op jit(solution)/shard_map/ppermute | solution.py:470
  8.6 6.3 %collective-permute-start.2 = (bf16[2,2,64,384]{3,2,1,0:T(8,128)(2,1)S(1)}, bf16[2,2,64,384]{3,2,1,0:T(8,128)(2,1)S(1)}, u32[]{:S(2)}, u32[]{:S(2)}) collective-permute-start(bf16[2,2,64,384]{3,2,1,0:T(8,128)(2,1)S(1)} %get-tuple-element.68), channel_id=1, source_target_pairs={{0,4},{4,0},{8,12},{12,8},{1,5},{5,1},{9,13},{13,9},{2,6},{6,2},{1... | collective-permute-start | bytes 589832 | tf_op jit(solution)/shard_map/ppermute | solution.py:470
  10.5 9.3 %collective-permute-start.4 = (bf16[2,512,384]{2,1,0:T(8,128)(2,1)S(1)}, bf16[2,512,384]{2,1,0:T(8,128)(2,1)S(1)}, u32[]{:S(2)}, u32[]{:S(2)}) collective-permute-start(bf16[2,512,384]{2,1,0:T(8,128)(2,1)S(1)} %get-tuple-element.57.tile_ref), channel_id=1, source_target_pairs={{0,16},{1,17},{2,18},{3,19},{4,20},{5,21},{6,22},{7,23},{8,24},{9,... | collective-permute-start | bytes 2359304 | tf_op jit(solution)/shard_map/ppermute | solution.py:517
  14.9 4.9 %collective-permute-start.5 = (bf16[2,288,384]{2,1,0:T(8,128)(2,1)S(1)}, bf16[2,288,384]{2,1,0:T(8,128)(2,1)S(1)}, u32[]{:S(2)}, u32[]{:S(2)}) collective-permute-start(bf16[2,288,384]{2,1,0:T(8,128)(2,1)S(1)} %edges.1.edge_ref), channel_id=1, source_target_pairs={{0,16},{1,17},{2,18},{3,19},{4,20},{5,21},{6,22},{7,23},{8,24},{9,... | collective-permute-start | bytes 1327112 | tf_op jit(solution)/shard_map/ppermute | solution.py:535
  16.3 7.1 %collective-permute-start.8 = (bf16[96,768]{1,0:T(8,128)(2,1)S(1)}, bf16[96,768]{1,0:T(8,128)(2,1)S(1)}, u32[]{:S(2)}, u32[]{:S(2)}) collective-permute-start(bf16[96,768]{1,0:T(8,128)(2,1)S(1)} %lone.1.refs_0_), channel_id=1, source_target_pairs={{0,12},{4,8},{8,4},{12,0},{1,13},{5,9},{9,5},{13,1},{2,14},{6,10},... | collective-permute-start | bytes 442376 | tf_op jit(solution)/shard_map/ppermute | solution.py:470
  17.8 7.0 %collective-permute-start.7 = (bf16[96,768]{1,0:T(8,128)(2,1)S(1)}, bf16[96,768]{1,0:T(8,128)(2,1)S(1)}, u32[]{:S(2)}, u32[]{:S(2)}) collective-permute-start(bf16[96,768]{1,0:T(8,128)(2,1)S(1)} %lone.1.refs_0_), channel_id=1, source_target_pairs={{0,8},{4,12},{8,0},{12,4},{1,9},{5,13},{9,1},{13,5},{2,10},{6,14},... | collective-permute-start | bytes 442376 | tf_op jit(solution)/shard_map/ppermute | solution.py:470
  18.4 6.4 %collective-permute-start.6 = (bf16[96,768]{1,0:T(8,128)(2,1)S(1)}, bf16[96,768]{1,0:T(8,128)(2,1)S(1)}, u32[]{:S(2)}, u32[]{:S(2)}) collective-permute-start(bf16[96,768]{1,0:T(8,128)(2,1)S(1)} %lone.1.refs_0_), channel_id=1, source_target_pairs={{0,4},{4,0},{8,12},{12,8},{1,5},{5,1},{9,13},{13,9},{2,6},{6,2},{1... | collective-permute-start | bytes 442376 | tf_op jit(solution)/shard_map/ppermute | solution.py:470
  20.5 5.6 %collective-permute-start.9 = (bf16[128,384]{1,0:T(8,128)(2,1)S(1)}, bf16[128,384]{1,0:T(8,128)(2,1)S(1)}, u32[]{:S(2)}, u32[]{:S(2)}) collective-permute-start(bf16[128,384]{1,0:T(8,128)(2,1)S(1)} %rest.3), channel_id=1, source_target_pairs={{0,2},{1,3},{2,0},{3,1},{4,6},{5,7},{6,4},{7,5},{8,10},{9,11},{10,... | collective-permute-start | bytes 294920 | tf_op jit(solution)/shard_map/ppermute | solution.py:470
  22.0 4.0 %copy-start = (bf16[384,1536]{1,0:T(8,128)(2,1)S(1)}, bf16[384,1536]{1,0:T(8,128)(2,1)}, u32[]{:S(2)}) copy-start(bf16[384,1536]{1,0:T(8,128)(2,1)} %w_ref.9) | copy-start | bytes 3538948
  24.8 6.2 %collective-permute-start.11 = (bf16[128,384]{1,0:T(8,128)(2,1)S(1)}, bf16[128,384]{1,0:T(8,128)(2,1)S(1)}, u32[]{:S(2)}, u32[]{:S(2)}) collective-permute-start(bf16[128,384]{1,0:T(8,128)(2,1)S(1)} %get-tuple-element.96), channel_id=1, source_target_pairs={{0,2},{1,3},{2,0},{3,1},{4,6},{5,7},{6,4},{7,5},{8,10},{9,11},{10,... | collective-permute-start | bytes 294920 | tf_op jit(solution)/shard_map/ppermute | solution.py:470
  26.4 7.4 %collective-permute-start.13 = (bf16[128,768]{1,0:T(8,128)(2,1)S(1)}, bf16[128,768]{1,0:T(8,128)(2,1)S(1)}, u32[]{:S(2)}, u32[]{:S(2)}) collective-permute-start(bf16[128,768]{1,0:T(8,128)(2,1)S(1)} %project.4), channel_id=1, source_target_pairs={{0,1},{1,0},{2,3},{3,2},{4,5},{5,4},{6,7},{7,6},{8,9},{9,8},{10,11... | collective-permute-start | bytes 589832 | tf_op jit(solution)/shard_map/ppermute | solution.py:470
  28.1 2.0 %collective-permute-start.10 = (bf16[384,768]{1,0:T(8,128)(2,1)S(1)}, bf16[384,768]{1,0:T(8,128)(2,1)S(1)}, u32[]{:S(2)}, u32[]{:S(2)}) collective-permute-start(bf16[384,768]{1,0:T(8,128)(2,1)S(1)} %stack.1.part_ref), channel_id=1, source_target_pairs={{0,16},{16,0},{1,17},{17,1},{2,18},{18,2},{3,19},{19,3},{4,20},{20... | collective-permute-start | bytes 1769480 | tf_op jit(solution)/shard_map/ppermute | solution.py:470
  30.5 7.3 %collective-permute-start.12 = (bf16[128,768]{1,0:T(8,128)(2,1)S(1)}, bf16[128,768]{1,0:T(8,128)(2,1)S(1)}, u32[]{:S(2)}, u32[]{:S(2)}) collective-permute-start(bf16[128,768]{1,0:T(8,128)(2,1)S(1)} %project.5), channel_id=1, source_target_pairs={{0,1},{1,0},{2,3},{3,2},{4,5},{5,4},{6,7},{7,6},{8,9},{9,8},{10,11... | collective-permute-start | bytes 589832 | tf_op jit(solution)/shard_map/ppermute | solution.py:470
